TPU v7x, 32 devices: a whole 2x2x4 slice. The times are simulated.
32 devices in a mesh: ctx: 8 (over y, x, core), fsdp: 4 (over z).
Axes of the slice: x: 2, y: 2, z: 4, core: 2. Of those that a mesh axis runs over, the one named last changes fastest.
Arguments:
- inputs: bfloat16 [4, 1024, 1600], P('fsdp', 'ctx'), may hold values from -6 to 6
- cotangent: bfloat16 [4, 1024, 1600], P('fsdp', 'ctx'), may hold values from -6 to 6
- norm_gain: float32 [1600], replicated, may hold values from 0.1 to 1.9
- query_proj: bfloat16 [1600, 1600], P('fsdp'), may hold values from -0.15625 to 0.15625
- key_proj: bfloat16 [1600, 320], P('fsdp'), may hold values from -0.15625 to 0.15625
- value_proj: bfloat16 [1600, 320], P('fsdp'), may hold values from -0.15625 to 0.15625
- attn_proj: bfloat16 [1600, 1600], P('fsdp'), may hold values from -0.15625 to 0.15625
- attn_gain: float32 [1600], replicated, may hold values from 0.1 to 1.9
- mixer_in: bfloat16 [1600, 6400], P('fsdp'), may hold values from -0.15625 to 0.15625
- conv_taps: float32 [4, 3200], replicated, may hold values from -3 to 3
- conv_bias: float32 [3200], replicated, may hold values from -3 to 3
- state_proj: bfloat16 [3200, 132], P('fsdp'), may hold values from -0.109375 to 0.109375
- step_proj: bfloat16 [100, 3200], P('fsdp'), may hold values from -0.625 to 0.625
- step_bias: float32 [3200], replicated, may hold values from -4 to 0
- decay_rate: float32 [3200, 16], replicated, may hold values from 9.765625e-05 to 0.5, as said below
- skip_gain: float32 [3200], replicated, may hold values from -6 to 6
- mixer_out: bfloat16 [3200, 1600], P('fsdp'), may hold values from -0.109375 to 0.109375
- ssm_gain: float32 [3200], replicated, may hold values from 0.1 to 1.9
- ffn_gain: float32 [1600], replicated, may hold values from 0.1 to 1.9
- gate_proj: bfloat16 [1600, 5504], P('fsdp'), may hold values from -0.15625 to 0.15625
- up_proj: bfloat16 [1600, 5504], P('fsdp'), may hold values from -0.15625 to 0.15625
- down_proj: bfloat16 [5504, 1600], P('fsdp'), may hold values from -0.078125 to 0.078125
Outputs:
- output: float32 [4, 1024, 1600], P('fsdp', 'ctx')
- input_grad: float32 [4, 1024, 1600], P('fsdp', 'ctx')
- norm_gain_grad: float32 [1600], replicated
- query_proj_grad: float32 [1600, 1600], P('fsdp', 'ctx')
- key_proj_grad: float32 [1600, 320], P('fsdp', 'ctx')
- value_proj_grad: float32 [1600, 320], P('fsdp', 'ctx')
- attn_proj_grad: float32 [1600, 1600], P('fsdp', 'ctx')
- attn_gain_grad: float32 [1600], replicated
- mixer_in_grad: float32 [1600, 6400], P('fsdp', 'ctx')
- conv_taps_grad: float32 [4, 3200], replicated
- conv_bias_grad: float32 [3200], replicated
- state_proj_grad: float32 [3200, 132], replicated
- step_proj_grad: float32 [100, 3200], P('fsdp', 'ctx')
- step_bias_grad: float32 [3200], replicated
- decay_rate_grad: float32 [3200, 16], replicated
- skip_gain_grad: float32 [3200], replicated
- mixer_out_grad: float32 [3200, 1600], P('fsdp', 'ctx')
- ssm_gain_grad: float32 [3200], replicated
- ffn_gain_grad: float32 [1600], replicated
- gate_proj_grad: float32 [1600, 5504], P('fsdp', 'ctx')
- up_proj_grad: float32 [1600, 5504], P('fsdp', 'ctx')
- down_proj_grad: float32 [5504, 1600], P('fsdp', 'ctx')
Inputs may be any that keep to these rules, and one draw needn't show every extreme that they name: `decay_rate`: decay rates, all positive.
All inputs are finite; a program needn't handle non-finite values.
Results may differ from a plain program's by a relative error of at most 0.028.
Values may be sent and summed in bfloat16 or wider, within the bound.
A program may use at most 384 MiB of HBM per device.

v0:
```python
import math

import jax
import jax.numpy as jnp
from jax import lax
from jax.sharding import PartitionSpec as P

D = 1600
HEADS = 25
KV_HEADS = 5
HEAD = 64
INNER = 3200
STATE = 16
CONV = 4
DT_RANK = 100
WINDOW = 1024
TOK_DEV = 128


epsilon = 1e-06


def passed_along(value, axis, steps):
    count = lax.axis_size(axis)
    first, last = (max(0, -steps), min(count, count - steps))
    return lax.ppermute(value, axis, [(source, source + steps) for source in range(first, last)])


def entering(part, axis, combine, identity):
    place = lax.axis_index(axis)
    gathered = jax.tree.map(lambda a: lax.all_gather(a, axis), part)
    state = jax.tree.map(lambda a, e: jnp.zeros_like(a) + jnp.asarray(e, a.dtype), part, identity)

    def entering_one(turn, state):
        return combine(
            state, jax.tree.map(lambda a: lax.dynamic_index_in_dim(a, turn, 0, False), gathered)
        )

    return lax.fori_loop(0, place, entering_one, state)


def prefix(array, axis, join, neutral):
    count = lax.axis_size(axis)
    place = lax.axis_index(axis)
    ahead = count - 1 - place
    gathered = jax.tree.map(
        lambda a, kind: lax.all_gather(a.astype(kind), axis),
        array,
        jax.tree.map(lambda a: jnp.bfloat16 if a.dtype == jnp.float32 else a.dtype, array),
    )
    state = jax.tree.map(lambda a, e: jnp.zeros_like(a) + jnp.asarray(e, a.dtype), array, neutral)

    def prefix_one(turn, state):
        source = count - 1 - turn
        return join(
            state,
            jax.tree.map(
                lambda a, own: lax.dynamic_index_in_dim(a, source, 0, False).astype(own.dtype),
                gathered,
                array,
            ),
        )

    return lax.fori_loop(0, ahead, prefix_one, state)


def matmul(left, right):
    return jnp.dot(left, right, preferred_element_type=jnp.float32)


def left_trans(left, right):
    return lax.dot_general(
        left, right, (((0,), (0,)), ((), ())), preferred_element_type=jnp.float32
    )


def right_trans(left, right):
    return lax.dot_general(
        left, right, (((1,), (1,)), ((), ())), preferred_element_type=jnp.float32
    )


def rms_scale(values):
    return lax.rsqrt(jnp.mean(values * values, axis=-1, keepdims=True) + epsilon)


def norm_back(grad_out, values, scale_in, gain_in):
    scaled = grad_out * gain_in
    grad_in = scale_in * scaled - values * scale_in**3 * jnp.mean(
        scaled * values, axis=-1, keepdims=True
    )
    return (grad_in, jnp.sum(grad_out * values * scale_in, axis=0))


def silu_slope(values):
    logistic = jax.nn.sigmoid(values)
    return logistic * (1.0 + values * (1.0 - logistic))


def affine_join(earlier, latter):
    return (latter[0] * earlier[0], latter[0] * earlier[1] + latter[1])


def decay_drive(step_block, input_block, drive_block, decay_rate):
    decays = jnp.exp(-step_block[:, :, None] * decay_rate[None])
    drives = (step_block * drive_block)[:, :, None] * input_block[:, None, :]
    return (decays, drives)


def settle(gradient):
    col_part = lax.psum_scatter(
        gradient.astype(jnp.bfloat16), "ctx", scatter_dimension=1, tiled=True
    )
    return lax.psum_scatter(col_part, "fsdp", scatter_dimension=0, tiled=True).astype(jnp.float32)


def body(
    inputs,
    cotangent,
    norm_gain,
    query_proj,
    key_proj,
    value_proj,
    attn_proj,
    attn_gain,
    mixer_in,
    conv_taps,
    conv_bias,
    state_proj,
    step_proj,
    step_bias,
    decay_rate,
    skip_gain,
    mixer_out,
    ssm_gain,
    ffn_gain,
    gate_proj,
    up_proj,
    down_proj,
):
    tokens = inputs[0].astype(jnp.float32)
    grad_top = cotangent[0]
    kv_width = KV_HEADS * HEAD
    group_size = HEADS // KV_HEADS
    score_scale = HEAD ** (-0.5)
    hop_count = WINDOW // TOK_DEV
    sharded = (
        query_proj,
        key_proj,
        value_proj,
        attn_proj,
        mixer_in,
        state_proj,
        step_proj,
        mixer_out,
        gate_proj,
        up_proj,
        down_proj,
    )
    (
        query_full,
        key_full,
        value_full,
        attn_full,
        mixin_full,
        state_full,
        step_full,
        mixout_full,
        gate_full,
        up_full,
        down_full,
    ) = (
        lax.all_gather(sharded[0], "fsdp", axis=0, tiled=True),
        lax.all_gather(sharded[1], "fsdp", axis=0, tiled=True),
        lax.all_gather(sharded[2], "fsdp", axis=0, tiled=True),
        lax.all_gather(sharded[3], "fsdp", axis=0, tiled=True),
        lax.all_gather(sharded[4], "fsdp", axis=0, tiled=True),
        lax.all_gather(sharded[5], "fsdp", axis=0, tiled=True),
        lax.all_gather(sharded[6], "fsdp", axis=0, tiled=True),
        lax.all_gather(sharded[7], "fsdp", axis=0, tiled=True),
        lax.all_gather(sharded[8], "fsdp", axis=0, tiled=True),
        lax.all_gather(sharded[9], "fsdp", axis=0, tiled=True),
        lax.all_gather(sharded[10], "fsdp", axis=0, tiled=True),
    )
    norm_scale = rms_scale(tokens)
    normed = (tokens * norm_scale * norm_gain).astype(jnp.bfloat16)
    queries = matmul(normed, query_full).astype(jnp.bfloat16)
    keyvals = jnp.concatenate([matmul(normed, key_full), matmul(normed, value_full)], 1).astype(
        jnp.bfloat16
    )
    mixed_in = matmul(normed, mixin_full).astype(jnp.bfloat16)
    conv_src = mixed_in[:, :INNER]
    gate_z = mixed_in[:, INNER:].astype(jnp.float32)
    recv_near, edge_in = passed_along((keyvals, conv_src[TOK_DEV - (CONV - 1) :]), "ctx", 1)
    far_pieces = []
    for distance in range(2, hop_count + 1):
        far_pieces.append(passed_along(keyvals, "ctx", distance))
    kv_all = jnp.concatenate(far_pieces[::-1] + [recv_near, keyvals], 0)
    keys_all = kv_all[:, :kv_width].reshape(-1, KV_HEADS, HEAD)
    vals_all = kv_all[:, kv_width:].reshape(-1, KV_HEADS, HEAD)
    heads_q = queries.reshape(TOK_DEV, KV_HEADS, group_size, HEAD)
    row_block = min(TOK_DEV, 512)
    key_span = WINDOW + row_block
    offset = lax.axis_index("ctx") * TOK_DEV

    def block_scores(row_start):
        row_ids = lax.broadcasted_iota(jnp.int32, (row_block, key_span), 0)
        col_ids = lax.broadcasted_iota(jnp.int32, (row_block, key_span), 1)
        allowed = (
            (col_ids > row_ids)
            & (col_ids <= row_ids + WINDOW)
            & (col_ids + offset + row_start >= WINDOW)
        )
        raw = (
            jnp.einsum("qhgd,khd->hgqk", heads_q, keys_all, preferred_element_type=jnp.float32)
            * score_scale
        )
        return jnp.where(allowed, raw, -1e30)

    row_start = 0
    scores = block_scores(row_start)
    row_top = jnp.max(scores, axis=-1, keepdims=True)
    log_total = row_top + jnp.log(jnp.sum(jnp.exp(scores - row_top), axis=-1, keepdims=True))
    probs_bf = jnp.exp(scores - log_total).astype(jnp.bfloat16)
    attn_rows = jnp.einsum(
        "hgqk,khd->qhgd", probs_bf, vals_all, preferred_element_type=jnp.float32
    ).reshape(row_block, D)
    log_totals = [log_total]
    attn_scale = rms_scale(attn_rows)
    branch_attn = (attn_rows * attn_scale * attn_gain).astype(jnp.bfloat16)
    padded_src = jnp.concatenate([edge_in, conv_src], 0).astype(jnp.float32)
    conv_pre = conv_bias + sum(
        (
            conv_taps[tap_index] * padded_src[tap_index : tap_index + TOK_DEV]
            for tap_index in range(CONV)
        )
    )
    conv_act = jax.nn.silu(conv_pre).astype(jnp.bfloat16)
    conv_vals = conv_act.astype(jnp.float32)
    projected = matmul(conv_act, state_full)
    step_low = projected[:, :DT_RANK].astype(jnp.bfloat16)
    input_mat = projected[:, DT_RANK : DT_RANK + STATE]
    output_mat = projected[:, DT_RANK + STATE :]
    step_pre = matmul(step_low, step_full) + step_bias
    steps_dt = jax.nn.softplus(step_pre)
    scan_block = math.gcd(TOK_DEV, 16)
    block_count = TOK_DEV // scan_block

    def blocked(values):
        return values.reshape((block_count, scan_block) + values.shape[1:])

    zero_state = jnp.zeros((INNER, STATE), jnp.float32)
    ones_state = jnp.ones((INNER, STATE), jnp.float32)
    cum_steps = jnp.cumsum(steps_dt, axis=0)
    tail_weights = jnp.exp(-(cum_steps[-1][None] - cum_steps)[:, :, None] * decay_rate[None])
    zero_end = jnp.einsum("tis,ti,ts->is", tail_weights, steps_dt * conv_vals, input_mat)
    total_decay = jnp.exp(-cum_steps[-1][:, None] * decay_rate)
    carry_pair = entering((total_decay, zero_end), "ctx", affine_join, (ones_state, zero_state))

    def out_step(carried, pieces):
        step_b, input_b, output_b, drive_b = pieces
        decays, drives = decay_drive(step_b, input_b, drive_b, decay_rate)
        cum_decay, cum_drive = lax.associative_scan(affine_join, (decays, drives), axis=0)
        states = cum_decay * carried[None] + cum_drive
        return (states[-1], (carried, jnp.einsum("tis,ts->ti", states, output_b)))

    unused, (block_starts, scan_out) = lax.scan(
        out_step,
        carry_pair[1],
        (blocked(steps_dt), blocked(input_mat), blocked(output_mat), blocked(conv_vals)),
    )
    scan_out = scan_out.reshape(TOK_DEV, INNER)
    ssm_raw = scan_out + skip_gain * conv_vals
    gate_act = jax.nn.silu(gate_z)
    ssm_gated = ssm_raw * gate_act
    ssm_scale = rms_scale(ssm_gated)
    branch_ssm = (ssm_gated * ssm_scale * ssm_gain).astype(jnp.bfloat16)
    both_branches = matmul(branch_attn, attn_full) + matmul(branch_ssm, mixout_full)
    middle = tokens + 0.5 * both_branches
    ffn_scale = rms_scale(middle)
    ffn_in = (middle * ffn_scale * ffn_gain).astype(jnp.bfloat16)
    gate_pre = matmul(ffn_in, gate_full)
    up_pre = matmul(ffn_in, up_full)
    gate_silu = jax.nn.silu(gate_pre)
    hidden = (gate_silu * up_pre).astype(jnp.bfloat16)
    output = middle + matmul(hidden, down_full)
    grad_down_proj = settle(left_trans(hidden, grad_top))
    grad_hidden = right_trans(grad_top, down_full)
    grad_gate = (grad_hidden * up_pre * silu_slope(gate_pre)).astype(jnp.bfloat16)
    grad_up = (grad_hidden * gate_silu).astype(jnp.bfloat16)
    grad_gate_proj = settle(left_trans(ffn_in, grad_gate))
    grad_up_proj = settle(left_trans(ffn_in, grad_up))
    grad_ffn_in = right_trans(grad_gate, gate_full) + right_trans(grad_up, up_full)
    grad_middle, grad_ffn_gain = norm_back(grad_ffn_in, middle, ffn_scale, ffn_gain)
    grad_middle = grad_middle + grad_top.astype(jnp.float32)
    grad_branch = (0.5 * grad_middle).astype(jnp.bfloat16)
    grad_attn_proj = settle(left_trans(branch_attn, grad_branch))
    grad_mixer_out = settle(left_trans(branch_ssm, grad_branch))
    grad_attn_raw, grad_attn_gain = norm_back(
        right_trans(grad_branch, attn_full), attn_rows, attn_scale, attn_gain
    )
    grad_heads = grad_attn_raw.astype(jnp.bfloat16).reshape(TOK_DEV, KV_HEADS, group_size, HEAD)
    grad_q_rows = []
    grad_keys = jnp.zeros((WINDOW + TOK_DEV, KV_HEADS, HEAD), jnp.float32)
    grad_vals = jnp.zeros((WINDOW + TOK_DEV, KV_HEADS, HEAD), jnp.float32)
    for block_index, row_start in enumerate(range(0, TOK_DEV, row_block)):
        scores = block_scores(row_start)
        attn_probs = jnp.exp(scores - log_totals[block_index])
        probs_bf = attn_probs.astype(jnp.bfloat16)
        grad_probs = jnp.einsum(
            "qhgd,khd->hgqk", grad_heads, vals_all, preferred_element_type=jnp.float32
        )
        row_dot = jnp.sum(attn_probs * grad_probs, axis=-1, keepdims=True)
        grad_scores = (attn_probs * (grad_probs - row_dot)).astype(jnp.bfloat16)
        grad_q_rows.append(
            score_scale
            * jnp.einsum(
                "hgqk,khd->qhgd", grad_scores, keys_all, preferred_element_type=jnp.float32
            ).reshape(row_block, D)
        )
        grad_keys = grad_keys.at[row_start : row_start + key_span].add(
            score_scale
            * jnp.einsum("hgqk,qhgd->khd", grad_scores, heads_q, preferred_element_type=jnp.float32)
        )
        grad_vals = grad_vals.at[row_start : row_start + key_span].add(
            jnp.einsum("hgqk,qhgd->khd", probs_bf, grad_heads, preferred_element_type=jnp.float32)
        )
    grad_queries = grad_q_rows[0].astype(jnp.bfloat16)
    grad_kv_all = jnp.concatenate(
        [grad_keys.reshape(-1, kv_width), grad_vals.reshape(-1, kv_width)], 1
    )
    grad_gated, grad_ssm_gain = norm_back(
        right_trans(grad_branch, mixout_full), ssm_gated, ssm_scale, ssm_gain
    )
    grad_scan = grad_gated * gate_act
    grad_gate_z = grad_gated * ssm_raw * silu_slope(gate_z)
    grad_skip = jnp.sum(grad_scan * conv_vals, axis=0)

    def adjoint_block(carried, decays, emits):
        next_decay = jnp.concatenate([decays[1:], ones_state[None]], 0)
        cum_decay, cum_emit = lax.associative_scan(
            affine_join, (next_decay, emits), axis=0, reverse=True
        )
        return cum_decay * carried[None] + cum_emit

    head_weights = jnp.exp(-cum_steps[:, :, None] * decay_rate[None])
    zero_carry = jnp.einsum("tis,ti,ts->is", head_weights, grad_scan, output_mat)
    carry_back = prefix((total_decay, zero_carry), "ctx", affine_join, (ones_state, zero_state))

    def full_back(carried, pieces):
        adjoint_in, rate_sum = carried
        start_b, step_b, input_b, output_b, drive_b, grad_b = pieces
        decays, drives = decay_drive(step_b, input_b, drive_b, decay_rate)
        cum_decay, cum_drive = lax.associative_scan(affine_join, (decays, drives), axis=0)
        states = cum_decay * start_b[None] + cum_drive
        previous = jnp.concatenate([start_b[None], states[:-1]], 0)
        adjoints = adjoint_block(adjoint_in, decays, grad_b[:, :, None] * output_b[:, None, :])
        held = adjoints * previous * decays
        input_dot = jnp.sum(adjoints * input_b[:, None, :], axis=2)
        grad_step = -jnp.sum(held * decay_rate[None], axis=2) + drive_b * input_dot
        grad_drive = step_b * input_dot
        grad_input = jnp.einsum("tis,ti->ts", adjoints, step_b * drive_b)
        grad_output = jnp.einsum("tis,ti->ts", states, grad_b)
        rate_sum = rate_sum - jnp.einsum("tis,ti->is", held, step_b)
        return (
            (decays[0] * adjoints[0], rate_sum),
            (grad_step, grad_drive, grad_input, grad_output),
        )

    (unused, grad_rate), (grad_steps, grad_drive_scan, grad_input_mat, grad_output_mat) = lax.scan(
        full_back,
        (carry_back[1], zero_state),
        (
            block_starts,
            blocked(steps_dt),
            blocked(input_mat),
            blocked(output_mat),
            blocked(conv_vals),
            blocked(grad_scan),
        ),
        reverse=True,
    )
    grad_pre_full = grad_steps.reshape(TOK_DEV, INNER) * jax.nn.sigmoid(step_pre)
    grad_step_bias = jnp.sum(grad_pre_full, axis=0)
    grad_pre = grad_pre_full.astype(jnp.bfloat16)
    grad_step_proj = settle(left_trans(step_low, grad_pre))
    grad_projected = jnp.concatenate(
        [
            right_trans(grad_pre, step_full),
            grad_input_mat.reshape(TOK_DEV, STATE),
            grad_output_mat.reshape(TOK_DEV, STATE),
        ],
        1,
    ).astype(jnp.bfloat16)
    grad_state_proj = left_trans(conv_act, grad_projected)
    grad_conv_act = (
        right_trans(grad_projected, state_full)
        + grad_scan * skip_gain
        + grad_drive_scan.reshape(TOK_DEV, INNER)
    ).astype(jnp.bfloat16)
    grad_conv = grad_conv_act.astype(jnp.float32) * silu_slope(conv_pre)
    grad_conv_bias = jnp.sum(grad_conv, axis=0)
    grad_taps = jnp.stack(
        [
            jnp.sum(grad_conv * padded_src[tap_index : tap_index + TOK_DEV], axis=0)
            for tap_index in range(CONV)
        ]
    )
    grad_padded = jnp.zeros((TOK_DEV + CONV - 1, INNER), jnp.float32)
    for tap_index in range(CONV):
        grad_padded = grad_padded.at[tap_index : tap_index + TOK_DEV].add(
            conv_taps[tap_index] * grad_conv
        )
    near_piece = grad_kv_all[(hop_count - 1) * TOK_DEV : hop_count * TOK_DEV]
    back_near, edge_back = (
        passed_along(near_piece.astype(jnp.bfloat16), "ctx", -1).astype(near_piece.dtype),
        passed_along(grad_padded[: CONV - 1].astype(jnp.bfloat16), "ctx", -1).astype(jnp.float32),
    )
    own_kv = grad_kv_all[WINDOW:] + back_near
    for distance in range(2, hop_count + 1):
        far_piece = grad_kv_all[
            (hop_count - distance) * TOK_DEV : (hop_count - distance + 1) * TOK_DEV
        ]
        own_kv = own_kv + passed_along(far_piece.astype(jnp.bfloat16), "ctx", -distance).astype(
            far_piece.dtype
        )
    own_kv_bf = own_kv.astype(jnp.bfloat16)
    grad_src = grad_padded[CONV - 1 :]
    grad_src = grad_src.at[TOK_DEV - (CONV - 1) :].add(edge_back)
    grad_mixed_in = jnp.concatenate([grad_src, grad_gate_z], 1).astype(jnp.bfloat16)
    grad_query_proj = settle(left_trans(normed, grad_queries))
    grad_key_proj = settle(left_trans(normed, own_kv_bf[:, :kv_width]))
    grad_value_proj = settle(left_trans(normed, own_kv_bf[:, kv_width:]))
    grad_mixer_in = settle(left_trans(normed, grad_mixed_in))
    grad_normed = (
        right_trans(grad_queries, query_full)
        + right_trans(own_kv_bf[:, :kv_width], key_full)
        + right_trans(own_kv_bf[:, kv_width:], value_full)
        + right_trans(grad_mixed_in, mixin_full)
    )
    grad_tokens, grad_norm_gain = norm_back(grad_normed, tokens, norm_scale, norm_gain)
    grad_tokens = grad_tokens + grad_middle
    (
        sum_norm_gain,
        sum_attn_gain,
        sum_taps,
        sum_conv_bias,
        sum_state_proj,
        sum_step_bias,
        sum_rate,
        sum_skip,
        sum_ssm_gain,
        sum_ffn_gain,
    ) = lax.psum(
        (
            grad_norm_gain,
            grad_attn_gain,
            grad_taps,
            grad_conv_bias,
            grad_state_proj,
            grad_step_bias,
            grad_rate,
            grad_skip,
            grad_ssm_gain,
            grad_ffn_gain,
        ),
        ("ctx", "fsdp"),
    )
    return (
        output[None],
        grad_tokens[None],
        sum_norm_gain,
        grad_query_proj,
        grad_key_proj,
        grad_value_proj,
        grad_attn_proj,
        sum_attn_gain,
        grad_mixer_in,
        sum_taps,
        sum_conv_bias,
        sum_state_proj,
        grad_step_proj,
        sum_step_bias,
        sum_rate,
        sum_skip,
        grad_mixer_out,
        sum_ssm_gain,
        sum_ffn_gain,
        grad_gate_proj,
        grad_up_proj,
        grad_down_proj,
    )


def solution(mesh):
    placed = (
        P("fsdp", "ctx", None),
        P("fsdp", "ctx", None),
        P(),
        P("fsdp", None),
        P("fsdp", None),
        P("fsdp", None),
        P("fsdp", None),
        P(),
        P("fsdp", None),
        P(),
        P(),
        P("fsdp", None),
        P("fsdp", None),
        P(),
        P(),
        P(),
        P("fsdp", None),
        P(),
        P(),
        P("fsdp", None),
        P("fsdp", None),
        P("fsdp", None),
    )
    return jax.shard_map(
        body,
        mesh=mesh,
        in_specs=placed,
        out_specs=(
            P("fsdp", "ctx", None),
            P("fsdp", "ctx", None),
            P(),
            P("fsdp", "ctx"),
            P("fsdp", "ctx"),
            P("fsdp", "ctx"),
            P("fsdp", "ctx"),
            P(),
            P("fsdp", "ctx"),
            P(),
            P(),
            P(),
            P("fsdp", "ctx"),
            P(),
            P(),
            P(),
            P("fsdp", "ctx"),
            P(),
            P(),
            P("fsdp", "ctx"),
            P("fsdp", "ctx"),
            P("fsdp", "ctx"),
        ),
        check_vma=False,
    )
```

profile of v0, /device:TPU:1, one launch (start us, length us, event | category | flops | bytes accessed | tf_op | source)
XLA Modules:
  0.0 5235.9 jit_solution(10775395905844119761)
XLA Ops:
  10.5 18.4 all-gather.5
  29.0 47.8 all-gather.4
  76.8 299.7 %all-gather.21.cloned.1.call-done = bf16[1600,6400]{1,0:T(8,128)(2,1)} async-done(((bf16[400,6400]{1,0:T(8,128)(2,1)}), bf16[1600,6400]{1,0:T(8,128)(2,1)}) %all-gather.21.cloned.1.call-update) | async-done | bytes 20480016 | tf_op jit(solution)/shard_map/all_gather | solution.py:177
  376.5 10.2 convolution_convert_fusion.5
  412.7 8.7 exponential_multiply_fusion.1
  421.4 8.5 fusion.34
  432.9 42.9 all_gather.57
  477.7 37.6 all_gather.58
  574.5 247.4 %all-gather.33.cloned.1.call-done = bf16[4,1376,1600]{1,2,0:T(8,128)(2,1)} async-done(((bf16[1,1376,1600]{1,2,0:T(8,128)(2,1)}), bf16[4,1376,1600]{1,2,0:T(8,128)(2,1)}) %all-gather.33.cloned.1.call-update) | async-done | bytes 17612816 | tf_op jit(solution)/shard_map/all_gather | solution.py:183
  821.9 23.5 copy.125
  847.5 11.0 all-gather.2
  862.5 15.4 all-gather.31.cloned.1.call-done
  884.7 728.7 %while.75 = (s32[]{:T(128)}, f32[3200,16]{0,1:T(8,128)S(1)}, f32[8,3200,16]{1,2,0:T(8,128)}, f32[8,16,3200]{2,1,0:T(8,128)}, f32[8,16,3200]{2,1,0:T(8,128)S(1)},...) while((s32[]{:T(128)}, f32[3200,16]{0,1:T(8,128)S(1)}, ...), condition=%wide.region_8.9_spmd, body=%wide.region_7.8_spmd.sunk | while | flops 14643202 | bytes 213613264 | solution.py:267
  1618.5 9.2 fusion.120
  1633.9 10.4 fusion.147
  1644.3 125.1 %all-gather.25.cloned.1.call-done = bf16[1600,5504]{1,0:T(8,128)(2,1)} async-done(((bf16[400,5504]{1,0:T(8,128)(2,1)}), bf16[1600,5504]{1,0:T(8,128)(2,1)}) %all-gather.25.cloned.1.call-update) | async-done | bytes 17612816 | tf_op jit(solution)/shard_map/all_gather | solution.py:181
  1769.4 10.8 fusion.146
  1780.2 11.6 multiply_convert_fusion.1
  1793.0 8.6 fusion.148
  1801.6 12.7 multiply_reduce_fusion.12
  1841.8 10.3 exponential_multiply_fusion
  1860.5 11.0 all-gather.3
  1881.5 1629.2 %while.77 = (s32[]{:T(128)}, f32[3200,16]{0,1:T(8,128)S(1)}, f32[3200,16]{0,1:T(8,128)}, f32[8,16,3200]{2,1,0:T(8,128)}, f32[8,16,3200]{2,1,0:T(8,128)}, /*index...) while((s32[]{:T(128)}, f32[3200,16]{0,1:T(8,128)S(1)}, ...), condition=%wide.region_20.21_spmd.clone, body=%wide.region_17.20_spmd.clone.sunk | while | flops 39628800 | bytes 510493216 | solution.py:370
  3515.2 11.1 multiply_convert_fusion
  3578.2 12.6 convolution_convert_fusion.2
  3590.8 12.7 convolution_convert_fusion.3
  3636.2 10.9 convolution_convert_fusion
  3648.2 10.2 convolution_convert_fusion.1
  3663.0 37.8 reduce-scatter.84.cloned.1.call-done
  3703.1 65.8 %reduce-scatter.78.cloned.1.call-done = bf16[1600,200]{0,1:T(8,128)(2,1)} async-done(((bf16[1600,1600]{0,1:T(8,128)(2,1)}), bf16[1600,200]{0,1:T(8,128)(2,1)}) %reduce-scatter.78.cloned.1.call-update) | async-done | bytes 640016
  3771.2 99.5 %reduce-scatter.86.cloned.1.call-done = bf16[3200,200]{0,1:T(8,128)(2,1)} async-done(((bf16[3200,1600]{0,1:T(8,128)(2,1)}), bf16[3200,200]{0,1:T(8,128)(2,1)}) %reduce-scatter.86.cloned.1.call-update) | async-done | bytes 1280016
  3873.4 158.8 %reduce-scatter.58.cloned.1.call-done = bf16[1600,688]{0,1:T(8,128)(2,1)} async-done(((bf16[1600,5504]{0,1:T(8,128)(2,1)}), bf16[1600,688]{0,1:T(8,128)(2,1)}) %reduce-scatter.58.cloned.1.call-update) | async-done | bytes 2201616 | tf_op jit(solution)/shard_map/reduce_scatter | solution.py:111
  4036.7 157.4 %reduce-scatter.56.cloned.1.call-done = bf16[1600,688]{0,1:T(8,128)(2,1)} async-done(((bf16[1600,5504]{0,1:T(8,128)(2,1)}), bf16[1600,688]{0,1:T(8,128)(2,1)}) %reduce-scatter.56.cloned.1.call-update) | async-done | bytes 2201616 | tf_op jit(solution)/shard_map/reduce_scatter | solution.py:111
  4198.6 144.8 %reduce-scatter.52.cloned.1.call-done = bf16[1600,800]{0,1:T(8,128)(2,1)} async-done(((bf16[1600,6400]{0,1:T(8,128)(2,1)}), bf16[1600,800]{0,1:T(8,128)(2,1)}) %reduce-scatter.52.cloned.1.call-update) | async-done | bytes 2560016 | tf_op jit(solution)/shard_map/reduce_scatter | solution.py:111
  4348.7 208.6 %reduce-scatter.88.cloned.1.call-done = bf16[5504,200]{0,1:T(8,128)(2,1)} async-done(((bf16[5504,1600]{0,1:T(8,128)(2,1)}), bf16[5504,200]{0,1:T(8,128)(2,1)}) %reduce-scatter.88.cloned.1.call-update) | async-done | bytes 2201616
  4568.4 9.8 fusion.62
  4583.6 14.6 fusion.49
  4602.6 12.2 reduce-scatter.62.cloned.1.call-done
  4616.5 20.3 reduce-scatter.64.cloned.1.call-done
  4638.4 23.5 reduce-scatter.66.cloned.1.call-done
  4663.9 23.9 reduce-scatter.60.cloned.1.call-done
  4689.7 36.5 reduce-scatter.70.cloned.1.call-done
  4728.3 48.7 reduce-scatter.74.cloned.1.call-done
  4779.6 48.7 reduce-scatter.72.cloned.1.call-done
  4830.9 55.4 %reduce-scatter.68.cloned.1.call-done = bf16[400,800]{1,0:T(8,128)(2,1)} async-done(((bf16[1600,800]{1,0:T(8,128)(2,1)}), bf16[400,800]{1,0:T(8,128)(2,1)}) %reduce-scatter.68.cloned.1.call-update) | async-done | bytes 640016
  4889.1 54.6 %reduce-scatter.76.cloned.1.call-done = bf16[1376,200]{1,0:T(8,128)(2,1)} async-done(((bf16[5504,200]{1,0:T(8,128)(2,1)}), bf16[1376,200]{1,0:T(8,128)(2,1)}) %reduce-scatter.76.cloned.1.call-update) | async-done | bytes 550416
  4946.2 131.2 %all-reduce.66.cloned.1.call-done = (f32[1600]{0:T(1024)}, f32[1600]{0:T(1024)}, f32[4,3200]{1,0:T(4,128)}, f32[3200]{0:T(1024)}, f32[3200]{0:T(1024)}, /*index=5*/f32[3200]{0:T(1024)}, f32[3200]{0:T(1024)}, f32[1600]{0:T(1024)}) async-done(((f32[1600]{0:T(1024)}, f32[1600]{0:T(1024)}, f32[4,3200]{1,0:T(4,128)}, f32[3200]{0:T(1024)}, f32[3200]{0:T(1024)}, /*index=5*/f32[3200]{0:T(1024)}, f32[3200]{0:T(1024)}, ...) | async-done | bytes 121616 | tf_op jit(solution)/shard_map/psum | solution.py:454
  5077.3 140.2 %all-reduce.68.cloned.1.call-done = (f32[3200,132]{0,1:T(8,128)}, f32[3200,16]{0,1:T(8,128)}) async-done(((f32[3200,132]{0,1:T(8,128)}, f32[3200,16]{0,1:T(8,128)}), (f32[3200,132]{0,1:T(8,128)}, f32[3200,16]{0,1:T(8,128)})) %all-reduce.68.cloned.1.call-update) | async-done | bytes 1894416 | tf_op jit(solution)/shard_map/psum | solution.py:454
  (2599 shorter events, 2691.3 us)
Async XLA Ops:
  7.2 369.3 %all-gather.21.cloned.1.call-start = ((), (), s32[]{:S(2)}) async-start(), calls=%async_computation.21 | async-start | bytes 25600000 | tf_op jit(solution)/shard_map/all_gather | solution.py:177
  7.9 537.0 %all-gather.17.cloned.1.call-start = ((), (), s32[]{:S(2)}) async-start(), calls=%async_computation.19 | async-start | bytes 6656000 | tf_op jit(solution)/shard_map/all_gather | solution.py:173
  8.7 813.2 %all-gather.33.cloned.1.call-start = ((), (), s32[]{:S(2)}) async-start(), calls=%async_computation.31 | async-start | bytes 22528000 | tf_op jit(solution)/shard_map/all_gather | solution.py:183
  9.4 850.1 %all-gather.29.cloned.1.call-start = ((), (), s32[]{:S(2)}) async-start(), calls=%async_computation.29 | async-start | bytes 1843200 | tf_op jit(solution)/shard_map/all_gather | solution.py:31
  387.4 10.1 collective-permute-start.8
  408.7 469.3 %all-gather.31.cloned.1.call-start = ((), (), s32[]{:S(2)}) async-start(), calls=%async_computation.30 | async-start | bytes 1843200 | tf_op jit(solution)/shard_map/all_gather | solution.py:31
  430.6 1187.3 %all-gather.23.cloned.1.call-start = ((), (), s32[]{:S(2)}) async-start(), calls=%async_computation.22 | async-start | bytes 13312000 | tf_op jit(solution)/shard_map/all_gather | solution.py:180
  431.2 1196.5 %all-gather.19.cloned.1.call-start = ((), (), s32[]{:S(2)}) async-start(), calls=%async_computation.20 | async-start | bytes 6656000 | tf_op jit(solution)/shard_map/all_gather | solution.py:176
  431.9 1201.7 %all-gather.27.cloned.1.call-start = ((), (), s32[]{:S(2)}) async-start(), calls=%async_computation.24 | async-start | bytes 22016000 | tf_op jit(solution)/shard_map/all_gather | solution.py:182
  432.7 1336.7 %all-gather.25.cloned.1.call-start = ((), (), s32[]{:S(2)}) async-start(), calls=%async_computation.23 | async-start | bytes 22016000 | tf_op jit(solution)/shard_map/all_gather | solution.py:181
  517.9 25.7 collective-permute-start.7
  521.6 20.9 collective-permute-start.6
  525.4 16.2 collective-permute-start.5
  527.9 5.9 collective-permute-start.1
  530.6 3127.9 %reduce-scatter.54.cloned.1.call-start = ((), (), s32[]{:S(2)}) async-start(), calls=%async_computation.26 | async-start | bytes 921600 | tf_op jit(solution)/shard_map/reduce_scatter | solution.py:111
  531.6 4.5 collective-permute-start.2
  533.9 5.4 collective-permute-start.3
  536.1 5.4 collective-permute-start.4
  3515.1 144.0 %reduce-scatter.80.cloned.1.call-start = ((), (), s32[]{:S(2)}) async-start(), calls=%async_computation.43 | async-start | bytes 1198080
  3529.7 9.1 collective-permute-start.9
  3532.8 7.3 collective-permute-start.16
  3533.5 7.9 collective-permute-start.15
  3534.2 9.2 collective-permute-start.14
  3535.5 10.2 collective-permute-start.13
  3538.8 14.2 collective-permute-start.12
  3540.1 13.0 collective-permute-start.11
  3541.5 11.6 collective-permute-start.10
  3554.9 106.1 %reduce-scatter.82.cloned.1.call-start = ((), (), s32[]{:S(2)}) async-start(), calls=%async_computation.44 | async-start | bytes 1198080
  3556.5 144.2 %reduce-scatter.84.cloned.1.call-start = ((), (), s32[]{:S(2)}) async-start(), calls=%async_computation.45 | async-start | bytes 5990400
  3560.6 208.3 %reduce-scatter.78.cloned.1.call-start = ((), (), s32[]{:S(2)}) async-start(), calls=%async_computation.42 | async-start | bytes 5990400
  3570.2 300.5 %reduce-scatter.86.cloned.1.call-start = ((), (), s32[]{:S(2)}) async-start(), calls=%async_computation.46 | async-start | bytes 11520000
  3577.2 455.0 %reduce-scatter.58.cloned.1.call-start = ((), (), s32[]{:S(2)}) async-start(), calls=%async_computation.28 | async-start | bytes 20606976 | tf_op jit(solution)/shard_map/reduce_scatter | solution.py:111
  3590.8 603.3 %reduce-scatter.56.cloned.1.call-start = ((), (), s32[]{:S(2)}) async-start(), calls=%async_computation.27 | async-start | bytes 20606976 | tf_op jit(solution)/shard_map/reduce_scatter | solution.py:111
  3603.5 739.9 %reduce-scatter.52.cloned.1.call-start = ((), (), s32[]{:S(2)}) async-start(), calls=%async_computation.25 | async-start | bytes 23961600 | tf_op jit(solution)/shard_map/reduce_scatter | solution.py:111
  3625.9 6.0 collective-permute-start.17
  3647.2 910.1 %reduce-scatter.88.cloned.1.call-start = ((), (), s32[]{:S(2)}) async-start(), calls=%async_computation.47 | async-start | bytes 19814400
  3658.4 942.4 %all-reduce.64.cloned.1.call-start = ((), (), s32[]{:S(2)}) async-start(), calls=%async_computation.41 | async-start | bytes 204800
  3659.0 955.8 %reduce-scatter.62.cloned.1.call-start = ((), (), s32[]{:S(2)}) async-start(), calls=%async_computation.33 | async-start | bytes 512000
  3661.0 975.8 %reduce-scatter.64.cloned.1.call-start = ((), (), s32[]{:S(2)}) async-start(), calls=%async_computation.34 | async-start | bytes 512000
  3662.9 999.0 %reduce-scatter.66.cloned.1.call-start = ((), (), s32[]{:S(2)}) async-start(), calls=%async_computation.35 | async-start | bytes 1024000
  3703.1 984.7 %reduce-scatter.60.cloned.1.call-start = ((), (), s32[]{:S(2)}) async-start(), calls=%async_computation.32 | async-start | bytes 1024000
  3771.2 955.0 %reduce-scatter.70.cloned.1.call-start = ((), (), s32[]{:S(2)}) async-start(), calls=%async_computation.37 | async-start | bytes 2048000
  3873.3 903.7 %reduce-scatter.74.cloned.1.call-start = ((), (), s32[]{:S(2)}) async-start(), calls=%async_computation.39 | async-start | bytes 3072000
  4036.7 791.6 %reduce-scatter.72.cloned.1.call-start = ((), (), s32[]{:S(2)}) async-start(), calls=%async_computation.38 | async-start | bytes 3072000
  4198.6 687.7 %reduce-scatter.68.cloned.1.call-start = ((), (), s32[]{:S(2)}) async-start(), calls=%async_computation.36 | async-start | bytes 3584000
  4348.6 595.0 %reduce-scatter.76.cloned.1.call-start = ((), (), s32[]{:S(2)}) async-start(), calls=%async_computation.40 | async-start | bytes 3522560
  4561.7 515.6 %all-reduce.66.cloned.1.call-start = ((), (), s32[]{:S(2)}) async-start(), calls=%async_computation.48 | async-start | bytes 282624 | tf_op jit(solution)/shard_map/psum | solution.py:454
  4581.7 635.9 %all-reduce.68.cloned.1.call-start = ((), (), s32[]{:S(2)}) async-start(), calls=%async_computation.49 | async-start | bytes 3891200 | tf_op jit(solution)/shard_map/psum | solution.py:454
  (617 other events, 5954.8 us)
Sparse Core Ops, SparseCore 0:
  9.6 366.8 all-gather.20
  378.0 132.6 all-gather.16
  512.4 309.5 all-gather.32
  824.3 25.3 all-gather.28
  852.0 25.9 all-gather.30
  879.4 186.3 all-gather.22
  1067.4 97.5 all-gather.18
  1166.5 300.1 all-gather.26
  1468.4 300.9 all-gather.24
  3515.2 35.0 reduce-scatter.53
  3555.0 36.1 reduce-scatter.79
  3595.4 36.4 reduce-scatter.81
  3635.7 65.0 reduce-scatter.83
  3704.0 64.8 reduce-scatter.77
  3772.6 98.0 reduce-scatter.85
  3874.1 158.0 reduce-scatter.57
  4035.6 158.4 reduce-scatter.55
  4197.6 145.7 reduce-scatter.51
  4345.7 211.5 reduce-scatter.87
  4559.5 30.8 all-reduce.63
  4593.4 21.4 reduce-scatter.61
  4617.7 19.0 reduce-scatter.63
  4639.2 22.7 reduce-scatter.65
  4664.7 22.9 reduce-scatter.59
  4690.2 35.9 reduce-scatter.69
  4728.4 48.5 reduce-scatter.73
  4779.1 49.1 reduce-scatter.71
  4830.6 55.6 reduce-scatter.67
  4888.6 54.9 reduce-scatter.75
  4952.8 124.4 all-reduce.65
  5083.3 134.1 all-reduce.67
where the time goes:
time: 5270 us; the launch traced here: 5240 us
  waiting for transfers between devices  2180 us (41%)
  local copies, waits for them, and re-layouts  1750 us (33%)
  other arithmetic  825 us (16%)
  matrix products  262 us (5%)
  blocking collectives  169 us (3%)
    unnamed x47, waiting for transfers between devices  740 us
    reduce_scatter x4, waiting for transfers between devices, settle(): lax.psum_scatter(gradient.astype(jnp.bfloat16), 'ctx', scatter_dimension=...  461 us
    pad x96, local copies, waits for them, and re-layouts, adjoint_block(): lax.associative_scan(affine_join, (next_decay, emits), axis=0, reverse=True)  456 us
    pad x96, local copies, waits for them, and re-layouts, out_step(): lax.associative_scan(affine_join, (decays, drives), axis=0)  434 us
    pad x96, local copies, waits for them, and re-layouts, full_back(): lax.associative_scan(affine_join, (decays, drives), axis=0)  432 us
    all_gather x1, waiting for transfers between devices, body(): lax.all_gather(sharded[4], 'fsdp', axis=0, tiled=True)  300 us
    psum x2, waiting for transfers between devices, body(): lax.psum((grad_norm_gain, grad_attn_gain, grad_taps, grad_conv_bias, grad...  271 us
    all_gather x1, waiting for transfers between devices, body(): lax.all_gather(sharded[10], 'fsdp', axis=0, tiled=True)  247 us
  transfers between devices with their start and end apart: 49, of which 29 were waited for; matrix products, arithmetic and copies ran while one was open for 20% of the time, Pallas kernels for 0%

commit v1 on v0

v1 whole, which is shorter than its diff:
```python
import functools
import jax
import jax.numpy as jnp
from jax import lax
from jax.experimental import pallas as pl
from jax.experimental.pallas import tpu as pltpu
from jax.sharding import PartitionSpec as P

LANES = 128
STATE = 16
CHUNK = 128
HEAD = 64
KV_HEADS = 5
CONV = 4
DT_RANK = 100
WINDOW = 1024
EPSILON = 1e-06
LOG2_E = 1.4426950408889634
BF16 = jnp.bfloat16


MESH = pl.DeviceIdType.MESH
VMEM_LIMIT = 56 * 1024 * 1024
IN_VMEM = pl.BlockSpec(memory_space=pltpu.VMEM)


def flip(index, bit):
    return index + (1 - 2 * ((index // (1 << bit)) % 2)) * (1 << bit)


def greet(me, bits):
    barrier = pltpu.get_barrier_semaphore()
    for bit in range(bits):
        pl.semaphore_signal(
            barrier, inc=1, device_id={"ctx": flip(me, bit)}, device_id_type=MESH
        )
    pl.semaphore_wait(barrier, bits)


def halves_of(rows):
    half = rows // 2
    return (pl.ds(0, half), pl.ds(half, rows - half))


class Copies:
    def __init__(self, axis, send_sem, recv_sem):
        self.axis, self.send_sem, self.recv_sem = axis, send_sem, recv_sem
        self.started = []
        self.count = 0

    def make(self, source, target, device):
        copy = pltpu.make_async_remote_copy(
            src_ref=source,
            dst_ref=target,
            send_sem=self.send_sem.at[self.count],
            recv_sem=self.recv_sem.at[self.count],
            device_id={self.axis: device},
            device_id_type=MESH,
        )
        self.count += 1
        return copy

    def send(self, source, target, device):
        copy = self.make(source, target, device)
        copy.start()
        self.started.append(copy)
        return copy

    def finish(self):
        for copy in self.started:
            copy.wait_send()


def gather_sems(bits):
    return 1 + 2 * sum(1 << p for p in range(bits - 1)) + 2 * ((1 << (bits - 1)) - 1)


def gather_steps(copies, bits, out_ref):
    me = lax.axis_index("ctx")
    parts = halves_of(out_ref.shape[1])
    orders = (list(range(1, bits)), list(range(bits - 1, 0, -1)))

    def send(bit, shard, part):
        at = out_ref.at[shard] if part is None else out_ref.at[shard, part]
        return copies.send(at, at, flip(me, bit))

    known = ([me], [me])
    last, flying = [], [None, None]

    def begin():
        for h in range(2):
            flying[h] = [send(orders[h][0], shard, parts[h]) for shard in known[h]]
        last.append(send(0, me, None))

    def turn(phase, h):
        bit = orders[h][phase]
        for copy in flying[h]:
            copy.wait_recv()
        fresh = [flip(shard, bit) for shard in known[h]]
        known[h].extend(fresh)
        if phase + 1 < bits - 1:
            flying[h] = [send(orders[h][phase + 1], shard, parts[h]) for shard in known[h]]
        last.extend(send(0, shard, parts[h]) for shard in fresh)

    def end():
        for copy in last:
            copy.wait_recv()

    turns = [functools.partial(turn, p, h) for p in range(bits - 1) for h in range(2)]
    return [begin] + turns + [end]


def gather_kernel(bits, x_ref, out_ref, send_sem, recv_sem):
    me = lax.axis_index("ctx")
    greet(me, bits)
    out_ref[me] = x_ref[...]
    copies = Copies("ctx", send_sem, recv_sem)
    for step in gather_steps(copies, bits, out_ref):
        step()
    copies.finish()


def ctx_bits():
    return lax.axis_size("ctx").bit_length() - 1


def params(collective_id):
    return pltpu.CompilerParams(
        collective_id=collective_id, has_side_effects=True, vmem_limit_bytes=VMEM_LIMIT
    )


def gather_shards(x, collective_id):
    bits, ctx = ctx_bits(), lax.axis_size("ctx")
    sems = pltpu.SemaphoreType.DMA((gather_sems(bits),))
    return pl.pallas_call(
        functools.partial(gather_kernel, bits),
        out_shape=jax.ShapeDtypeStruct((ctx,) + x.shape, x.dtype),
        in_specs=[IN_VMEM],
        out_specs=IN_VMEM,
        scratch_shapes=[sems, sems],
        compiler_params=params(collective_id),
        name="gather_shards",
    )(x)


def gather_tokens(x, collective_id):
    return gather_shards(x, collective_id).reshape(-1, x.shape[1])


def row_parts(rows, count):
    tiles = rows // 16
    edges = [16 * (tiles * i // count) for i in range(count)] + [rows]
    return [pl.ds(a, b - a) for a, b in zip(edges[:-1], edges[1:]) if b > a]


def line_steps(copies, out_refs, pieces):
    me, size = lax.axis_index("fsdp"), lax.axis_size("fsdp")
    plans = []
    for way in (1, -1):
        for distance in range(size - 1):
            for ref, part in pieces:
                shard = me - way * distance
                inside = jnp.logical_and(shard >= 0, shard < size)
                held = jnp.where(inside, shard, me)
                to = me + way
                go = jnp.logical_and(inside, jnp.logical_and(to >= 0, to < size))
                target = jnp.where(jnp.logical_and(to >= 0, to < size), to, me - way)
                at = out_refs[ref].at[held, part]
                plans.append((way, distance, go, copies.make(at, at, target)))
    table = {}
    for way, distance, go, copy in plans:
        table.setdefault((way, distance), []).append((go, copy))

    def begin():
        for index in range(len(pieces)):
            for way in (1, -1):
                go, copy = table[way, 0][index]
                pl.when(go)(copy.start)

    def turn(distance, index):
        for way in (1, -1):
            _, came = table[way, distance - 1][index]
            origin = me - way * distance
            pl.when(jnp.logical_and(origin >= 0, origin < size))(came.wait_recv)
            if distance < size - 1:
                go, copy = table[way, distance][index]
                pl.when(go)(copy.start)

    def end():
        for way in (1, -1):
            for distance in range(size - 1):
                for go, copy in table[way, distance]:
                    pl.when(go)(copy.wait_send)

    turns = [
        functools.partial(turn, d, i) for d in range(1, size) for i in range(len(pieces))
    ]
    return [begin] + turns, end


def front_kernel(
    bits, count, x_ref, gain_ref, top_ref, in_ref, state_ref, step_ref,
    normed_ref, tops_ref, in_out, state_out, step_out,
    ctx_send, ctx_recv, line_send, line_recv,
):
    me, row, rows = lax.axis_index("ctx"), lax.axis_index("fsdp"), lax.axis_size("fsdp")
    barrier = pltpu.get_barrier_semaphore()
    for bit in range(bits):
        pl.semaphore_signal(
            barrier, inc=1, device_id={"ctx": flip(me, bit)}, device_id_type=MESH
        )
    for to in (row - 1, row + 1):
        there = jnp.logical_and(to >= 0, to < rows)

        @pl.when(there)
        def _():
            pl.semaphore_signal(
                barrier, inc=1, device_id={"fsdp": jnp.where(there, to, row)}, device_id_type=MESH
            )

    in_out[row] = in_ref[...]
    state_out[row] = state_ref[...]
    step_out[row] = step_ref[...]
    tokens = x_ref[...].astype(jnp.float32)
    scale = lax.rsqrt(jnp.mean(tokens * tokens, axis=-1, keepdims=True) + EPSILON)
    normed_ref[me] = (tokens * scale * gain_ref[...]).astype(normed_ref.dtype)
    tops_ref[me] = top_ref[...]
    neighbours = jnp.where(row > 0, 1, 0) + jnp.where(row < rows - 1, 1, 0)
    pl.semaphore_wait(barrier, bits + neighbours)

    line = Copies("fsdp", line_send, line_recv)
    across = Copies("ctx", ctx_send, ctx_recv)
    pieces = [(0, part) for part in row_parts(in_ref.shape[0], count)]
    pieces = [(1, pl.ds(0, state_ref.shape[0])), (2, pl.ds(0, step_ref.shape[0]))] + pieces
    line_list, line_end = line_steps(line, (in_out, state_out, step_out), pieces)
    first = gather_steps(across, bits, normed_ref)
    second = gather_steps(across, bits, tops_ref)
    token_list = first[:-1] + second[:-1] + [first[-1], second[-1]]
    line_list[0]()
    token_list[0]()
    line_rest, token_rest = line_list[1:], token_list[1:]
    done = 0
    for i, step in enumerate(line_rest):
        step()
        upto = len(token_rest) * (i + 1) // len(line_rest)
        for token_step in token_rest[done:upto]:
            token_step()
        done = upto
    across.finish()
    line_end()


def front(x, gain, top, in_part, state_part, step_part, collective_id):
    bits, ctx, fsdp = ctx_bits(), lax.axis_size("ctx"), lax.axis_size("fsdp")
    count = 4
    ctx_sems = pltpu.SemaphoreType.DMA((2 * gather_sems(bits),))
    line_sems = pltpu.SemaphoreType.DMA((2 * fsdp * (count + 2),))

    def stacked(array, size):
        return jax.ShapeDtypeStruct((size,) + array.shape, array.dtype)

    return pl.pallas_call(
        functools.partial(front_kernel, bits, count),
        out_shape=[
            stacked(x, ctx), stacked(top, ctx), stacked(in_part, fsdp), stacked(state_part, fsdp),
            stacked(step_part, fsdp),
        ],
        in_specs=[IN_VMEM] * 6,
        out_specs=[IN_VMEM] * 5,
        scratch_shapes=[ctx_sems, ctx_sems, line_sems, line_sems],
        compiler_params=params(collective_id),
        name="front",
    )(x, gain, top, in_part, state_part, step_part)


def product(x, weight, trans):
    dims = (((1,), (1 if trans else 0,)), ((), ()))
    return lax.dot_general(x, weight, dims, preferred_element_type=jnp.float32)


def subsets(chosen):
    out = [()]
    for bit in chosen:
        out = out + [s + (bit,) for s in out]
    return out


def flipped(shard, flips):
    for bit in flips:
        shard = flip(shard, bit)
    return shard


class Reducer:
    def __init__(self, copies, bits, part_ref, inbox, out_ref):
        self.copies, self.bits, self.part_ref = copies, bits, part_ref
        self.inbox, self.out_ref = inbox, out_ref
        self.me = lax.axis_index("ctx")
        self.parts = halves_of(out_ref.shape[0])
        self.orders = (list(range(1, bits)), list(range(bits - 1, 0, -1)))
        self.everyone = subsets(range(1, bits))[::-1]
        self.slots = {flips: slot for slot, flips in enumerate(self.everyone)}
        self.first = {}
        self.flying = [{}, {}]

    def to_sibling(self, flips, partial):
        slot = self.slots[flips]
        self.part_ref[slot] = partial.astype(self.part_ref.dtype)
        self.first[flips] = self.copies.send(
            self.part_ref.at[slot], self.inbox[0].at[slot], flip(self.me, 0)
        )

    def pass_on(self, h, phase, flips, following):
        bit = self.orders[h][phase]
        if bit in flips:
            kept = tuple(b for b in flips if b != bit)
            following[kept] = self.copies.send(
                self.inbox[0].at[self.slots[flips], self.parts[h]],
                self.inbox[1 + phase].at[len(following), self.parts[h]],
                flip(self.me, bit),
            )

    def own(self, flips, partial):
        self.first[flips].wait_recv()
        kept_ref, slot = self.inbox[0], self.slots[flips]
        kept_ref[slot] = (partial + kept_ref[slot].astype(jnp.float32)).astype(kept_ref.dtype)
        for h in range(2):
            self.pass_on(h, 0, flips, self.flying[h])

    def finish(self):
        kept_ref = self.inbox[0]
        for phase in range(self.bits - 1):
            for h in range(2):
                part, following = self.parts[h], {}
                for box, (flips, copy) in enumerate(list(self.flying[h].items())):
                    copy.wait_recv()
                    slot = self.slots[flips]
                    total = kept_ref[slot, part].astype(jnp.float32) + self.inbox[1 + phase][
                        box, part
                    ].astype(jnp.float32)
                    if phase == self.bits - 2:
                        self.out_ref[part] = total
                    else:
                        kept_ref[slot, part] = total.astype(kept_ref.dtype)
                        self.pass_on(h, phase + 1, flips, following)
                self.flying[h] = following


def reducer_boxes(ctx, bits, rows, columns):
    boxes = [ctx // 2, ctx // 2] + [ctx // 4 >> p for p in range(bits - 1)]
    sems = boxes[0] + 2 * sum(boxes[2:])
    return [pltpu.VMEM((box, rows, columns), BF16) for box in boxes], sems


def reduce_kernel(bits, trans, *refs):
    count = len(trans)
    x_refs, w_refs, out_ref = refs[:count], refs[count : 2 * count], refs[2 * count]
    part_ref, inbox = refs[2 * count + 1], refs[2 * count + 2 : -2]
    me = lax.axis_index("ctx")
    greet(me, bits)
    copies = Copies("ctx", *refs[-2:])
    reducer = Reducer(copies, bits, part_ref, inbox, out_ref)

    def partial(flips):
        shard = flipped(me, flips)
        return sum(
            product(x_ref[shard], w_ref[...], way)
            for x_ref, w_ref, way in zip(x_refs, w_refs, trans)
        )

    for flips in reducer.everyone:
        reducer.to_sibling(flips, partial(flips + (0,)))
    for flips in reducer.everyone:
        reducer.own(flips, partial(flips))
    reducer.finish()
    copies.finish()


def reduce_products(pairs, trans, collective_id):
    ctx, bits = lax.axis_size("ctx"), ctx_bits()
    rows = pairs[0][0].shape[0] // ctx
    columns = pairs[0][1].shape[0 if trans[0] else 1]
    boxes, count = reducer_boxes(ctx, bits, rows, columns)
    sems = pltpu.SemaphoreType.DMA((count,))
    return pl.pallas_call(
        functools.partial(reduce_kernel, bits, trans),
        out_shape=jax.ShapeDtypeStruct((rows, columns), jnp.float32),
        in_specs=[IN_VMEM] * (2 * len(pairs)),
        out_specs=IN_VMEM,
        scratch_shapes=boxes + [sems, sems],
        compiler_params=params(collective_id),
        name="reduce_products",
    )(*[x.reshape(ctx, rows, -1) for x, _ in pairs], *[w for _, w in pairs])


def greet_all(me, size):
    barrier = pltpu.get_barrier_semaphore()
    for turn in range(1, size):
        pl.semaphore_signal(
            barrier, inc=1, device_id={"ctx": (me + turn) % size}, device_id_type=MESH
        )
    pl.semaphore_wait(barrier, size - 1)


def sum_kernel(size, x_ref, out_ref, inbox, send_sem, recv_sem):
    me = lax.axis_index("ctx")
    greet_all(me, size)
    copies = Copies("ctx", send_sem, recv_sem)
    come = []
    for turn in range(1, size):
        to = (me + turn) % size
        come.append(copies.send(x_ref.at[to], inbox.at[turn - 1], to))
    total = x_ref[me].astype(jnp.float32)
    for turn in range(1, size):
        come[turn - 1].wait_recv()
        total = total + inbox[turn - 1].astype(jnp.float32)
    out_ref[me] = total.astype(out_ref.dtype)
    come = [
        copies.send(out_ref.at[me], out_ref.at[me], (me + turn) % size) for turn in range(1, size)
    ]
    for copy in come:
        copy.wait_recv()
    copies.finish()


def sum_everywhere(partial, collective_id):
    ctx = lax.axis_size("ctx")
    rows, columns = partial.shape[0] // ctx, partial.shape[1]
    sems = pltpu.SemaphoreType.DMA((2 * (ctx - 1),))
    return pl.pallas_call(
        functools.partial(sum_kernel, ctx),
        out_shape=jax.ShapeDtypeStruct((ctx, rows, columns), partial.dtype),
        in_specs=[IN_VMEM],
        out_specs=IN_VMEM,
        scratch_shapes=[pltpu.VMEM((ctx - 1, rows, columns), partial.dtype), sems, sems],
        compiler_params=params(collective_id),
        name="sum_everywhere",
    )(partial.reshape(ctx, rows, columns)).reshape(partial.shape)


def total_kernel(size, x_ref, out_ref, inbox, send_sem, recv_sem):
    me = lax.axis_index("ctx")
    greet_all(me, size)
    copies = Copies("ctx", send_sem, recv_sem)
    come = [
        copies.send(x_ref, inbox.at[turn - 1], (me + turn) % size) for turn in range(1, size)
    ]
    inbox_total = x_ref[...]
    for turn in range(1, size):
        come[turn - 1].wait_recv()
        inbox_total = inbox_total + inbox[turn - 1]
    out_ref[...] = inbox_total
    copies.finish()


def total_of(rows_sum, collective_id):
    ctx = lax.axis_size("ctx")
    flat = rows_sum.reshape(-1, LANES)
    sems = pltpu.SemaphoreType.DMA((ctx - 1,))
    return pl.pallas_call(
        functools.partial(total_kernel, ctx),
        out_shape=jax.ShapeDtypeStruct(flat.shape, flat.dtype),
        in_specs=[IN_VMEM],
        out_specs=IN_VMEM,
        scratch_shapes=[pltpu.VMEM((ctx - 1,) + flat.shape, flat.dtype), sems, sems],
        compiler_params=params(collective_id),
        name="total_of",
    )(flat).reshape(rows_sum.shape)


def settle_kernel(
    bits, size, count, channel_ref, gain_ref, all_ref, sums_ref,
    row_inbox, gain_inbox, line_inbox, ctx_send, ctx_recv, line_send, line_recv,
):
    me, row = lax.axis_index("ctx"), lax.axis_index("fsdp")
    barrier = pltpu.get_barrier_semaphore()
    for turn in range(1, size):
        pl.semaphore_signal(
            barrier, inc=1, device_id={"ctx": (me + turn) % size}, device_id_type=MESH
        )
    for turn in range(1, count):
        pl.semaphore_signal(
            barrier, inc=1, device_id={"fsdp": (row + turn) % count}, device_id_type=MESH
        )
    pl.semaphore_wait(barrier, size - 1 + count - 1)
    across, line = Copies("ctx", ctx_send, ctx_recv), Copies("fsdp", line_send, line_recv)
    band = channel_ref.shape[0] // count

    def band_of(index):
        return pl.ds(pl.multiple_of(index * band, 8), band)

    rows_come = []
    for turn in range(1, count):
        to = (row + turn) % count
        rows_come.append(line.send(channel_ref.at[band_of(to)], row_inbox.at[turn - 1], to))
    gains_come = [
        across.send(gain_ref, gain_inbox.at[turn - 1], (me + turn) % size)
        for turn in range(1, size)
    ]
    total = channel_ref[band_of(row)]
    for turn in range(1, count):
        rows_come[turn - 1].wait_recv()
        total = total + row_inbox[turn - 1]
    all_ref[me, band_of(row)] = total
    at = all_ref.at[me, band_of(row)]
    bands_come = [line.send(at, at, (row + turn) % count) for turn in range(1, count)]
    total = gain_ref[...]
    for turn in range(1, size):
        gains_come[turn - 1].wait_recv()
        total = total + gain_inbox[turn - 1]
    line_inbox[0] = total
    line_come = [
        line.send(line_inbox.at[0], line_inbox.at[turn], (row + turn) % count)
        for turn in range(1, count)
    ]
    for copy in bands_come:
        copy.wait_recv()
    for step in gather_steps(across, bits, all_ref):
        step()
    total = line_inbox[0]
    for turn in range(1, count):
        line_come[turn - 1].wait_recv()
        total = total + line_inbox[turn]
    sums_ref[...] = total
    across.finish()
    line.finish()


def settle_small(channel, gains, collective_id):
    ctx, fsdp, bits = lax.axis_size("ctx"), lax.axis_size("fsdp"), ctx_bits()
    ctx_sems = pltpu.SemaphoreType.DMA((ctx - 1 + gather_sems(bits),))
    line_sems = pltpu.SemaphoreType.DMA((3 * (fsdp - 1),))
    rows, columns = channel.shape
    return pl.pallas_call(
        functools.partial(settle_kernel, bits, ctx, fsdp),
        out_shape=[
            jax.ShapeDtypeStruct((ctx, rows, columns), jnp.float32),
            jax.ShapeDtypeStruct(gains.shape, jnp.float32),
        ],
        in_specs=[IN_VMEM] * 2,
        out_specs=[IN_VMEM] * 2,
        scratch_shapes=[
            pltpu.VMEM((fsdp - 1, rows // fsdp, columns), jnp.float32),
            pltpu.VMEM((ctx - 1,) + gains.shape, jnp.float32),
            pltpu.VMEM((fsdp,) + gains.shape, jnp.float32),
            ctx_sems, ctx_sems, line_sems, line_sems,
        ],
        compiler_params=params(collective_id),
        name="settle_small",
    )(channel, gains)


def plane_gather(copies, out_ref):
    me = lax.axis_index("ctx")
    parts = halves_of(out_ref.shape[1])
    held = {}

    def send(name, bit, flips, part=None):
        shard = flipped(me, flips)
        at = out_ref.at[shard] if part is None else out_ref.at[shard, part]
        held[name] = copies.send(at, at, flip(me, bit))

    def start():
        for bit in (1, 2, 0):
            send(("own", bit), bit, ())

    def forward():
        held["own", 1].wait_recv()
        send(("corner", 2), 2, (1,), parts[0])
        held["own", 2].wait_recv()
        send(("corner", 1), 1, (2,), parts[1])
        send(("core", (1,)), 0, (1,))
        send(("core", (2,)), 0, (2,))

    def corner():
        held["corner", 2].wait_recv()
        held["corner", 1].wait_recv()
        send(("core", (1, 2)), 0, (1, 2))

    def wait(flips):
        held["core", flips].wait_recv() if flips else held["own", 0].wait_recv()

    return start, forward, corner, wait


def ffn_kernel(
    x_ref, top_ref, pair_w, down_w,
    all_ref, hidden_ref, pair_ref, out_ref, grad_ref,
    own_ref, part_out, part_grad, *rest,
):
    bits = 3
    boxes = (len(rest) - 2) // 2
    inbox_out, inbox_grad = rest[:boxes], rest[boxes : 2 * boxes]
    me = lax.axis_index("ctx")
    greet(me, bits)
    all_ref[me] = x_ref[...]
    copies = Copies("ctx", *rest[-2:])
    start, forward, corner, wait = plane_gather(copies, all_ref)
    reducers = (
        Reducer(copies, bits, part_grad, inbox_grad, grad_ref),
        Reducer(copies, bits, part_out, inbox_out, out_ref),
    )
    rows, model = x_ref.shape
    hid = hidden_ref.shape[2]
    core = me % 2

    def work(slot, flips):
        first = 2 * (flipped(me, flips) // 2)
        pair = pl.ds(first, 2)
        x = all_ref[pair].reshape(2 * rows, model)
        pre = product(x, pair_w[...], False)
        gate, up = pre[:, :hid], pre[:, hid:]
        logistic = jax.nn.sigmoid(gate)
        gate_silu = gate * logistic
        hidden = (gate_silu * up).astype(BF16)
        hidden_ref[pair] = hidden.reshape(2, rows, hid)
        top = top_ref[pair].reshape(2 * rows, model)
        grad_hidden = product(top, down_w[...], True)
        slope = logistic * (1.0 + gate * (1.0 - logistic))
        pair_ref[pair, :, :hid] = (grad_hidden * up * slope).astype(BF16).reshape(2, rows, hid)
        pair_ref[pair, :, hid:] = (grad_hidden * gate_silu).astype(BF16).reshape(2, rows, hid)
        grads = pair_ref[pair].reshape(2 * rows, 2 * hid)
        for index, value in enumerate(
            (product(grads, pair_w[...], True), product(hidden, down_w[...], False))
        ):
            low, high = value[:rows], value[rows:]
            own_ref[index, slot] = jnp.where(core == 0, low, high)
            reducers[index].to_sibling(flips, jnp.where(core == 0, high, low))

    def settle(slot, flips):
        for index, reducer in enumerate(reducers):
            reducer.own(flips, own_ref[index, slot])

    start()
    wait(())
    work(0, ())
    forward()
    wait((1,))
    work(1, (1,))
    settle(0, ())
    corner()
    wait((2,))
    work(2, (2,))
    settle(1, (1,))
    wait((1, 2))
    work(3, (1, 2))
    settle(2, (2,))
    settle(3, (1, 2))
    for reducer in reducers:
        reducer.finish()
    copies.finish()


def ffn_both_ways(ffn_in, top, pair_full, down_full, collective_id):
    ctx, bits = lax.axis_size("ctx"), ctx_bits()
    rows, model = ffn_in.shape
    hid = down_full.shape[0]
    boxes, count = reducer_boxes(ctx, bits, rows, model)
    sems = pltpu.SemaphoreType.DMA((2 * count + 8,))
    all_rows, hidden, pair, out, grad = pl.pallas_call(
        ffn_kernel,
        out_shape=[
            jax.ShapeDtypeStruct((ctx, rows, model), BF16),
            jax.ShapeDtypeStruct((ctx, rows, hid), BF16),
            jax.ShapeDtypeStruct((ctx, rows, 2 * hid), BF16),
            jax.ShapeDtypeStruct((rows, model), jnp.float32),
            jax.ShapeDtypeStruct((rows, model), jnp.float32),
        ],
        in_specs=[IN_VMEM] * 4,
        out_specs=[IN_VMEM] * 5,
        scratch_shapes=[pltpu.VMEM((2, ctx // 2, rows, model), jnp.float32), boxes[0], boxes[0]]
        + boxes[1:]
        + boxes[1:]
        + [sems, sems],
        compiler_params=params(collective_id),
        name="ffn_both_ways",
    )(ffn_in, top.reshape(ctx, rows, model), pair_full, down_full)
    flat = [a.reshape(ctx * rows, -1) for a in (all_rows, hidden, pair)]
    return flat[0], flat[1], flat[2], out, grad


def scan_fwd_kernel(steps_ref, drive_ref, in_ref, out_ref, rate_ref, scan_ref, prev_ref, state_ref):
    tiles = steps_ref.shape[1] // LANES
    chunk = steps_ref.shape[0]

    @pl.when(pl.program_id(0) == 0)
    def _():
        state_ref[...] = jnp.zeros_like(state_ref)

    rates = [rate_ref[:, j * LANES : (j + 1) * LANES] for j in range(tiles)]

    def group(g, states):
        states = list(states)
        base = pl.multiple_of(g * 8, 8)
        for j in range(tiles):
            lanes = slice(j * LANES, (j + 1) * LANES)
            step_8 = steps_ref[pl.ds(base, 8), lanes]
            drive_8 = step_8 * drive_ref[pl.ds(base, 8), lanes]
            rows = []
            for t in range(8):
                in_t = in_ref[base + t]
                out_t = out_ref[base + t]
                decay = jnp.exp2(step_8[t : t + 1] * rates[j])
                prev_ref[base + t, :, lanes] = states[j]
                states[j] = decay * states[j] + drive_8[t : t + 1] * in_t
                rows.append(jnp.sum(states[j] * out_t, axis=0, keepdims=True))
            scan_ref[pl.ds(base, 8), lanes] = jnp.concatenate(rows, 0)
        return tuple(states)

    start = tuple(state_ref[:, j * LANES : (j + 1) * LANES] for j in range(tiles))
    final = lax.fori_loop(0, chunk // 8, group, start)
    for j in range(tiles):
        state_ref[:, j * LANES : (j + 1) * LANES] = final[j]


def scan_fwd(steps, drive, in_b, out_b, rates):
    length, width = steps.shape
    chunk = CHUNK
    row = pl.BlockSpec((chunk, width), lambda i: (i, 0))
    mat = pl.BlockSpec((chunk, STATE, LANES), lambda i: (i, 0, 0))
    rate = pl.BlockSpec((STATE, width), lambda i: (0, 0))
    return pl.pallas_call(
        scan_fwd_kernel,
        grid=(length // chunk,),
        in_specs=[row, row, mat, mat, rate],
        out_specs=[row, pl.BlockSpec((chunk, STATE, width), lambda i: (i, 0, 0))],
        out_shape=[
            jax.ShapeDtypeStruct((length, width), jnp.float32),
            jax.ShapeDtypeStruct((length, STATE, width), jnp.float32),
        ],
        scratch_shapes=[pltpu.VMEM((STATE, width), jnp.float32)],
        compiler_params=pltpu.CompilerParams(vmem_limit_bytes=48 * 1024 * 1024),
        name="scan_forward",
    )(steps, drive, in_b, out_b, rates)


def scan_bwd_kernel(
    steps_ref, drive_ref, grad_ref, in_ref, out_ref, rate_ref, prev_ref,
    gstep_ref, gdrive_ref, gin_ref, gout_ref, grate_ref,
    carry_ref, pin_ref, pout_ref,
):
    tiles = steps_ref.shape[1] // LANES
    chunk = steps_ref.shape[0]

    @pl.when(pl.program_id(0) == 0)
    def _():
        carry_ref[...] = jnp.zeros_like(carry_ref)
        grate_ref[...] = jnp.zeros_like(grate_ref)

    for j in range(tiles):
        lanes = slice(j * LANES, (j + 1) * LANES)
        rates = rate_ref[:, lanes]

        def group(k, kept):
            carry, acc = kept
            base = pl.multiple_of(chunk - 8 - k * 8, 8)
            step_8 = steps_ref[pl.ds(base, 8), lanes]
            x_8 = drive_ref[pl.ds(base, 8), lanes]
            drive_8 = step_8 * x_8
            grad_8 = grad_ref[pl.ds(base, 8), lanes]
            held_rows, dot_rows = [None] * 8, [None] * 8
            for t in range(7, -1, -1):
                in_t = in_ref[base + t]
                out_t = out_ref[base + t]
                previous = prev_ref[base + t, :, lanes]
                step_t = step_8[t : t + 1]
                drive_t = drive_8[t : t + 1]
                grad_t = grad_8[t : t + 1]
                decay = jnp.exp2(step_t * rates)
                adjoint = grad_t * out_t + carry
                carry = decay * adjoint
                held = carry * previous
                state = decay * previous + drive_t * in_t
                acc = acc + held * step_t
                held_rows[t] = jnp.sum(held * rates, axis=0, keepdims=True)
                dot_rows[t] = jnp.sum(adjoint * in_t, axis=0, keepdims=True)
                part_in = adjoint * drive_t
                part_out = state * grad_t
                at = pl.ds(pl.multiple_of((base + t) * STATE, STATE), STATE)
                if j == 0:
                    pin_ref[at] = part_in
                    pout_ref[at] = part_out
                else:
                    pin_ref[at] += part_in
                    pout_ref[at] += part_out
            held_8 = jnp.concatenate(held_rows, 0)
            dot_8 = jnp.concatenate(dot_rows, 0)
            gstep_ref[pl.ds(base, 8), lanes] = held_8 * 0.6931471805599453 + x_8 * dot_8
            gdrive_ref[pl.ds(base, 8), lanes] = step_8 * dot_8
            return carry, acc

        carry, acc = lax.fori_loop(
            0, chunk // 8, group, (carry_ref[:, lanes], grate_ref[:, lanes])
        )
        carry_ref[:, lanes] = carry
        grate_ref[:, lanes] = acc
    ones = jnp.ones((8, LANES), jnp.float32)
    dims = (((1,), (1,)), ((), ()))
    gin_ref[0] = lax.dot_general(ones, pin_ref[...], dims, preferred_element_type=jnp.float32)
    gout_ref[0] = lax.dot_general(ones, pout_ref[...], dims, preferred_element_type=jnp.float32)


def scan_bwd(steps, drive, grad, in_b, out_b, rates, previous):
    length, width = steps.shape
    chunk = CHUNK
    count = length // chunk
    row = pl.BlockSpec((chunk, width), lambda i: (count - 1 - i, 0))
    mat = pl.BlockSpec((chunk, STATE, LANES), lambda i: (count - 1 - i, 0, 0))
    rate = pl.BlockSpec((STATE, width), lambda i: (0, 0))
    red = pl.BlockSpec((1, 8, chunk * STATE), lambda i: (count - 1 - i, 0, 0))
    gstep, gdrive, gin, gout, grate = pl.pallas_call(
        scan_bwd_kernel,
        grid=(count,),
        in_specs=[row, row, row, mat, mat, rate,
                  pl.BlockSpec((chunk, STATE, width), lambda i: (count - 1 - i, 0, 0))],
        out_specs=[row, row, red, red, rate],
        out_shape=[
            jax.ShapeDtypeStruct((length, width), jnp.float32),
            jax.ShapeDtypeStruct((length, width), jnp.float32),
            jax.ShapeDtypeStruct((count, 8, chunk * STATE), jnp.float32),
            jax.ShapeDtypeStruct((count, 8, chunk * STATE), jnp.float32),
            jax.ShapeDtypeStruct((STATE, width), jnp.float32),
        ],
        scratch_shapes=[
            pltpu.VMEM((STATE, width), jnp.float32),
            pltpu.VMEM((chunk * STATE, LANES), jnp.float32),
            pltpu.VMEM((chunk * STATE, LANES), jnp.float32),
        ],
        compiler_params=pltpu.CompilerParams(vmem_limit_bytes=48 * 1024 * 1024),
        name="scan_backward",
    )(steps, drive, grad, in_b, out_b, rates, previous)
    return (gstep, gdrive, gin[:, 0].reshape(length, STATE), gout[:, 0].reshape(length, STATE), grate)


def matmul(left, right):
    return jnp.dot(left, right, preferred_element_type=jnp.float32)


def left_trans(left, right):
    return lax.dot_general(
        left, right, (((0,), (0,)), ((), ())), preferred_element_type=jnp.float32
    )


def right_trans(left, right):
    return lax.dot_general(
        left, right, (((1,), (1,)), ((), ())), preferred_element_type=jnp.float32
    )


def rms_scale(values):
    return lax.rsqrt(jnp.mean(values * values, axis=-1, keepdims=True) + EPSILON)


def norm_back(grad_out, values, scale_in, gain_in):
    scaled = grad_out * gain_in
    grad_in = scale_in * scaled - values * scale_in**3 * jnp.mean(
        scaled * values, axis=-1, keepdims=True
    )
    return (grad_in, jnp.sum(grad_out * values * scale_in, axis=0))


def silu_slope(values):
    logistic = jax.nn.sigmoid(values)
    return logistic * (1.0 + values * (1.0 - logistic))


def unit_count(width, ctx, fsdp):
    return ctx if width % (ctx * ctx) == 0 and ctx % fsdp == 0 else fsdp


def my_columns(array, units):
    span = array.shape[1] // units
    width = span // lax.axis_size("ctx")
    start = lax.axis_index("ctx") * width
    return [
        lax.dynamic_slice_in_dim(array, unit * span + start, width, 1) for unit in range(units)
    ]


def my_rows(array, units):
    span = array.shape[0] // units
    width = span // lax.axis_size("ctx")
    start = lax.axis_index("ctx") * width
    return [
        lax.dynamic_slice_in_dim(array, unit * span + start, width, 0) for unit in range(units)
    ]


def block_columns(array):
    width = array.shape[1] // lax.axis_size("ctx")
    return lax.dynamic_slice_in_dim(array, lax.axis_index("ctx") * width, width, 1)


def over_fsdp(array):
    return lax.all_gather(array, "fsdp", axis=0, tiled=True)


def to_blocks(array, units):
    ctx = lax.axis_size("ctx")
    rows = array.shape[0]
    width = array.shape[1] // units
    repeat = ctx // units
    pieces = array.reshape(rows, units, width).transpose(1, 0, 2)
    slots = jnp.repeat(pieces, repeat, axis=0) if repeat > 1 else pieces
    got = lax.all_to_all(slots, "ctx", 0, 0, tiled=True)
    if repeat > 1:
        first = units * lax.rem(lax.axis_index("ctx"), repeat)
        got = lax.dynamic_slice_in_dim(got, first, units, 0)
    return got.transpose(1, 0, 2).reshape(rows, units * width).astype(jnp.float32)


def rows_to_blocks(array, units):
    ctx = lax.axis_size("ctx")
    rows, columns = array.shape
    pieces = array.reshape(rows, ctx, columns // ctx).transpose(1, 0, 2)
    got = lax.all_to_all(pieces, "ctx", 0, 0, tiled=True)
    got = got.reshape(ctx, units, rows // units, columns // ctx).transpose(1, 0, 2, 3)
    return got.reshape(ctx * rows, columns // ctx).astype(jnp.float32)


def scatter_fsdp(*gradients):
    fsdp = lax.axis_size("fsdp")
    parts = [g.astype(BF16).reshape(fsdp, -1, g.shape[1]) for g in gradients]
    sizes = [part.shape[1] for part in parts]
    pad = -sum(sizes) % 16
    if pad:
        parts.append(jnp.zeros((fsdp, pad, gradients[0].shape[1]), BF16))
    joined = jnp.concatenate(parts, 1) if len(parts) > 1 else parts[0]
    joined = joined.reshape(-1, joined.shape[2])
    out = lax.psum_scatter(joined, "fsdp", scatter_dimension=0, tiled=True)
    starts = [sum(sizes[:i]) for i in range(len(sizes))]
    return [out[start : start + size] for start, size in zip(starts, sizes)]


def body(
    inputs,
    cotangent,
    norm_gain,
    query_proj,
    key_proj,
    value_proj,
    attn_proj,
    attn_gain,
    mixer_in,
    conv_taps,
    conv_bias,
    state_proj,
    step_proj,
    step_bias,
    decay_rate,
    skip_gain,
    mixer_out,
    ssm_gain,
    ffn_gain,
    gate_proj,
    up_proj,
    down_proj,
):
    ctx, fsdp = lax.axis_size("ctx"), lax.axis_size("fsdp")
    place = lax.axis_index("ctx")
    tokens = inputs[0].astype(jnp.float32)
    own, model = tokens.shape
    length = own * ctx
    inner = conv_bias.shape[0]
    mine = inner // ctx
    kv_mine = key_proj.shape[1] // ctx
    q_mine = query_proj.shape[1] // ctx
    hidden_units = unit_count(gate_proj.shape[1], ctx, fsdp)
    hidden_rows = hidden_units // fsdp
    hid = gate_proj.shape[1] // ctx
    group_size = query_proj.shape[1] // key_proj.shape[1]
    score_scale = HEAD ** (-0.5)

    src_part = jnp.concatenate(my_columns(mixer_in[:, :inner], fsdp), 1)
    state_part = my_rows(state_proj, 1)[0]
    step_part = jnp.concatenate(my_columns(step_proj, fsdp), 1)
    state_rows, step_rows = state_part.shape[0], step_part.shape[0]
    normed_all, grad_top, src_full, state_full, step_full = front(
        inputs[0],
        norm_gain[None],
        cotangent[0],
        src_part,
        jnp.pad(state_part, ((0, -state_rows % 16), (0, 0))),
        jnp.pad(step_part, ((0, -step_rows % 16), (0, 0))),
        0,
    )
    normed_all = normed_all.reshape(length, model)
    grad_top = grad_top.reshape(length, model)
    src_full = src_full.reshape(model, -1)
    state_full = state_full[:, :state_rows].reshape(-1, state_proj.shape[1])
    step_full = step_full[:, :step_rows].reshape(-1, mine)
    norm_scale = rms_scale(tokens)

    attn_pad = -attn_proj.shape[0] % ctx
    attn_rows_mine = (attn_proj.shape[0] + attn_pad) // ctx
    (
        query_proj, key_proj, value_proj, mixer_late, attn_proj, mixer_out, down_proj, gate_proj,
        up_proj, normed_all,
    ) = lax.optimization_barrier(
        (
            query_proj, key_proj, value_proj, mixer_in, attn_proj, mixer_out, down_proj, gate_proj,
            up_proj, normed_all,
        )
    )
    early_part = jnp.concatenate(
        [block_columns(query_proj), block_columns(key_proj), block_columns(value_proj)]
        + my_columns(mixer_late[:, inner:], fsdp),
        1,
    )
    out_part = jnp.concatenate(
        my_rows(jnp.pad(attn_proj, ((0, attn_pad), (0, 0))), 1) + my_rows(mixer_out, 1), 0
    )
    down_part = jnp.concatenate(my_rows(down_proj, hidden_rows), 0)
    ffn_part = jnp.concatenate(
        my_columns(gate_proj, hidden_units) + my_columns(up_proj, hidden_units), 1
    )
    rows_part = jnp.concatenate([out_part, down_part], 0)
    early_full = over_fsdp(early_part)
    rows_full = lax.all_gather(rows_part, "fsdp", axis=0)
    ffn_full = over_fsdp(ffn_part)
    attn_full = rows_full[:, :attn_rows_mine].reshape(-1, model)
    mixout_full = rows_full[:, attn_rows_mine : out_part.shape[0]].reshape(-1, model)
    down_full = rows_full[:, out_part.shape[0] :].reshape(-1, model)
    attn_width = attn_full.shape[0]

    def mine_of(vector):
        return jnp.concatenate(my_columns(vector.reshape(-1, inner), fsdp), 1)

    taps, bias, skip, gain_ssm, bias_step = (
        mine_of(conv_taps),
        mine_of(conv_bias),
        mine_of(skip_gain),
        mine_of(ssm_gain),
        mine_of(step_bias),
    )
    rates = jnp.concatenate(
        [
            lax.dynamic_slice_in_dim(
                decay_rate, unit * (inner // fsdp) + place * (mine // fsdp), mine // fsdp, 0
            )
            for unit in range(fsdp)
        ],
        0,
    ).T
    pad = -mine % LANES

    def padded(values):
        return jnp.pad(values, ((0, 0), (0, pad)))

    conv_src = matmul(normed_all, src_full).astype(BF16)

    padded_src = jnp.concatenate(
        [jnp.zeros((CONV - 1, mine), jnp.float32), conv_src.astype(jnp.float32)], 0
    )
    conv_pre = bias + sum(taps[tap][None] * padded_src[tap : tap + length] for tap in range(CONV))
    conv_act = jax.nn.silu(conv_pre).astype(BF16)
    conv_vals = conv_act.astype(jnp.float32)
    projected = sum_everywhere(matmul(conv_act, state_full).astype(BF16), 2).astype(jnp.float32)
    step_low = projected[:, :DT_RANK].astype(BF16)
    input_mat = projected[:, DT_RANK : DT_RANK + STATE]
    output_mat = projected[:, DT_RANK + STATE :]
    step_pre = matmul(step_low, step_full) + bias_step
    steps_dt = jax.nn.softplus(step_pre)
    in_b = jnp.broadcast_to(input_mat[:, :, None], (length, STATE, LANES))
    out_b = jnp.broadcast_to(output_mat[:, :, None], (length, STATE, LANES))
    rates_log2 = padded(-LOG2_E * rates)
    steps_pad, vals_pad = padded(steps_dt), padded(conv_vals)
    scan_out, states = scan_fwd(steps_pad, vals_pad, in_b, out_b, rates_log2)
    scan_out = scan_out[:, :mine]

    projected_in = matmul(normed_all, early_full).astype(BF16)
    queries = lax.all_to_all(projected_in[:, :q_mine], "ctx", 0, 1, tiled=True)
    keyvals = gather_shards(projected_in[:, q_mine : q_mine + 2 * kv_mine], 1)
    keys_all = keyvals[:, :, :kv_mine].transpose(1, 0, 2).reshape(length, KV_HEADS, HEAD)
    vals_all = keyvals[:, :, kv_mine:].transpose(1, 0, 2).reshape(length, KV_HEADS, HEAD)
    gate_z = projected_in[:, q_mine + 2 * kv_mine :].astype(jnp.float32)
    heads_q = queries.reshape(own, KV_HEADS, group_size, HEAD)
    row_ids = place * own + lax.broadcasted_iota(jnp.int32, (own, length), 0)
    col_ids = lax.broadcasted_iota(jnp.int32, (own, length), 1)
    allowed = (col_ids <= row_ids) & (col_ids > row_ids - WINDOW)

    def scores_of():
        raw = jnp.einsum("qhgd,khd->hgqk", heads_q, keys_all, preferred_element_type=jnp.float32)
        return jnp.where(allowed, raw * score_scale, -1e30)

    scores = scores_of()
    row_top = jnp.max(scores, axis=-1, keepdims=True)
    log_total = row_top + jnp.log(jnp.sum(jnp.exp(scores - row_top), axis=-1, keepdims=True))
    probs = jnp.exp(scores - log_total)
    probs_bf = probs.astype(BF16)
    attn_rows = jnp.einsum(
        "hgqk,khd->qhgd", probs_bf, vals_all, preferred_element_type=jnp.float32
    ).reshape(own, -1)
    attn_scale = rms_scale(attn_rows)
    branch_attn = (attn_rows * attn_scale * attn_gain).astype(BF16)

    def attn_to_channels(values):
        parts = jnp.pad(values.reshape(own, fsdp, -1), ((0, 0), (0, 0), (0, attn_pad)))
        parts = parts.reshape(own, fsdp, ctx, -1).transpose(2, 0, 1, 3).reshape(ctx, own, -1)
        return lax.all_to_all(parts, "ctx", 0, 0, tiled=True).reshape(length, -1)

    def attn_to_tokens(values):
        parts = values.reshape(ctx, own, -1)
        got = lax.all_to_all(parts, "ctx", 0, 0, tiled=True)
        got = got.reshape(ctx, own, fsdp, -1).transpose(1, 2, 0, 3).reshape(own, fsdp, -1)
        return got[:, :, : attn_proj.shape[0]].reshape(own, -1)

    branch_attn_c = attn_to_channels(branch_attn)

    ssm_raw = scan_out + skip * conv_vals
    gate_act = jax.nn.silu(gate_z)
    ssm_gated = ssm_raw * gate_act
    square = total_of(jnp.sum(ssm_gated * ssm_gated, axis=-1), 3)
    ssm_scale = lax.rsqrt(square / inner + EPSILON)[:, None]
    branch_ssm = (ssm_gated * ssm_scale * gain_ssm).astype(BF16)
    middle = tokens + 0.5 * reduce_products(
        [(branch_attn_c, attn_full), (branch_ssm, mixout_full)], (False, False), 4
    )
    ffn_scale = rms_scale(middle)
    ffn_in = (middle * ffn_scale * ffn_gain).astype(BF16)
    if ctx == 8:
        ffn_all, hidden, grad_pair, ffn_out, grad_ffn_in = ffn_both_ways(
            ffn_in, grad_top, ffn_full, down_full, 5
        )
    else:
        ffn_all = gather_tokens(ffn_in, 5)
        pre = matmul(ffn_all, ffn_full)
        gate_pre, up_pre = pre[:, :hid], pre[:, hid:]
        gate_silu = jax.nn.silu(gate_pre)
        hidden = (gate_silu * up_pre).astype(BF16)
        ffn_out = reduce_products([(hidden, down_full)], (False,), 6)
        grad_hidden = right_trans(grad_top, down_full)
        grad_gate = (grad_hidden * up_pre * silu_slope(gate_pre)).astype(BF16)
        grad_up = (grad_hidden * gate_silu).astype(BF16)
        grad_pair = jnp.concatenate([grad_gate, grad_up], 1)
        grad_ffn_in = reduce_products([(grad_pair, ffn_full)], (True,), 7)
    output = middle + ffn_out

    down_dw = left_trans(hidden, grad_top).astype(BF16)
    pair_dw = left_trans(ffn_all, grad_pair).astype(BF16)
    grad_ffn_in, down_dw, pair_dw = lax.optimization_barrier((grad_ffn_in, down_dw, pair_dw))
    (down_grad,) = scatter_fsdp(down_dw)
    (pair_grad,) = scatter_fsdp(pair_dw)
    grad_middle, grad_ffn_gain = norm_back(grad_ffn_in, middle, ffn_scale, ffn_gain)
    grad_middle = grad_middle + cotangent[0].astype(jnp.float32)
    grad_branch = (0.5 * grad_middle).astype(BF16)
    branch_all = gather_tokens(grad_branch, 8)
    branch_all, down_grad = lax.optimization_barrier((branch_all, down_grad))
    attn_grad, mixout_grad = scatter_fsdp(
        left_trans(branch_attn_c, branch_all), left_trans(branch_ssm, branch_all)
    )

    grad_attn = attn_to_tokens(right_trans(branch_all, attn_full).astype(BF16)).astype(jnp.float32)
    grad_attn_raw, grad_attn_gain = norm_back(grad_attn, attn_rows, attn_scale, attn_gain)
    grad_heads = grad_attn_raw.astype(BF16).reshape(own, KV_HEADS, group_size, HEAD)
    grad_probs = jnp.einsum(
        "qhgd,khd->hgqk", grad_heads, vals_all, preferred_element_type=jnp.float32
    )
    row_dot = jnp.sum(probs * grad_probs, axis=-1, keepdims=True)
    grad_scores = (probs * (grad_probs - row_dot)).astype(BF16)
    grad_queries = score_scale * jnp.einsum(
        "hgqk,khd->qhgd", grad_scores, keys_all, preferred_element_type=jnp.float32
    ).reshape(own, -1)
    grad_keys = score_scale * jnp.einsum(
        "hgqk,qhgd->khd", grad_scores, heads_q, preferred_element_type=jnp.float32
    )
    grad_vals = jnp.einsum(
        "hgqk,qhgd->khd", probs_bf, grad_heads, preferred_element_type=jnp.float32
    )
    grad_queries = lax.all_to_all(
        grad_queries.astype(BF16).reshape(own, ctx, -1).transpose(1, 0, 2), "ctx", 0, 0, tiled=True
    ).reshape(length, -1)
    grad_kv = jnp.concatenate(
        [
            grad_keys.reshape(length, ctx, kv_mine).transpose(1, 0, 2),
            grad_vals.reshape(length, ctx, kv_mine).transpose(1, 0, 2),
        ],
        2,
    ).astype(BF16)
    grad_kv = jnp.sum(
        lax.all_to_all(grad_kv, "ctx", 0, 0, tiled=True).astype(jnp.float32), axis=0
    ).astype(BF16)

    grad_norm = right_trans(branch_all, mixout_full)
    grad_ssm_gain = jnp.sum(grad_norm * ssm_gated * ssm_scale, axis=0)
    grad_norm, pair_grad = lax.optimization_barrier((grad_norm, pair_grad))
    scaled = grad_norm * gain_ssm
    mean_dot = total_of(jnp.sum(scaled * ssm_gated, axis=-1), 9)[:, None] / inner
    grad_gated = ssm_scale * scaled - ssm_gated * ssm_scale**3 * mean_dot
    grad_scan = grad_gated * gate_act
    grad_gate_z = grad_gated * ssm_raw * silu_slope(gate_z)
    grad_skip = jnp.sum(grad_scan * conv_vals, axis=0)
    grad_gate_bf = grad_gate_z.astype(BF16)
    grad_early = jnp.concatenate([grad_queries, grad_kv, grad_gate_bf], 1)
    (early_grad,) = scatter_fsdp(left_trans(normed_all, grad_early))
    grad_steps, grad_drive, grad_input_mat, grad_output_mat, grad_rate = scan_bwd(
        steps_pad, vals_pad, padded(grad_scan), in_b, out_b, rates_log2, states
    )
    grad_steps, attn_grad, mixout_grad = lax.optimization_barrier(
        (grad_steps, attn_grad, mixout_grad)
    )
    grad_steps, grad_drive, grad_rate = (
        grad_steps[:, :mine],
        grad_drive[:, :mine],
        -grad_rate[:, :mine],
    )
    grad_pre_full = grad_steps * jax.nn.sigmoid(step_pre)
    grad_step_bias = jnp.sum(grad_pre_full, axis=0)
    grad_pre = grad_pre_full.astype(BF16)
    step_dw = left_trans(step_low, grad_pre)
    grad_projected = sum_everywhere(
        jnp.concatenate(
            [right_trans(grad_pre, step_full), grad_input_mat, grad_output_mat], 1
        ).astype(BF16),
        10,
    )
    grad_state_proj = left_trans(conv_act, grad_projected)
    grad_conv_act = (
        right_trans(grad_projected, state_full) + grad_scan * skip + grad_drive
    ).astype(BF16)
    grad_conv_act, early_grad = lax.optimization_barrier((grad_conv_act, early_grad))
    grad_conv = grad_conv_act.astype(jnp.float32) * silu_slope(conv_pre)
    grad_conv_bias = jnp.sum(grad_conv, axis=0)
    grad_taps = jnp.stack(
        [jnp.sum(grad_conv * padded_src[tap : tap + length], axis=0) for tap in range(CONV)]
    )
    conv_tail = jnp.concatenate([grad_conv, jnp.zeros((CONV - 1, mine), jnp.float32)], 0)
    grad_src = sum(
        taps[tap][None] * conv_tail[CONV - 1 - tap : CONV - 1 - tap + length]
        for tap in range(CONV)
    )
    grad_src = grad_src.astype(BF16)
    src_grad, step_grad = scatter_fsdp(left_trans(normed_all, grad_src), step_dw)
    grad_normed = reduce_products(
        [(grad_early, early_full), (grad_src, src_full)], (True, True), 11
    )
    grad_tokens, grad_norm_gain = norm_back(grad_normed, tokens, norm_scale, norm_gain)
    grad_tokens = grad_tokens + grad_middle

    channel = jnp.concatenate(
        [
            grad_taps,
            jnp.stack([grad_conv_bias, grad_step_bias, grad_skip, grad_ssm_gain]),
            grad_rate,
            grad_state_proj.T,
        ],
        0,
    )
    gains = jnp.stack([grad_norm_gain, grad_attn_gain, grad_ffn_gain])
    channel, gains = settle_small(
        jnp.pad(channel, ((0, -channel.shape[0] % (8 * fsdp)), (0, 0))),
        jnp.pad(gains, ((0, 5), (0, 0))),
        12,
    )
    channel = channel.reshape(ctx, -1, fsdp, mine // fsdp).transpose(1, 2, 0, 3)
    channel = channel.reshape(-1, inner)
    sum_norm_gain, sum_attn_gain, sum_ffn_gain = gains[0], gains[1], gains[2]
    pair_blocks = to_blocks(
        jnp.concatenate(
            [
                pair_grad[:, :hid].reshape(-1, hidden_units, hid // hidden_units),
                pair_grad[:, hid:].reshape(-1, hidden_units, hid // hidden_units),
            ],
            0,
        ).reshape(-1, hid),
        hidden_units,
    )
    half = pair_grad.shape[0]
    return (
        output[None],
        grad_tokens[None],
        sum_norm_gain,
        early_grad[:, :q_mine].astype(jnp.float32),
        early_grad[:, q_mine : q_mine + kv_mine].astype(jnp.float32),
        early_grad[:, q_mine + kv_mine : q_mine + 2 * kv_mine].astype(jnp.float32),
        rows_to_blocks(attn_grad, 1)[: attn_proj.shape[0]],
        sum_attn_gain,
        to_blocks(jnp.concatenate([src_grad, early_grad[:, q_mine + 2 * kv_mine :]], 1), 2 * fsdp),
        channel[:CONV],
        channel[CONV],
        channel[CONV + 4 + STATE : CONV + 4 + STATE + state_proj.shape[1]].T,
        to_blocks(step_grad, fsdp),
        channel[CONV + 1],
        channel[CONV + 4 : CONV + 4 + STATE].T,
        channel[CONV + 2],
        rows_to_blocks(mixout_grad, 1),
        channel[CONV + 3],
        sum_ffn_gain,
        pair_blocks[:half],
        pair_blocks[half:],
        rows_to_blocks(down_grad, hidden_rows),
    )


def solution(mesh):
    rows, whole = P("fsdp", None), P()
    blocks, sequence = P("fsdp", "ctx"), P("fsdp", "ctx", None)
    return jax.shard_map(
        body,
        mesh=mesh,
        in_specs=(
            sequence, sequence, whole, rows, rows, rows, rows, whole, rows, whole, whole,
            rows, rows, whole, whole, whole, rows, whole, whole, rows, rows, rows,
        ),
        out_specs=(
            sequence, sequence, whole, blocks, blocks, blocks, blocks, whole, blocks, whole, whole,
            whole, blocks, whole, whole, whole, blocks, whole, whole, blocks, blocks, blocks,
        ),
        check_vma=False,
    )
```

time: 5270 us -> 857 us (0.16)
  waiting for transfers between devices: 2180 us -> 51.2 us
  local copies, waits for them, and re-layouts: 1750 us -> 202 us
  other arithmetic: 825 us -> 78.8 us
  Pallas kernels: 0 us -> 367 us
  matrix products: 262 us -> 84 us
  blocking collectives: 169 us -> 0 us
    pad x288 -> x6, local copies, waits for them, and re-layouts: 1320 us -> 4.73 us  [the longest x4 3.35 us: padded(): return jnp.pad(values, ((0, 0), (0, pad)))]
    unnamed x47 -> x8, waiting for transfers between devices: 740 us -> 0.65 us
    all_gather x9 -> x3, waiting for transfers between devices: 688 us -> 16.1 us  [the longest x2 16.1 us: over_fsdp(): return lax.all_gather(array, 'fsdp', axis=0, tiled=True)]
    reduce_scatter x4 -> x5, waiting for transfers between devices: 461 us -> 18.9 us  [scatter_fsdp(): out = lax.psum_scatter(joined, 'fsdp', scatter_dimension=0, tiled=True)]
    pallas_call x0 -> x13, Pallas kernels: none -> 367 us  [the longest x1 69.6 us: ffn_both_ways(): pl.pallas_call(ffn_kernel, out_shape=[jax.ShapeDtypeStruct((ctx, rows, mo...]
    add x187 -> x1, other arithmetic: 315 us -> 0.01 us  [body(): row_ids = place * own + lax.broadcasted_iota(jnp.int32, (own, length), 0)]
    psum x2 -> x0, waiting for transfers between devices: 271 us -> none  [body(): lax.psum((grad_norm_gain, grad_attn_gain, grad_taps, grad_conv_bias, grad...]
    mul x152 -> x1, other arithmetic: 192 us -> 0.08 us  [body(): rates_log2 = padded(-LOG2_E * rates)]
  transfers between devices with their start and end apart: 49 -> 19, of which waited for: 29 -> 7; matrix products, arithmetic and copies ran while one was open for 20% -> 36% of each run, Pallas kernels for 0% -> 30%
where the time goes in v1:
time: 857 us; the launch traced here: 847 us
  Pallas kernels  367 us (43%)
  local copies, waits for them, and re-layouts  202 us (24%)
  matrix products  84 us (10%)
  other arithmetic  78.8 us (9%)
  waiting for transfers between devices  51.2 us (6%)
  starting transfers between devices  47.7 us (6%)
  between operations  16 us (2%)
    pallas_call x1, Pallas kernels, ffn_both_ways(): pl.pallas_call(ffn_kernel, out_shape=[jax.ShapeDtypeStruct((ctx, rows, mo...  69.6 us
    pallas_call x2, Pallas kernels, reduce_products(): pl.pallas_call(functools.partial(reduce_kernel, bits, trans), out_shape=j...  57.9 us
    pallas_call x1, Pallas kernels, front(): pl.pallas_call(functools.partial(front_kernel, bits, count), out_shape=[s...  44.4 us
    pallas_call x2, Pallas kernels, gather_shards(): pl.pallas_call(functools.partial(gather_kernel, bits), out_shape=jax.Shap...  40.4 us
    pallas_call x2, Pallas kernels, sum_everywhere(): pl.pallas_call(functools.partial(sum_kernel, ctx), out_shape=jax.ShapeDty...  40 us
    pallas_call x1, Pallas kernels, scan_bwd(): pl.pallas_call(scan_bwd_kernel, grid=(count,), in_specs=[row, row, row, m...  38.8 us
    pallas_call x1, Pallas kernels, settle_small(): pl.pallas_call(functools.partial(settle_kernel, bits, ctx, fsdp), out_sha...  37.8 us
    dot_general x8, matrix products, left_trans(): lax.dot_general(left, right, (((0,), (0,)), ((), ())), preferred_element_...  32.6 us
  transfers between devices with their start and end apart: 19, of which 7 were waited for; matrix products, arithmetic and copies ran while one was open for 36% of the time, Pallas kernels for 30%

profile of v1, /device:TPU:1, one launch (start us, length us, event | category | flops | bytes accessed | tf_op | source)
XLA Modules:
  0.0 846.6 jit_solution(13196042412221426945)
XLA Ops:
  21.7 44.4 %front.1 = (bf16[8,128,1600]{2,1,0:T(8,128)(2,1)}, bf16[8,128,1600]{2,1,0:T(8,128)(2,1)}, bf16[4,400,400]{2,1,0:T(8,128)(2,1)}, bf16[4,112,132]{2,1,0:T(8,128)(2,1)}, bf16[4,32,400]{2,1,0:T(8,128)(2,1)}) custom-call(bf16[128,1600]{1,0:T(8,128)(2,1)} %bitcast.277, f32[1,1600]{1,0:T(1,128)} %broadcast_in_dim.24.gain_ref, bf16[128,1600]{1,0:T(8,128)(2,1)} %bitcast.298, ...), custom_call_target="tpu_custom_call" | custom-call | tf_op jit(solution)/shard_map/front/pallas_call | solution.py:263
  71.6 7.1 copy.354
  85.1 4.3 concatenate.91
  91.8 4.1 fusion.21
  101.4 18.4 %sum_everywhere.2 = bf16[8,128,132]{2,1,0:T(8,128)(2,1)} custom-call(bf16[8,128,132]{2,1,0:T(8,128)(2,1)} %bitcast.308), custom_call_target="tpu_custom_call" | custom-call | tf_op jit(solution)/shard_map/sum_everywhere/pallas_call | solution.py:431
  125.8 5.9 broadcast_in_dim.27.in_ref
  131.7 5.8 broadcast_in_dim.28.out_ref
  137.6 22.7 %scan_forward.1 = (f32[1024,512]{1,0:T(8,128)S(1)}, f32[1024,16,512]{2,1,0:T(8,128)}) custom-call(f32[1024,512]{1,0:T(8,128)S(1)} %pad.35.steps_ref, f32[1024,512]{1,0:T(8,128)} %pad.36.drive_ref, f32[1024,16,128]{2,1,0:T(8,128)} %broadcast_in_dim.27.in_ref, f32[1024,16,128]{2,1,0:T(8,128)} %broadcast_in_dim.28.out_ref, f32[16,512]{1,0:T(8,128)S(1)} %pad.37.rate_ref), custom_call_target="tpu_custom_call" | custom-call | tf_op jit(solution)/shard_map/scan_forward/pallas_call | solution.py:723
  162.8 5.7 convolution_convert_fusion.4
  169.8 17.8 %gather_shards.2 = bf16[8,1024,80]{2,1,0:T(8,128)(2,1)} custom-call(bf16[1024,80]{1,0:T(8,128)(2,1)} %slice.250.x_ref), custom_call_target="tpu_custom_call" | custom-call | tf_op jit(solution)/shard_map/gather_shards/pallas_call | solution.py:136
  187.7 4.3 slice_bitcast_fusion
  200.5 4.5 multiply_reduce_fusion.7
  205.0 6.2 total_of.2
  224.6 4.0 all-to-all-start.1
  250.8 24.4 %reduce_products.2 = f32[128,1600]{1,0:T(8,128)} custom-call(bf16[8,128,200]{2,1,0:T(8,128)(2,1)} %copy.356.refs_0_, bf16[8,128,400]{2,1,0:T(8,128)(2,1)} %bitcast.296, bf16[200,1600]{1,0:T(8,128)(2,1)} %reshape.415.refs_2_, bf16[400,1600]{1,0:T(8,128)(2,1)} %reshape.416.refs_3_), custom_call_target="tpu_custom_call" | custom-call | tf_op jit(solution)/shard_map/reduce_products/pallas_call | solution.py:386
  278.1 16.1 %all-gather.8.cloned.1.call-done.pair_w = bf16[1600,1376]{1,0:T(8,128)(2,1)} async-done(((bf16[400,1376]{1,0:T(8,128)(2,1)}), bf16[1600,1376]{1,0:T(8,128)(2,1)}) %all-gather.8.cloned.1.call-update) | async-done | bytes 4403216 | tf_op jit(solution)/shard_map/all_gather | solution.py:897
  294.2 69.6 %ffn_both_ways.1 = (bf16[8,128,1600]{2,1,0:T(8,128)(2,1)}, bf16[8,128,688]{2,1,0:T(8,128)(2,1)}, bf16[8,128,1376]{2,1,0:T(8,128)(2,1)}, f32[128,1600]{1,0:T(8,128)}, f32[128,1600]{1,0:T(8,128)}) custom-call(bf16[128,1600]{1,0:T(8,128)(2,1)} %multiply_convert_fusion.4.x_ref, bf16[8,128,1600]{2,1,0:T(8,128)(2,1)} %get-tuple-element.76.top_ref, ...), custom_call_target="tpu_custom_call" | custom-call | tf_op jit(solution)/shard_map/ffn_both_ways/pallas_call | solution.py:661
  363.8 6.2 bitcast_convert_fusion.1
  370.0 7.2 bitcast_convert_fusion
  387.5 22.6 %gather_shards.3 = bf16[8,128,1600]{2,1,0:T(8,128)(2,1)} custom-call(bf16[128,1600]{1,0:T(8,128)(2,1)} %get-tuple-element.279.x_ref), custom_call_target="tpu_custom_call" | custom-call | tf_op jit(solution)/shard_map/gather_shards/pallas_call | solution.py:136
  410.1 18.8 %reduce-scatter.6.cloned.1.call-done = bf16[176,1600]{1,0:T(8,128)(2,1)} async-done(((bf16[704,1600]{1,0:T(8,128)(2,1)}), bf16[176,1600]{1,0:T(8,128)(2,1)}) %reduce-scatter.6.cloned.1.call-update) | async-done | bytes 563216 | tf_op jit(solution)/shard_map/reduce_scatter | solution.py:932
  433.0 4.8 all-to-all-start.2
  437.9 5.1 convolution_convert_fusion.2
  460.4 7.0 fusion.27
  467.5 9.5 %fusion = (f32[5,5,128]{2,1,0:T(8,128)S(1)}, f32[5,1024,128,5]{2,1,3,0:T(8,128)}) fusion(f32[5,5,128,1024]{2,3,1,0:T(8,128)} %copy-done.7, f32[5,5,128]{2,1,0:T(8,128)S(1)} %log_add_fusion, bf16[1024,5,64,1]{0,2,3,1:T(8,128)(2,1)S(1)} %bitcast.292, bf16[128,5,5,64]{0,3,2,1:T(8,128)(2,1)S(1)} %subtract_convert_fusion), kind=kOutput, calls=%fused_computation.2 | convolution fusion | flops 429257600 | bytes 27304960 | tf_op jit(solution)/shard_map/qhgd,khd->hgqk/dot_general | solution.py:1158
  477.0 6.6 fusion.2
  486.4 4.3 all-to-all-start.3
  490.7 5.0 fusion.26
  497.2 6.3 all-to-all-start.4
  503.5 5.2 fusion.74
  513.1 5.1 all-to-all-done.4
  522.9 4.2 multiply_reduce_fusion
  527.1 9.5 %total_of.3 = f32[8,128]{1,0:T(8,128)} custom-call(f32[8,128]{1,0:T(8,128)} %bitcast.337), custom_call_target="tpu_custom_call" | custom-call | tf_op jit(solution)/shard_map/total_of/pallas_call | solution.py:461
  537.3 5.1 multiply_reduce_fusion.1
  543.3 4.5 convolution_convert_fusion
  551.0 4.3 all-to-all-start.10
  557.8 5.9 all-to-all-done.10
  570.2 38.8 %scan_backward.1 = (f32[1024,512]{1,0:T(8,128)S(1)}, f32[1024,512]{1,0:T(8,128)S(1)}, f32[8,8,2048]{2,1,0:T(8,128)S(1)}, f32[8,8,2048]{2,1,0:T(8,128)S(1)}, f32[16,512]{1,0:T(8,128)S(1)}) custom-call(f32[1024,512]{1,0:T(8,128)} %copy-done.2, f32[1024,512]{1,0:T(8,128)} %pad.36.drive_ref, f32[1024,512]{1,0:T(8,128)} %pad.38.grad_ref, ...), custom_call_target="tpu_custom_call" | custom-call | tf_op jit(solution)/shard_map/scan_backward/pallas_call | solution.py:812
  616.4 21.6 %sum_everywhere.3 = bf16[8,128,132]{2,1,0:T(8,128)(2,1)} custom-call(bf16[8,128,132]{2,1,0:T(8,128)(2,1)} %pad_maximum_fusion.3.x_ref), custom_call_target="tpu_custom_call" | custom-call | tf_op jit(solution)/shard_map/sum_everywhere/pallas_call | solution.py:431
  659.3 6.2 multiply_reduce_fusion.2
  671.2 5.0 convolution_convert_fusion.1
  679.0 4.9 all-to-all-start.9
  712.4 33.5 %reduce_products.3 = f32[128,1600]{1,0:T(8,128)} custom-call(bf16[8,128,680]{2,1,0:T(8,128)(2,1)} %pad_maximum_fusion.refs_0_, bf16[8,128,400]{2,1,0:T(8,128)(2,1)} %bitcast.297, bf16[1600,680]{1,0:T(8,128)(2,1)} %all-gather.6.cloned.1.call-done.refs_2_, bf16[1600,400]{1,0:T(8,128)(2,1)} %bitcast.314), custom_call_target="tpu_custom_call" | custom-call | tf_op jit(solution)/shard_map/reduce_products/pallas_call | solution.py:386
  748.2 37.8 %settle_small.1 = (f32[8,160,400]{2,1,0:T(8,128)}, f32[8,1600]{1,0:T(8,128)}) custom-call(f32[160,400]{1,0:T(8,128)} %pad.39.channel_ref, f32[8,1600]{1,0:T(8,128)} %select_maximum_fusion.gain_ref), custom_call_target="tpu_custom_call" | custom-call | tf_op jit(solution)/shard_map/settle_small/pallas_call | solution.py:535
  786.0 4.8 reshape.437
  790.9 4.8 copy.434
  798.5 3.9 all-to-all-start.7
  809.7 4.2 all-to-all-start.6
  (416 shorter events, 252.6 us)
Async XLA Ops:
  7.2 72.5 %copy-start = (bf16[800,1600]{1,0:T(8,128)(2,1)S(1)}, bf16[800,1600]{1,0:T(8,128)(2,1)}, u32[]{:S(2)}) copy-start(bf16[800,1600]{1,0:T(8,128)(2,1)} %param.38) | copy-start | bytes 7680004
  7.2 155.6 %all-gather.6.cloned.1.call-start = ((), (), s32[]{:S(2)}) async-start(), calls=%async_computation.16 | async-start | bytes 3072000 | tf_op jit(solution)/shard_map/all_gather | solution.py:897
  71.5 164.6 %all-gather.10.cloned.1.call-start = ((), (), s32[]{:S(2)}) async-start(), calls=%async_computation.23 | async-start | bytes 5457920 | tf_op jit(solution)/shard_map/all_gather | solution.py:1021
  82.3 211.9 %all-gather.8.cloned.1.call-start = ((), (), s32[]{:S(2)}) async-start(), calls=%async_computation.17 | async-start | bytes 5632000 | tf_op jit(solution)/shard_map/all_gather | solution.py:897
  91.4 30.2 %copy-start.62 = (bf16[100,400]{1,0:T(8,128)(2,1)}, bf16[100,400]{1,0:T(8,128)(2,1)S(1)}, u32[]{:S(2)}) copy-start(bf16[100,400]{1,0:T(8,128)(2,1)S(1)} %reshape.412) | copy-start | bytes 240004
  91.8 8.1 copy-start.53
  99.9 21.6 %copy-start.9 = (bf16[1024,400]{1,0:T(8,128)(2,1)}, bf16[1024,400]{1,0:T(8,128)(2,1)S(1)}, u32[]{:S(2)}) copy-start(bf16[1024,400]{1,0:T(8,128)(2,1)S(1)} %get-tuple-element.285) | copy-start | bytes 2457604
  124.4 13.2 %copy-start.2 = (f32[1024,512]{1,0:T(8,128)}, f32[1024,512]{1,0:T(8,128)S(1)}, u32[]{:S(2)}) copy-start(f32[1024,512]{1,0:T(8,128)S(1)} %pad.35.steps_ref) | copy-start | bytes 6291460
  196.0 15.3 %copy-start.21 = (bf16[1024,8,40]{0,2,1:T(8,128)(2,1)}, bf16[1024,8,40]{0,2,1:T(8,128)(2,1)S(1)}, u32[]{:S(2)}) copy-start(bf16[1024,8,40]{0,2,1:T(8,128)(2,1)S(1)} %copy.345) | copy-start | bytes 1966084
  197.0 14.2 %all-to-all-start = ((bf16[8,128,200]{1,2,0:T(8,128)(2,1)}), bf16[8,128,200]{1,2,0:T(8,128)(2,1)S(1)}, u32[]{:S(2)}, u32[]{:S(2)}) async-start(bf16[8,128,200]{1,2,0:T(8,128)(2,1)} %copy.346), calls=%async_computation | async-start | bytes 819200 | tf_op jit(solution)/shard_map/all_to_all | solution.py:1074
  224.6 10.5 %all-to-all-start.1 = ((bf16[8,128,200]{1,2,0:T(8,128)(2,1)}), bf16[8,128,200]{1,2,0:T(8,128)(2,1)S(1)}, u32[]{:S(2)}, u32[]{:S(2)}) async-start(bf16[8,128,200]{1,2,0:T(8,128)(2,1)} %copy.349), calls=%async_computation.1 | async-start | bytes 819200 | tf_op jit(solution)/shard_map/all_to_all | solution.py:1102
  228.6 200.3 %reduce-scatter.6.cloned.1.call-start = ((), (), s32[]{:S(2)}) async-start(), calls=%async_computation.18 | async-start | bytes 2928640 | tf_op jit(solution)/shard_map/reduce_scatter | solution.py:932
  250.8 24.4 %copy-start.18 = (bf16[1,128,1600]{2,1,0:T(8,128)(2,1)S(1)}, bf16[1,128,1600]{2,1,0:T(8,128)(2,1)}, u32[]{:S(2)}) copy-start(bf16[1,128,1600]{2,1,0:T(8,128)(2,1)} %copy.340) | copy-start | bytes 1228804
  294.2 69.6 %copy-start.42 = (bf16[8,128,1600]{2,1,0:T(8,128)(2,1)S(1)}, bf16[8,128,1600]{2,1,0:T(8,128)(2,1)}, u32[]{:S(2)}) copy-start(bf16[8,128,1600]{2,1,0:T(8,128)(2,1)} %get-tuple-element.76.top_ref) | copy-start | bytes 9830404
  383.4 136.6 %reduce-scatter.8.cloned.1.call-start = ((), (), s32[]{:S(2)}) async-start(), calls=%async_computation.19 | async-start | bytes 5632000 | tf_op jit(solution)/shard_map/reduce_scatter | solution.py:932
  387.5 41.4 %copy-start.47 = (bf16[200,1600]{1,0:T(8,128)(2,1)S(1)}, bf16[200,1600]{1,0:T(8,128)(2,1)}, u32[]{:S(2)}) copy-start(bf16[200,1600]{1,0:T(8,128)(2,1)} %reshape.415.refs_2_) | copy-start | bytes 1920004
  433.0 20.9 %all-to-all-start.2 = ((bf16[8,128,200]{1,2,0:T(8,128)(2,1)}), bf16[8,128,200]{1,2,0:T(8,128)(2,1)}, u32[]{:S(2)}, u32[]{:S(2)}) async-start(bf16[8,128,200]{1,2,0:T(8,128)(2,1)} %bitcast.268), calls=%async_computation.3 | async-start | bytes 819200 | tf_op jit(solution)/shard_map/all_to_all | solution.py:1106
  437.9 128.0 %reduce-scatter.10.cloned.1.call-start = ((), (), s32[]{:S(2)}) async-start(), calls=%async_computation.20 | async-start | bytes 2662400 | tf_op jit(solution)/shard_map/reduce_scatter | solution.py:932
  460.4 16.5 %slice-start = ((s8[13107200]{0:T(1024)(128)(4,1)}), s8[4194304]{0:T(1024)(128)(4,1)S(1)}, s32[]{:S(2)}) async-start(s8[13107200]{0:T(1024)(128)(4,1)} %bitcast.271), calls=%async_computation.24 | async-start | bytes 8388608
  460.4 16.5 %slice-start.1 = ((s8[13107200]{0:T(1024)(128)(4,1)}), s8[4194304]{0:T(1024)(128)(4,1)S(1)}, s32[]{:S(2)}) async-start(s8[13107200]{0:T(1024)(128)(4,1)} %bitcast.271), calls=%async_computation.25 | async-start | bytes 8388608
  467.5 9.5 %slice-start.2 = ((s8[13107200]{0:T(1024)(128)(4,1)}), s8[4194304]{0:T(1024)(128)(4,1)S(1)}, s32[]{:S(2)}) async-start(s8[13107200]{0:T(1024)(128)(4,1)} %bitcast.271), calls=%async_computation.26 | async-start | bytes 8388608
  467.5 9.5 %slice-start.3 = ((s8[13107200]{0:T(1024)(128)(4,1)}), s8[524288]{0:T(1024)(128)(4,1)S(1)}, s32[]{:S(2)}) async-start(s8[13107200]{0:T(1024)(128)(4,1)} %bitcast.271), calls=%async_computation.27 | async-start | bytes 1048576
  486.4 10.8 %all-to-all-start.3 = ((bf16[8,128,200]{1,2,0:T(8,128)(2,1)}), bf16[8,128,200]{1,2,0:T(8,128)(2,1)}, u32[]{:S(2)}, u32[]{:S(2)}) async-start(bf16[8,128,200]{1,2,0:T(8,128)(2,1)} %bitcast.309), calls=%async_computation.4 | async-start | bytes 819200 | tf_op jit(solution)/shard_map/all_to_all | solution.py:1172
  497.2 21.0 %all-to-all-start.4 = ((bf16[8,1024,80]{1,2,0:T(8,128)(2,1)}), bf16[8,1024,80]{1,2,0:T(8,128)(2,1)}, u32[]{:S(2)}, u32[]{:S(2)}) async-start(bf16[8,1024,80]{1,2,0:T(8,128)(2,1)} %pad_maximum_fusion.1), calls=%async_computation.5 | async-start | bytes 2621440 | tf_op jit(solution)/shard_map/all_to_all | solution.py:1183
  503.5 155.8 %reduce-scatter.12.cloned.1.call-start = ((), (), s32[]{:S(2)}) async-start(), calls=%async_computation.21 | async-start | bytes 3072000 | tf_op jit(solution)/shard_map/reduce_scatter | solution.py:932
  513.1 29.2 %copy-start.48 = (bf16[8,128,200]{2,1,0:T(8,128)(2,1)}, bf16[8,128,200]{2,1,0:T(8,128)(2,1)S(1)}, u32[]{:S(2)}) copy-start(bf16[8,128,200]{2,1,0:T(8,128)(2,1)S(1)} %copy.369) | copy-start | bytes 1228804
  519.9 22.4 %copy-start.57 = (bf16[1024,80]{1,0:T(8,128)(2,1)}, bf16[1024,80]{1,0:T(8,128)(2,1)S(1)}, u32[]{:S(2)}) copy-start(bf16[1024,80]{1,0:T(8,128)(2,1)S(1)} %copy.367) | copy-start | bytes 491524
  522.9 14.4 %copy-start.10 = (bf16[1024,400]{1,0:T(8,128)(2,1)S(1)}, bf16[1024,400]{1,0:T(8,128)(2,1)}, u32[]{:S(2)}) copy-start(bf16[1024,400]{1,0:T(8,128)(2,1)} %copy-done.9) | copy-start | bytes 2457604
  522.9 14.4 %copy-start.12 = (f32[1024,400]{1,0:T(8,128)S(1)}, f32[1024,400]{1,0:T(8,128)}, u32[]{:S(2)}) copy-start(f32[1024,400]{1,0:T(8,128)} %get-tuple-element.284) | copy-start | bytes 4915204
  522.9 14.4 %copy-start.13 = (f32[1024,400]{1,0:T(8,128)S(1)}, f32[1024,400]{1,0:T(8,128)}, u32[]{:S(2)}) copy-start(f32[1024,400]{1,0:T(8,128)} %copy.368) | copy-start | bytes 4915204
  551.0 12.7 %all-to-all-start.10 = ((bf16[8,172,200]{2,1,0:T(8,128)(2,1)}), bf16[8,172,200]{2,1,0:T(8,128)(2,1)}, u32[]{:S(2)}, u32[]{:S(2)}) async-start(bf16[8,172,200]{2,1,0:T(8,128)(2,1)} %copy.391), calls=%async_computation.15 | async-start | bytes 1441792 | tf_op jit(solution)/shard_map/all_to_all | solution.py:918
  556.5 12.1 %copy-start.14 = (f32[1024,400]{1,0:T(8,128)S(1)}, f32[1024,400]{1,0:T(8,128)}, u32[]{:S(2)}) copy-start(f32[1024,400]{1,0:T(8,128)} %get-tuple-element.275) | copy-start | bytes 4915204
  570.2 41.0 %copy-start.80 = (f32[1,400]{1,0:T(1,128)S(1)}, f32[1,400]{1,0:T(1,128)}, u32[]{:S(2)}) copy-start(f32[1,400]{1,0:T(1,128)} %copy-done.79) | copy-start | bytes 4804
  614.9 28.6 %copy-start.24 = (bf16[1024,400]{1,0:T(8,128)(2,1)S(1)}, bf16[1024,400]{1,0:T(8,128)(2,1)}, u32[]{:S(2)}) copy-start(bf16[1024,400]{1,0:T(8,128)(2,1)} %copy-done.23) | copy-start | bytes 2457604
  614.9 28.6 %copy-start.45 = (bf16[8,128,132]{2,1,0:T(8,128)(2,1)S(1)}, bf16[8,128,132]{2,1,0:T(8,128)(2,1)}, u32[]{:S(2)}) copy-start(bf16[8,128,132]{2,1,0:T(8,128)(2,1)} %sum_everywhere.2) | copy-start | bytes 811012
  639.9 27.5 %all-to-all-start.5 = ((bf16[8,50,200]{2,1,0:T(8,128)(2,1)}), bf16[8,50,200]{2,1,0:T(8,128)(2,1)S(1)}, u32[]{:S(2)}, u32[]{:S(2)}) async-start(bf16[8,50,200]{2,1,0:T(8,128)(2,1)} %copy.379), calls=%async_computation.9 | async-start | bytes 458752 | tf_op jit(solution)/shard_map/all_to_all | solution.py:918
  650.0 7.8 copy-start.54
  667.5 8.7 %copy-start.59 = (bf16[8,50,200]{2,1,0:T(8,128)(2,1)}, bf16[8,50,200]{2,1,0:T(8,128)(2,1)S(1)}, u32[]{:S(2)}) copy-start(bf16[8,50,200]{2,1,0:T(8,128)(2,1)S(1)} %all-to-all-done.5) | copy-start | bytes 480004
  667.5 11.5 %all-to-all-start.8 = ((bf16[8,100,200]{1,2,0:T(8,128)(2,1)}), bf16[8,100,200]{1,2,0:T(8,128)(2,1)S(1)}, u32[]{:S(2)}, u32[]{:S(2)}) async-start(bf16[8,100,200]{1,2,0:T(8,128)(2,1)} %copy.387), calls=%async_computation.13 | async-start | bytes 819200 | tf_op jit(solution)/shard_map/all_to_all | solution.py:918
  679.0 19.1 %all-to-all-start.9 = ((bf16[8,800,86]{1,2,0:T(8,128)(2,1)}), bf16[8,800,86]{1,2,0:T(8,128)(2,1)}, u32[]{:S(2)}, u32[]{:S(2)}) async-start(bf16[8,800,86]{1,2,0:T(8,128)(2,1)} %maximum_bitcast_fusion), calls=%async_computation.14 | async-start | bytes 2523136 | tf_op jit(solution)/shard_map/all_to_all | solution.py:907
  683.9 113.1 %reduce-scatter.14.cloned.1.call-start = ((), (), s32[]{:S(2)}) async-start(), calls=%async_computation.22 | async-start | bytes 2211840 | tf_op jit(solution)/shard_map/reduce_scatter | solution.py:932
  712.4 33.5 %copy-start.19 = (bf16[1,128,1600]{2,1,0:T(8,128)(2,1)S(1)}, bf16[1,128,1600]{2,1,0:T(8,128)(2,1)}, u32[]{:S(2)}) copy-start(bf16[1,128,1600]{2,1,0:T(8,128)(2,1)} %copy.340) | copy-start | bytes 1228804
  712.4 33.5 %copy-start.67 = (f32[1600]{0:T(1024)S(1)}, f32[1600]{0:T(1024)}, u32[]{:S(2)}) copy-start(f32[1600]{0:T(1024)} %param.24) | copy-start | bytes 19204
  712.4 33.5 %copy-start.82 = (f32[128]{0:T(128)S(1)}, f32[128]{0:T(128)}, u32[]{:S(2)}) copy-start(f32[128]{0:T(128)} %get-tuple-element.363) | copy-start | bytes 1540
  712.4 34.9 %copy-start.55 = (bf16[400,680]{1,0:T(8,128)(2,1)S(1)}, bf16[400,680]{1,0:T(8,128)(2,1)}, u32[]{:S(2)}) copy-start(bf16[400,680]{1,0:T(8,128)(2,1)} %reduce-scatter.12.cloned.1.call-done) | copy-start | bytes 1632004
  798.5 11.2 %all-to-all-start.7 = ((bf16[8,25,100]{2,1,0:T(8,128)(2,1)}), bf16[8,25,100]{2,1,0:T(8,128)(2,1)}, u32[]{:S(2)}, u32[]{:S(2)}) async-start(bf16[8,25,100]{2,1,0:T(8,128)(2,1)} %bitcast.103), calls=%async_computation.12 | async-start | bytes 131072 | tf_op jit(solution)/shard_map/all_to_all | solution.py:907
  804.6 9.3 %copy-start.20 = (f32[8,160,4,100]{3,0,2,1:T(8,128)S(1)}, f32[8,160,4,100]{3,0,2,1:T(8,128)}, u32[]{:S(2)}) copy-start(f32[8,160,4,100]{3,0,2,1:T(8,128)} %copy.434) | copy-start | bytes 6144004
  809.7 24.0 %all-to-all-start.6 = ((bf16[8,400,100]{2,1,0:T(8,128)(2,1)}), bf16[8,400,100]{2,1,0:T(8,128)(2,1)}, u32[]{:S(2)}, u32[]{:S(2)}) async-start(bf16[8,400,100]{2,1,0:T(8,128)(2,1)} %bitcast.299), calls=%async_computation.11 | async-start | bytes 1638400 | tf_op jit(solution)/shard_map/all_to_all | solution.py:907
  (64 other events, 284.9 us)
Sparse Core Ops, SparseCore 0:
  71.6 51.2 all-gather.5
  125.1 82.4 all-gather.9
  209.7 84.4 all-gather.7
  383.5 45.4 reduce-scatter.5
  431.1 81.7 reduce-scatter.7
  515.1 44.7 reduce-scatter.9
  562.3 48.8 reduce-scatter.11
  687.1 38.0 reduce-scatter.13

commit v2 on v1

--- a/solution.py
+++ b/solution.py
@@ -38,7 +38,7 @@
 
 
 def halves_of(rows):
-    half = rows // 2
+    half = rows // 2 if rows % 32 == 0 else rows // 32 * 16
     return (pl.ds(0, half), pl.ds(half, rows - half))
 
 
@@ -200,10 +200,12 @@
 
 
 def front_kernel(
-    bits, count, x_ref, gain_ref, top_ref, in_ref, state_ref, step_ref,
-    normed_ref, tops_ref, in_out, state_out, step_out,
-    ctx_send, ctx_recv, line_send, line_recv,
+    bits, count, pack, x_ref, gain_ref, top_ref, in_ref, state_ref, step_ref, *rest,
 ):
+    weights, rest = rest[: pack["inputs"]], rest[pack["inputs"] :]
+    normed_ref, tops_ref, in_out, state_out, step_out = rest[:5]
+    packed, rest = rest[5 : 5 + pack["outputs"]], rest[5 + pack["outputs"] :]
+    ctx_send, ctx_recv, line_send, line_recv = rest[:4]
     me, row, rows = lax.axis_index("ctx"), lax.axis_index("fsdp"), lax.axis_size("fsdp")
     barrier = pltpu.get_barrier_semaphore()
     for bit in range(bits):
@@ -222,10 +224,6 @@
     in_out[row] = in_ref[...]
     state_out[row] = state_ref[...]
     step_out[row] = step_ref[...]
-    tokens = x_ref[...].astype(jnp.float32)
-    scale = lax.rsqrt(jnp.mean(tokens * tokens, axis=-1, keepdims=True) + EPSILON)
-    normed_ref[me] = (tokens * scale * gain_ref[...]).astype(normed_ref.dtype)
-    tops_ref[me] = top_ref[...]
     neighbours = jnp.where(row > 0, 1, 0) + jnp.where(row < rows - 1, 1, 0)
     pl.semaphore_wait(barrier, bits + neighbours)
 
@@ -234,44 +232,56 @@
     pieces = [(0, part) for part in row_parts(in_ref.shape[0], count)]
     pieces = [(1, pl.ds(0, state_ref.shape[0])), (2, pl.ds(0, step_ref.shape[0]))] + pieces
     line_list, line_end = line_steps(line, (in_out, state_out, step_out), pieces)
+    line_list[0]()
+    tokens = x_ref[...].astype(jnp.float32)
+    scale = lax.rsqrt(jnp.mean(tokens * tokens, axis=-1, keepdims=True) + EPSILON)
+    normed_ref[me] = (tokens * scale * gain_ref[...]).astype(normed_ref.dtype)
     first = gather_steps(across, bits, normed_ref)
+    first[0]()
+    tops_ref[me] = top_ref[...]
     second = gather_steps(across, bits, tops_ref)
-    token_list = first[:-1] + second[:-1] + [first[-1], second[-1]]
-    line_list[0]()
-    token_list[0]()
-    line_rest, token_rest = line_list[1:], token_list[1:]
-    done = 0
+    steps = list(pack["steps"](me, weights, packed, rest[4:])) if weights else []
+    token_rest = first[1:-1] + [second[0]] + second[1:-1] + [first[-1], second[-1]]
+    line_rest = line_list[1:]
+    tokens_done = packs_done = 0
+    spread = len(line_rest) * 3 // 4
     for i, step in enumerate(line_rest):
+        upto = min(len(steps), len(steps) * (i + 1) // max(1, spread))
+        for pack_step in steps[packs_done:upto]:
+            pack_step()
+        packs_done = max(packs_done, upto)
         step()
-        upto = len(token_rest) * (i + 1) // len(line_rest)
-        for token_step in token_rest[done:upto]:
+        upto = min(len(token_rest), len(token_rest) * (i + 1) // spread)
+        for token_step in token_rest[tokens_done:upto]:
             token_step()
-        done = upto
+        tokens_done = max(tokens_done, upto)
     across.finish()
     line_end()
 
 
-def front(x, gain, top, in_part, state_part, step_part, collective_id):
+def front(x, gain, top, in_part, state_part, step_part, later, hidden_units, collective_id):
     bits, ctx, fsdp = ctx_bits(), lax.axis_size("ctx"), lax.axis_size("fsdp")
-    count = 4
+    count = 5
     ctx_sems = pltpu.SemaphoreType.DMA((2 * gather_sems(bits),))
     line_sems = pltpu.SemaphoreType.DMA((2 * fsdp * (count + 2),))
+    pack = pack_out_plan(later, hidden_units)
 
     def stacked(array, size):
         return jax.ShapeDtypeStruct((size,) + array.shape, array.dtype)
 
     return pl.pallas_call(
-        functools.partial(front_kernel, bits, count),
+        functools.partial(front_kernel, bits, count, pack),
         out_shape=[
-            stacked(x, ctx), stacked(top, ctx), stacked(in_part, fsdp), stacked(state_part, fsdp),
-            stacked(step_part, fsdp),
-        ],
-        in_specs=[IN_VMEM] * 6,
-        out_specs=[IN_VMEM] * 5,
-        scratch_shapes=[ctx_sems, ctx_sems, line_sems, line_sems],
+            stacked(x, ctx), stacked(top, ctx), stacked(in_part, fsdp),
+            stacked(state_part, fsdp), stacked(step_part, fsdp),
+        ]
+        + pack["shapes"],
+        in_specs=[IN_VMEM] * 6 + [pl.BlockSpec(memory_space=pl.ANY)] * len(later),
+        out_specs=[IN_VMEM] * (5 + pack["outputs"]),
+        scratch_shapes=[ctx_sems, ctx_sems, line_sems, line_sems] + pack["scratch"],
         compiler_params=params(collective_id),
         name="front",
-    )(x, gain, top, in_part, state_part, step_part)
+    )(x, gain, top, in_part, state_part, step_part, *later)
 
 
 def product(x, weight, trans):
@@ -328,23 +338,28 @@
         for h in range(2):
             self.pass_on(h, 0, flips, self.flying[h])
 
+    def turn(self, phase, h):
+        kept_ref = self.inbox[0]
+        part, following = self.parts[h], {}
+        for box, (flips, copy) in enumerate(list(self.flying[h].items())):
+            copy.wait_recv()
+            slot = self.slots[flips]
+            total = kept_ref[slot, part].astype(jnp.float32) + self.inbox[1 + phase][
+                box, part
+            ].astype(jnp.float32)
+            if phase == self.bits - 2:
+                self.out_ref[part] = total
+            else:
+                kept_ref[slot, part] = total.astype(kept_ref.dtype)
+                self.pass_on(h, phase + 1, flips, following)
+        self.flying[h] = following
+
+    def turns(self):
+        return [functools.partial(self.turn, p, h) for p in range(self.bits - 1) for h in range(2)]
+
     def finish(self):
-        kept_ref = self.inbox[0]
-        for phase in range(self.bits - 1):
-            for h in range(2):
-                part, following = self.parts[h], {}
-                for box, (flips, copy) in enumerate(list(self.flying[h].items())):
-                    copy.wait_recv()
-                    slot = self.slots[flips]
-                    total = kept_ref[slot, part].astype(jnp.float32) + self.inbox[1 + phase][
-                        box, part
-                    ].astype(jnp.float32)
-                    if phase == self.bits - 2:
-                        self.out_ref[part] = total
-                    else:
-                        kept_ref[slot, part] = total.astype(kept_ref.dtype)
-                        self.pass_on(h, phase + 1, flips, following)
-                self.flying[h] = following
+        for turn in self.turns():
+            turn()
 
 
 def reducer_boxes(ctx, bits, rows, columns):
@@ -353,12 +368,20 @@
     return [pltpu.VMEM((box, rows, columns), BF16) for box in boxes], sems
 
 
-def reduce_kernel(bits, trans, *refs):
+def reduce_kernel(bits, trans, joint, *refs):
     count = len(trans)
-    x_refs, w_refs, out_ref = refs[:count], refs[count : 2 * count], refs[2 * count]
-    part_ref, inbox = refs[2 * count + 1], refs[2 * count + 2 : -2]
+    weights = 1 if joint else count
+    x_refs, w_refs, out_ref = refs[:count], refs[count : count + weights], refs[count + weights]
+    part_ref, inbox = refs[count + weights + 1], refs[count + weights + 2 : -2]
     me = lax.axis_index("ctx")
     greet(me, bits)
+    if joint:
+        whole, w_refs, inbox = w_refs[0], inbox[-count:], inbox[:-count]
+        at = 0
+        for w_ref in w_refs:
+            wide = w_ref.shape[1]
+            w_ref[...] = whole[:, at : at + wide]
+            at += wide
     copies = Copies("ctx", *refs[-2:])
     reducer = Reducer(copies, bits, part_ref, inbox, out_ref)
 
@@ -377,21 +400,24 @@
     copies.finish()
 
 
-def reduce_products(pairs, trans, collective_id):
+def reduce_products(lefts, weights, trans, collective_id):
     ctx, bits = lax.axis_size("ctx"), ctx_bits()
-    rows = pairs[0][0].shape[0] // ctx
-    columns = pairs[0][1].shape[0 if trans[0] else 1]
+    rows = lefts[0].shape[0] // ctx
+    columns = weights[0].shape[0 if trans else 1]
+    joint = len(weights) < len(lefts)
     boxes, count = reducer_boxes(ctx, bits, rows, columns)
+    if joint:
+        boxes = boxes + [pltpu.VMEM((columns, x.shape[1]), BF16) for x in lefts]
     sems = pltpu.SemaphoreType.DMA((count,))
     return pl.pallas_call(
-        functools.partial(reduce_kernel, bits, trans),
+        functools.partial(reduce_kernel, bits, (trans,) * len(lefts), joint),
         out_shape=jax.ShapeDtypeStruct((rows, columns), jnp.float32),
-        in_specs=[IN_VMEM] * (2 * len(pairs)),
+        in_specs=[IN_VMEM] * (len(lefts) + len(weights)),
         out_specs=IN_VMEM,
         scratch_shapes=boxes + [sems, sems],
         compiler_params=params(collective_id),
         name="reduce_products",
-    )(*[x.reshape(ctx, rows, -1) for x, _ in pairs], *[w for _, w in pairs])
+    )(*[x.reshape(ctx, rows, -1) for x in lefts], *weights)
 
 
 def greet_all(me, size):
@@ -586,8 +612,8 @@
 
 def ffn_kernel(
     x_ref, top_ref, pair_w, down_w,
-    all_ref, hidden_ref, pair_ref, out_ref, grad_ref,
-    own_ref, part_out, part_grad, *rest,
+    pair_dw, down_dw, out_ref, grad_ref,
+    all_ref, hidden_ref, pair_ref, own_ref, part_out, part_grad, *rest,
 ):
     bits = 3
     boxes = (len(rest) - 2) // 2
@@ -647,8 +673,33 @@
     work(3, (1, 2))
     settle(2, (2,))
     settle(3, (1, 2))
-    for reducer in reducers:
-        reducer.finish()
+
+    def band(out, left_ref, right_ref, low, high):
+        left = left_ref[:, :, low:high].reshape(size * rows, high - low)
+        right = right_ref[...].reshape(size * rows, right_ref.shape[2])
+        out[low:high] = lax.dot_general(
+            left, right, (((0,), (0,)), ((), ())), preferred_element_type=jnp.float32
+        ).astype(out.dtype)
+
+    def bands(out, left_ref, right_ref, count):
+        wide = left_ref.shape[2]
+        tiles = -(-wide // 128)
+        edges = [min(wide, 128 * (tiles * i // count)) for i in range(count + 1)]
+        return [
+            functools.partial(band, out, left_ref, right_ref, low, high)
+            for low, high in zip(edges[:-1], edges[1:])
+        ]
+
+    size = all_ref.shape[0]
+    work_left = bands(down_dw, hidden_ref, top_ref, 2) + bands(pair_dw, all_ref, pair_ref, 4)
+    turns = [turn for pair in zip(*(reducer.turns() for reducer in reducers)) for turn in pair]
+    done = 0
+    for i, turn in enumerate(turns):
+        upto = len(work_left) * (i + 1) // len(turns)
+        for item in work_left[done:upto]:
+            item()
+        done = upto
+        turn()
     copies.finish()
 
 
@@ -658,26 +709,626 @@
     hid = down_full.shape[0]
     boxes, count = reducer_boxes(ctx, bits, rows, model)
     sems = pltpu.SemaphoreType.DMA((2 * count + 8,))
-    all_rows, hidden, pair, out, grad = pl.pallas_call(
+    return pl.pallas_call(
         ffn_kernel,
         out_shape=[
-            jax.ShapeDtypeStruct((ctx, rows, model), BF16),
-            jax.ShapeDtypeStruct((ctx, rows, hid), BF16),
-            jax.ShapeDtypeStruct((ctx, rows, 2 * hid), BF16),
+            jax.ShapeDtypeStruct((model, 2 * hid), BF16),
+            jax.ShapeDtypeStruct((hid, model), BF16),
             jax.ShapeDtypeStruct((rows, model), jnp.float32),
             jax.ShapeDtypeStruct((rows, model), jnp.float32),
         ],
         in_specs=[IN_VMEM] * 4,
-        out_specs=[IN_VMEM] * 5,
-        scratch_shapes=[pltpu.VMEM((2, ctx // 2, rows, model), jnp.float32), boxes[0], boxes[0]]
+        out_specs=[IN_VMEM] * 4,
+        scratch_shapes=[
+            pltpu.VMEM((ctx, rows, model), BF16),
+            pltpu.VMEM((ctx, rows, hid), BF16),
+            pltpu.VMEM((ctx, rows, 2 * hid), BF16),
+            pltpu.VMEM((2, ctx // 2, rows, model), jnp.float32),
+            boxes[0],
+            boxes[0],
+        ]
         + boxes[1:]
         + boxes[1:]
         + [sems, sems],
         compiler_params=params(collective_id),
         name="ffn_both_ways",
     )(ffn_in, top.reshape(ctx, rows, model), pair_full, down_full)
-    flat = [a.reshape(ctx * rows, -1) for a in (all_rows, hidden, pair)]
-    return flat[0], flat[1], flat[2], out, grad
+
+
+def pieces_of(start, width, span):
+    out = []
+    at = start
+    while at < start + width:
+        block = at // span
+        end = min(start + width, (block + 1) * span)
+        out.append((block, at - start, end - start, at - block * span))
+        at = end
+    return out
+
+
+def exchange(copies, send_ref, recv_ref, me, size):
+    recv_ref[me] = send_ref[me]
+    return [
+        copies.send(send_ref.at[(me + turn) % size], recv_ref.at[me], (me + turn) % size)
+        for turn in range(1, size)
+    ]
+
+
+def attention_kernel(
+    size, fsdp, proj_ref, gain_ref,
+    branch_ref, rows_ref, prob_ref, inverse_ref, q_ref, k_ref, v_ref,
+    q_send, q_recv, kv_all, score_ref, attn_send, send_sem, recv_sem,
+):
+    bits = size.bit_length() - 1
+    me = lax.axis_index("ctx")
+    own, q_mine = q_send.shape[1], q_send.shape[2]
+    kv_mine = kv_all.shape[2] // 2
+    groups, keys, _ = k_ref.shape
+    heads = q_ref.shape[1] // own
+    queries = heads * own
+    chunk = 128
+    greet_all(me, size)
+    copies = Copies("ctx", send_sem, recv_sem)
+    for s in range(size):
+        q_send[s] = proj_ref[s * own : (s + 1) * own, :q_mine]
+    kv_all[me] = proj_ref[:, q_mine : q_mine + 2 * kv_mine]
+    steps = gather_steps(copies, bits, kv_all)
+    steps[0]()
+    come = exchange(copies, q_send, q_recv, me, size)
+    for step in steps[1:]:
+        step()
+    for copy in come:
+        copy.wait_recv()
+
+    for g in range(groups):
+        for s, low, high, at in pieces_of(g * HEAD, HEAD, kv_mine):
+            k_ref[g, :, low:high] = kv_all[s, :, at : at + high - low]
+            v_ref[g, :, low:high] = kv_all[s, :, kv_mine + at : kv_mine + at + high - low]
+        for h in range(heads):
+            for s, low, high, at in pieces_of((g * heads + h) * HEAD, HEAD, q_mine):
+                q_ref[g, h * own : (h + 1) * own, low:high] = q_recv[s, :, at : at + high - low]
+
+    query_ids = me * own + lax.broadcasted_iota(jnp.int32, (chunk, queries), 1) % own
+    key_ids = lax.broadcasted_iota(jnp.int32, (chunk, queries), 0)
+    for g in range(groups):
+        q_g = q_ref[g]
+
+        def scores(i, top):
+            at = pl.ds(pl.multiple_of(i * chunk, chunk), chunk)
+            raw = product(k_ref[g, at], q_g, True) * (HEAD**-0.5)
+            ids = key_ids + i * chunk
+            kept = jnp.logical_and(ids <= query_ids, ids > query_ids - WINDOW)
+            raw = jnp.where(kept, raw, -1e30)
+            score_ref[at] = raw
+            return jnp.maximum(top, jnp.max(raw, axis=0, keepdims=True))
+
+        top = lax.fori_loop(
+            0, keys // chunk, scores, jnp.full((1, queries), -1e30, jnp.float32)
+        )
+
+        def weights(i, total):
+            at = pl.ds(pl.multiple_of(i * chunk, chunk), chunk)
+            value = jnp.exp(score_ref[at] - top)
+            prob_ref[g, at] = value.astype(BF16)
+            return total + jnp.sum(value, axis=0, keepdims=True)
+
+        total = lax.fori_loop(
+            0, keys // chunk, weights, jnp.zeros((1, queries), jnp.float32)
+        )
+        inverse = 1.0 / total
+        inverse_ref[g] = inverse
+        out = lax.dot_general(
+            v_ref[g], prob_ref[g], (((0,), (0,)), ((), ())), preferred_element_type=jnp.float32
+        )
+        out = (out * inverse).T
+        for h in range(heads):
+            at = (g * heads + h) * HEAD
+            rows_ref[:, at : at + HEAD] = out[h * own : (h + 1) * own]
+
+    values = rows_ref[...]
+    scale = lax.rsqrt(jnp.mean(values * values, axis=-1, keepdims=True) + EPSILON)
+    branch = (values * scale * gain_ref[...]).astype(BF16)
+    part = values.shape[1] // fsdp
+    width = part // size
+    for d in range(size):
+        for f in range(fsdp):
+            at = f * part + d * width
+            attn_send[d, :, f * width : (f + 1) * width] = branch[:, at : at + width]
+    for copy in exchange(copies, attn_send, branch_ref, me, size):
+        copy.wait_recv()
+    copies.finish()
+
+
+def attention_forward(projected, gain, kv_width, collective_id):
+    ctx, fsdp, bits = lax.axis_size("ctx"), lax.axis_size("fsdp"), ctx_bits()
+    length, model = projected.shape[0], gain.shape[0]
+    own, q_mine, kv_mine = length // ctx, model // ctx, kv_width // ctx
+    heads = model // kv_width
+    sems = pltpu.SemaphoreType.DMA((2 * (ctx - 1) + gather_sems(bits),))
+    shape = jax.ShapeDtypeStruct
+    return pl.pallas_call(
+        functools.partial(attention_kernel, ctx, fsdp),
+        out_shape=[
+            shape((ctx, own, q_mine), BF16),
+            shape((own, model), jnp.float32),
+            shape((KV_HEADS, length, heads * own), BF16),
+            shape((KV_HEADS, 1, heads * own), jnp.float32),
+            shape((KV_HEADS, heads * own, HEAD), BF16),
+            shape((KV_HEADS, length, HEAD), BF16),
+            shape((KV_HEADS, length, HEAD), BF16),
+        ],
+        in_specs=[IN_VMEM] * 2,
+        out_specs=[IN_VMEM] * 7,
+        scratch_shapes=[
+            pltpu.VMEM((ctx, own, q_mine), BF16),
+            pltpu.VMEM((ctx, own, q_mine), BF16),
+            pltpu.VMEM((ctx, length, 2 * kv_mine), BF16),
+            pltpu.VMEM((length, heads * own), jnp.float32),
+            pltpu.VMEM((ctx, own, q_mine), BF16),
+            sems, sems,
+        ],
+        compiler_params=params(collective_id),
+        name="attention_forward",
+    )(projected, gain[None])
+
+
+def attention_back_kernel(
+    size, fsdp, grad_ref, rows_ref, gain_ref, prob_ref, inverse_ref, q_ref, k_ref, v_ref,
+    early_ref, gain_grad_ref,
+    recv_ref, heads_ref, dp_ref, dq_ref, dkv_ref, dq_send, dq_recv, kv_part, kv_sum, *rest,
+):
+    bits = size.bit_length() - 1
+    me = lax.axis_index("ctx")
+    own, model = rows_ref.shape
+    q_mine = model // size
+    groups, keys, queries = prob_ref.shape
+    heads = queries // own
+    kv_mine = groups * HEAD // size
+    chunk = 128
+    scale_qk = HEAD**-0.5
+    inbox = rest[:-2]
+    greet_all(me, size)
+    copies = Copies("ctx", *rest[-2:])
+    come = exchange(copies, grad_ref, recv_ref, me, size)
+    values = rows_ref[...]
+    scale = lax.rsqrt(jnp.mean(values * values, axis=-1, keepdims=True) + EPSILON)
+    for copy in come:
+        copy.wait_recv()
+    part = model // fsdp
+    width = part // size
+    for s in range(size):
+        for f in range(fsdp):
+            at = f * part + s * width
+            dq_ref[:, at : at + width] = recv_ref[s, :, f * width : (f + 1) * width].astype(
+                jnp.float32
+            )
+    grad = dq_ref[...]
+    gain_grad_ref[...] = jnp.sum(grad * values * scale, axis=0, keepdims=True)
+    scaled = grad * gain_ref[...]
+    grad = scale * scaled - values * (scale * scale * scale) * jnp.mean(
+        scaled * values, axis=-1, keepdims=True
+    )
+    grad = grad.astype(BF16)
+    for h in range(groups * heads):
+        at = (h % heads) * own
+        heads_ref[h // heads, at : at + own] = grad[:, h * HEAD : (h + 1) * HEAD]
+
+    for g in range(groups):
+        q_g, do_g, inverse = q_ref[g], heads_ref[g], inverse_ref[g]
+        q_t = q_g.astype(jnp.float32).T.astype(BF16)
+        do_t = do_g.astype(jnp.float32).T.astype(BF16)
+
+        def first(i, row_dot):
+            at = pl.ds(pl.multiple_of(i * chunk, chunk), chunk)
+            prob = prob_ref[g, at].astype(jnp.float32) * inverse
+            grad_prob = product(v_ref[g, at], do_g, True)
+            dp_ref[at] = grad_prob
+            dkv_ref[groups + g, :, at] = product(do_t, prob.astype(BF16), True)
+            return row_dot + jnp.sum(prob * grad_prob, axis=0, keepdims=True)
+
+        row_dot = lax.fori_loop(
+            0, keys // chunk, first, jnp.zeros((1, queries), jnp.float32)
+        )
+
+        def second(i, dq_t):
+            at = pl.ds(pl.multiple_of(i * chunk, chunk), chunk)
+            prob = prob_ref[g, at].astype(jnp.float32) * inverse
+            grad_score = (prob * (dp_ref[at] - row_dot)).astype(BF16)
+            dkv_ref[g, :, at] = scale_qk * product(q_t, grad_score, True)
+            return dq_t + lax.dot_general(
+                k_ref[g, at], grad_score, (((0,), (0,)), ((), ())),
+                preferred_element_type=jnp.float32,
+            )
+
+        dq_t = lax.fori_loop(
+            0, keys // chunk, second, jnp.zeros((HEAD, queries), jnp.float32)
+        )
+        dq_g = (scale_qk * dq_t).T
+        for h in range(heads):
+            at = (g * heads + h) * HEAD
+            dq_ref[:, at : at + HEAD] = dq_g[h * own : (h + 1) * own]
+
+    for d in range(size):
+        dq_send[d] = dq_ref[:, d * q_mine : (d + 1) * q_mine].astype(BF16)
+    come = exchange(copies, dq_send, dq_recv, me, size)
+    flat = dkv_ref.reshape(2 * groups * HEAD, keys)
+    for d in range(size):
+        kv_part[d, :kv_mine] = flat[d * kv_mine : (d + 1) * kv_mine].astype(BF16)
+        at = groups * HEAD + d * kv_mine
+        kv_part[d, kv_mine:] = flat[at : at + kv_mine].astype(BF16)
+    reducer = Reducer(copies, bits, None, inbox, kv_sum)
+    for flips in reducer.everyone:
+        reducer.first[flips] = copies.send(
+            kv_part.at[flipped(me, flips + (0,))],
+            inbox[0].at[reducer.slots[flips]],
+            flip(me, 0),
+        )
+    for flips in reducer.everyone:
+        reducer.own(flips, kv_part[flipped(me, flips)].astype(jnp.float32))
+    for copy in come:
+        copy.wait_recv()
+    for s in range(size):
+        early_ref[s * own : (s + 1) * own, :q_mine] = dq_recv[s]
+    reducer.finish()
+    early_ref[:, q_mine:] = kv_sum[...].T.astype(BF16)
+    copies.finish()
+
+
+def attention_backward(grad_c, rows, gain, kept, collective_id):
+    ctx, fsdp, bits = lax.axis_size("ctx"), lax.axis_size("fsdp"), ctx_bits()
+    prob = kept[0]
+    own, model = rows.shape
+    length = own * ctx
+    q_mine, kv_mine = model // ctx, KV_HEADS * HEAD // ctx
+    boxes, count = reducer_boxes(ctx, bits, 2 * kv_mine, length)
+    sems = pltpu.SemaphoreType.DMA((2 * (ctx - 1) + count,))
+    shape = jax.ShapeDtypeStruct
+    return pl.pallas_call(
+        functools.partial(attention_back_kernel, ctx, fsdp),
+        out_shape=[
+            shape((length, q_mine + 2 * kv_mine), BF16),
+            shape((1, model), jnp.float32),
+        ],
+        in_specs=[IN_VMEM] * (3 + len(kept)),
+        out_specs=[IN_VMEM] * 2,
+        scratch_shapes=[
+            pltpu.VMEM((ctx, own, q_mine), BF16),
+            pltpu.VMEM(kept[2].shape, BF16),
+            pltpu.VMEM((length, prob.shape[2]), jnp.float32),
+            pltpu.VMEM((own, model), jnp.float32),
+            pltpu.VMEM((2 * KV_HEADS, HEAD, length), jnp.float32),
+            pltpu.VMEM((ctx, own, q_mine), BF16),
+            pltpu.VMEM((ctx, own, q_mine), BF16),
+            pltpu.VMEM((ctx, 2 * kv_mine, length), BF16),
+            pltpu.VMEM((2 * kv_mine, length), jnp.float32),
+        ]
+        + boxes[1:]
+        + [sems, sems],
+        compiler_params=params(collective_id),
+        name="attention_backward",
+    )(grad_c.reshape(ctx, own, q_mine), rows, gain[None], *kept)
+
+
+def finish_kernel(
+    size, fsdp, early_ref, src_ref, step_ref, attn_ref, mix_ref, channel_ref, gain_ref,
+    query_out, key_out, value_out, mixer_out, step_out, attn_out, mix_out, channel_out, sums_ref,
+    all_ref, row_inbox, gain_inbox, line_inbox, c_send, c_recv, r_send, r_recv,
+    ctx_send, ctx_recv, line_send, line_recv,
+):
+    bits = size.bit_length() - 1
+    me, row = lax.axis_index("ctx"), lax.axis_index("fsdp")
+    barrier = pltpu.get_barrier_semaphore()
+    for turn in range(1, size):
+        pl.semaphore_signal(
+            barrier, inc=1, device_id={"ctx": (me + turn) % size}, device_id_type=MESH
+        )
+    for turn in range(1, fsdp):
+        pl.semaphore_signal(
+            barrier, inc=1, device_id={"fsdp": (row + turn) % fsdp}, device_id_type=MESH
+        )
+    q_mine, kv_mine = query_out.shape[1], key_out.shape[1]
+    late = q_mine + 2 * kv_mine
+    rows, width = src_ref.shape[0], src_ref.shape[1] // fsdp
+    low, high = step_ref.shape[0], mix_ref.shape[0]
+    attn_at = -(-high // 16) * 16
+    block = mix_out.shape[1]
+    repeat = size // fsdp
+    pl.semaphore_wait(barrier, size - 1 + fsdp - 1)
+    across, line = Copies("ctx", ctx_send, ctx_recv), Copies("fsdp", line_send, line_recv)
+    band = channel_ref.shape[0] // fsdp
+
+    def band_of(index):
+        return pl.ds(pl.multiple_of(index * band, 8), band)
+
+    bands = []
+    for turn in range(1, fsdp):
+        to = (row + turn) % fsdp
+        bands.append(line.send(channel_ref.at[band_of(to)], row_inbox.at[turn - 1], to))
+    gains = [
+        across.send(gain_ref, gain_inbox.at[turn - 1], (me + turn) % size)
+        for turn in range(1, size)
+    ]
+    c_send[:, rows:] = jnp.zeros((size, c_send.shape[1] - rows, width), BF16)
+    r_send[...] = jnp.zeros(r_send.shape, BF16)
+    for d in range(size):
+        unit = d % fsdp
+        if d < fsdp:
+            c_send[d, :rows] = src_ref[:, unit * width : (unit + 1) * width]
+        else:
+            at = late + unit * width
+            c_send[d, :rows] = early_ref[:, at : at + width]
+        at = d // repeat * width
+        c_send[d, rows : rows + low] = step_ref[:, at : at + width]
+        r_send[d, :high] = mix_ref[:, d * block : (d + 1) * block]
+        r_send[d, attn_at : attn_at + attn_ref.shape[0]] = attn_ref[:, d * block : (d + 1) * block]
+    moved = exchange(across, c_send, c_recv, me, size) + exchange(across, r_send, r_recv, me, size)
+    query_out[...] = early_ref[:, :q_mine].astype(jnp.float32)
+    key_out[...] = early_ref[:, q_mine : q_mine + kv_mine].astype(jnp.float32)
+    value_out[...] = early_ref[:, q_mine + kv_mine : late].astype(jnp.float32)
+
+    total = channel_ref[band_of(row)]
+    for turn in range(1, fsdp):
+        bands[turn - 1].wait_recv()
+        total = total + row_inbox[turn - 1]
+    all_ref[me, band_of(row)] = total
+    at = all_ref.at[me, band_of(row)]
+    bands = [line.send(at, at, (row + turn) % fsdp) for turn in range(1, fsdp)]
+    total = gain_ref[...]
+    for turn in range(1, size):
+        gains[turn - 1].wait_recv()
+        total = total + gain_inbox[turn - 1]
+    line_inbox[0] = total
+    gains = [
+        line.send(line_inbox.at[0], line_inbox.at[turn], (row + turn) % fsdp)
+        for turn in range(1, fsdp)
+    ]
+    for copy in bands:
+        copy.wait_recv()
+    steps = gather_steps(across, bits, all_ref)
+    steps[0]()
+    for copy in moved:
+        copy.wait_recv()
+    for step in steps[1:-1]:
+        step()
+    for s in range(size):
+        mixer_out[:, s * width : (s + 1) * width] = c_recv[s, :rows].astype(jnp.float32)
+        mix_out[s * high : (s + 1) * high] = r_recv[s, :high].astype(jnp.float32)
+        count = attn_ref.shape[0]
+        attn_out[s * count : (s + 1) * count] = r_recv[s, attn_at : attn_at + count].astype(
+            jnp.float32
+        )
+    for j in range(fsdp):
+        source = fsdp * (me % repeat) + j
+        step_out[:, j * width : (j + 1) * width] = c_recv[source, rows : rows + low].astype(
+            jnp.float32
+        )
+    steps[-1]()
+    part = channel_out.shape[1] // fsdp
+    for s in range(size):
+        for f in range(fsdp):
+            at = f * part + s * width
+            channel_out[:, at : at + width] = all_ref[s, :, f * width : (f + 1) * width]
+    total = line_inbox[0]
+    for turn in range(1, fsdp):
+        gains[turn - 1].wait_recv()
+        total = total + line_inbox[turn]
+    sums_ref[...] = total
+    across.finish()
+    line.finish()
+
+
+def finish(early, src, step, attn, mix, channel, gains, q_mine, kv_mine, collective_id):
+    ctx, fsdp, bits = lax.axis_size("ctx"), lax.axis_size("fsdp"), ctx_bits()
+    rows, mine = src.shape
+    model = attn.shape[1]
+    width, block = mine // fsdp, model // ctx
+    pad_rows = rows + -(-step.shape[0] // 16) * 16
+    stack_rows = -(-mix.shape[0] // 16) * 16 + -(-attn.shape[0] // 16) * 16
+    ctx_sems = pltpu.SemaphoreType.DMA((3 * (ctx - 1) + gather_sems(bits),))
+    line_sems = pltpu.SemaphoreType.DMA((3 * (fsdp - 1),))
+
+    def shape(*sizes):
+        return jax.ShapeDtypeStruct(sizes, jnp.float32)
+
+    return pl.pallas_call(
+        functools.partial(finish_kernel, ctx, fsdp),
+        out_shape=[
+            shape(rows, q_mine), shape(rows, kv_mine), shape(rows, kv_mine),
+            shape(rows, ctx * width), shape(step.shape[0], mine),
+            shape(ctx * attn.shape[0], block), shape(ctx * mix.shape[0], block),
+            shape(channel.shape[0], ctx * mine), shape(*gains.shape),
+        ],
+        in_specs=[IN_VMEM] * 7,
+        out_specs=[IN_VMEM] * 9,
+        scratch_shapes=[
+            pltpu.VMEM((ctx,) + channel.shape, jnp.float32),
+            pltpu.VMEM((fsdp - 1, channel.shape[0] // fsdp, mine), jnp.float32),
+            pltpu.VMEM((ctx - 1,) + gains.shape, jnp.float32),
+            pltpu.VMEM((fsdp,) + gains.shape, jnp.float32),
+            pltpu.VMEM((ctx, pad_rows, width), BF16),
+            pltpu.VMEM((ctx, pad_rows, width), BF16),
+            pltpu.VMEM((ctx, stack_rows, block), BF16),
+            pltpu.VMEM((ctx, stack_rows, block), BF16),
+            ctx_sems, ctx_sems, line_sems, line_sems,
+        ],
+        compiler_params=params(collective_id),
+        name="finish",
+    )(early, src, step, attn, mix, channel, gains)
+
+
+def window(start, size, total, step):
+    return pl.multiple_of(jnp.minimum(start // step * step, total - size), step)
+
+
+def shifted(values, offset, axis):
+    size = values.shape[axis]
+    return pltpu.roll(values.astype(jnp.float32), lax.rem(size - offset, size), axis)
+
+
+def pack_in_kernel(
+    size, query_ref, key_ref, value_ref, mixer_ref, state_ref, step_ref,
+    in_out, state_out, step_out, inbox, sems,
+):
+    me = lax.axis_index("ctx")
+    units, _, span = inbox.shape
+    total = mixer_ref.shape[1]
+    width = total // units // size
+    copies = []
+    for u in range(units):
+        at = window(u * (total // units) + me * width, span, total, 128)
+        copy = pltpu.make_async_copy(mixer_ref.at[:, pl.ds(at, span)], inbox.at[u], sems.at[u])
+        copy.start()
+        copies.append(copy)
+    at = 0
+    for ref in (query_ref, key_ref, value_ref):
+        wide = ref.shape[1] // size
+        in_out[:, at : at + wide] = shifted(ref[...], me * wide, 1)[:, :wide].astype(BF16)
+        at += wide
+    high = state_ref.shape[0] // size
+    first = window(me * high, 128, state_ref.shape[0], 16)
+    rows = shifted(state_ref[pl.ds(first, 128)], me * high - first, 0)
+    state_out[...] = rows[: state_out.shape[0]].astype(BF16)
+    part = step_ref.shape[1] * 2 // units
+    step_out[...] = jnp.zeros(step_out.shape, BF16)
+    for f in range(units // 2):
+        band = shifted(step_ref[:, f * part : (f + 1) * part], me * width, 1)
+        step_out[: step_ref.shape[0], f * width : (f + 1) * width] = band[:, :width].astype(BF16)
+    for u in range(units):
+        copies[u].wait()
+        start = u * (total // units) + me * width
+        piece = shifted(inbox[u], start - window(start, span, total, 128), 1)[:, :width]
+        to = at + (u + units // 2) % units * width
+        in_out[:, to : to + width] = piece.astype(BF16)
+
+
+def pack_in(query, key, value, mixer, state, step):
+    ctx, fsdp = lax.axis_size("ctx"), lax.axis_size("fsdp")
+    rows = mixer.shape[0]
+    mine = mixer.shape[1] // 2 // ctx
+    qkv = (query.shape[1] + key.shape[1] + value.shape[1]) // ctx
+    state_rows = state.shape[0] // ctx
+    shape = jax.ShapeDtypeStruct
+    return pl.pallas_call(
+        functools.partial(pack_in_kernel, ctx),
+        out_shape=[
+            shape((rows, qkv + 2 * mine), BF16),
+            shape((state_rows + -state_rows % 16, state.shape[1]), BF16),
+            shape((step.shape[0] + -step.shape[0] % 16, mine), BF16),
+        ],
+        in_specs=[IN_VMEM] * 3 + [pl.BlockSpec(memory_space=pl.ANY)] + [IN_VMEM] * 2,
+        out_specs=[IN_VMEM] * 3,
+        scratch_shapes=[
+            pltpu.VMEM((2 * fsdp, rows, 256), BF16), pltpu.SemaphoreType.DMA((2 * fsdp,))
+        ],
+        compiler_params=pltpu.CompilerParams(vmem_limit_bytes=VMEM_LIMIT),
+        name="pack_in",
+    )(query, key, value, mixer, state, step)
+
+
+def pack_out_plan(later, hidden_units):
+    if not later:
+        return {"inputs": 0, "outputs": 0, "shapes": [], "scratch": [], "steps": None}
+    ctx, fsdp = lax.axis_size("ctx"), lax.axis_size("fsdp")
+    gate, _, down, mix, attn = later
+    rows, model, total = gate.shape[0], down.shape[0], gate.shape[1]
+    hid_part = total // ctx // fsdp
+    pad = -hid_part % 16
+    units = hidden_units // fsdp
+    width = hid_part // units
+    high = (hid_part + pad) + (mix.shape[0] + attn.shape[0]) // ctx
+    span = 256
+
+    def box_rows(array):
+        need = array.shape[0] // ctx
+        return need + 15 + -(need + 15) % 16
+
+    def steps(me, weights, outs, scratch):
+        gate_ref, up_ref, down_ref, mix_ref, attn_ref = weights
+        pair_out, rows_out = outs
+        inbox, down_box, tail_box, mix_box, attn_box, sems = scratch
+        copies = []
+
+        def start_copy(source, target):
+            copy = pltpu.make_async_copy(source, target, sems.at[len(copies)])
+            copy.start()
+            copies.append(copy)
+
+        plans = []
+        half = pair_out.shape[1] // 2
+        for index, ref in enumerate((gate_ref, up_ref)):
+            for u in range(hidden_units):
+                start = u * (total // hidden_units) + me * width
+                at = window(start, span, total, 128)
+                start_copy(ref.at[:, pl.ds(at, span)], inbox.at[index, u])
+                to = index * half + u * width + u // units * pad
+                plans.append(("columns", inbox, (index, u), start - at, to, width))
+        to = 0
+        down_at = to
+        to += units * width + pad
+        for ref, box in ((mix_ref, mix_box), (attn_ref, attn_box)):
+            tall = ref.shape[0] // size
+            at = window(me * tall, box.shape[1], ref.shape[0], 16)
+            start_copy(ref.at[pl.ds(at, box.shape[1])], box.at[0])
+            plans.append(("rows", box, (0,), me * tall - at, to, tall))
+            to += tall
+        start_copy(down_ref, down_box)
+        full = down.shape[1] // 128
+        tail = down.shape[1] % 128
+
+        def tile_of(index):
+            at = pl.multiple_of(jnp.minimum(index, full - 1) * 128, 128)
+            whole = down_box[:, pl.ds(at, 128)].astype(jnp.float32)
+            return jnp.where(index >= full, tail_box[...], whole) if tail else whole
+
+        def begin_down():
+            copies[-1].wait()
+            if tail:
+                tail_box[...] = jnp.zeros(tail_box.shape, jnp.float32)
+                tail_box[:, :tail] = down_box[:, full * 128 :].astype(jnp.float32)
+
+        def place_down(u):
+            start = u * (down.shape[1] // units) + me * width
+            first = start // 128
+            pair = jnp.concatenate([tile_of(first), tile_of(first + 1)], 1)
+            turned = shifted(pair, start - first * 128, 1)[:, :128].T
+            at = down_at + u * width
+            rows_out[at : at + width] = turned[:width].astype(BF16)
+
+        def clear():
+            pair_out[...] = jnp.zeros(pair_out.shape, BF16)
+            rows_out[...] = jnp.zeros(rows_out.shape, BF16)
+
+        def place(copy, kind, box, index, offset, to, extent):
+            copy.wait()
+            values = box[index]
+            if kind == "columns":
+                pair_out[:, to : to + extent] = shifted(values, offset, 1)[:, :extent].astype(BF16)
+            else:
+                rows_out[to : to + extent] = shifted(values, offset, 0)[:extent].astype(BF16)
+
+        placed = [functools.partial(place, copy, *plan) for copy, plan in zip(copies, plans)]
+        downs = [functools.partial(place_down, u) for u in range(units)]
+        return [clear] + placed + [begin_down] + downs
+
+    size = ctx
+    shape = jax.ShapeDtypeStruct
+    return {
+        "inputs": 5,
+        "outputs": 2,
+        "shapes": [
+            shape((rows, 2 * fsdp * (hid_part + pad)), BF16),
+            shape((high + -high % 16, model), BF16),
+        ],
+        "scratch": [
+            pltpu.VMEM((2, hidden_units, rows, span), BF16),
+            pltpu.VMEM(down.shape, BF16),
+            pltpu.VMEM((model, 128), jnp.float32),
+            pltpu.VMEM((1, box_rows(mix), model), BF16),
+            pltpu.VMEM((1, box_rows(attn), model), BF16),
+            pltpu.SemaphoreType.DMA((2 * hidden_units + 3,)),
+        ],
+        "steps": steps,
+    }
 
 
 def scan_fwd_kernel(steps_ref, drive_ref, in_ref, out_ref, rate_ref, scan_ref, prev_ref, state_ref):
@@ -699,8 +1350,8 @@
             drive_8 = step_8 * drive_ref[pl.ds(base, 8), lanes]
             rows = []
             for t in range(8):
-                in_t = in_ref[base + t]
-                out_t = out_ref[base + t]
+                in_t = in_ref[base + t].astype(jnp.float32)
+                out_t = out_ref[base + t].astype(jnp.float32)
                 decay = jnp.exp2(step_8[t : t + 1] * rates[j])
                 prev_ref[base + t, :, lanes] = states[j]
                 states[j] = decay * states[j] + drive_8[t : t + 1] * in_t
@@ -761,8 +1412,8 @@
             grad_8 = grad_ref[pl.ds(base, 8), lanes]
             held_rows, dot_rows = [None] * 8, [None] * 8
             for t in range(7, -1, -1):
-                in_t = in_ref[base + t]
-                out_t = out_ref[base + t]
+                in_t = in_ref[base + t].astype(jnp.float32)
+                out_t = out_ref[base + t].astype(jnp.float32)
                 previous = prev_ref[base + t, :, lanes]
                 step_t = step_8[t : t + 1]
                 drive_t = drive_8[t : t + 1]
@@ -897,27 +1548,42 @@
     return lax.all_gather(array, "fsdp", axis=0, tiled=True)
 
 
-def to_blocks(array, units):
-    ctx = lax.axis_size("ctx")
-    rows = array.shape[0]
-    width = array.shape[1] // units
-    repeat = ctx // units
+def to_slots(array, units):
+    repeat = lax.axis_size("ctx") // units
+    rows, width = array.shape[0], array.shape[1] // units
     pieces = array.reshape(rows, units, width).transpose(1, 0, 2)
-    slots = jnp.repeat(pieces, repeat, axis=0) if repeat > 1 else pieces
-    got = lax.all_to_all(slots, "ctx", 0, 0, tiled=True)
+    return jnp.repeat(pieces, repeat, axis=0) if repeat > 1 else pieces
+
+
+def from_slots(got, units):
+    repeat = lax.axis_size("ctx") // units
     if repeat > 1:
         first = units * lax.rem(lax.axis_index("ctx"), repeat)
         got = lax.dynamic_slice_in_dim(got, first, units, 0)
+    rows, width = got.shape[1:]
     return got.transpose(1, 0, 2).reshape(rows, units * width).astype(jnp.float32)
 
 
-def rows_to_blocks(array, units):
+def to_blocks(array, units):
+    got = lax.all_to_all(to_slots(array, units), "ctx", 0, 0, tiled=True)
+    return from_slots(got, units)
+
+
+def rows_to_slots(array):
     ctx = lax.axis_size("ctx")
     rows, columns = array.shape
-    pieces = array.reshape(rows, ctx, columns // ctx).transpose(1, 0, 2)
-    got = lax.all_to_all(pieces, "ctx", 0, 0, tiled=True)
-    got = got.reshape(ctx, units, rows // units, columns // ctx).transpose(1, 0, 2, 3)
-    return got.reshape(ctx * rows, columns // ctx).astype(jnp.float32)
+    return array.reshape(rows, ctx, columns // ctx).transpose(1, 0, 2)
+
+
+def rows_from_slots(got, units):
+    ctx, rows, columns = got.shape
+    got = got.reshape(ctx, units, rows // units, columns).transpose(1, 0, 2, 3)
+    return got.reshape(ctx * rows, columns).astype(jnp.float32)
+
+
+def rows_to_blocks(array, units):
+    got = lax.all_to_all(rows_to_slots(array), "ctx", 0, 0, tiled=True)
+    return rows_from_slots(got, units)
 
 
 def scatter_fsdp(*gradients):
@@ -973,56 +1639,65 @@
     group_size = query_proj.shape[1] // key_proj.shape[1]
     score_scale = HEAD ** (-0.5)
 
-    src_part = jnp.concatenate(my_columns(mixer_in[:, :inner], fsdp), 1)
-    state_part = my_rows(state_proj, 1)[0]
-    step_part = jnp.concatenate(my_columns(step_proj, fsdp), 1)
-    state_rows, step_rows = state_part.shape[0], step_part.shape[0]
-    normed_all, grad_top, src_full, state_full, step_full = front(
-        inputs[0],
-        norm_gain[None],
-        cotangent[0],
-        src_part,
-        jnp.pad(state_part, ((0, -state_rows % 16), (0, 0))),
-        jnp.pad(step_part, ((0, -step_rows % 16), (0, 0))),
-        0,
+    hid_part = hid // fsdp
+    hid_pad = -hid_part % 16
+    hid_all = hid + fsdp * hid_pad
+    attn_pad = -attn_proj.shape[0] % ctx
+    attn_rows_mine = (attn_proj.shape[0] + attn_pad) // ctx
+    state_rows, step_rows = state_proj.shape[0] // ctx, step_proj.shape[0]
+    if ctx == 8:
+        in_part, state_part, step_part = pack_in(
+            query_proj, key_proj, value_proj, mixer_in, state_proj, step_proj
+        )
+        later = (gate_proj, up_proj, down_proj.T, mixer_out, attn_proj)
+    else:
+        in_part = jnp.concatenate(
+            [block_columns(array) for array in (query_proj, key_proj, value_proj)]
+            + my_columns(mixer_in[:, inner:], fsdp)
+            + my_columns(mixer_in[:, :inner], fsdp),
+            1,
+        )
+        later = ()
+        state_part = jnp.pad(my_rows(state_proj, 1)[0], ((0, -state_rows % 16), (0, 0)))
+        step_part = jnp.pad(
+            jnp.concatenate(my_columns(step_proj, fsdp), 1), ((0, -step_rows % 16), (0, 0))
+        )
+
+        def hidden_columns(array):
+            pieces = my_columns(array, hidden_units)
+            if hid_pad:
+                for f in range(fsdp, 0, -1):
+                    pieces.insert(f * hidden_rows, jnp.zeros((array.shape[0], hid_pad), BF16))
+            return pieces
+
+        ffn_part = jnp.concatenate(hidden_columns(gate_proj) + hidden_columns(up_proj), 1)
+        rows_part = jnp.concatenate(
+            my_rows(down_proj, hidden_rows)
+            + [jnp.zeros((hid_pad, model), BF16)]
+            + my_rows(mixer_out, 1)
+            + my_rows(jnp.pad(attn_proj, ((0, attn_pad), (0, 0))), 1),
+            0,
+        )
+    mix_rows = mixer_out.shape[0] // ctx
+    normed_all, grad_top, in_full, state_full, step_full, *parts = front(
+        inputs[0], norm_gain[None], cotangent[0], in_part, state_part, step_part, later,
+        hidden_units, 0,
     )
+    if parts:
+        ffn_part, rows_part = parts
     normed_all = normed_all.reshape(length, model)
     grad_top = grad_top.reshape(length, model)
-    src_full = src_full.reshape(model, -1)
+    in_full = in_full.reshape(model, -1)
     state_full = state_full[:, :state_rows].reshape(-1, state_proj.shape[1])
     step_full = step_full[:, :step_rows].reshape(-1, mine)
     norm_scale = rms_scale(tokens)
-
-    attn_pad = -attn_proj.shape[0] % ctx
-    attn_rows_mine = (attn_proj.shape[0] + attn_pad) // ctx
-    (
-        query_proj, key_proj, value_proj, mixer_late, attn_proj, mixer_out, down_proj, gate_proj,
-        up_proj, normed_all,
-    ) = lax.optimization_barrier(
-        (
-            query_proj, key_proj, value_proj, mixer_in, attn_proj, mixer_out, down_proj, gate_proj,
-            up_proj, normed_all,
-        )
-    )
-    early_part = jnp.concatenate(
-        [block_columns(query_proj), block_columns(key_proj), block_columns(value_proj)]
-        + my_columns(mixer_late[:, inner:], fsdp),
-        1,
-    )
-    out_part = jnp.concatenate(
-        my_rows(jnp.pad(attn_proj, ((0, attn_pad), (0, 0))), 1) + my_rows(mixer_out, 1), 0
-    )
-    down_part = jnp.concatenate(my_rows(down_proj, hidden_rows), 0)
-    ffn_part = jnp.concatenate(
-        my_columns(gate_proj, hidden_units) + my_columns(up_proj, hidden_units), 1
-    )
-    rows_part = jnp.concatenate([out_part, down_part], 0)
-    early_full = over_fsdp(early_part)
     rows_full = lax.all_gather(rows_part, "fsdp", axis=0)
     ffn_full = over_fsdp(ffn_part)
-    attn_full = rows_full[:, :attn_rows_mine].reshape(-1, model)
-    mixout_full = rows_full[:, attn_rows_mine : out_part.shape[0]].reshape(-1, model)
-    down_full = rows_full[:, out_part.shape[0] :].reshape(-1, model)
+    down_at = hid_part + hid_pad
+    down_full = rows_full[:, :down_at].reshape(-1, model)
+    mixout_full = rows_full[:, down_at : down_at + mix_rows].reshape(-1, model)
+    attn_at = down_at + mix_rows
+    attn_full = rows_full[:, attn_at : attn_at + attn_rows_mine].reshape(-1, model)
     attn_width = attn_full.shape[0]
 
     def mine_of(vector):
@@ -1049,7 +1724,8 @@
     def padded(values):
         return jnp.pad(values, ((0, 0), (0, pad)))
 
-    conv_src = matmul(normed_all, src_full).astype(BF16)
+    projected_in = matmul(normed_all, in_full).astype(BF16)
+    conv_src = projected_in[:, q_mine + 2 * kv_mine + mine :]
 
     padded_src = jnp.concatenate(
         [jnp.zeros((CONV - 1, mine), jnp.float32), conv_src.astype(jnp.float32)], 0
@@ -1063,39 +1739,14 @@
     output_mat = projected[:, DT_RANK + STATE :]
     step_pre = matmul(step_low, step_full) + bias_step
     steps_dt = jax.nn.softplus(step_pre)
-    in_b = jnp.broadcast_to(input_mat[:, :, None], (length, STATE, LANES))
-    out_b = jnp.broadcast_to(output_mat[:, :, None], (length, STATE, LANES))
+    in_b = jnp.broadcast_to(input_mat.astype(BF16)[:, :, None], (length, STATE, LANES))
+    out_b = jnp.broadcast_to(output_mat.astype(BF16)[:, :, None], (length, STATE, LANES))
     rates_log2 = padded(-LOG2_E * rates)
     steps_pad, vals_pad = padded(steps_dt), padded(conv_vals)
     scan_out, states = scan_fwd(steps_pad, vals_pad, in_b, out_b, rates_log2)
     scan_out = scan_out[:, :mine]
 
-    projected_in = matmul(normed_all, early_full).astype(BF16)
-    queries = lax.all_to_all(projected_in[:, :q_mine], "ctx", 0, 1, tiled=True)
-    keyvals = gather_shards(projected_in[:, q_mine : q_mine + 2 * kv_mine], 1)
-    keys_all = keyvals[:, :, :kv_mine].transpose(1, 0, 2).reshape(length, KV_HEADS, HEAD)
-    vals_all = keyvals[:, :, kv_mine:].transpose(1, 0, 2).reshape(length, KV_HEADS, HEAD)
-    gate_z = projected_in[:, q_mine + 2 * kv_mine :].astype(jnp.float32)
-    heads_q = queries.reshape(own, KV_HEADS, group_size, HEAD)
-    row_ids = place * own + lax.broadcasted_iota(jnp.int32, (own, length), 0)
-    col_ids = lax.broadcasted_iota(jnp.int32, (own, length), 1)
-    allowed = (col_ids <= row_ids) & (col_ids > row_ids - WINDOW)
-
-    def scores_of():
-        raw = jnp.einsum("qhgd,khd->hgqk", heads_q, keys_all, preferred_element_type=jnp.float32)
-        return jnp.where(allowed, raw * score_scale, -1e30)
-
-    scores = scores_of()
-    row_top = jnp.max(scores, axis=-1, keepdims=True)
-    log_total = row_top + jnp.log(jnp.sum(jnp.exp(scores - row_top), axis=-1, keepdims=True))
-    probs = jnp.exp(scores - log_total)
-    probs_bf = probs.astype(BF16)
-    attn_rows = jnp.einsum(
-        "hgqk,khd->qhgd", probs_bf, vals_all, preferred_element_type=jnp.float32
-    ).reshape(own, -1)
-    attn_scale = rms_scale(attn_rows)
-    branch_attn = (attn_rows * attn_scale * attn_gain).astype(BF16)
-
+    gate_z = projected_in[:, q_mine + 2 * kv_mine : q_mine + 2 * kv_mine + mine].astype(jnp.float32)
     def attn_to_channels(values):
         parts = jnp.pad(values.reshape(own, fsdp, -1), ((0, 0), (0, 0), (0, attn_pad)))
         parts = parts.reshape(own, fsdp, ctx, -1).transpose(2, 0, 1, 3).reshape(ctx, own, -1)
@@ -1107,7 +1758,36 @@
         got = got.reshape(ctx, own, fsdp, -1).transpose(1, 2, 0, 3).reshape(own, fsdp, -1)
         return got[:, :, : attn_proj.shape[0]].reshape(own, -1)
 
-    branch_attn_c = attn_to_channels(branch_attn)
+    if ctx == 8:
+        branch_attn_c, attn_rows, *attn_kept = attention_forward(
+            projected_in, attn_gain, key_proj.shape[1], 1
+        )
+        branch_attn_c = branch_attn_c.reshape(length, -1)
+    else:
+        queries = lax.all_to_all(projected_in[:, :q_mine], "ctx", 0, 1, tiled=True)
+        keyvals = gather_shards(projected_in[:, q_mine : q_mine + 2 * kv_mine], 1)
+        keys_all = keyvals[:, :, :kv_mine].transpose(1, 0, 2).reshape(length, KV_HEADS, HEAD)
+        vals_all = keyvals[:, :, kv_mine:].transpose(1, 0, 2).reshape(length, KV_HEADS, HEAD)
+        heads_q = queries.reshape(own, KV_HEADS, group_size, HEAD)
+        row_ids = place * own + lax.broadcasted_iota(jnp.int32, (own, length), 0)
+        col_ids = lax.broadcasted_iota(jnp.int32, (own, length), 1)
+        allowed = (col_ids <= row_ids) & (col_ids > row_ids - WINDOW)
+
+        def scores_of():
+            raw = jnp.einsum("qhgd,khd->hgqk", heads_q, keys_all, preferred_element_type=jnp.float32)
+            return jnp.where(allowed, raw * score_scale, -1e30)
+
+        scores = scores_of()
+        row_top = jnp.max(scores, axis=-1, keepdims=True)
+        log_total = row_top + jnp.log(jnp.sum(jnp.exp(scores - row_top), axis=-1, keepdims=True))
+        probs = jnp.exp(scores - log_total)
+        probs_bf = probs.astype(BF16)
+        attn_rows = jnp.einsum(
+            "hgqk,khd->qhgd", probs_bf, vals_all, preferred_element_type=jnp.float32
+        ).reshape(own, -1)
+        attn_scale = rms_scale(attn_rows)
+        branch_attn = (attn_rows * attn_scale * attn_gain).astype(BF16)
+        branch_attn_c = attn_to_channels(branch_attn)
 
     ssm_raw = scan_out + skip * conv_vals
     gate_act = jax.nn.silu(gate_z)
@@ -1116,30 +1796,30 @@
     ssm_scale = lax.rsqrt(square / inner + EPSILON)[:, None]
     branch_ssm = (ssm_gated * ssm_scale * gain_ssm).astype(BF16)
     middle = tokens + 0.5 * reduce_products(
-        [(branch_attn_c, attn_full), (branch_ssm, mixout_full)], (False, False), 4
+        [branch_attn_c, branch_ssm], [attn_full, mixout_full], False, 4
     )
     ffn_scale = rms_scale(middle)
     ffn_in = (middle * ffn_scale * ffn_gain).astype(BF16)
     if ctx == 8:
-        ffn_all, hidden, grad_pair, ffn_out, grad_ffn_in = ffn_both_ways(
+        pair_dw, down_dw, ffn_out, grad_ffn_in = ffn_both_ways(
             ffn_in, grad_top, ffn_full, down_full, 5
         )
     else:
         ffn_all = gather_tokens(ffn_in, 5)
         pre = matmul(ffn_all, ffn_full)
-        gate_pre, up_pre = pre[:, :hid], pre[:, hid:]
+        gate_pre, up_pre = pre[:, :hid_all], pre[:, hid_all:]
         gate_silu = jax.nn.silu(gate_pre)
         hidden = (gate_silu * up_pre).astype(BF16)
-        ffn_out = reduce_products([(hidden, down_full)], (False,), 6)
+        ffn_out = reduce_products([hidden], [down_full], False, 6)
         grad_hidden = right_trans(grad_top, down_full)
         grad_gate = (grad_hidden * up_pre * silu_slope(gate_pre)).astype(BF16)
         grad_up = (grad_hidden * gate_silu).astype(BF16)
         grad_pair = jnp.concatenate([grad_gate, grad_up], 1)
-        grad_ffn_in = reduce_products([(grad_pair, ffn_full)], (True,), 7)
+        grad_ffn_in = reduce_products([grad_pair], [ffn_full], True, 7)
+        down_dw = left_trans(hidden, grad_top).astype(BF16)
+        pair_dw = left_trans(ffn_all, grad_pair).astype(BF16)
     output = middle + ffn_out
 
-    down_dw = left_trans(hidden, grad_top).astype(BF16)
-    pair_dw = left_trans(ffn_all, grad_pair).astype(BF16)
     grad_ffn_in, down_dw, pair_dw = lax.optimization_barrier((grad_ffn_in, down_dw, pair_dw))
     (down_grad,) = scatter_fsdp(down_dw)
     (pair_grad,) = scatter_fsdp(pair_dw)
@@ -1147,45 +1827,53 @@
     grad_middle = grad_middle + cotangent[0].astype(jnp.float32)
     grad_branch = (0.5 * grad_middle).astype(BF16)
     branch_all = gather_tokens(grad_branch, 8)
-    branch_all, down_grad = lax.optimization_barrier((branch_all, down_grad))
-    attn_grad, mixout_grad = scatter_fsdp(
-        left_trans(branch_attn_c, branch_all), left_trans(branch_ssm, branch_all)
+    attn_dw, mixout_dw = left_trans(branch_attn_c, branch_all), left_trans(branch_ssm, branch_all)
+    grad_attn_c = right_trans(branch_all, attn_full).astype(BF16)
+    if ctx == 8:
+        grad_early, grad_attn_gain = attention_backward(
+            grad_attn_c, attn_rows, attn_gain, attn_kept, 13
+        )
+        grad_attn_gain = grad_attn_gain[0]
+    else:
+        grad_attn = attn_to_tokens(grad_attn_c).astype(jnp.float32)
+        grad_attn_raw, grad_attn_gain = norm_back(grad_attn, attn_rows, attn_scale, attn_gain)
+        grad_heads = grad_attn_raw.astype(BF16).reshape(own, KV_HEADS, group_size, HEAD)
+        grad_probs = jnp.einsum(
+            "qhgd,khd->hgqk", grad_heads, vals_all, preferred_element_type=jnp.float32
+        )
+        row_dot = jnp.sum(probs * grad_probs, axis=-1, keepdims=True)
+        grad_scores = (probs * (grad_probs - row_dot)).astype(BF16)
+        grad_queries = score_scale * jnp.einsum(
+            "hgqk,khd->qhgd", grad_scores, keys_all, preferred_element_type=jnp.float32
+        ).reshape(own, -1)
+        grad_keys = score_scale * jnp.einsum(
+            "hgqk,qhgd->khd", grad_scores, heads_q, preferred_element_type=jnp.float32
+        )
+        grad_vals = jnp.einsum(
+            "hgqk,qhgd->khd", probs_bf, grad_heads, preferred_element_type=jnp.float32
+        )
+        grad_queries = lax.all_to_all(
+            grad_queries.astype(BF16).reshape(own, ctx, -1).transpose(1, 0, 2), "ctx", 0, 0, tiled=True
+        ).reshape(length, -1)
+        grad_kv = jnp.concatenate(
+            [
+                grad_keys.reshape(length, ctx, kv_mine).transpose(1, 0, 2),
+                grad_vals.reshape(length, ctx, kv_mine).transpose(1, 0, 2),
+            ],
+            2,
+        ).astype(BF16)
+        grad_kv = jnp.sum(
+            lax.all_to_all(grad_kv, "ctx", 0, 0, tiled=True).astype(jnp.float32), axis=0
+        ).astype(BF16)
+        grad_early = jnp.concatenate([grad_queries, grad_kv], 1)
+
+    grad_early, attn_dw, mixout_dw, pair_grad = lax.optimization_barrier(
+        (grad_early, attn_dw.astype(BF16), mixout_dw.astype(BF16), pair_grad)
     )
-
-    grad_attn = attn_to_tokens(right_trans(branch_all, attn_full).astype(BF16)).astype(jnp.float32)
-    grad_attn_raw, grad_attn_gain = norm_back(grad_attn, attn_rows, attn_scale, attn_gain)
-    grad_heads = grad_attn_raw.astype(BF16).reshape(own, KV_HEADS, group_size, HEAD)
-    grad_probs = jnp.einsum(
-        "qhgd,khd->hgqk", grad_heads, vals_all, preferred_element_type=jnp.float32
-    )
-    row_dot = jnp.sum(probs * grad_probs, axis=-1, keepdims=True)
-    grad_scores = (probs * (grad_probs - row_dot)).astype(BF16)
-    grad_queries = score_scale * jnp.einsum(
-        "hgqk,khd->qhgd", grad_scores, keys_all, preferred_element_type=jnp.float32
-    ).reshape(own, -1)
-    grad_keys = score_scale * jnp.einsum(
-        "hgqk,qhgd->khd", grad_scores, heads_q, preferred_element_type=jnp.float32
-    )
-    grad_vals = jnp.einsum(
-        "hgqk,qhgd->khd", probs_bf, grad_heads, preferred_element_type=jnp.float32
-    )
-    grad_queries = lax.all_to_all(
-        grad_queries.astype(BF16).reshape(own, ctx, -1).transpose(1, 0, 2), "ctx", 0, 0, tiled=True
-    ).reshape(length, -1)
-    grad_kv = jnp.concatenate(
-        [
-            grad_keys.reshape(length, ctx, kv_mine).transpose(1, 0, 2),
-            grad_vals.reshape(length, ctx, kv_mine).transpose(1, 0, 2),
-        ],
-        2,
-    ).astype(BF16)
-    grad_kv = jnp.sum(
-        lax.all_to_all(grad_kv, "ctx", 0, 0, tiled=True).astype(jnp.float32), axis=0
-    ).astype(BF16)
+    attn_grad, mixout_grad = scatter_fsdp(attn_dw, mixout_dw)
 
     grad_norm = right_trans(branch_all, mixout_full)
     grad_ssm_gain = jnp.sum(grad_norm * ssm_gated * ssm_scale, axis=0)
-    grad_norm, pair_grad = lax.optimization_barrier((grad_norm, pair_grad))
     scaled = grad_norm * gain_ssm
     mean_dot = total_of(jnp.sum(scaled * ssm_gated, axis=-1), 9)[:, None] / inner
     grad_gated = ssm_scale * scaled - ssm_gated * ssm_scale**3 * mean_dot
@@ -1193,14 +1881,21 @@
     grad_gate_z = grad_gated * ssm_raw * silu_slope(gate_z)
     grad_skip = jnp.sum(grad_scan * conv_vals, axis=0)
     grad_gate_bf = grad_gate_z.astype(BF16)
-    grad_early = jnp.concatenate([grad_queries, grad_kv, grad_gate_bf], 1)
+    grad_early = jnp.concatenate([grad_early, grad_gate_bf], 1)
     (early_grad,) = scatter_fsdp(left_trans(normed_all, grad_early))
+    pair_grad = pair_grad.reshape(-1, 2, fsdp, down_at)[..., :hid_part]
+    pair_slots = to_slots(pair_grad.transpose(1, 0, 2, 3).reshape(-1, hid), hidden_units)
+    down_slots = rows_to_slots(down_grad[:hid_part])
+    pair_slots = lax.all_to_all(pair_slots, "ctx", 0, 0, tiled=True)
+    down_slots = lax.all_to_all(down_slots, "ctx", 0, 0, tiled=True)
     grad_steps, grad_drive, grad_input_mat, grad_output_mat, grad_rate = scan_bwd(
         steps_pad, vals_pad, padded(grad_scan), in_b, out_b, rates_log2, states
     )
-    grad_steps, attn_grad, mixout_grad = lax.optimization_barrier(
-        (grad_steps, attn_grad, mixout_grad)
+    grad_steps, pair_slots, down_slots, attn_grad, mixout_grad = lax.optimization_barrier(
+        (grad_steps, pair_slots, down_slots, attn_grad, mixout_grad)
     )
+    pair_blocks = from_slots(pair_slots, hidden_units)
+    down_blocks = rows_from_slots(down_slots, hidden_rows)
     grad_steps, grad_drive, grad_rate = (
         grad_steps[:, :mine],
         grad_drive[:, :mine],
@@ -1233,9 +1928,7 @@
     )
     grad_src = grad_src.astype(BF16)
     src_grad, step_grad = scatter_fsdp(left_trans(normed_all, grad_src), step_dw)
-    grad_normed = reduce_products(
-        [(grad_early, early_full), (grad_src, src_full)], (True, True), 11
-    )
+    grad_normed = reduce_products([grad_early, grad_src], [in_full], True, 11)
     grad_tokens, grad_norm_gain = norm_back(grad_normed, tokens, norm_scale, norm_gain)
     grad_tokens = grad_tokens + grad_middle
 
@@ -1249,48 +1942,54 @@
         0,
     )
     gains = jnp.stack([grad_norm_gain, grad_attn_gain, grad_ffn_gain])
-    channel, gains = settle_small(
-        jnp.pad(channel, ((0, -channel.shape[0] % (8 * fsdp)), (0, 0))),
-        jnp.pad(gains, ((0, 5), (0, 0))),
-        12,
-    )
-    channel = channel.reshape(ctx, -1, fsdp, mine // fsdp).transpose(1, 2, 0, 3)
-    channel = channel.reshape(-1, inner)
+    channel = jnp.pad(channel, ((0, -channel.shape[0] % (8 * fsdp)), (0, 0)))
+    gains = jnp.pad(gains, ((0, 5), (0, 0)))
+    if ctx == 8 and ctx == 2 * fsdp and not attn_pad:
+        (
+            query_grad, key_grad, value_grad, mixer_grad, step_grad, attn_grad, mixout_grad, channel, gains,
+        ) = finish(
+            early_grad, src_grad, step_grad, attn_grad, mixout_grad, channel, gains,
+            q_mine, kv_mine, 12,
+        )
+    else:
+        channel, gains = settle_small(channel, gains, 12)
+        channel = channel.reshape(ctx, -1, fsdp, mine // fsdp).transpose(1, 2, 0, 3)
+        channel = channel.reshape(-1, inner)
+        late_at = q_mine + 2 * kv_mine
+        query_grad = early_grad[:, :q_mine].astype(jnp.float32)
+        key_grad = early_grad[:, q_mine : q_mine + kv_mine].astype(jnp.float32)
+        value_grad = early_grad[:, q_mine + kv_mine : late_at].astype(jnp.float32)
+        mixer_grad = to_blocks(
+            jnp.concatenate([src_grad, early_grad[:, late_at:]], 1), 2 * fsdp
+        )
+        step_grad = to_blocks(step_grad, fsdp)
+        attn_grad = rows_to_blocks(attn_grad, 1)[: attn_proj.shape[0]]
+        mixout_grad = rows_to_blocks(mixout_grad, 1)
     sum_norm_gain, sum_attn_gain, sum_ffn_gain = gains[0], gains[1], gains[2]
-    pair_blocks = to_blocks(
-        jnp.concatenate(
-            [
-                pair_grad[:, :hid].reshape(-1, hidden_units, hid // hidden_units),
-                pair_grad[:, hid:].reshape(-1, hidden_units, hid // hidden_units),
-            ],
-            0,
-        ).reshape(-1, hid),
-        hidden_units,
-    )
-    half = pair_grad.shape[0]
+    half = pair_blocks.shape[0] // 2
     return (
         output[None],
         grad_tokens[None],
         sum_norm_gain,
-        early_grad[:, :q_mine].astype(jnp.float32),
-        early_grad[:, q_mine : q_mine + kv_mine].astype(jnp.float32),
-        early_grad[:, q_mine + kv_mine : q_mine + 2 * kv_mine].astype(jnp.float32),
-        rows_to_blocks(attn_grad, 1)[: attn_proj.shape[0]],
+        query_grad,
+        key_grad,
+        value_grad,
+        attn_grad,
         sum_attn_gain,
-        to_blocks(jnp.concatenate([src_grad, early_grad[:, q_mine + 2 * kv_mine :]], 1), 2 * fsdp),
+        mixer_grad,
         channel[:CONV],
         channel[CONV],
         channel[CONV + 4 + STATE : CONV + 4 + STATE + state_proj.shape[1]].T,
-        to_blocks(step_grad, fsdp),
+        step_grad,
         channel[CONV + 1],
         channel[CONV + 4 : CONV + 4 + STATE].T,
         channel[CONV + 2],
-        rows_to_blocks(mixout_grad, 1),
+        mixout_grad,
         channel[CONV + 3],
         sum_ffn_gain,
         pair_blocks[:half],
         pair_blocks[half:],
-        rows_to_blocks(down_grad, hidden_rows),
+        down_blocks,
     )
 
 

time: 857 us -> 725 us (0.85)
  Pallas kernels: 367 us -> 496 us
  local copies, waits for them, and re-layouts: 202 us -> 99.8 us
  matrix products: 84 us -> 35.4 us
  waiting for transfers between devices: 51.2 us -> 11.7 us
  other arithmetic: 78.8 us -> 44.3 us
  starting transfers between devices: 47.7 us -> 13.2 us
    pallas_call x5 -> x8, Pallas kernels: 210 us -> 361 us  [the longest x1 76.4 us: front(): pl.pallas_call(functools.partial(front_kernel, bits, count, pack), out_sh...]
    all_to_all x11 -> x2, starting transfers between devices: 47.5 us -> 12.8 us  [the longest x1 7.84 us: body(): pair_slots = lax.all_to_all(pair_slots, 'ctx', 0, 0, tiled=True)]
    dot_general x6 -> x0, matrix products: 28.2 us -> none  [the longest x1 9.45 us: body(): jnp.einsum('qhgd,khd->hgqk', grad_heads, vals_all, preferred_element_type...]
    reshape x18 -> x4, local copies, waits for them, and re-layouts: 34.8 us -> 8.16 us  [the longest x2 3.29 us: rows_to_slots(): return array.reshape(rows, ctx, columns // ctx).transpose(1, 0, 2)]
    dot_general x8 -> x6, matrix products: 32.6 us -> 12.3 us  [left_trans(): lax.dot_general(left, right, (((0,), (0,)), ((), ())), preferred_element_...]
    pallas_call x2 -> x1, Pallas kernels: 40.4 us -> 23 us  [gather_shards(): pl.pallas_call(functools.partial(gather_kernel, bits), out_shape=jax.Shap...]
    all_gather x2 -> x1, waiting for transfers between devices: 16.1 us -> 0.01 us  [over_fsdp(): return lax.all_gather(array, 'fsdp', axis=0, tiled=True)]
    slice x14 -> x3, local copies, waits for them, and re-layouts: 21.7 us -> 7.97 us  [the longest x1 3.24 us: body(): down_full = rows_full[:, :down_at].reshape(-1, model)]
  transfers between devices with their start and end apart: 19 -> 9, of which waited for: 7 -> 2; matrix products, arithmetic and copies ran while one was open for 36% -> 19% of each run, Pallas kernels for 30% -> 42%
where the time goes in v2:
time: 725 us; the launch traced here: 716 us
  Pallas kernels  496 us (68%)
  local copies, waits for them, and re-layouts  99.8 us (14%)
  other arithmetic  44.3 us (6%)
  matrix products  35.4 us (5%)
  between operations  15.3 us (2%)
  starting transfers between devices  13.2 us (2%)
  waiting for transfers between devices  11.7 us (2%)
    pallas_call x1, Pallas kernels, front(): pl.pallas_call(functools.partial(front_kernel, bits, count, pack), out_sh...  76.4 us
    pallas_call x1, Pallas kernels, ffn_both_ways(): pl.pallas_call(ffn_kernel, out_shape=[jax.ShapeDtypeStruct((model, 2 * hi...  69.4 us
    pallas_call x2, Pallas kernels, reduce_products(): pl.pallas_call(functools.partial(reduce_kernel, bits, (trans,) * len(left...  57.2 us
    pallas_call x1, Pallas kernels, attention_forward(): pl.pallas_call(functools.partial(attention_kernel, ctx, fsdp), out_shape=...  52.6 us
    pallas_call x1, Pallas kernels, attention_backward(): pl.pallas_call(functools.partial(attention_back_kernel, ctx, fsdp), out_s...  52 us
    pallas_call x1, Pallas kernels, finish(): pl.pallas_call(functools.partial(finish_kernel, ctx, fsdp), out_shape=[sh...  45.5 us
    pallas_call x1, Pallas kernels, scan_bwd(): pl.pallas_call(scan_bwd_kernel, grid=(count,), in_specs=[row, row, row, m...  40.7 us
    pallas_call x2, Pallas kernels, sum_everywhere(): pl.pallas_call(functools.partial(sum_kernel, ctx), out_shape=jax.ShapeDty...  40.1 us
  transfers between devices with their start and end apart: 9, of which 2 were waited for; matrix products, arithmetic and copies ran while one was open for 19% of the time, Pallas kernels for 42%

profile of v2, /device:TPU:1, one launch (start us, length us, event | category | flops | bytes accessed | tf_op | source)
XLA Modules:
  0.0 715.5 jit_solution(8996759900176305249)
XLA Ops:
  13.7 7.5 %pack_in.1 = (bf16[400,1080]{1,0:T(8,128)(2,1)}, bf16[112,132]{1,0:T(8,128)(2,1)}, bf16[32,400]{1,0:T(8,128)(2,1)}) custom-call(bf16[400,1600]{1,0:T(8,128)(2,1)} %query_ref.1, bf16[400,320]{1,0:T(8,128)(2,1)} %key_ref.1, bf16[400,320]{1,0:T(8,128)(2,1)} %value_ref.1, bf16[400,6400]{1,0:T(8,128)(2,1)} %mixer_ref.1, bf16[800,132]{1,0:T(8,128)(2,1)} %copy.154.state_ref, ...), custom_call_target="tpu_custom_call" | custom-call | tf_op jit(solution)/shard_map/pack_in/pallas_call | solution.py:1211
  21.2 76.4 %front.1 = (bf16[8,128,1600]{2,1,0:T(8,128)(2,1)}, bf16[8,128,1600]{2,1,0:T(8,128)(2,1)}, bf16[4,400,1080]{2,1,0:T(8,128)(2,1)}, bf16[4,112,132]{2,1,0:T(8,128)(...) custom-call(bf16[128,1600]{1,0:T(8,128)(2,1)} %bitcast.150, ...), custom_call_target="tpu_custom_call" | custom-call | tf_op jit(solution)/shard_map/front/pallas_call | solution.py:272
  101.0 7.9 %convolution_convert_fusion.proj_ref = bf16[1024,1080]{1,0:T(8,128)(2,1)S(1)} fusion(bf16[1024,1600]{1,0:T(8,128)(2,1)} %bitcast.208, bf16[1600,1080]{1,0:T(8,128)(2,1)} %bitcast.168), kind=kOutput, calls=%fused_computation.1 | convolution fusion | flops 3540049920 | bytes 8944640 | tf_op jit(solution)/shard_map/dot_general | solution.py:1488
  110.4 2.7 multiply_convert_fusion.1
  114.7 20.8 %sum_everywhere.2 = bf16[8,128,132]{2,1,0:T(8,128)(2,1)} custom-call(bf16[8,128,132]{2,1,0:T(8,128)(2,1)} %bitcast.178), custom_call_target="tpu_custom_call" | custom-call | tf_op jit(solution)/shard_map/sum_everywhere/pallas_call | solution.py:457
  137.2 2.6 compare_select_fusion
  141.3 4.3 broadcast_in_dim.18.in_ref
  145.6 3.8 broadcast_in_dim.19.out_ref
  149.4 19.2 %scan_forward.1 = (f32[1024,512]{1,0:T(8,128)S(1)}, f32[1024,16,512]{2,1,0:T(8,128)}) custom-call(f32[1024,512]{1,0:T(8,128)S(1)} %pad.24.steps_ref, f32[1024,512]{1,0:T(8,128)} %pad.25.drive_ref, bf16[1024,16,128]{2,1,0:T(8,128)(2,1)} %broadcast_in_dim.18.in_ref, bf16[1024,16,128]{2,1,0:T(8,128)(2,1)} %broadcast_in_dim.19.out_ref, f32[16,512]{1,0:T(8,128)S(1)} %pad.26.rate_ref), custom_call_target="tpu_custom_call" | custom-call | tf_op jit(solution)/shard_map/scan_forward/pallas_call | solution.py:1374
  169.9 3.2 multiply_reduce_fusion.7
  173.1 5.9 total_of.2
  179.6 52.6 %attention_forward.1 = (bf16[8,128,200]{2,1,0:T(8,128)(2,1)}, f32[128,1600]{1,0:T(8,128)}, bf16[5,1024,640]{2,1,0:T(8,128)(2,1)}, f32[5,1,640]{2,1,0:T(1,128)}, ...) custom-call(bf16[1024,1080]{1,0:T(8,128)(2,1)} %copy-done.9, ...), custom_call_target="tpu_custom_call" | custom-call | tf_op jit(solution)/shard_map/attention_forward/pallas_call | solution.py:849
  233.5 2.5 slice.206
  236.0 2.2 slice.205
  238.2 3.2 slice.207
  241.5 2.6 reshape.236.refs_3_
  244.1 2.3 reshape.235.refs_2_
  246.4 24.9 %reduce_products.2 = f32[128,1600]{1,0:T(8,128)} custom-call(bf16[8,128,200]{2,1,0:T(8,128)(2,1)} %get-tuple-element.80.refs_0_, bf16[8,128,400]{2,1,0:T(8,128)(2,1)} %bitcast.166, bf16[200,1600]{1,0:T(8,128)(2,1)} %reshape.235.refs_2_, bf16[400,1600]{1,0:T(8,128)(2,1)} %reshape.236.refs_3_), custom_call_target="tpu_custom_call" | custom-call | tf_op jit(solution)/shard_map/reduce_products/pallas_call | solution.py:412
  275.0 69.4 %ffn_both_ways.1 = (bf16[1600,1408]{1,0:T(8,128)(2,1)}, bf16[704,1600]{1,0:T(8,128)(2,1)}, f32[128,1600]{1,0:T(8,128)}, f32[128,1600]{1,0:T(8,128)}) custom-call(bf16[128,1600]{1,0:T(8,128)(2,1)} %multiply_convert_fusion.3.x_ref, bf16[8,128,1600]{2,1,0:T(8,128)(2,1)} %get-tuple-element.85.top_ref, bf16[1600,1408]{1,0:T(8,128)(2,1)} %all-gather.4.cloned.1.call-done.pair_w, ...), custom_call_target="tpu_custom_call" | custom-call | tf_op jit(solution)/shard_map/ffn_both_ways/pallas_call | solution.py:712
  345.2 2.3 multiply_reduce_fusion.8
  347.5 3.0 multiply_convert_fusion.2
  350.6 23.0 %gather_shards.1 = bf16[8,128,1600]{2,1,0:T(8,128)(2,1)} custom-call(bf16[128,1600]{1,0:T(8,128)(2,1)} %get-tuple-element.264.x_ref), custom_call_target="tpu_custom_call" | custom-call | tf_op jit(solution)/shard_map/gather_shards/pallas_call | solution.py:136
  373.6 4.0 convolution_convert_fusion.4
  379.6 52.0 %attention_backward.1 = (bf16[1024,280]{1,0:T(8,128)(2,1)}, f32[1,1600]{1,0:T(1,128)}) custom-call(bf16[8,128,200]{2,1,0:T(8,128)(2,1)} %bitcast.177, f32[128,1600]{1,0:T(8,128)} %get-tuple-element.92.rows_ref, f32[1,1600]{1,0:T(1,128)} %broadcast_in_dim.17.gain_ref, bf16[5,1024,640]{2,1,0:T(8,128)(2,1)} %get-tuple-element.93.prob_ref, ...), custom_call_target="tpu_custom_call" | custom-call | tf_op jit(solution)/shard_map/attention_backward/pallas_call | solution.py:986
  433.5 2.8 convolution_convert_fusion.3
  436.2 2.3 reshape.245
  440.7 3.5 maximum_maximum_fusion
  444.4 5.4 multiply_reduce_fusion
  449.8 6.3 total_of.3
  456.8 5.1 multiply_reduce_fusion.1
  464.5 4.2 convolution_convert_fusion.1
  468.8 6.8 reduce-scatter.8.cloned.1.call-done
  475.5 2.3 reshape.243
  478.8 4.9 all-to-all-start.1
  486.3 2.3 reshape_reshape.3
  488.5 3.6 all-to-all-done.1
  492.1 7.8 %all-to-all-start = ((bf16[8,800,86]{1,2,0:T(8,128)(2,1)}), bf16[8,800,86]{1,2,0:T(8,128)(2,1)}, u32[]{:S(2)}, u32[]{:S(2)}) async-start(bf16[8,800,86]{1,2,0:T(8,128)(2,1)} %bitcast.158), calls=%async_computation.1 | async-start | bytes 2523136 | tf_op jit(solution)/shard_map/all_to_all | solution.py:1889
  501.6 40.7 %scan_backward.1 = (f32[1024,512]{1,0:T(8,128)S(1)}, f32[1024,512]{1,0:T(8,128)S(1)}, f32[8,8,2048]{2,1,0:T(8,128)S(1)}, f32[8,8,2048]{2,1,0:T(8,128)S(1)}, f32[16,512]{1,0:T(8,128)S(1)}) custom-call(f32[1024,512]{1,0:T(8,128)} %copy-done, f32[1024,512]{1,0:T(8,128)} %pad.25.drive_ref, f32[1024,512]{1,0:T(8,128)} %pad.27.grad_ref, ...), custom_call_target="tpu_custom_call" | custom-call | tf_op jit(solution)/shard_map/scan_backward/pallas_call | solution.py:1463
  549.2 2.3 fusion.29
  552.9 2.5 pad_maximum_fusion.1.x_ref
  555.4 19.3 %sum_everywhere.3 = bf16[8,128,132]{2,1,0:T(8,128)(2,1)} custom-call(bf16[8,128,132]{2,1,0:T(8,128)(2,1)} %pad_maximum_fusion.1.x_ref), custom_call_target="tpu_custom_call" | custom-call | tf_op jit(solution)/shard_map/sum_everywhere/pallas_call | solution.py:457
  576.4 2.2 add_convert_fusion.1
  578.6 5.6 fusion.27
  595.6 2.8 copy.181
  602.7 2.4 copy.175
  607.3 32.3 %reduce_products.3 = f32[128,1600]{1,0:T(8,128)} custom-call(bf16[8,128,680]{2,1,0:T(8,128)(2,1)} %bitcast.156, bf16[8,128,400]{2,1,0:T(8,128)(2,1)} %bitcast.165, bf16[1600,1080]{1,0:T(8,128)(2,1)} %bitcast.169), custom_call_target="tpu_custom_call" | custom-call | tf_op jit(solution)/shard_map/reduce_products/pallas_call | solution.py:412
  647.5 45.5 %finish.1 = (f32[400,200]{1,0:T(8,128)}, f32[400,40]{1,0:T(8,128)}, f32[400,40]{1,0:T(8,128)}, f32[400,800]{1,0:T(8,128)}, f32[25,400]{1,0:T(8,128)}, /*index=5*...) custom-call(bf16[400,680]{1,0:T(8,128)(2,1)} %reduce-scatter.12.cloned.1.call-done.early_ref, ...), custom_call_target="tpu_custom_call" | custom-call | tf_op jit(solution)/shard_map/finish/pallas_call | solution.py:1133
  693.0 2.9 slice_bitcast_fusion
  (239 shorter events, 85.9 us)
Async XLA Ops:
  7.2 5.9 copy-start.41
  7.2 226.3 %all-gather.6.cloned.1.call-start = ((), (), s32[]{:S(2)}) async-start(), calls=%async_computation.13 | async-start | bytes 5591040 | tf_op jit(solution)/shard_map/all_gather | solution.py:1694
  97.7 177.4 %all-gather.4.cloned.1.call-start = ((), (), s32[]{:S(2)}) async-start(), calls=%async_computation.7 | async-start | bytes 5632000 | tf_op jit(solution)/shard_map/all_gather | solution.py:1548
  98.4 337.8 %reduce-scatter.6.cloned.1.call-start = ((), (), s32[]{:S(2)}) async-start(), calls=%async_computation.8 | async-start | bytes 5632000 | tf_op jit(solution)/shard_map/reduce_scatter | solution.py:1598
  99.1 14.1 %copy-start.26 = (bf16[400,132]{0,1:T(8,128)(2,1)}, bf16[400,132]{0,1:T(8,128)(2,1)S(1)}, u32[]{:S(2)}) copy-start(bf16[400,132]{0,1:T(8,128)(2,1)S(1)} %reshape.230) | copy-start | bytes 316804
  101.0 9.4 %copy-start.45 = (f32[1,400]{1,0:T(1,128)}, f32[1,400]{1,0:T(1,128)S(1)}, u32[]{:S(2)}) copy-start(f32[1,400]{1,0:T(1,128)S(1)} %get-tuple-element.304) | copy-start | bytes 4804
  101.0 9.4 %copy-start.47 = (f32[1,400]{1,0:T(1,128)}, f32[1,400]{1,0:T(1,128)S(1)}, u32[]{:S(2)}) copy-start(f32[1,400]{1,0:T(1,128)S(1)} %get-tuple-element.305) | copy-start | bytes 4804
  101.0 9.4 %copy-start.49 = (f32[1,400]{1,0:T(1,128)}, f32[1,400]{1,0:T(1,128)S(1)}, u32[]{:S(2)}) copy-start(f32[1,400]{1,0:T(1,128)S(1)} %get-tuple-element.306) | copy-start | bytes 4804
  109.4 3.8 copy-start.8
  113.2 343.6 %copy-start.5 = (bf16[1024,400]{1,0:T(8,128)(2,1)}, bf16[1024,400]{1,0:T(8,128)(2,1)S(1)}, u32[]{:S(2)}) copy-start(bf16[1024,400]{1,0:T(8,128)(2,1)S(1)} %get-tuple-element.270) | copy-start | bytes 2457604
  113.2 22.3 %copy-start.39 = (bf16[4,32,400]{2,1,0:T(8,128)(2,1)S(1)}, bf16[4,32,400]{2,1,0:T(8,128)(2,1)}, u32[]{:S(2)}) copy-start(bf16[4,32,400]{2,1,0:T(8,128)(2,1)} %get-tuple-element.82) | copy-start | bytes 307204
  135.5 4.3 copy-start.32
  140.0 9.4 %copy-start = (f32[1024,512]{1,0:T(8,128)}, f32[1024,512]{1,0:T(8,128)S(1)}, u32[]{:S(2)}) copy-start(f32[1024,512]{1,0:T(8,128)S(1)} %pad.24.steps_ref) | copy-start | bytes 6291460
  168.6 4.5 copy-start.1
  169.9 9.1 %copy-start.54 = (f32[1600]{0:T(1024)S(1)}, f32[1600]{0:T(1024)}, u32[]{:S(2)}) copy-start(f32[1600]{0:T(1024)} %param.29) | copy-start | bytes 19204
  179.0 53.3 %copy-start.43 = (f32[8,128]{1,0:T(8,128)S(1)}, f32[8,128]{1,0:T(8,128)}, u32[]{:S(2)}) copy-start(f32[8,128]{1,0:T(8,128)} %total_of.2) | copy-start | bytes 12292
  246.4 24.9 %copy-start.12 = (bf16[1,128,1600]{2,1,0:T(8,128)(2,1)S(1)}, bf16[1,128,1600]{2,1,0:T(8,128)(2,1)}, u32[]{:S(2)}) copy-start(bf16[1,128,1600]{2,1,0:T(8,128)(2,1)} %copy.152) | copy-start | bytes 1228804
  271.3 2.9 copy-start.40
  344.4 131.1 %reduce-scatter.8.cloned.1.call-start = ((), (), s32[]{:S(2)}) async-start(), calls=%async_computation.9 | async-start | bytes 2928640 | tf_op jit(solution)/shard_map/reduce_scatter | solution.py:1598
  345.0 200.8 %reduce-scatter.10.cloned.1.call-start = ((), (), s32[]{:S(2)}) async-start(), calls=%async_computation.10 | async-start | bytes 2662400 | tf_op jit(solution)/shard_map/reduce_scatter | solution.py:1598
  350.6 23.0 %copy-start.24 = (bf16[200,1600]{1,0:T(8,128)(2,1)S(1)}, bf16[200,1600]{1,0:T(8,128)(2,1)}, u32[]{:S(2)}) copy-start(bf16[200,1600]{1,0:T(8,128)(2,1)} %reshape.235.refs_2_) | copy-start | bytes 1920004
  379.6 52.0 %copy-start.21 = (bf16[8,128,1600]{2,1,0:T(8,128)(2,1)S(1)}, bf16[8,128,1600]{2,1,0:T(8,128)(2,1)}, u32[]{:S(2)}) copy-start(bf16[8,128,1600]{2,1,0:T(8,128)(2,1)} %gather_shards.1) | copy-start | bytes 9830404
  379.6 52.0 %copy-start.31 = (bf16[8,128,200]{2,1,0:T(8,128)(2,1)S(1)}, bf16[8,128,200]{2,1,0:T(8,128)(2,1)}, u32[]{:S(2)}) copy-start(bf16[8,128,200]{2,1,0:T(8,128)(2,1)} %get-tuple-element.80.refs_0_) | copy-start | bytes 1228804
  444.3 134.3 %reduce-scatter.12.cloned.1.call-start = ((), (), s32[]{:S(2)}) async-start(), calls=%async_computation.11 | async-start | bytes 3072000 | tf_op jit(solution)/shard_map/reduce_scatter | solution.py:1598
  444.4 12.5 %copy-start.2 = (f32[1024,512]{1,0:T(8,128)S(1)}, f32[1024,512]{1,0:T(8,128)}, u32[]{:S(2)}) copy-start(f32[1024,512]{1,0:T(8,128)} %copy-done.1) | copy-start | bytes 6291460
  456.8 5.1 copy-start.30
  468.7 15.0 %copy-start.28 = (bf16[400,1408]{1,0:T(8,128)(2,1)S(1)}, bf16[400,1408]{1,0:T(8,128)(2,1)}, u32[]{:S(2)}) copy-start(bf16[400,1408]{1,0:T(8,128)(2,1)} %reduce-scatter.6.cloned.1.call-done) | copy-start | bytes 3379204
  478.8 13.3 %all-to-all-start.1 = ((bf16[8,172,200]{2,1,0:T(8,128)(2,1)}), bf16[8,172,200]{2,1,0:T(8,128)(2,1)}, u32[]{:S(2)}, u32[]{:S(2)}) async-start(bf16[8,172,200]{2,1,0:T(8,128)(2,1)} %bitcast.147), calls=%async_computation.3 | async-start | bytes 1441792 | tf_op jit(solution)/shard_map/all_to_all | solution.py:1890
  486.3 13.8 %copy-start.7 = (f32[1024,400]{1,0:T(8,128)S(1)}, f32[1024,400]{1,0:T(8,128)}, u32[]{:S(2)}) copy-start(f32[1024,400]{1,0:T(8,128)} %get-tuple-element.260) | copy-start | bytes 4915204
  492.1 57.1 %all-to-all-start = ((bf16[8,800,86]{1,2,0:T(8,128)(2,1)}), bf16[8,800,86]{1,2,0:T(8,128)(2,1)}, u32[]{:S(2)}, u32[]{:S(2)}) async-start(bf16[8,800,86]{1,2,0:T(8,128)(2,1)} %bitcast.158), calls=%async_computation.1 | async-start | bytes 2523136 | tf_op jit(solution)/shard_map/all_to_all | solution.py:1889
  500.0 144.3 %reduce-scatter.14.cloned.1.call-start = ((), (), s32[]{:S(2)}) async-start(), calls=%async_computation.12 | async-start | bytes 2211840 | tf_op jit(solution)/shard_map/reduce_scatter | solution.py:1598
  501.6 47.7 %copy-start.53 = (f32[1,400]{1,0:T(1,128)S(1)}, f32[1,400]{1,0:T(1,128)}, u32[]{:S(2)}) copy-start(f32[1,400]{1,0:T(1,128)} %copy-done.52) | copy-start | bytes 4804
  552.9 23.4 %copy-start.4 = (f32[1024,512]{1,0:T(8,128)S(1)}, f32[1024,512]{1,0:T(8,128)}, u32[]{:S(2)}) copy-start(f32[1024,512]{1,0:T(8,128)} %copy-done.3) | copy-start | bytes 6291460
  552.9 23.4 %copy-start.27 = (bf16[400,132]{0,1:T(8,128)(2,1)S(1)}, bf16[400,132]{0,1:T(8,128)(2,1)}, u32[]{:S(2)}) copy-start(bf16[400,132]{0,1:T(8,128)(2,1)} %copy-done.26) | copy-start | bytes 316804
  578.6 5.6 copy-start.46
  578.6 5.6 copy-start.48
  578.6 5.6 copy-start.50
  578.6 7.6 %copy-start.59 = (bf16[8,128,1600]{2,1,0:T(8,128)(2,1)S(1)}, bf16[8,128,1600]{2,1,0:T(8,128)(2,1)}, u32[]{:S(2)}) copy-start(bf16[8,128,1600]{2,1,0:T(8,128)(2,1)} %get-tuple-element.78) | copy-start | bytes 9830404
  607.3 32.3 %copy-start.13 = (bf16[1,128,1600]{2,1,0:T(8,128)(2,1)S(1)}, bf16[1,128,1600]{2,1,0:T(8,128)(2,1)}, u32[]{:S(2)}) copy-start(bf16[1,128,1600]{2,1,0:T(8,128)(2,1)} %copy.152) | copy-start | bytes 1228804
  607.3 33.9 %copy-start.51 = (f32[400]{0:T(512)S(1)}, f32[400]{0:T(512)}, u32[]{:S(2)}) copy-start(f32[400]{0:T(512)} %get-tuple-element.259) | copy-start | bytes 4804
  607.3 33.9 %copy-start.56 = (f32[400]{0:T(512)S(1)}, f32[400]{0:T(512)}, u32[]{:S(2)}) copy-start(f32[400]{0:T(512)} %get-tuple-element.238) | copy-start | bytes 4804
  692.9 8.0 %copy-start.29 = (f32[800,200]{1,0:T(8,128)S(1)}, f32[800,200]{1,0:T(8,128)}, u32[]{:S(2)}) copy-start(f32[800,200]{1,0:T(8,128)} %get-tuple-element.232) | copy-start | bytes 1920004
  693.0 9.2 %copy-start.37 = (f32[400,40]{1,0:T(8,128)S(1)}, f32[400,40]{1,0:T(8,128)}, u32[]{:S(2)}) copy-start(f32[400,40]{1,0:T(8,128)} %get-tuple-element.220) | copy-start | bytes 192004
  695.8 7.1 copy-start.36
  695.8 9.4 %copy-start.35 = (f32[400,200]{1,0:T(8,128)S(1)}, f32[400,200]{1,0:T(8,128)}, u32[]{:S(2)}) copy-start(f32[400,200]{1,0:T(8,128)} %get-tuple-element.349) | copy-start | bytes 960004
  695.8 10.1 %copy-start.34 = (f32[400,200]{1,0:T(8,128)S(1)}, f32[400,200]{1,0:T(8,128)}, u32[]{:S(2)}) copy-start(f32[400,200]{1,0:T(8,128)} %get-tuple-element.352) | copy-start | bytes 960004
  697.5 9.2 %copy-start.25 = (f32[400,800]{1,0:T(8,128)S(1)}, f32[400,800]{1,0:T(8,128)}, u32[]{:S(2)}) copy-start(f32[400,800]{1,0:T(8,128)} %get-tuple-element.354) | copy-start | bytes 3840004
  705.2 2.6 copy-start.42
  (21 other events, 37.9 us)
Sparse Core Ops, SparseCore 0:
  97.8 86.3 all-gather.5
  185.8 84.3 all-gather.3
  344.6 80.3 reduce-scatter.5
  427.2 48.2 reduce-scatter.7
  477.8 43.9 reduce-scatter.9
  524.0 48.8 reduce-scatter.11
  591.3 36.2 reduce-scatter.13

commit v3 on v2

--- a/solution.py
+++ b/solution.py
@@ -200,12 +200,15 @@
 
 
 def front_kernel(
-    bits, count, pack, x_ref, gain_ref, top_ref, in_ref, state_ref, step_ref, *rest,
+    bits, count, turned, pack_first, pack, x_ref, gain_ref, top_ref, *rest,
 ):
+    number = 6 if pack_first["scratch"] else 3
+    first_refs, rest = rest[:number], rest[number:]
     weights, rest = rest[: pack["inputs"]], rest[pack["inputs"] :]
     normed_ref, tops_ref, in_out, state_out, step_out = rest[:5]
     packed, rest = rest[5 : 5 + pack["outputs"]], rest[5 + pack["outputs"] :]
     ctx_send, ctx_recv, line_send, line_recv = rest[:4]
+    first_scratch, rest = rest[4 : 4 + len(pack_first["scratch"])], rest[4 + len(pack_first["scratch"]) :]
     me, row, rows = lax.axis_index("ctx"), lax.axis_index("fsdp"), lax.axis_size("fsdp")
     barrier = pltpu.get_barrier_semaphore()
     for bit in range(bits):
@@ -221,26 +224,32 @@
                 barrier, inc=1, device_id={"fsdp": jnp.where(there, to, row)}, device_id_type=MESH
             )
 
-    in_out[row] = in_ref[...]
-    state_out[row] = state_ref[...]
-    step_out[row] = step_ref[...]
+    if first_scratch:
+        copies = pack_in_begin(first_refs, first_scratch)
+        pack_in(row, copies, first_refs, first_scratch, in_out, state_out, step_out)
+    else:
+        for out, ref in zip((in_out, state_out, step_out), first_refs):
+            out[row] = ref[...]
     neighbours = jnp.where(row > 0, 1, 0) + jnp.where(row < rows - 1, 1, 0)
     pl.semaphore_wait(barrier, bits + neighbours)
 
     line = Copies("fsdp", line_send, line_recv)
     across = Copies("ctx", ctx_send, ctx_recv)
-    pieces = [(0, part) for part in row_parts(in_ref.shape[0], count)]
-    pieces = [(1, pl.ds(0, state_ref.shape[0])), (2, pl.ds(0, step_ref.shape[0]))] + pieces
+    pieces = [(0, part) for part in row_parts(in_out.shape[1], count)]
+    pieces = [(1, pl.ds(0, state_out.shape[1])), (2, pl.ds(0, step_out.shape[1]))] + pieces
     line_list, line_end = line_steps(line, (in_out, state_out, step_out), pieces)
     line_list[0]()
     tokens = x_ref[...].astype(jnp.float32)
+    if turned:
+        tokens = tokens.T
     scale = lax.rsqrt(jnp.mean(tokens * tokens, axis=-1, keepdims=True) + EPSILON)
     normed_ref[me] = (tokens * scale * gain_ref[...]).astype(normed_ref.dtype)
     first = gather_steps(across, bits, normed_ref)
     first[0]()
-    tops_ref[me] = top_ref[...]
+    tops = top_ref[...].astype(jnp.float32)
+    tops_ref[me] = (tops.T if turned else tops).astype(tops_ref.dtype)
     second = gather_steps(across, bits, tops_ref)
-    steps = list(pack["steps"](me, weights, packed, rest[4:])) if weights else []
+    steps = list(pack["steps"](me, weights, packed, rest)) if weights else []
     token_rest = first[1:-1] + [second[0]] + second[1:-1] + [first[-1], second[-1]]
     line_rest = line_list[1:]
     tokens_done = packs_done = 0
@@ -259,29 +268,34 @@
     line_end()
 
 
-def front(x, gain, top, in_part, state_part, step_part, later, hidden_units, collective_id):
+def front(x, gain, top, first, later, hidden_units, collective_id):
     bits, ctx, fsdp = ctx_bits(), lax.axis_size("ctx"), lax.axis_size("fsdp")
     count = 5
     ctx_sems = pltpu.SemaphoreType.DMA((2 * gather_sems(bits),))
     line_sems = pltpu.SemaphoreType.DMA((2 * fsdp * (count + 2),))
-    pack = pack_out_plan(later, hidden_units)
+    pack_first, pack = pack_in_plan(first), pack_out_plan(later, hidden_units)
+    turned = bool(later)
+    tokens = jax.ShapeDtypeStruct(x.shape[::-1] if turned else x.shape, x.dtype)
+    in_any = pl.BlockSpec(memory_space=pl.ANY)
 
     def stacked(array, size):
         return jax.ShapeDtypeStruct((size,) + array.shape, array.dtype)
 
     return pl.pallas_call(
-        functools.partial(front_kernel, bits, count, pack),
-        out_shape=[
-            stacked(x, ctx), stacked(top, ctx), stacked(in_part, fsdp),
-            stacked(state_part, fsdp), stacked(step_part, fsdp),
-        ]
+        functools.partial(front_kernel, bits, count, turned, pack_first, pack),
+        out_shape=[stacked(tokens, ctx), stacked(tokens, ctx)]
+        + [stacked(part, fsdp) for part in pack_first["shapes"]]
         + pack["shapes"],
-        in_specs=[IN_VMEM] * 6 + [pl.BlockSpec(memory_space=pl.ANY)] * len(later),
+        in_specs=[IN_VMEM] * 3
+        + [in_any if i in pack_first["any"] else IN_VMEM for i in range(len(first))]
+        + [in_any] * len(later),
         out_specs=[IN_VMEM] * (5 + pack["outputs"]),
-        scratch_shapes=[ctx_sems, ctx_sems, line_sems, line_sems] + pack["scratch"],
+        scratch_shapes=[ctx_sems, ctx_sems, line_sems, line_sems]
+        + pack_first["scratch"]
+        + pack["scratch"],
         compiler_params=params(collective_id),
         name="front",
-    )(x, gain, top, in_part, state_part, step_part, *later)
+    )(x, gain, top, *first, *later)
 
 
 def product(x, weight, trans):
@@ -329,6 +343,14 @@
                 self.inbox[0].at[self.slots[flips], self.parts[h]],
                 self.inbox[1 + phase].at[len(following), self.parts[h]],
                 flip(self.me, bit),
+            )
+
+    def send_parts(self, parts_ref):
+        for flips in self.everyone:
+            self.first[flips] = self.copies.send(
+                parts_ref.at[flipped(self.me, flips + (0,))],
+                self.inbox[0].at[self.slots[flips]],
+                flip(self.me, 0),
             )
 
     def own(self, flips, partial):
@@ -420,6 +442,47 @@
     )(*[x.reshape(ctx, rows, -1) for x in lefts], *weights)
 
 
+def relay_copies(pair_send, pair_recv, down_send, down_recv, send_sem, recv_sem):
+    size = pair_send.shape[0]
+    me = lax.axis_index("ctx")
+    copies = Copies("ctx", send_sem, recv_sem)
+    return [
+        copies.make(send.at[(me + turn) % size], recv.at[me], (me + turn) % size)
+        for send, recv in ((pair_send, pair_recv), (down_send, down_recv))
+        for turn in range(1, size)
+    ]
+
+
+def relay_begin(units, pair_ref, down_ref, pair_send, pair_recv, down_send, down_recv, *sems):
+    size = pair_send.shape[0]
+    me = lax.axis_index("ctx")
+    greet_all(me, size)
+    wide, block = pair_send.shape[2] // 2, down_send.shape[2]
+    half, part = pair_ref.shape[1] // 2, down_ref.shape[0]
+    for d in range(size):
+        at = d // units * part + d % units * wide
+        pair_send[d, :, :wide] = pair_ref[:, at : at + wide]
+        pair_send[d, :, wide:] = pair_ref[:, half + at : half + at + wide]
+        down_send[d] = down_ref[:, d * block : (d + 1) * block]
+    for copy in relay_copies(pair_send, pair_recv, down_send, down_recv, *sems):
+        copy.start()
+    pair_recv[me] = pair_send[me]
+    down_recv[me] = down_send[me]
+
+
+def relay_end(units, gate_out, up_out, down_out, pair_send, pair_recv, down_send, down_recv, *sems):
+    size, wide = pair_send.shape[0], pair_send.shape[2] // 2
+    for copy in relay_copies(pair_send, pair_recv, down_send, down_recv, *sems):
+        copy.wait()
+    for s in range(size):
+        at = s * wide
+        gate_out[:, at : at + wide] = pair_recv[s, :, :wide].astype(jnp.float32)
+        up_out[:, at : at + wide] = pair_recv[s, :, wide:].astype(jnp.float32)
+        for u in range(units):
+            to = u * size * wide + at
+            down_out[to : to + wide] = down_recv[s, u * wide : (u + 1) * wide].astype(jnp.float32)
+
+
 def greet_all(me, size):
     barrier = pltpu.get_barrier_semaphore()
     for turn in range(1, size):
@@ -429,37 +492,49 @@
     pl.semaphore_wait(barrier, size - 1)
 
 
-def sum_kernel(size, x_ref, out_ref, inbox, send_sem, recv_sem):
+def sum_kernel(size, x_ref, out_ref, send_ref, inbox, all_ref, send_sem, recv_sem):
     me = lax.axis_index("ctx")
     greet_all(me, size)
+    columns = x_ref.shape[2]
     copies = Copies("ctx", send_sem, recv_sem)
+    send_ref[:, columns:] = jnp.zeros((size, send_ref.shape[1] - columns, x_ref.shape[1]), BF16)
+    for e in range(size):
+        send_ref[e, :columns] = x_ref[e].astype(jnp.float32).T.astype(BF16)
     come = []
     for turn in range(1, size):
         to = (me + turn) % size
-        come.append(copies.send(x_ref.at[to], inbox.at[turn - 1], to))
-    total = x_ref[me].astype(jnp.float32)
+        come.append(copies.send(send_ref.at[to], inbox.at[turn - 1], to))
+    total = send_ref[me].astype(jnp.float32)
     for turn in range(1, size):
         come[turn - 1].wait_recv()
         total = total + inbox[turn - 1].astype(jnp.float32)
-    out_ref[me] = total.astype(out_ref.dtype)
+    all_ref[me] = total.astype(BF16)
     come = [
-        copies.send(out_ref.at[me], out_ref.at[me], (me + turn) % size) for turn in range(1, size)
+        copies.send(all_ref.at[me], all_ref.at[me], (me + turn) % size) for turn in range(1, size)
     ]
     for copy in come:
         copy.wait_recv()
+    for e in range(size):
+        out_ref[e] = all_ref[e].astype(jnp.float32).T[:, :columns].astype(out_ref.dtype)
     copies.finish()
 
 
 def sum_everywhere(partial, collective_id):
     ctx = lax.axis_size("ctx")
     rows, columns = partial.shape[0] // ctx, partial.shape[1]
+    high = columns + -columns % 16
     sems = pltpu.SemaphoreType.DMA((2 * (ctx - 1),))
     return pl.pallas_call(
         functools.partial(sum_kernel, ctx),
         out_shape=jax.ShapeDtypeStruct((ctx, rows, columns), partial.dtype),
         in_specs=[IN_VMEM],
         out_specs=IN_VMEM,
-        scratch_shapes=[pltpu.VMEM((ctx - 1, rows, columns), partial.dtype), sems, sems],
+        scratch_shapes=[
+            pltpu.VMEM((ctx, high, rows), BF16),
+            pltpu.VMEM((ctx - 1, high, rows), BF16),
+            pltpu.VMEM((ctx, high, rows), BF16),
+            sems, sems,
+        ],
         compiler_params=params(collective_id),
         name="sum_everywhere",
     )(partial.reshape(ctx, rows, columns)).reshape(partial.shape)
@@ -613,20 +688,15 @@
 def ffn_kernel(
     x_ref, top_ref, pair_w, down_w,
     pair_dw, down_dw, out_ref, grad_ref,
-    all_ref, hidden_ref, pair_ref, own_ref, part_out, part_grad, *rest,
+    all_ref, hidden_ref, pair_ref, own_ref, part_grad, *rest,
 ):
     bits = 3
-    boxes = (len(rest) - 2) // 2
-    inbox_out, inbox_grad = rest[:boxes], rest[boxes : 2 * boxes]
     me = lax.axis_index("ctx")
     greet(me, bits)
     all_ref[me] = x_ref[...]
     copies = Copies("ctx", *rest[-2:])
     start, forward, corner, wait = plane_gather(copies, all_ref)
-    reducers = (
-        Reducer(copies, bits, part_grad, inbox_grad, grad_ref),
-        Reducer(copies, bits, part_out, inbox_out, out_ref),
-    )
+    reducer = Reducer(copies, bits, part_grad, rest[:-2], grad_ref)
     rows, model = x_ref.shape
     hid = hidden_ref.shape[2]
     core = me % 2
@@ -647,16 +717,15 @@
         pair_ref[pair, :, :hid] = (grad_hidden * up * slope).astype(BF16).reshape(2, rows, hid)
         pair_ref[pair, :, hid:] = (grad_hidden * gate_silu).astype(BF16).reshape(2, rows, hid)
         grads = pair_ref[pair].reshape(2 * rows, 2 * hid)
-        for index, value in enumerate(
-            (product(grads, pair_w[...], True), product(hidden, down_w[...], False))
-        ):
-            low, high = value[:rows], value[rows:]
-            own_ref[index, slot] = jnp.where(core == 0, low, high)
-            reducers[index].to_sibling(flips, jnp.where(core == 0, high, low))
+        value = product(grads, pair_w[...], True)
+        low, high = value[:rows], value[rows:]
+        own_ref[slot] = jnp.where(core == 0, low, high)
+        reducer.to_sibling(flips, jnp.where(core == 0, high, low))
+        value = product(hidden, down_w[...], False)
+        out_ref[pair] = value.astype(BF16).reshape(2, rows, model)
 
     def settle(slot, flips):
-        for index, reducer in enumerate(reducers):
-            reducer.own(flips, own_ref[index, slot])
+        reducer.own(flips, own_ref[slot])
 
     start()
     wait(())
@@ -692,7 +761,7 @@
 
     size = all_ref.shape[0]
     work_left = bands(down_dw, hidden_ref, top_ref, 2) + bands(pair_dw, all_ref, pair_ref, 4)
-    turns = [turn for pair in zip(*(reducer.turns() for reducer in reducers)) for turn in pair]
+    turns = reducer.turns()
     done = 0
     for i, turn in enumerate(turns):
         upto = len(work_left) * (i + 1) // len(turns)
@@ -708,13 +777,13 @@
     rows, model = ffn_in.shape
     hid = down_full.shape[0]
     boxes, count = reducer_boxes(ctx, bits, rows, model)
-    sems = pltpu.SemaphoreType.DMA((2 * count + 8,))
+    sems = pltpu.SemaphoreType.DMA((count + 8,))
     return pl.pallas_call(
         ffn_kernel,
         out_shape=[
             jax.ShapeDtypeStruct((model, 2 * hid), BF16),
             jax.ShapeDtypeStruct((hid, model), BF16),
-            jax.ShapeDtypeStruct((rows, model), jnp.float32),
+            jax.ShapeDtypeStruct((ctx, rows, model), BF16),
             jax.ShapeDtypeStruct((rows, model), jnp.float32),
         ],
         in_specs=[IN_VMEM] * 4,
@@ -723,12 +792,9 @@
             pltpu.VMEM((ctx, rows, model), BF16),
             pltpu.VMEM((ctx, rows, hid), BF16),
             pltpu.VMEM((ctx, rows, 2 * hid), BF16),
-            pltpu.VMEM((2, ctx // 2, rows, model), jnp.float32),
-            boxes[0],
-            boxes[0],
+            pltpu.VMEM((ctx // 2, rows, model), jnp.float32),
         ]
-        + boxes[1:]
-        + boxes[1:]
+        + boxes
         + [sems, sems],
         compiler_params=params(collective_id),
         name="ffn_both_ways",
@@ -873,8 +939,9 @@
 
 
 def attention_back_kernel(
-    size, fsdp, grad_ref, rows_ref, gain_ref, prob_ref, inverse_ref, q_ref, k_ref, v_ref,
-    early_ref, gain_grad_ref,
+    size, fsdp, grad_ref, rows_ref, gain_ref, parts_ref, branch_ref, ssm_ref, top_ref,
+    prob_ref, inverse_ref, q_ref, k_ref, v_ref,
+    early_ref, gain_grad_ref, ffn_ref, dw_ref,
     recv_ref, heads_ref, dp_ref, dq_ref, dkv_ref, dq_send, dq_recv, kv_part, kv_sum, *rest,
 ):
     bits = size.bit_length() - 1
@@ -886,12 +953,31 @@
     kv_mine = groups * HEAD // size
     chunk = 128
     scale_qk = HEAD**-0.5
-    inbox = rest[:-2]
+    boxes = (len(rest) - 2) // 2
+    inbox, ffn_inbox = rest[:boxes], rest[boxes : 2 * boxes]
     greet_all(me, size)
     copies = Copies("ctx", *rest[-2:])
     come = exchange(copies, grad_ref, recv_ref, me, size)
+    ffn_sum = Reducer(copies, bits, None, ffn_inbox, ffn_ref)
+    ffn_sum.send_parts(parts_ref)
+
+    def add_parts():
+        for flips in ffn_sum.everyone:
+            ffn_sum.own(flips, parts_ref[flipped(me, flips)].astype(jnp.float32))
+
+    beside = [add_parts] + ffn_sum.turns()
     values = rows_ref[...]
     scale = lax.rsqrt(jnp.mean(values * values, axis=-1, keepdims=True) + EPSILON)
+    at = 0
+    for ref in (ssm_ref, branch_ref):
+        wide = ref.shape[1] // fsdp
+        weights = lax.dot_general(
+            ref[...], top_ref[...], (((0,), (0,)), ((), ())), preferred_element_type=jnp.float32
+        ).astype(BF16)
+        for f in range(fsdp):
+            dw_ref[f, at : at + wide] = weights[f * wide : (f + 1) * wide]
+        at += wide
+    dw_ref[:, at:] = jnp.zeros((fsdp, dw_ref.shape[1] - at, model), BF16)
     for copy in come:
         copy.wait_recv()
     part = model // fsdp
@@ -947,7 +1033,11 @@
         for h in range(heads):
             at = (g * heads + h) * HEAD
             dq_ref[:, at : at + HEAD] = dq_g[h * own : (h + 1) * own]
-
+        if beside:
+            beside.pop(0)()
+
+    for step in beside:
+        step()
     for d in range(size):
         dq_send[d] = dq_ref[:, d * q_mine : (d + 1) * q_mine].astype(BF16)
     come = exchange(copies, dq_send, dq_recv, me, size)
@@ -957,12 +1047,7 @@
         at = groups * HEAD + d * kv_mine
         kv_part[d, kv_mine:] = flat[at : at + kv_mine].astype(BF16)
     reducer = Reducer(copies, bits, None, inbox, kv_sum)
-    for flips in reducer.everyone:
-        reducer.first[flips] = copies.send(
-            kv_part.at[flipped(me, flips + (0,))],
-            inbox[0].at[reducer.slots[flips]],
-            flip(me, 0),
-        )
+    reducer.send_parts(kv_part)
     for flips in reducer.everyone:
         reducer.own(flips, kv_part[flipped(me, flips)].astype(jnp.float32))
     for copy in come:
@@ -974,23 +1059,27 @@
     copies.finish()
 
 
-def attention_backward(grad_c, rows, gain, kept, collective_id):
+def attention_backward(grad_c, rows, gain, parts, branches, top, kept, collective_id):
     ctx, fsdp, bits = lax.axis_size("ctx"), lax.axis_size("fsdp"), ctx_bits()
     prob = kept[0]
     own, model = rows.shape
     length = own * ctx
     q_mine, kv_mine = model // ctx, KV_HEADS * HEAD // ctx
     boxes, count = reducer_boxes(ctx, bits, 2 * kv_mine, length)
-    sems = pltpu.SemaphoreType.DMA((2 * (ctx - 1) + count,))
+    ffn_boxes, ffn_count = reducer_boxes(ctx, bits, own, model)
+    dw_rows = sum(branch.shape[1] for branch in branches) // fsdp
+    sems = pltpu.SemaphoreType.DMA((2 * (ctx - 1) + count + ffn_count,))
     shape = jax.ShapeDtypeStruct
     return pl.pallas_call(
         functools.partial(attention_back_kernel, ctx, fsdp),
         out_shape=[
             shape((length, q_mine + 2 * kv_mine), BF16),
             shape((1, model), jnp.float32),
+            shape((own, model), jnp.float32),
+            shape((fsdp, dw_rows + -dw_rows % 16, model), BF16),
         ],
-        in_specs=[IN_VMEM] * (3 + len(kept)),
-        out_specs=[IN_VMEM] * 2,
+        in_specs=[IN_VMEM] * (7 + len(kept)),
+        out_specs=[IN_VMEM] * 4,
         scratch_shapes=[
             pltpu.VMEM((ctx, own, q_mine), BF16),
             pltpu.VMEM(kept[2].shape, BF16),
@@ -1003,14 +1092,15 @@
             pltpu.VMEM((2 * kv_mine, length), jnp.float32),
         ]
         + boxes[1:]
+        + ffn_boxes[1:]
         + [sems, sems],
         compiler_params=params(collective_id),
         name="attention_backward",
-    )(grad_c.reshape(ctx, own, q_mine), rows, gain[None], *kept)
+    )(grad_c.reshape(ctx, own, q_mine), rows, gain[None], parts, *branches, top, *kept)
 
 
 def finish_kernel(
-    size, fsdp, early_ref, src_ref, step_ref, attn_ref, mix_ref, channel_ref, gain_ref,
+    size, fsdp, early_ref, src_ref, stack_ref, channel_ref, gain_ref,
     query_out, key_out, value_out, mixer_out, step_out, attn_out, mix_out, channel_out, sums_ref,
     all_ref, row_inbox, gain_inbox, line_inbox, c_send, c_recv, r_send, r_recv,
     ctx_send, ctx_recv, line_send, line_recv,
@@ -1028,9 +1118,8 @@
         )
     q_mine, kv_mine = query_out.shape[1], key_out.shape[1]
     late = q_mine + 2 * kv_mine
-    rows, width = src_ref.shape[0], src_ref.shape[1] // fsdp
-    low, high = step_ref.shape[0], mix_ref.shape[0]
-    attn_at = -(-high // 16) * 16
+    rows, width = early_ref.shape[0], src_ref.shape[1] // fsdp
+    low, high = step_out.shape[0], mix_out.shape[0] // size
     block = mix_out.shape[1]
     repeat = size // fsdp
     pl.semaphore_wait(barrier, size - 1 + fsdp - 1)
@@ -1048,19 +1137,16 @@
         across.send(gain_ref, gain_inbox.at[turn - 1], (me + turn) % size)
         for turn in range(1, size)
     ]
-    c_send[:, rows:] = jnp.zeros((size, c_send.shape[1] - rows, width), BF16)
-    r_send[...] = jnp.zeros(r_send.shape, BF16)
     for d in range(size):
         unit = d % fsdp
         if d < fsdp:
-            c_send[d, :rows] = src_ref[:, unit * width : (unit + 1) * width]
+            c_send[d, :rows] = src_ref[:rows, unit * width : (unit + 1) * width]
         else:
             at = late + unit * width
             c_send[d, :rows] = early_ref[:, at : at + width]
         at = d // repeat * width
-        c_send[d, rows : rows + low] = step_ref[:, at : at + width]
-        r_send[d, :high] = mix_ref[:, d * block : (d + 1) * block]
-        r_send[d, attn_at : attn_at + attn_ref.shape[0]] = attn_ref[:, d * block : (d + 1) * block]
+        c_send[d, rows:] = src_ref[rows:, at : at + width]
+        r_send[d] = stack_ref[:, d * block : (d + 1) * block]
     moved = exchange(across, c_send, c_recv, me, size) + exchange(across, r_send, r_recv, me, size)
     query_out[...] = early_ref[:, :q_mine].astype(jnp.float32)
     key_out[...] = early_ref[:, q_mine : q_mine + kv_mine].astype(jnp.float32)
@@ -1093,10 +1179,8 @@
     for s in range(size):
         mixer_out[:, s * width : (s + 1) * width] = c_recv[s, :rows].astype(jnp.float32)
         mix_out[s * high : (s + 1) * high] = r_recv[s, :high].astype(jnp.float32)
-        count = attn_ref.shape[0]
-        attn_out[s * count : (s + 1) * count] = r_recv[s, attn_at : attn_at + count].astype(
-            jnp.float32
-        )
+        count = attn_out.shape[0] // size
+        attn_out[s * count : (s + 1) * count] = r_recv[s, high : high + count].astype(jnp.float32)
     for j in range(fsdp):
         source = fsdp * (me % repeat) + j
         step_out[:, j * width : (j + 1) * width] = c_recv[source, rows : rows + low].astype(
@@ -1117,13 +1201,11 @@
     line.finish()
 
 
-def finish(early, src, step, attn, mix, channel, gains, q_mine, kv_mine, collective_id):
+def finish(early, src, stack, channel, gains, sizes, collective_id):
     ctx, fsdp, bits = lax.axis_size("ctx"), lax.axis_size("fsdp"), ctx_bits()
-    rows, mine = src.shape
-    model = attn.shape[1]
-    width, block = mine // fsdp, model // ctx
-    pad_rows = rows + -(-step.shape[0] // 16) * 16
-    stack_rows = -(-mix.shape[0] // 16) * 16 + -(-attn.shape[0] // 16) * 16
+    q_mine, kv_mine, step_rows, mix_rows, attn_rows = sizes
+    rows, mine = early.shape[0], src.shape[1]
+    width, block = mine // fsdp, stack.shape[1] // ctx
     ctx_sems = pltpu.SemaphoreType.DMA((3 * (ctx - 1) + gather_sems(bits),))
     line_sems = pltpu.SemaphoreType.DMA((3 * (fsdp - 1),))
 
@@ -1134,26 +1216,26 @@
         functools.partial(finish_kernel, ctx, fsdp),
         out_shape=[
             shape(rows, q_mine), shape(rows, kv_mine), shape(rows, kv_mine),
-            shape(rows, ctx * width), shape(step.shape[0], mine),
-            shape(ctx * attn.shape[0], block), shape(ctx * mix.shape[0], block),
+            shape(rows, ctx * width), shape(step_rows, mine),
+            shape(ctx * attn_rows, block), shape(ctx * mix_rows, block),
             shape(channel.shape[0], ctx * mine), shape(*gains.shape),
         ],
-        in_specs=[IN_VMEM] * 7,
+        in_specs=[IN_VMEM] * 5,
         out_specs=[IN_VMEM] * 9,
         scratch_shapes=[
             pltpu.VMEM((ctx,) + channel.shape, jnp.float32),
             pltpu.VMEM((fsdp - 1, channel.shape[0] // fsdp, mine), jnp.float32),
             pltpu.VMEM((ctx - 1,) + gains.shape, jnp.float32),
             pltpu.VMEM((fsdp,) + gains.shape, jnp.float32),
-            pltpu.VMEM((ctx, pad_rows, width), BF16),
-            pltpu.VMEM((ctx, pad_rows, width), BF16),
-            pltpu.VMEM((ctx, stack_rows, block), BF16),
-            pltpu.VMEM((ctx, stack_rows, block), BF16),
+            pltpu.VMEM((ctx, src.shape[0], width), BF16),
+            pltpu.VMEM((ctx, src.shape[0], width), BF16),
+            pltpu.VMEM((ctx, stack.shape[0], block), BF16),
+            pltpu.VMEM((ctx, stack.shape[0], block), BF16),
             ctx_sems, ctx_sems, line_sems, line_sems,
         ],
         compiler_params=params(collective_id),
         name="finish",
-    )(early, src, step, attn, mix, channel, gains)
+    )(early, src, stack, channel, gains)
 
 
 def window(start, size, total, step):
@@ -1165,11 +1247,9 @@
     return pltpu.roll(values.astype(jnp.float32), lax.rem(size - offset, size), axis)
 
 
-def pack_in_kernel(
-    size, query_ref, key_ref, value_ref, mixer_ref, state_ref, step_ref,
-    in_out, state_out, step_out, inbox, sems,
-):
-    me = lax.axis_index("ctx")
+def pack_in_begin(weights, scratch):
+    mixer_ref, (inbox, sems) = weights[3], scratch
+    me, size = lax.axis_index("ctx"), lax.axis_size("ctx")
     units, _, span = inbox.shape
     total = mixer_ref.shape[1]
     width = total // units // size
@@ -1179,50 +1259,58 @@
         copy = pltpu.make_async_copy(mixer_ref.at[:, pl.ds(at, span)], inbox.at[u], sems.at[u])
         copy.start()
         copies.append(copy)
+    return copies
+
+
+def pack_in(row, copies, weights, scratch, in_out, state_out, step_out):
+    query_ref, key_ref, value_ref, mixer_ref, state_ref, step_ref = weights
+    inbox = scratch[0]
+    me, size = lax.axis_index("ctx"), lax.axis_size("ctx")
+    units, _, span = inbox.shape
+    total = mixer_ref.shape[1]
+    width = total // units // size
     at = 0
     for ref in (query_ref, key_ref, value_ref):
         wide = ref.shape[1] // size
-        in_out[:, at : at + wide] = shifted(ref[...], me * wide, 1)[:, :wide].astype(BF16)
+        in_out[row, :, at : at + wide] = shifted(ref[...], me * wide, 1)[:, :wide].astype(BF16)
         at += wide
-    high = state_ref.shape[0] // size
-    first = window(me * high, 128, state_ref.shape[0], 16)
-    rows = shifted(state_ref[pl.ds(first, 128)], me * high - first, 0)
-    state_out[...] = rows[: state_out.shape[0]].astype(BF16)
+    high = state_ref.shape[1] // size
+    turned = shifted(state_ref[...], me * high, 1)[:, :128].T
+    state_out[row] = turned[: state_out.shape[1]].astype(BF16)
     part = step_ref.shape[1] * 2 // units
-    step_out[...] = jnp.zeros(step_out.shape, BF16)
+    step_out[row] = jnp.zeros(step_out.shape[1:], BF16)
     for f in range(units // 2):
-        band = shifted(step_ref[:, f * part : (f + 1) * part], me * width, 1)
-        step_out[: step_ref.shape[0], f * width : (f + 1) * width] = band[:, :width].astype(BF16)
+        band = shifted(step_ref[:, f * part : (f + 1) * part], me * width, 1)[:, :width]
+        step_out[row, : step_ref.shape[0], f * width : (f + 1) * width] = band.astype(BF16)
     for u in range(units):
         copies[u].wait()
         start = u * (total // units) + me * width
         piece = shifted(inbox[u], start - window(start, span, total, 128), 1)[:, :width]
         to = at + (u + units // 2) % units * width
-        in_out[:, to : to + width] = piece.astype(BF16)
-
-
-def pack_in(query, key, value, mixer, state, step):
+        in_out[row, :, to : to + width] = piece.astype(BF16)
+
+
+def pack_in_plan(first):
+    shape = jax.ShapeDtypeStruct
+    if len(first) == 3:
+        return {"shapes": [shape(a.shape, a.dtype) for a in first], "scratch": [], "any": ()}
+    query, key, value, mixer, state, step = first
     ctx, fsdp = lax.axis_size("ctx"), lax.axis_size("fsdp")
     rows = mixer.shape[0]
     mine = mixer.shape[1] // 2 // ctx
     qkv = (query.shape[1] + key.shape[1] + value.shape[1]) // ctx
-    state_rows = state.shape[0] // ctx
-    shape = jax.ShapeDtypeStruct
-    return pl.pallas_call(
-        functools.partial(pack_in_kernel, ctx),
-        out_shape=[
+    state_rows = state.shape[1] // ctx
+    return {
+        "shapes": [
             shape((rows, qkv + 2 * mine), BF16),
-            shape((state_rows + -state_rows % 16, state.shape[1]), BF16),
+            shape((state_rows + -state_rows % 16, state.shape[0]), BF16),
             shape((step.shape[0] + -step.shape[0] % 16, mine), BF16),
         ],
-        in_specs=[IN_VMEM] * 3 + [pl.BlockSpec(memory_space=pl.ANY)] + [IN_VMEM] * 2,
-        out_specs=[IN_VMEM] * 3,
-        scratch_shapes=[
+        "scratch": [
             pltpu.VMEM((2 * fsdp, rows, 256), BF16), pltpu.SemaphoreType.DMA((2 * fsdp,))
         ],
-        compiler_params=pltpu.CompilerParams(vmem_limit_bytes=VMEM_LIMIT),
-        name="pack_in",
-    )(query, key, value, mixer, state, step)
+        "any": (3,),
+    }
 
 
 def pack_out_plan(later, hidden_units):
@@ -1387,12 +1475,17 @@
 
 
 def scan_bwd_kernel(
-    steps_ref, drive_ref, grad_ref, in_ref, out_ref, rate_ref, prev_ref,
-    gstep_ref, gdrive_ref, gin_ref, gout_ref, grate_ref,
-    carry_ref, pin_ref, pout_ref,
+    units, steps_ref, drive_ref, grad_ref, in_ref, out_ref, rate_ref, prev_ref, *refs
 ):
+    exchanged, refs = refs[: 2 if units else 0], refs[2 if units else 0 :]
+    gstep_ref, gdrive_ref, gin_ref, gout_ref, grate_ref = refs[:5]
+    received, refs = refs[5 : 8 if units else 5], refs[8 if units else 5 :]
+    carry_ref, pin_ref, pout_ref = refs[:3]
+    slots = refs[3:]
     tiles = steps_ref.shape[1] // LANES
     chunk = steps_ref.shape[0]
+    if units:
+        pl.when(pl.program_id(0) == 0)(functools.partial(relay_begin, units, *exchanged, *slots))
 
     @pl.when(pl.program_id(0) == 0)
     def _():
@@ -1450,9 +1543,12 @@
     dims = (((1,), (1,)), ((), ()))
     gin_ref[0] = lax.dot_general(ones, pin_ref[...], dims, preferred_element_type=jnp.float32)
     gout_ref[0] = lax.dot_general(ones, pout_ref[...], dims, preferred_element_type=jnp.float32)
-
-
-def scan_bwd(steps, drive, grad, in_b, out_b, rates, previous):
+    if units:
+        last = pl.num_programs(0) - 1
+        pl.when(pl.program_id(0) == last)(functools.partial(relay_end, units, *received, *slots))
+
+
+def scan_bwd(steps, drive, grad, in_b, out_b, rates, previous, relay=(), units=0, hidden=0, collective_id=None):
     length, width = steps.shape
     chunk = CHUNK
     count = length // chunk
@@ -1460,28 +1556,56 @@
     mat = pl.BlockSpec((chunk, STATE, LANES), lambda i: (count - 1 - i, 0, 0))
     rate = pl.BlockSpec((STATE, width), lambda i: (0, 0))
     red = pl.BlockSpec((1, 8, chunk * STATE), lambda i: (count - 1 - i, 0, 0))
-    gstep, gdrive, gin, gout, grate = pl.pallas_call(
-        scan_bwd_kernel,
+    shape = jax.ShapeDtypeStruct
+    relay_out, slots = [], []
+    settings = dict(vmem_limit_bytes=56 * 1024 * 1024)
+    if relay:
+        ctx = lax.axis_size("ctx")
+        pair, down = relay
+        wide, block = hidden // ctx, down.shape[1] // ctx
+        relay_out = [
+            shape((pair.shape[0], ctx * wide), jnp.float32),
+            shape((pair.shape[0], ctx * wide), jnp.float32),
+            shape((units * ctx * wide, block), jnp.float32),
+        ]
+        slots = [
+            pltpu.VMEM((ctx, pair.shape[0], 2 * wide), BF16),
+            pltpu.VMEM((ctx, pair.shape[0], 2 * wide), BF16),
+            pltpu.VMEM((ctx, down.shape[0], block), BF16),
+            pltpu.VMEM((ctx, down.shape[0], block), BF16),
+            pltpu.SemaphoreType.DMA((2 * (ctx - 1),)),
+            pltpu.SemaphoreType.DMA((2 * (ctx - 1),)),
+        ]
+        settings.update(collective_id=collective_id, has_side_effects=True)
+    gstep, gdrive, gin, gout, grate, *relayed = pl.pallas_call(
+        functools.partial(scan_bwd_kernel, units),
         grid=(count,),
         in_specs=[row, row, row, mat, mat, rate,
-                  pl.BlockSpec((chunk, STATE, width), lambda i: (count - 1 - i, 0, 0))],
-        out_specs=[row, row, red, red, rate],
+                  pl.BlockSpec((chunk, STATE, width), lambda i: (count - 1 - i, 0, 0))]
+        + [pl.BlockSpec(a.shape, lambda i: (0, 0)) for a in relay],
+        out_specs=[row, row, red, red, rate]
+        + [pl.BlockSpec(a.shape, lambda i: (0, 0)) for a in relay_out],
         out_shape=[
-            jax.ShapeDtypeStruct((length, width), jnp.float32),
-            jax.ShapeDtypeStruct((length, width), jnp.float32),
-            jax.ShapeDtypeStruct((count, 8, chunk * STATE), jnp.float32),
-            jax.ShapeDtypeStruct((count, 8, chunk * STATE), jnp.float32),
-            jax.ShapeDtypeStruct((STATE, width), jnp.float32),
-        ],
+            shape((length, width), jnp.float32),
+            shape((length, width), jnp.float32),
+            shape((count, 8, chunk * STATE), jnp.float32),
+            shape((count, 8, chunk * STATE), jnp.float32),
+            shape((STATE, width), jnp.float32),
+        ]
+        + relay_out,
         scratch_shapes=[
             pltpu.VMEM((STATE, width), jnp.float32),
             pltpu.VMEM((chunk * STATE, LANES), jnp.float32),
             pltpu.VMEM((chunk * STATE, LANES), jnp.float32),
-        ],
-        compiler_params=pltpu.CompilerParams(vmem_limit_bytes=48 * 1024 * 1024),
+        ]
+        + slots,
+        compiler_params=pltpu.CompilerParams(**settings),
         name="scan_backward",
-    )(steps, drive, grad, in_b, out_b, rates, previous)
-    return (gstep, gdrive, gin[:, 0].reshape(length, STATE), gout[:, 0].reshape(length, STATE), grate)
+    )(steps, drive, grad, in_b, out_b, rates, previous, *relay)
+    return (
+        gstep, gdrive, gin[:, 0].reshape(length, STATE), gout[:, 0].reshape(length, STATE), grate,
+        relayed,
+    )
 
 
 def matmul(left, right):
@@ -1589,15 +1713,12 @@
 def scatter_fsdp(*gradients):
     fsdp = lax.axis_size("fsdp")
     parts = [g.astype(BF16).reshape(fsdp, -1, g.shape[1]) for g in gradients]
-    sizes = [part.shape[1] for part in parts]
-    pad = -sum(sizes) % 16
+    pad = -sum(part.shape[1] for part in parts) % 16
     if pad:
         parts.append(jnp.zeros((fsdp, pad, gradients[0].shape[1]), BF16))
     joined = jnp.concatenate(parts, 1) if len(parts) > 1 else parts[0]
     joined = joined.reshape(-1, joined.shape[2])
-    out = lax.psum_scatter(joined, "fsdp", scatter_dimension=0, tiled=True)
-    starts = [sum(sizes[:i]) for i in range(len(sizes))]
-    return [out[start : start + size] for start, size in zip(starts, sizes)]
+    return lax.psum_scatter(joined, "fsdp", scatter_dimension=0, tiled=True)
 
 
 def body(
@@ -1646,10 +1767,9 @@
     attn_rows_mine = (attn_proj.shape[0] + attn_pad) // ctx
     state_rows, step_rows = state_proj.shape[0] // ctx, step_proj.shape[0]
     if ctx == 8:
-        in_part, state_part, step_part = pack_in(
-            query_proj, key_proj, value_proj, mixer_in, state_proj, step_proj
-        )
+        first = (query_proj, key_proj, value_proj, mixer_in, state_proj.T, step_proj)
         later = (gate_proj, up_proj, down_proj.T, mixer_out, attn_proj)
+        x_in, top_in = inputs[0].T, cotangent[0].T
     else:
         in_part = jnp.concatenate(
             [block_columns(array) for array in (query_proj, key_proj, value_proj)]
@@ -1658,10 +1778,13 @@
             1,
         )
         later = ()
+        x_in, top_in = inputs[0], cotangent[0]
         state_part = jnp.pad(my_rows(state_proj, 1)[0], ((0, -state_rows % 16), (0, 0)))
         step_part = jnp.pad(
             jnp.concatenate(my_columns(step_proj, fsdp), 1), ((0, -step_rows % 16), (0, 0))
         )
+
+        first = (in_part, state_part, step_part)
 
         def hidden_columns(array):
             pieces = my_columns(array, hidden_units)
@@ -1680,8 +1803,7 @@
         )
     mix_rows = mixer_out.shape[0] // ctx
     normed_all, grad_top, in_full, state_full, step_full, *parts = front(
-        inputs[0], norm_gain[None], cotangent[0], in_part, state_part, step_part, later,
-        hidden_units, 0,
+        x_in, norm_gain[None], top_in, first, later, hidden_units, 0
     )
     if parts:
         ffn_part, rows_part = parts
@@ -1818,21 +1940,20 @@
         grad_ffn_in = reduce_products([grad_pair], [ffn_full], True, 7)
         down_dw = left_trans(hidden, grad_top).astype(BF16)
         pair_dw = left_trans(ffn_all, grad_pair).astype(BF16)
-    output = middle + ffn_out
-
     grad_ffn_in, down_dw, pair_dw = lax.optimization_barrier((grad_ffn_in, down_dw, pair_dw))
-    (down_grad,) = scatter_fsdp(down_dw)
-    (pair_grad,) = scatter_fsdp(pair_dw)
+    down_grad = scatter_fsdp(down_dw)
+    pair_grad = scatter_fsdp(pair_dw)
     grad_middle, grad_ffn_gain = norm_back(grad_ffn_in, middle, ffn_scale, ffn_gain)
     grad_middle = grad_middle + cotangent[0].astype(jnp.float32)
     grad_branch = (0.5 * grad_middle).astype(BF16)
     branch_all = gather_tokens(grad_branch, 8)
-    attn_dw, mixout_dw = left_trans(branch_attn_c, branch_all), left_trans(branch_ssm, branch_all)
     grad_attn_c = right_trans(branch_all, attn_full).astype(BF16)
     if ctx == 8:
-        grad_early, grad_attn_gain = attention_backward(
-            grad_attn_c, attn_rows, attn_gain, attn_kept, 13
-        )
+        grad_early, grad_attn_gain, ffn_out, out_dw = attention_backward(
+            grad_attn_c, attn_rows, attn_gain, ffn_out, (branch_attn_c, branch_ssm), branch_all,
+            attn_kept, 13,
+        )
+        out_dw = [out_dw.reshape(-1, model)]
         grad_attn_gain = grad_attn_gain[0]
     else:
         grad_attn = attn_to_tokens(grad_attn_c).astype(jnp.float32)
@@ -1866,11 +1987,15 @@
             lax.all_to_all(grad_kv, "ctx", 0, 0, tiled=True).astype(jnp.float32), axis=0
         ).astype(BF16)
         grad_early = jnp.concatenate([grad_queries, grad_kv], 1)
-
-    grad_early, attn_dw, mixout_dw, pair_grad = lax.optimization_barrier(
-        (grad_early, attn_dw.astype(BF16), mixout_dw.astype(BF16), pair_grad)
-    )
-    attn_grad, mixout_grad = scatter_fsdp(attn_dw, mixout_dw)
+        out_dw = [
+            left_trans(branch_ssm, branch_all).astype(BF16),
+            left_trans(branch_attn_c, branch_all).astype(BF16),
+        ]
+
+    grad_early, out_dw, pair_grad = lax.optimization_barrier((grad_early, out_dw, pair_grad))
+    out_grad = scatter_fsdp(*out_dw)
+
+    output = middle + ffn_out
 
     grad_norm = right_trans(branch_all, mixout_full)
     grad_ssm_gain = jnp.sum(grad_norm * ssm_gated * ssm_scale, axis=0)
@@ -1882,20 +2007,13 @@
     grad_skip = jnp.sum(grad_scan * conv_vals, axis=0)
     grad_gate_bf = grad_gate_z.astype(BF16)
     grad_early = jnp.concatenate([grad_early, grad_gate_bf], 1)
-    (early_grad,) = scatter_fsdp(left_trans(normed_all, grad_early))
-    pair_grad = pair_grad.reshape(-1, 2, fsdp, down_at)[..., :hid_part]
-    pair_slots = to_slots(pair_grad.transpose(1, 0, 2, 3).reshape(-1, hid), hidden_units)
-    down_slots = rows_to_slots(down_grad[:hid_part])
-    pair_slots = lax.all_to_all(pair_slots, "ctx", 0, 0, tiled=True)
-    down_slots = lax.all_to_all(down_slots, "ctx", 0, 0, tiled=True)
-    grad_steps, grad_drive, grad_input_mat, grad_output_mat, grad_rate = scan_bwd(
-        steps_pad, vals_pad, padded(grad_scan), in_b, out_b, rates_log2, states
+    early_grad = scatter_fsdp(left_trans(normed_all, grad_early))
+    with_relay = ctx == 8 and hidden_units == ctx
+    grad_steps, grad_drive, grad_input_mat, grad_output_mat, grad_rate, relayed = scan_bwd(
+        steps_pad, vals_pad, padded(grad_scan), in_b, out_b, rates_log2, states,
+        *(((pair_grad, down_grad), hidden_rows, hid, 14) if with_relay else ()),
     )
-    grad_steps, pair_slots, down_slots, attn_grad, mixout_grad = lax.optimization_barrier(
-        (grad_steps, pair_slots, down_slots, attn_grad, mixout_grad)
-    )
-    pair_blocks = from_slots(pair_slots, hidden_units)
-    down_blocks = rows_from_slots(down_slots, hidden_rows)
+    grad_steps, out_grad = lax.optimization_barrier((grad_steps, out_grad))
     grad_steps, grad_drive, grad_rate = (
         grad_steps[:, :mine],
         grad_drive[:, :mine],
@@ -1915,7 +2033,6 @@
     grad_conv_act = (
         right_trans(grad_projected, state_full) + grad_scan * skip + grad_drive
     ).astype(BF16)
-    grad_conv_act, early_grad = lax.optimization_barrier((grad_conv_act, early_grad))
     grad_conv = grad_conv_act.astype(jnp.float32) * silu_slope(conv_pre)
     grad_conv_bias = jnp.sum(grad_conv, axis=0)
     grad_taps = jnp.stack(
@@ -1927,8 +2044,15 @@
         for tap in range(CONV)
     )
     grad_src = grad_src.astype(BF16)
-    src_grad, step_grad = scatter_fsdp(left_trans(normed_all, grad_src), step_dw)
+    src_grad = scatter_fsdp(left_trans(normed_all, grad_src), step_dw)
     grad_normed = reduce_products([grad_early, grad_src], [in_full], True, 11)
+    if with_relay:
+        gate_blocks, up_blocks, down_blocks = relayed
+    else:
+        pair_grad = pair_grad.reshape(-1, 2, fsdp, down_at)[..., :hid_part]
+        gate_blocks = to_blocks(pair_grad[:, 0].reshape(-1, hid), hidden_units)
+        up_blocks = to_blocks(pair_grad[:, 1].reshape(-1, hid), hidden_units)
+        down_blocks = rows_to_blocks(down_grad[:hid_part], hidden_rows)
     grad_tokens, grad_norm_gain = norm_back(grad_normed, tokens, norm_scale, norm_gain)
     grad_tokens = grad_tokens + grad_middle
 
@@ -1948,14 +2072,18 @@
         (
             query_grad, key_grad, value_grad, mixer_grad, step_grad, attn_grad, mixout_grad, channel, gains,
         ) = finish(
-            early_grad, src_grad, step_grad, attn_grad, mixout_grad, channel, gains,
-            q_mine, kv_mine, 12,
+            early_grad, src_grad, out_grad, channel, gains,
+            (q_mine, kv_mine, step_rows, mix_rows, attn_rows_mine), 12,
         )
     else:
         channel, gains = settle_small(channel, gains, 12)
         channel = channel.reshape(ctx, -1, fsdp, mine // fsdp).transpose(1, 2, 0, 3)
         channel = channel.reshape(-1, inner)
         late_at = q_mine + 2 * kv_mine
+        step_grad = src_grad[early_grad.shape[0] :][:step_rows]
+        src_grad = src_grad[: early_grad.shape[0]]
+        mixout_grad = out_grad[:mix_rows]
+        attn_grad = out_grad[mix_rows : mix_rows + attn_rows_mine]
         query_grad = early_grad[:, :q_mine].astype(jnp.float32)
         key_grad = early_grad[:, q_mine : q_mine + kv_mine].astype(jnp.float32)
         value_grad = early_grad[:, q_mine + kv_mine : late_at].astype(jnp.float32)
@@ -1966,7 +2094,6 @@
         attn_grad = rows_to_blocks(attn_grad, 1)[: attn_proj.shape[0]]
         mixout_grad = rows_to_blocks(mixout_grad, 1)
     sum_norm_gain, sum_attn_gain, sum_ffn_gain = gains[0], gains[1], gains[2]
-    half = pair_blocks.shape[0] // 2
     return (
         output[None],
         grad_tokens[None],
@@ -1987,8 +2114,8 @@
         mixout_grad,
         channel[CONV + 3],
         sum_ffn_gain,
-        pair_blocks[:half],
-        pair_blocks[half:],
+        gate_blocks,
+        up_blocks,
         down_blocks,
     )
 

time: 725 us -> 669 us (0.923)
  local copies, waits for them, and re-layouts: 99.8 us -> 76.3 us
  starting transfers between devices: 13.2 us -> 0.78 us
  other arithmetic: 44.3 us -> 36.3 us
  waiting for transfers between devices: 11.7 us -> 3.98 us
    all_to_all x2 -> x0, starting transfers between devices: 12.8 us -> none  [the longest x1 7.84 us: body(): pair_slots = lax.all_to_all(pair_slots, 'ctx', 0, 0, tiled=True)]
    pallas_call x1, Pallas kernels: 69.4 us -> 57 us  [ffn_both_ways(): pl.pallas_call(ffn_kernel, out_shape=[jax.ShapeDtypeStruct((model, 2 * hi...]
    pallas_call x1, Pallas kernels: 52 us -> 63.3 us  [attention_backward(): pl.pallas_call(functools.partial(attention_back_kernel, ctx, fsdp), out_s...]
    pallas_call x2, Pallas kernels: 40.1 us -> 31 us  [sum_everywhere(): pl.pallas_call(functools.partial(sum_kernel, ctx), out_shape=jax.ShapeDty...]
    slice x7 -> x0, local copies, waits for them, and re-layouts: 8.5 us -> none  [the longest x4 6.56 us: scatter_fsdp(): return [out[start:start + size] for start, size in zip(starts, sizes)]]
    pallas_call x3 -> x2, Pallas kernels: 125 us -> 130 us  [the longest x1 81.1 us: front(): pl.pallas_call(functools.partial(front_kernel, bits, count, turned, pack_...]
    unnamed x134 -> x130, local copies, waits for them, and re-layouts: 24.8 us -> 19.1 us
  transfers between devices with their start and end apart: 9 -> 7, of which waited for: 2 -> 2; matrix products, arithmetic and copies ran while one was open for 19% -> 19% of each run, Pallas kernels for 42% -> 47%
where the time goes in v3:
time: 669 us; the launch traced here: 660 us
  Pallas kernels  491 us (73%)
  local copies, waits for them, and re-layouts  76.3 us (11%)
  matrix products  36.6 us (5%)
  other arithmetic  36.3 us (5%)
  between operations  15.2 us (2%)
    pallas_call x1, Pallas kernels, front(): pl.pallas_call(functools.partial(front_kernel, bits, count, turned, pack_...  81.1 us
    pallas_call x1, Pallas kernels, attention_backward(): pl.pallas_call(functools.partial(attention_back_kernel, ctx, fsdp), out_s...  63.3 us
    pallas_call x2, Pallas kernels, reduce_products(): pl.pallas_call(functools.partial(reduce_kernel, bits, (trans,) * len(left...  57.8 us
    pallas_call x1, Pallas kernels, ffn_both_ways(): pl.pallas_call(ffn_kernel, out_shape=[jax.ShapeDtypeStruct((model, 2 * hi...  57 us
    pallas_call x1, Pallas kernels, attention_forward(): pl.pallas_call(functools.partial(attention_kernel, ctx, fsdp), out_shape=...  52.6 us
    pallas_call x1, Pallas kernels, scan_bwd(): pl.pallas_call(functools.partial(scan_bwd_kernel, units), grid=(count,),...  49.3 us
    pallas_call x1, Pallas kernels, finish(): pl.pallas_call(functools.partial(finish_kernel, ctx, fsdp), out_shape=[sh...  44.9 us
    pallas_call x2, Pallas kernels, sum_everywhere(): pl.pallas_call(functools.partial(sum_kernel, ctx), out_shape=jax.ShapeDty...  31 us
  transfers between devices with their start and end apart: 7, of which 2 were waited for; matrix products, arithmetic and copies ran while one was open for 19% of the time, Pallas kernels for 47%

profile of v3, /device:TPU:1, one launch (start us, length us, event | category | flops | bytes accessed | tf_op | source)
XLA Modules:
  0.0 660.3 jit_solution(15661927349235940513)
XLA Ops:
  8.5 81.1 %front.1 = (bf16[8,128,1600]{2,1,0:T(8,128)(2,1)}, bf16[8,128,1600]{2,1,0:T(8,128)(2,1)}, bf16[4,400,1080]{2,1,0:T(8,128)(2,1)}, bf16[4,112,132]{2,1,0:T(8,128)(...) custom-call(bf16[1600,128]{1,0:T(8,128)(2,1)} %bitcast.149, ...), custom_call_target="tpu_custom_call" | custom-call | tf_op jit(solution)/shard_map/front/pallas_call | solution.py:284
  94.6 8.0 %convolution_convert_fusion.proj_ref = bf16[1024,1080]{1,0:T(8,128)(2,1)S(1)} fusion(bf16[1024,1600]{1,0:T(8,128)(2,1)} %bitcast.180, bf16[1600,1080]{1,0:T(8,128)(2,1)} %bitcast.138), kind=kOutput, calls=%fused_computation.1 | convolution fusion | flops 3540049920 | bytes 8944640 | tf_op jit(solution)/shard_map/dot_general | solution.py:1612
  103.1 2.7 multiply_convert_fusion.1
  106.9 2.0 copy.95
  108.9 16.6 %sum_everywhere.2 = bf16[8,128,132]{2,1,0:T(8,128)(2,1)} custom-call(bf16[8,128,132]{2,1,0:T(8,128)(2,1)} %bitcast.148), custom_call_target="tpu_custom_call" | custom-call | tf_op jit(solution)/shard_map/sum_everywhere/pallas_call | solution.py:527
  125.5 1.6 reshape.212
  127.1 1.7 pad.25.drive_ref
  129.5 2.6 compare_select_fusion
  133.6 4.3 broadcast_in_dim.16.in_ref
  137.9 3.9 broadcast_in_dim.17.out_ref
  141.8 19.1 %scan_forward.1 = (f32[1024,512]{1,0:T(8,128)S(1)}, f32[1024,16,512]{2,1,0:T(8,128)}) custom-call(f32[1024,512]{1,0:T(8,128)S(1)} %pad.24.steps_ref, f32[1024,512]{1,0:T(8,128)} %pad.25.drive_ref, bf16[1024,16,128]{2,1,0:T(8,128)(2,1)} %broadcast_in_dim.16.in_ref, bf16[1024,16,128]{2,1,0:T(8,128)(2,1)} %broadcast_in_dim.17.out_ref, f32[16,512]{1,0:T(8,128)S(1)} %pad.26.rate_ref), custom_call_target="tpu_custom_call" | custom-call | tf_op jit(solution)/shard_map/scan_forward/pallas_call | solution.py:1462
  162.2 1.9 multiply_reduce_fusion.7
  164.0 5.8 total_of.2
  170.5 52.6 %attention_forward.1 = (bf16[8,128,200]{2,1,0:T(8,128)(2,1)}, f32[128,1600]{1,0:T(8,128)}, bf16[5,1024,640]{2,1,0:T(8,128)(2,1)}, f32[5,1,640]{2,1,0:T(1,128)}, ...) custom-call(bf16[1024,1080]{1,0:T(8,128)(2,1)} %copy-done.8, ...), custom_call_target="tpu_custom_call" | custom-call | tf_op jit(solution)/shard_map/attention_forward/pallas_call | solution.py:915
  227.2 3.2 slice.167
  233.1 24.9 %reduce_products.2 = f32[128,1600]{1,0:T(8,128)} custom-call(bf16[8,128,200]{2,1,0:T(8,128)(2,1)} %get-tuple-element.73.refs_0_, bf16[8,128,400]{2,1,0:T(8,128)(2,1)} %bitcast.127, bf16[200,1600]{1,0:T(8,128)(2,1)} %reshape.215.refs_2_, bf16[400,1600]{1,0:T(8,128)(2,1)} %reshape.216.refs_3_), custom_call_target="tpu_custom_call" | custom-call | tf_op jit(solution)/shard_map/reduce_products/pallas_call | solution.py:434
  258.1 1.9 multiply_reduce_fusion.10
  261.9 57.0 %ffn_both_ways.1 = (bf16[1600,1408]{1,0:T(8,128)(2,1)}, bf16[704,1600]{1,0:T(8,128)(2,1)}, bf16[8,128,1600]{2,1,0:T(8,128)(2,1)}, f32[128,1600]{1,0:T(8,128)}) custom-call(bf16[128,1600]{1,0:T(8,128)(2,1)} %multiply_convert_fusion.3.x_ref, bf16[8,128,1600]{2,1,0:T(8,128)(2,1)} %get-tuple-element.78.top_ref, ...), custom_call_target="tpu_custom_call" | custom-call | tf_op jit(solution)/shard_map/ffn_both_ways/pallas_call | solution.py:781
  319.6 2.0 copy.90
  321.8 2.5 multiply_convert_fusion.2
  324.3 22.6 %gather_shards.1 = bf16[8,128,1600]{2,1,0:T(8,128)(2,1)} custom-call(bf16[128,1600]{1,0:T(8,128)(2,1)} %get-tuple-element.211.x_ref), custom_call_target="tpu_custom_call" | custom-call | tf_op jit(solution)/shard_map/gather_shards/pallas_call | solution.py:136
  346.9 4.0 convolution_convert_fusion.3
  350.9 2.0 copy.97
  352.9 63.3 %attention_backward.1 = (bf16[1024,280]{1,0:T(8,128)(2,1)}, f32[1,1600]{1,0:T(1,128)}, f32[128,1600]{1,0:T(8,128)}, bf16[4,160,1600]{2,1,0:T(8,128)(2,1)}) custom-call(bf16[8,128,200]{2,1,0:T(8,128)(2,1)} %bitcast.145, f32[128,1600]{1,0:T(8,128)} %get-tuple-element.84.rows_ref, f32[1,1600]{1,0:T(1,128)} %broadcast_in_dim.15.gain_ref, ...), custom_call_target="tpu_custom_call" | custom-call | tf_op jit(solution)/shard_map/attention_backward/pallas_call | solution.py:1073
  416.4 7.3 %multiply_reduce_fusion = (f32[400]{0:T(512)}, f32[1024]{0:T(1024)}, f32[1024,400]{1,0:T(8,128)}) fusion(f32[1024,400]{1,0:T(8,128)} %copy-done.4, f32[1024]{0:T(1024)S(1)} %rsqrt_bitcast_fusion, f32[400]{0:T(512)S(1)} %bitcast.165, bf16[1024,1600]{1,0:T(8,128)(2,1)} %bitcast.126, bf16[400,1600]{1,0:T(8,128)(2,1)} %reshape.216.refs_3_), kind=kOutput, calls=%fused_computation.14 | convolution fusion | flops 1313176192 | bytes 7844992 | tf_op jit(solution)/shard_map/dot_general | solution.py:1622
  423.8 6.4 total_of.3
  430.9 5.3 multiply_reduce_fusion.1
  438.7 4.3 convolution_convert_fusion.1
  443.9 3.1 pad.27.grad_ref
  447.0 1.7 reduce-scatter.8.cloned.1.call-done.refs_1_
  448.7 49.3 %scan_backward.1 = (f32[1024,512]{1,0:T(8,128)}, f32[1024,512]{1,0:T(8,128)}, f32[8,8,2048]{2,1,0:T(8,128)}, f32[8,8,2048]{2,1,0:T(8,128)}, f32[16,512]{1,0:T(8,...) custom-call(f32[1024,512]{1,0:T(8,128)} %copy-done, f32[1024,512]{1,0:T(8,128)} %pad.25.drive_ref, ...), custom_call_target="tpu_custom_call" | custom-call | tf_op jit(solution)/shard_map/scan_backward/pallas_call | solution.py:1580
  502.3 3.9 fusion.28
  507.3 1.8 copy.102
  509.1 2.5 pad_maximum_fusion.1.x_ref
  511.6 14.4 %sum_everywhere.3 = bf16[8,128,132]{2,1,0:T(8,128)(2,1)} custom-call(bf16[8,128,132]{2,1,0:T(8,128)(2,1)} %pad_maximum_fusion.1.x_ref), custom_call_target="tpu_custom_call" | custom-call | tf_op jit(solution)/shard_map/sum_everywhere/pallas_call | solution.py:527
  526.1 3.5 multiply_multiply_fusion
  529.7 3.6 fusion.26
  534.3 2.8 convolution_convert_fusion.2
  537.1 3.8 copy.122
  542.6 3.1 maximum_maximum_fusion
  548.2 2.8 copy.112
  551.0 32.9 %reduce_products.3 = f32[128,1600]{1,0:T(8,128)} custom-call(bf16[8,128,680]{2,1,0:T(8,128)(2,1)} %bitcast.132, bf16[8,128,400]{2,1,0:T(8,128)(2,1)} %bitcast.137, bf16[1600,1080]{1,0:T(8,128)(2,1)} %bitcast.139), custom_call_target="tpu_custom_call" | custom-call | tf_op jit(solution)/shard_map/reduce_products/pallas_call | solution.py:434
  590.7 44.9 %finish.1 = (f32[400,200]{1,0:T(8,128)}, f32[400,40]{1,0:T(8,128)}, f32[400,40]{1,0:T(8,128)}, f32[400,800]{1,0:T(8,128)}, f32[25,400]{1,0:T(8,128)}, /*index=5*...) custom-call(bf16[400,680]{1,0:T(8,128)(2,1)} %reduce-scatter.12.cloned.1.call-done.early_ref, ...), custom_call_target="tpu_custom_call" | custom-call | tf_op jit(solution)/shard_map/finish/pallas_call | solution.py:1215
  635.7 2.9 slice_bitcast_fusion
  638.6 1.7 slice_bitcast_fusion.1
  640.3 1.9 slice_reduce_fusion
  642.2 1.5 slice.148
  646.4 1.6 slice_reduce_fusion.4
  (205 shorter events, 50.9 us)
Async XLA Ops:
  7.2 217.2 %all-gather.6.cloned.1.call-start = ((), (), s32[]{:S(2)}) async-start(), calls=%async_computation.11 | async-start | bytes 5591040 | tf_op jit(solution)/shard_map/all_gather | solution.py:1816
  89.7 172.2 %all-gather.4.cloned.1.call-start = ((), (), s32[]{:S(2)}) async-start(), calls=%async_computation.5 | async-start | bytes 5632000 | tf_op jit(solution)/shard_map/all_gather | solution.py:1672
  90.4 325.8 %reduce-scatter.6.cloned.1.call-start = ((), (), s32[]{:S(2)}) async-start(), calls=%async_computation.6 | async-start | bytes 5632000 | tf_op jit(solution)/shard_map/reduce_scatter | solution.py:1721
  94.5 8.5 %copy-start.40 = (f32[1,400]{1,0:T(1,128)}, f32[1,400]{1,0:T(1,128)S(1)}, u32[]{:S(2)}) copy-start(f32[1,400]{1,0:T(1,128)S(1)} %get-tuple-element.248) | copy-start | bytes 4804
  94.5 8.5 %copy-start.42 = (f32[1,400]{1,0:T(1,128)}, f32[1,400]{1,0:T(1,128)S(1)}, u32[]{:S(2)}) copy-start(f32[1,400]{1,0:T(1,128)S(1)} %get-tuple-element.249) | copy-start | bytes 4804
  94.6 8.5 %copy-start.44 = (f32[1,400]{1,0:T(1,128)}, f32[1,400]{1,0:T(1,128)S(1)}, u32[]{:S(2)}) copy-start(f32[1,400]{1,0:T(1,128)S(1)} %get-tuple-element.250) | copy-start | bytes 4804
  94.6 8.5 %copy-start.46 = (f32[1,400]{1,0:T(1,128)}, f32[1,400]{1,0:T(1,128)S(1)}, u32[]{:S(2)}) copy-start(f32[1,400]{1,0:T(1,128)S(1)} %get-tuple-element.251) | copy-start | bytes 4804
  102.6 59.5 %copy-start.8 = (bf16[1024,1080]{1,0:T(8,128)(2,1)}, bf16[1024,1080]{1,0:T(8,128)(2,1)S(1)}, u32[]{:S(2)}) copy-start(bf16[1024,1080]{1,0:T(8,128)(2,1)S(1)} %convolution_convert_fusion.proj_ref) | copy-start | bytes 6635524
  103.0 2.7 copy-start.6
  132.2 9.5 %copy-start = (f32[1024,512]{1,0:T(8,128)}, f32[1024,512]{1,0:T(8,128)S(1)}, u32[]{:S(2)}) copy-start(f32[1024,512]{1,0:T(8,128)S(1)} %pad.24.steps_ref) | copy-start | bytes 6291460
  133.4 8.4 %copy-start.3 = (f32[16,512]{1,0:T(8,128)}, f32[16,512]{1,0:T(8,128)S(1)}, u32[]{:S(2)}) copy-start(f32[16,512]{1,0:T(8,128)S(1)} %pad.26.rate_ref) | copy-start | bytes 98308
  160.9 3.1 copy-start.1
  162.1 7.7 %copy-start.51 = (f32[1600]{0:T(1024)S(1)}, f32[1600]{0:T(1024)}, u32[]{:S(2)}) copy-start(f32[1600]{0:T(1024)} %param.29) | copy-start | bytes 19204
  164.0 59.2 %copy-start.4 = (f32[1024,400]{1,0:T(8,128)}, f32[1024,400]{1,0:T(8,128)S(1)}, u32[]{:S(2)}) copy-start(f32[1024,400]{1,0:T(8,128)S(1)} %get-tuple-element.216) | copy-start | bytes 4915204
  169.9 53.3 %copy-start.35 = (f32[8,128]{1,0:T(8,128)S(1)}, f32[8,128]{1,0:T(8,128)}, u32[]{:S(2)}) copy-start(f32[8,128]{1,0:T(8,128)} %total_of.2) | copy-start | bytes 12292
  233.1 24.9 %copy-start.11 = (bf16[1,128,1600]{2,1,0:T(8,128)(2,1)S(1)}, bf16[1,128,1600]{2,1,0:T(8,128)(2,1)}, u32[]{:S(2)}) copy-start(bf16[1,128,1600]{2,1,0:T(8,128)(2,1)} %copy.89) | copy-start | bytes 1228804
  319.0 129.7 %reduce-scatter.8.cloned.1.call-start = ((), (), s32[]{:S(2)}) async-start(), calls=%async_computation.7 | async-start | bytes 2928640 | tf_op jit(solution)/shard_map/reduce_scatter | solution.py:1721
  319.6 182.7 %reduce-scatter.10.cloned.1.call-start = ((), (), s32[]{:S(2)}) async-start(), calls=%async_computation.8 | async-start | bytes 2662400 | tf_op jit(solution)/shard_map/reduce_scatter | solution.py:1721
  324.3 22.6 %copy-start.17 = (bf16[200,1600]{1,0:T(8,128)(2,1)S(1)}, bf16[200,1600]{1,0:T(8,128)(2,1)}, u32[]{:S(2)}) copy-start(bf16[200,1600]{1,0:T(8,128)(2,1)} %reshape.215.refs_2_) | copy-start | bytes 1920004
  416.3 174.4 %reduce-scatter.12.cloned.1.call-start = ((), (), s32[]{:S(2)}) async-start(), calls=%async_computation.9 | async-start | bytes 3072000 | tf_op jit(solution)/shard_map/reduce_scatter | solution.py:1721
  416.4 14.5 %copy-start.2 = (f32[1024,512]{1,0:T(8,128)S(1)}, f32[1024,512]{1,0:T(8,128)}, u32[]{:S(2)}) copy-start(f32[1024,512]{1,0:T(8,128)} %copy-done.1) | copy-start | bytes 6291460
  416.4 14.5 %copy-start.5 = (f32[1024,400]{1,0:T(8,128)S(1)}, f32[1024,400]{1,0:T(8,128)}, u32[]{:S(2)}) copy-start(f32[1024,400]{1,0:T(8,128)} %copy-done.4) | copy-start | bytes 4915204
  416.4 14.5 %copy-start.38 = (f32[1,400]{1,0:T(1,128)S(1)}, f32[1,400]{1,0:T(1,128)}, u32[]{:S(2)}) copy-start(f32[1,400]{1,0:T(1,128)} %copy-done.37) | copy-start | bytes 4804
  430.9 5.3 copy-start.24
  443.0 147.7 %reduce-scatter.14.cloned.1.call-start = ((), (), s32[]{:S(2)}) async-start(), calls=%async_computation.10 | async-start | bytes 2211840 | tf_op jit(solution)/shard_map/reduce_scatter | solution.py:1721
  502.3 3.9 copy-start.26
  506.2 19.9 %copy-start.39 = (f32[1,400]{1,0:T(1,128)S(1)}, f32[1,400]{1,0:T(1,128)}, u32[]{:S(2)}) copy-start(f32[1,400]{1,0:T(1,128)} %copy-done.37) | copy-start | bytes 4804
  509.1 16.9 %copy-start.9 = (f32[1024,400]{1,0:T(8,128)S(1)}, f32[1024,400]{1,0:T(8,128)}, u32[]{:S(2)}) copy-start(f32[1024,400]{1,0:T(8,128)} %get-tuple-element.208) | copy-start | bytes 4915204
  526.1 3.6 copy-start.7
  526.1 3.6 copy-start.41
  526.1 3.6 copy-start.43
  526.1 3.6 copy-start.45
  526.1 3.6 copy-start.47
  529.7 4.6 copy-start.57
  537.1 5.5 copy-start.53
  542.6 3.1 copy-start.55
  547.0 4.0 copy-start.36
  550.9 33.0 %copy-start.33 = (f32[1600]{0:T(1024)S(1)}, f32[1600]{0:T(1024)}, u32[]{:S(2)}) copy-start(f32[1600]{0:T(1024)} %param.24) | copy-start | bytes 19204
  550.9 34.5 %copy-start.18 = (bf16[8,128,132]{2,1,0:T(8,128)(2,1)S(1)}, bf16[8,128,132]{2,1,0:T(8,128)(2,1)}, u32[]{:S(2)}) copy-start(bf16[8,128,132]{2,1,0:T(8,128)(2,1)} %sum_everywhere.3) | copy-start | bytes 811012
  583.9 4.6 copy-start.10
  583.9 4.6 copy-start.15
  635.7 8.0 %copy-start.23 = (f32[800,200]{1,0:T(8,128)S(1)}, f32[800,200]{1,0:T(8,128)}, u32[]{:S(2)}) copy-start(f32[800,200]{1,0:T(8,128)} %get-tuple-element.180) | copy-start | bytes 1920004
  635.7 9.2 %copy-start.30 = (f32[400,40]{1,0:T(8,128)S(1)}, f32[400,40]{1,0:T(8,128)}, u32[]{:S(2)}) copy-start(f32[400,40]{1,0:T(8,128)} %get-tuple-element.168) | copy-start | bytes 192004
  638.6 7.1 %copy-start.29 = (f32[400,40]{1,0:T(8,128)S(1)}, f32[400,40]{1,0:T(8,128)}, u32[]{:S(2)}) copy-start(f32[400,40]{1,0:T(8,128)} %get-tuple-element.169) | copy-start | bytes 192004
  638.6 9.4 %copy-start.28 = (f32[400,200]{1,0:T(8,128)S(1)}, f32[400,200]{1,0:T(8,128)}, u32[]{:S(2)}) copy-start(f32[400,200]{1,0:T(8,128)} %get-tuple-element.294) | copy-start | bytes 960004
  638.6 10.1 %copy-start.27 = (f32[400,200]{1,0:T(8,128)S(1)}, f32[400,200]{1,0:T(8,128)}, u32[]{:S(2)}) copy-start(f32[400,200]{1,0:T(8,128)} %get-tuple-element.297) | copy-start | bytes 960004
  640.3 9.2 %copy-start.20 = (f32[400,800]{1,0:T(8,128)S(1)}, f32[400,800]{1,0:T(8,128)}, u32[]{:S(2)}) copy-start(f32[400,800]{1,0:T(8,128)} %get-tuple-element.299) | copy-start | bytes 3840004
  649.5 2.8 copy-start.21
  (17 other events, 36.4 us)
Sparse Core Ops, SparseCore 0:
  89.8 86.0 all-gather.5
  177.5 84.3 all-gather.3
  319.1 79.0 reduce-scatter.5
  400.4 48.2 reduce-scatter.7
  451.0 43.9 reduce-scatter.9
  497.2 48.9 reduce-scatter.11
  548.6 37.9 reduce-scatter.13

commit v4 on v3

--- a/solution.py
+++ b/solution.py
@@ -453,17 +453,30 @@
     ]
 
 
-def relay_begin(units, pair_ref, down_ref, pair_send, pair_recv, down_send, down_recv, *sems):
+def relay_begin(units, stack_ref, pair_send, pair_recv, down_send, down_recv, *sems):
     size = pair_send.shape[0]
     me = lax.axis_index("ctx")
     greet_all(me, size)
     wide, block = pair_send.shape[2] // 2, down_send.shape[2]
-    half, part = pair_ref.shape[1] // 2, down_ref.shape[0]
+    high, part, span = pair_send.shape[1], down_send.shape[1], stack_ref.shape[1]
+    half = span // 2
+    model = size * block
+    pieces, tall = spill_of(part, model, span)
     for d in range(size):
         at = d // units * part + d % units * wide
-        pair_send[d, :, :wide] = pair_ref[:, at : at + wide]
-        pair_send[d, :, wide:] = pair_ref[:, half + at : half + at + wide]
-        down_send[d] = down_ref[:, d * block : (d + 1) * block]
+        pair_send[d, :, :wide] = stack_ref[:high, at : at + wide]
+        pair_send[d, :, wide:] = stack_ref[:high, half + at : half + at + wide]
+        low, up = d * block, (d + 1) * block
+        if low < span:
+            down_send[d, :, : min(up, span) - low] = stack_ref[high : high + part, low : min(up, span)]
+        if up > span:
+            first = max(low, span)
+            for k in range(pieces):
+                begin, end = k * tall, min(part, (k + 1) * tall)
+                lane = k * (model - span) + first - span
+                down_send[d, begin:end, first - low :] = stack_ref[
+                    high + part : high + part + end - begin, lane : lane + up - first
+                ]
     for copy in relay_copies(pair_send, pair_recv, down_send, down_recv, *sems):
         copy.start()
     pair_recv[me] = pair_send[me]
@@ -687,7 +700,7 @@
 
 def ffn_kernel(
     x_ref, top_ref, pair_w, down_w,
-    pair_dw, down_dw, out_ref, grad_ref,
+    dw_ref, out_ref, grad_ref,
     all_ref, hidden_ref, pair_ref, own_ref, part_grad, *rest,
 ):
     bits = 3
@@ -721,8 +734,11 @@
         low, high = value[:rows], value[rows:]
         own_ref[slot] = jnp.where(core == 0, low, high)
         reducer.to_sibling(flips, jnp.where(core == 0, high, low))
-        value = product(hidden, down_w[...], False)
-        out_ref[pair] = value.astype(BF16).reshape(2, rows, model)
+
+    def project(first):
+        pair = pl.ds(first, 2)
+        hidden = hidden_ref[pair].reshape(2 * rows, hid)
+        out_ref[pair] = product(hidden, down_w[...], False).astype(BF16).reshape(2, rows, model)
 
     def settle(slot, flips):
         reducer.own(flips, own_ref[slot])
@@ -743,24 +759,34 @@
     settle(2, (2,))
     settle(3, (1, 2))
 
-    def band(out, left_ref, right_ref, low, high):
-        left = left_ref[:, :, low:high].reshape(size * rows, high - low)
+    size, blocks = all_ref.shape[0], dw_ref.shape[0]
+    high, part, wide = model // blocks, hid // blocks, 2 * hid
+    pieces, tall = spill_of(part, model, wide)
+
+    def over_tokens(left_ref, right_ref, low, count):
+        left = left_ref[:, :, low : low + count].reshape(size * rows, count)
         right = right_ref[...].reshape(size * rows, right_ref.shape[2])
-        out[low:high] = lax.dot_general(
+        return lax.dot_general(
             left, right, (((0,), (0,)), ((), ())), preferred_element_type=jnp.float32
-        ).astype(out.dtype)
-
-    def bands(out, left_ref, right_ref, count):
-        wide = left_ref.shape[2]
-        tiles = -(-wide // 128)
-        edges = [min(wide, 128 * (tiles * i // count)) for i in range(count + 1)]
-        return [
-            functools.partial(band, out, left_ref, right_ref, low, high)
-            for low, high in zip(edges[:-1], edges[1:])
-        ]
-
-    size = all_ref.shape[0]
-    work_left = bands(down_dw, hidden_ref, top_ref, 2) + bands(pair_dw, all_ref, pair_ref, 4)
+        ).astype(BF16)
+
+    def pair_band(f):
+        dw_ref[f, :high] = over_tokens(all_ref, pair_ref, f * high, high)
+
+    def down_band(f):
+        values = over_tokens(hidden_ref, top_ref, f * part, part)
+        dw_ref[f, high : high + part] = values[:, :wide]
+        dw_ref[f, high + part :] = jnp.zeros((dw_ref.shape[1] - high - part, wide), BF16)
+        spill = model - wide
+        for k in range(pieces):
+            low, up = k * tall, min(part, (k + 1) * tall)
+            dw_ref[f, high + part : high + part + up - low, k * spill : (k + 1) * spill] = values[
+                low:up, wide:
+            ]
+
+    work_left = [functools.partial(down_band, f) for f in range(blocks)]
+    work_left += [functools.partial(pair_band, f) for f in range(blocks)]
+    work_left += [functools.partial(project, first) for first in range(0, size, 2)]
     turns = reducer.turns()
     done = 0
     for i, turn in enumerate(turns):
@@ -772,8 +798,18 @@
     copies.finish()
 
 
+def spill_of(part, model, wide):
+    pieces = wide // (model - wide)
+    return pieces, -(-part // pieces)
+
+
+def stack_rows(model, hid, blocks):
+    _, tall = spill_of(hid // blocks, model, 2 * hid)
+    return model // blocks + hid // blocks + tall + -tall % 16
+
+
 def ffn_both_ways(ffn_in, top, pair_full, down_full, collective_id):
-    ctx, bits = lax.axis_size("ctx"), ctx_bits()
+    ctx, fsdp, bits = lax.axis_size("ctx"), lax.axis_size("fsdp"), ctx_bits()
     rows, model = ffn_in.shape
     hid = down_full.shape[0]
     boxes, count = reducer_boxes(ctx, bits, rows, model)
@@ -781,13 +817,12 @@
     return pl.pallas_call(
         ffn_kernel,
         out_shape=[
-            jax.ShapeDtypeStruct((model, 2 * hid), BF16),
-            jax.ShapeDtypeStruct((hid, model), BF16),
+            jax.ShapeDtypeStruct((fsdp, stack_rows(model, hid, fsdp), 2 * hid), BF16),
             jax.ShapeDtypeStruct((ctx, rows, model), BF16),
             jax.ShapeDtypeStruct((rows, model), jnp.float32),
         ],
         in_specs=[IN_VMEM] * 4,
-        out_specs=[IN_VMEM] * 4,
+        out_specs=[IN_VMEM] * 3,
         scratch_shapes=[
             pltpu.VMEM((ctx, rows, model), BF16),
             pltpu.VMEM((ctx, rows, hid), BF16),
@@ -939,10 +974,11 @@
 
 
 def attention_back_kernel(
-    size, fsdp, grad_ref, rows_ref, gain_ref, parts_ref, branch_ref, ssm_ref, top_ref,
+    size, fsdp, attn_w, mix_w, rows_ref, gain_ref, ssm_gain_ref, gated_ref,
+    parts_ref, branch_ref, ssm_ref, top_ref,
     prob_ref, inverse_ref, q_ref, k_ref, v_ref,
-    early_ref, gain_grad_ref, ffn_ref, dw_ref,
-    recv_ref, heads_ref, dp_ref, dq_ref, dkv_ref, dq_send, dq_recv, kv_part, kv_sum, *rest,
+    early_ref, gain_grad_ref, ffn_ref, dw_ref, norm_grad_ref, dot_ref,
+    grad_ref, dot_part, dot_inbox, recv_ref, heads_ref, dp_ref, dq_ref, dkv_ref, dq_send, dq_recv, kv_part, kv_sum, *rest,
 ):
     bits = size.bit_length() - 1
     me = lax.axis_index("ctx")
@@ -957,7 +993,20 @@
     inbox, ffn_inbox = rest[:boxes], rest[boxes : 2 * boxes]
     greet_all(me, size)
     copies = Copies("ctx", *rest[-2:])
+    for s in range(size):
+        grad_ref[s] = product(top_ref[s * own : (s + 1) * own], attn_w[...], True).astype(BF16)
     come = exchange(copies, grad_ref, recv_ref, me, size)
+    norm_grad_ref[...] = product(top_ref[...], mix_w[...], True)
+    scaled = norm_grad_ref[...] * ssm_gain_ref[...] * gated_ref[...]
+    dot_part[...] = lax.dot_general(
+        jnp.ones((dot_ref.shape[0], scaled.shape[1]), jnp.float32), scaled,
+        (((1,), (1,)), ((), ())),
+        precision=lax.Precision.HIGHEST, preferred_element_type=jnp.float32,
+    )
+    dots = [
+        copies.send(dot_part, dot_inbox.at[turn - 1], (me + turn) % size)
+        for turn in range(1, size)
+    ]
     ffn_sum = Reducer(copies, bits, None, ffn_inbox, ffn_ref)
     ffn_sum.send_parts(parts_ref)
 
@@ -1038,6 +1087,12 @@
 
     for step in beside:
         step()
+    for copy in dots:
+        copy.wait_recv()
+    total = dot_part[...]
+    for turn in range(1, size):
+        total = total + dot_inbox[turn - 1]
+    dot_ref[...] = total
     for d in range(size):
         dq_send[d] = dq_ref[:, d * q_mine : (d + 1) * q_mine].astype(BF16)
     come = exchange(copies, dq_send, dq_recv, me, size)
@@ -1059,7 +1114,7 @@
     copies.finish()
 
 
-def attention_backward(grad_c, rows, gain, parts, branches, top, kept, collective_id):
+def attention_backward(weights, rows, gains, gated, parts, branches, top, kept, collective_id):
     ctx, fsdp, bits = lax.axis_size("ctx"), lax.axis_size("fsdp"), ctx_bits()
     prob = kept[0]
     own, model = rows.shape
@@ -1068,7 +1123,7 @@
     boxes, count = reducer_boxes(ctx, bits, 2 * kv_mine, length)
     ffn_boxes, ffn_count = reducer_boxes(ctx, bits, own, model)
     dw_rows = sum(branch.shape[1] for branch in branches) // fsdp
-    sems = pltpu.SemaphoreType.DMA((2 * (ctx - 1) + count + ffn_count,))
+    sems = pltpu.SemaphoreType.DMA((3 * (ctx - 1) + count + ffn_count,))
     shape = jax.ShapeDtypeStruct
     return pl.pallas_call(
         functools.partial(attention_back_kernel, ctx, fsdp),
@@ -1077,10 +1132,15 @@
             shape((1, model), jnp.float32),
             shape((own, model), jnp.float32),
             shape((fsdp, dw_rows + -dw_rows % 16, model), BF16),
+            shape(gated.shape, jnp.float32),
+            shape((8, length), jnp.float32),
         ],
-        in_specs=[IN_VMEM] * (7 + len(kept)),
-        out_specs=[IN_VMEM] * 4,
+        in_specs=[IN_VMEM] * (10 + len(kept)),
+        out_specs=[IN_VMEM] * 6,
         scratch_shapes=[
+            pltpu.VMEM((ctx, own, q_mine), BF16),
+            pltpu.VMEM((8, length), jnp.float32),
+            pltpu.VMEM((ctx - 1, 8, length), jnp.float32),
             pltpu.VMEM((ctx, own, q_mine), BF16),
             pltpu.VMEM(kept[2].shape, BF16),
             pltpu.VMEM((length, prob.shape[2]), jnp.float32),
@@ -1096,69 +1156,204 @@
         + [sems, sems],
         compiler_params=params(collective_id),
         name="attention_backward",
-    )(grad_c.reshape(ctx, own, q_mine), rows, gain[None], parts, *branches, top, *kept)
-
-
-def finish_kernel(
-    size, fsdp, early_ref, src_ref, stack_ref, channel_ref, gain_ref,
-    query_out, key_out, value_out, mixer_out, step_out, attn_out, mix_out, channel_out, sums_ref,
-    all_ref, row_inbox, gain_inbox, line_inbox, c_send, c_recv, r_send, r_recv,
-    ctx_send, ctx_recv, line_send, line_recv,
-):
-    bits = size.bit_length() - 1
-    me, row = lax.axis_index("ctx"), lax.axis_index("fsdp")
+    )(*weights, rows, *[gain.reshape(1, -1) for gain in gains], gated, parts, *branches, top, *kept)
+
+
+def greet_planes(me, size, row, rows):
     barrier = pltpu.get_barrier_semaphore()
     for turn in range(1, size):
         pl.semaphore_signal(
             barrier, inc=1, device_id={"ctx": (me + turn) % size}, device_id_type=MESH
         )
-    for turn in range(1, fsdp):
+    for turn in range(1, rows):
         pl.semaphore_signal(
-            barrier, inc=1, device_id={"fsdp": (row + turn) % fsdp}, device_id_type=MESH
-        )
+            barrier, inc=1, device_id={"fsdp": (row + turn) % rows}, device_id_type=MESH
+        )
+    pl.semaphore_wait(barrier, size - 1 + rows - 1)
+
+
+class SomeExchange:
+    def __init__(self, copies, send_ref, recv_ref, me, size, chosen):
+        self.send_ref, self.recv_ref, self.me, self.mine = send_ref, recv_ref, me, chosen(me)
+        self.plans = []
+        for turn in range(1, size):
+            to = (me + turn) % size
+            self.plans.append((chosen(to), copies.make(send_ref.at[to], recv_ref.at[me], to)))
+
+    def start(self):
+        for chosen, copy in self.plans:
+            pl.when(chosen)(copy.start)
+
+        @pl.when(self.mine)
+        def _():
+            self.recv_ref[self.me] = self.send_ref[self.me]
+
+    def wait(self):
+        for _, copy in self.plans:
+            pl.when(self.mine)(copy.wait_recv)
+
+    def finish(self):
+        for chosen, copy in self.plans:
+            pl.when(chosen)(copy.wait_send)
+
+
+def back_kernel(
+    size, fsdp, first_ref, second_ref, weight_ref, early_ref, stack_ref, head_ref, state_ref,
+    sum_ref, query_out, key_out, value_out, gate_recv, attn_out, mix_out, head_sum, state_sum,
+    first_w, second_w, head_inbox, state_inbox, c_send, r_send, r_recv,
+    ctx_send, ctx_recv, line_send, line_recv, part_ref, *inbox,
+):
+    bits = size.bit_length() - 1
+    me, row = lax.axis_index("ctx"), lax.axis_index("fsdp")
+    greet_planes(me, size, row, fsdp)
     q_mine, kv_mine = query_out.shape[1], key_out.shape[1]
     late = q_mine + 2 * kv_mine
-    rows, width = early_ref.shape[0], src_ref.shape[1] // fsdp
-    low, high = step_out.shape[0], mix_out.shape[0] // size
-    block = mix_out.shape[1]
-    repeat = size // fsdp
-    pl.semaphore_wait(barrier, size - 1 + fsdp - 1)
+    rows, width = c_send.shape[1], c_send.shape[2]
+    high, block = mix_out.shape[0] // size, mix_out.shape[1]
     across, line = Copies("ctx", ctx_send, ctx_recv), Copies("fsdp", line_send, line_recv)
-    band = channel_ref.shape[0] // fsdp
-
-    def band_of(index):
-        return pl.ds(pl.multiple_of(index * band, 8), band)
+    small = ((head_ref, head_inbox, head_sum), (state_ref, state_inbox, state_sum))
+
+    def band_of(ref, index):
+        band = ref.shape[0] // fsdp
+        return pl.ds(pl.multiple_of(index * band, band), band)
 
     bands = []
     for turn in range(1, fsdp):
         to = (row + turn) % fsdp
-        bands.append(line.send(channel_ref.at[band_of(to)], row_inbox.at[turn - 1], to))
+        for ref, box, _ in small:
+            bands.append(line.send(ref.at[band_of(ref, to)], box.at[turn - 1], to))
+    for d in range(size):
+        r_send[d] = stack_ref[:, d * block : (d + 1) * block]
+        if d >= fsdp:
+            at = late + (d - fsdp) * width
+            c_send[d] = early_ref[:, at : at + width]
+    gates = SomeExchange(across, c_send, gate_recv, me, size, lambda d: d >= fsdp)
+    gates.start()
+    moved = exchange(across, r_send, r_recv, me, size)
+    cut = first_w.shape[1]
+    first_w[...] = weight_ref[:, :cut]
+    second_w[...] = weight_ref[:, cut:]
+    reducer = Reducer(across, bits, part_ref, inbox, sum_ref)
+
+    def partial(flips):
+        shard = flipped(me, flips)
+        return product(first_ref[shard], first_w[...], True) + product(
+            second_ref[shard], second_w[...], True
+        )
+
+    for flips in reducer.everyone:
+        reducer.to_sibling(flips, partial(flips + (0,)))
+    for flips in reducer.everyone:
+        reducer.own(flips, partial(flips))
+    for copy in bands:
+        copy.wait_recv()
+    bands = []
+    for ref, box, sum_of in small:
+        total = ref[band_of(ref, row)].astype(jnp.float32)
+        for turn in range(1, fsdp):
+            total = total + box[turn - 1].astype(jnp.float32)
+        sum_of[band_of(ref, row)] = total.astype(sum_of.dtype)
+        at = sum_of.at[band_of(ref, row)]
+        bands += [line.send(at, at, (row + turn) % fsdp) for turn in range(1, fsdp)]
+    turns = reducer.turns()
+    for turn in turns[:2]:
+        turn()
+
+    @pl.when(me < fsdp)
+    def _():
+        gate_recv[...] = jnp.zeros(gate_recv.shape, BF16)
+
+    query_out[...] = early_ref[:, :q_mine].astype(jnp.float32)
+    key_out[...] = early_ref[:, q_mine : q_mine + kv_mine].astype(jnp.float32)
+    value_out[...] = early_ref[:, q_mine + kv_mine : late].astype(jnp.float32)
+    for turn in turns[2:]:
+        turn()
+    for copy in moved:
+        copy.wait_recv()
+    count = attn_out.shape[0] // size
+    for s in range(size):
+        mix_out[s * high : (s + 1) * high] = r_recv[s, :high].astype(jnp.float32)
+        attn_out[s * count : (s + 1) * count] = r_recv[s, high : high + count].astype(jnp.float32)
+    gates.wait()
+    gates.finish()
+    for copy in bands:
+        copy.wait_recv()
+    across.finish()
+    line.finish()
+
+
+def reduce_and_place(first, second, weight, early, stack, head, state, sizes, collective_id):
+    ctx, fsdp, bits = lax.axis_size("ctx"), lax.axis_size("fsdp"), ctx_bits()
+    q_mine, kv_mine, mix_rows, attn_rows = sizes
+    own, columns = first.shape[0] // ctx, weight.shape[0]
+    rows, mine = early.shape[0], second.shape[1]
+    width, block = mine // fsdp, stack.shape[1] // ctx
+    boxes, count = reducer_boxes(ctx, bits, own, columns)
+    ctx_sems = pltpu.SemaphoreType.DMA((count + 2 * (ctx - 1),))
+    line_sems = pltpu.SemaphoreType.DMA((4 * (fsdp - 1),))
+
+    def shape(*sizes):
+        return jax.ShapeDtypeStruct(sizes, jnp.float32)
+
+    return pl.pallas_call(
+        functools.partial(back_kernel, ctx, fsdp),
+        out_shape=[
+            shape(own, columns), shape(rows, q_mine), shape(rows, kv_mine), shape(rows, kv_mine),
+            jax.ShapeDtypeStruct((ctx, rows, width), BF16),
+            shape(ctx * attn_rows, block), shape(ctx * mix_rows, block),
+            shape(*head.shape),
+            jax.ShapeDtypeStruct(state.shape, BF16),
+        ],
+        in_specs=[IN_VMEM] * 7,
+        out_specs=[IN_VMEM] * 9,
+        scratch_shapes=[
+            pltpu.VMEM((columns, first.shape[1]), BF16),
+            pltpu.VMEM((columns, second.shape[1]), BF16),
+            pltpu.VMEM((fsdp - 1, head.shape[0] // fsdp, mine), jnp.float32),
+            pltpu.VMEM((fsdp - 1, state.shape[0] // fsdp, mine), BF16),
+            pltpu.VMEM((ctx, rows, width), BF16),
+            pltpu.VMEM((ctx, stack.shape[0], block), BF16),
+            pltpu.VMEM((ctx, stack.shape[0], block), BF16),
+            ctx_sems, ctx_sems, line_sems, line_sems,
+        ]
+        + boxes,
+        compiler_params=params(collective_id),
+        name="reduce_and_place",
+    )(
+        first.reshape(ctx, own, -1), second.reshape(ctx, own, -1), weight, early, stack, head, state
+    )
+
+
+def finish_kernel(
+    size, fsdp, src_ref, gate_ref, head_ref, state_ref, gain_ref,
+    mixer_out, step_out, head_out, state_out, sums_ref,
+    head_all, state_all, gain_inbox, line_inbox, c_send, c_recv, s_send, s_recv, ctx_send, ctx_recv, line_send, line_recv,
+):
+    me, row = lax.axis_index("ctx"), lax.axis_index("fsdp")
+    greet_planes(me, size, row, fsdp)
+    rows, width, low = c_send.shape[1], c_send.shape[2], step_out.shape[0]
+    repeat = size // fsdp
+    across, line = Copies("ctx", ctx_send, ctx_recv), Copies("fsdp", line_send, line_recv)
+    head_all[me] = head_ref[...]
+    state_all[me] = state_ref[...]
+    lists = [gather_steps(across, size.bit_length() - 1, ref) for ref in (state_all, head_all)]
+    steps = [step for pair in zip(*lists) for step in pair]
+    steps[0]()
+    steps[1]()
     gains = [
         across.send(gain_ref, gain_inbox.at[turn - 1], (me + turn) % size)
         for turn in range(1, size)
     ]
     for d in range(size):
-        unit = d % fsdp
         if d < fsdp:
-            c_send[d, :rows] = src_ref[:rows, unit * width : (unit + 1) * width]
-        else:
-            at = late + unit * width
-            c_send[d, :rows] = early_ref[:, at : at + width]
+            c_send[d] = src_ref[:rows, d * width : (d + 1) * width]
         at = d // repeat * width
-        c_send[d, rows:] = src_ref[rows:, at : at + width]
-        r_send[d] = stack_ref[:, d * block : (d + 1) * block]
-    moved = exchange(across, c_send, c_recv, me, size) + exchange(across, r_send, r_recv, me, size)
-    query_out[...] = early_ref[:, :q_mine].astype(jnp.float32)
-    key_out[...] = early_ref[:, q_mine : q_mine + kv_mine].astype(jnp.float32)
-    value_out[...] = early_ref[:, q_mine + kv_mine : late].astype(jnp.float32)
-
-    total = channel_ref[band_of(row)]
-    for turn in range(1, fsdp):
-        bands[turn - 1].wait_recv()
-        total = total + row_inbox[turn - 1]
-    all_ref[me, band_of(row)] = total
-    at = all_ref.at[me, band_of(row)]
-    bands = [line.send(at, at, (row + turn) % fsdp) for turn in range(1, fsdp)]
+        s_send[d] = src_ref[rows:, at : at + width]
+    parts = SomeExchange(across, c_send, c_recv, me, size, lambda d: d < fsdp)
+    parts.start()
+    moved = exchange(across, s_send, s_recv, me, size)
+    for step in steps[2:6]:
+        step()
     total = gain_ref[...]
     for turn in range(1, size):
         gains[turn - 1].wait_recv()
@@ -1168,46 +1363,50 @@
         line.send(line_inbox.at[0], line_inbox.at[turn], (row + turn) % fsdp)
         for turn in range(1, fsdp)
     ]
-    for copy in bands:
-        copy.wait_recv()
-    steps = gather_steps(across, bits, all_ref)
-    steps[0]()
+
+    @pl.when(me >= fsdp)
+    def _():
+        for s in range(size):
+            mixer_out[:, s * width : (s + 1) * width] = gate_ref[s].astype(jnp.float32)
+
+    for step in steps[6:-2]:
+        step()
+    parts.wait()
+
+    @pl.when(me < fsdp)
+    def _():
+        for s in range(size):
+            mixer_out[:, s * width : (s + 1) * width] = c_recv[s].astype(jnp.float32)
+
+    steps[-2]()
+    steps[-1]()
+    part = head_out.shape[1] // fsdp
+    for out, ref in ((state_out, state_all), (head_out, head_all)):
+        for s in range(size):
+            for f in range(fsdp):
+                at = f * part + s * width
+                out[:, at : at + width] = ref[s, :, f * width : (f + 1) * width].astype(out.dtype)
+
     for copy in moved:
         copy.wait_recv()
-    for step in steps[1:-1]:
-        step()
-    for s in range(size):
-        mixer_out[:, s * width : (s + 1) * width] = c_recv[s, :rows].astype(jnp.float32)
-        mix_out[s * high : (s + 1) * high] = r_recv[s, :high].astype(jnp.float32)
-        count = attn_out.shape[0] // size
-        attn_out[s * count : (s + 1) * count] = r_recv[s, high : high + count].astype(jnp.float32)
     for j in range(fsdp):
         source = fsdp * (me % repeat) + j
-        step_out[:, j * width : (j + 1) * width] = c_recv[source, rows : rows + low].astype(
-            jnp.float32
-        )
-    steps[-1]()
-    part = channel_out.shape[1] // fsdp
-    for s in range(size):
-        for f in range(fsdp):
-            at = f * part + s * width
-            channel_out[:, at : at + width] = all_ref[s, :, f * width : (f + 1) * width]
+        step_out[:, j * width : (j + 1) * width] = s_recv[source, :low].astype(jnp.float32)
     total = line_inbox[0]
     for turn in range(1, fsdp):
         gains[turn - 1].wait_recv()
         total = total + line_inbox[turn]
     sums_ref[...] = total
+    parts.finish()
     across.finish()
     line.finish()
 
 
-def finish(early, src, stack, channel, gains, sizes, collective_id):
-    ctx, fsdp, bits = lax.axis_size("ctx"), lax.axis_size("fsdp"), ctx_bits()
-    q_mine, kv_mine, step_rows, mix_rows, attn_rows = sizes
-    rows, mine = early.shape[0], src.shape[1]
-    width, block = mine // fsdp, stack.shape[1] // ctx
-    ctx_sems = pltpu.SemaphoreType.DMA((3 * (ctx - 1) + gather_sems(bits),))
-    line_sems = pltpu.SemaphoreType.DMA((3 * (fsdp - 1),))
+def finish(src, gates, head, state, gains, step_rows, collective_id):
+    ctx, fsdp = lax.axis_size("ctx"), lax.axis_size("fsdp")
+    rows, width = gates.shape[1:]
+    ctx_sems = pltpu.SemaphoreType.DMA((3 * (ctx - 1) + 2 * gather_sems(ctx_bits()),))
+    line_sems = pltpu.SemaphoreType.DMA((fsdp - 1,))
 
     def shape(*sizes):
         return jax.ShapeDtypeStruct(sizes, jnp.float32)
@@ -1215,27 +1414,26 @@
     return pl.pallas_call(
         functools.partial(finish_kernel, ctx, fsdp),
         out_shape=[
-            shape(rows, q_mine), shape(rows, kv_mine), shape(rows, kv_mine),
-            shape(rows, ctx * width), shape(step_rows, mine),
-            shape(ctx * attn_rows, block), shape(ctx * mix_rows, block),
-            shape(channel.shape[0], ctx * mine), shape(*gains.shape),
+            shape(rows, ctx * width), shape(step_rows, fsdp * width),
+            shape(head.shape[0], ctx * head.shape[1]), shape(state.shape[0], ctx * head.shape[1]),
+            shape(*gains.shape),
         ],
         in_specs=[IN_VMEM] * 5,
-        out_specs=[IN_VMEM] * 9,
+        out_specs=[IN_VMEM] * 5,
         scratch_shapes=[
-            pltpu.VMEM((ctx,) + channel.shape, jnp.float32),
-            pltpu.VMEM((fsdp - 1, channel.shape[0] // fsdp, mine), jnp.float32),
+            pltpu.VMEM((ctx,) + head.shape, jnp.float32),
+            pltpu.VMEM((ctx,) + state.shape, BF16),
             pltpu.VMEM((ctx - 1,) + gains.shape, jnp.float32),
             pltpu.VMEM((fsdp,) + gains.shape, jnp.float32),
-            pltpu.VMEM((ctx, src.shape[0], width), BF16),
-            pltpu.VMEM((ctx, src.shape[0], width), BF16),
-            pltpu.VMEM((ctx, stack.shape[0], block), BF16),
-            pltpu.VMEM((ctx, stack.shape[0], block), BF16),
+            pltpu.VMEM((ctx, rows, width), BF16),
+            pltpu.VMEM((ctx, rows, width), BF16),
+            pltpu.VMEM((ctx, src.shape[0] - rows, width), BF16),
+            pltpu.VMEM((ctx, src.shape[0] - rows, width), BF16),
             ctx_sems, ctx_sems, line_sems, line_sems,
         ],
         compiler_params=params(collective_id),
         name="finish",
-    )(early, src, stack, channel, gains)
+    )(src, gates, head, state, gains)
 
 
 def window(start, size, total, step):
@@ -1477,7 +1675,7 @@
 def scan_bwd_kernel(
     units, steps_ref, drive_ref, grad_ref, in_ref, out_ref, rate_ref, prev_ref, *refs
 ):
-    exchanged, refs = refs[: 2 if units else 0], refs[2 if units else 0 :]
+    exchanged, refs = refs[: 1 if units else 0], refs[1 if units else 0 :]
     gstep_ref, gdrive_ref, gin_ref, gout_ref, grate_ref = refs[:5]
     received, refs = refs[5 : 8 if units else 5], refs[8 if units else 5 :]
     carry_ref, pin_ref, pout_ref = refs[:3]
@@ -1548,7 +1746,7 @@
         pl.when(pl.program_id(0) == last)(functools.partial(relay_end, units, *received, *slots))
 
 
-def scan_bwd(steps, drive, grad, in_b, out_b, rates, previous, relay=(), units=0, hidden=0, collective_id=None):
+def scan_bwd(steps, drive, grad, in_b, out_b, rates, previous, relay=None, units=0, hidden=0, part=0, model=0, collective_id=None):
     length, width = steps.shape
     chunk = CHUNK
     count = length // chunk
@@ -1558,21 +1756,21 @@
     red = pl.BlockSpec((1, 8, chunk * STATE), lambda i: (count - 1 - i, 0, 0))
     shape = jax.ShapeDtypeStruct
     relay_out, slots = [], []
+    extra = [] if relay is None else [relay]
     settings = dict(vmem_limit_bytes=56 * 1024 * 1024)
-    if relay:
-        ctx = lax.axis_size("ctx")
-        pair, down = relay
-        wide, block = hidden // ctx, down.shape[1] // ctx
+    if relay is not None:
+        ctx, fsdp = lax.axis_size("ctx"), lax.axis_size("fsdp")
+        wide, block, high = hidden // ctx, model // ctx, model // fsdp
         relay_out = [
-            shape((pair.shape[0], ctx * wide), jnp.float32),
-            shape((pair.shape[0], ctx * wide), jnp.float32),
+            shape((high, ctx * wide), jnp.float32),
+            shape((high, ctx * wide), jnp.float32),
             shape((units * ctx * wide, block), jnp.float32),
         ]
         slots = [
-            pltpu.VMEM((ctx, pair.shape[0], 2 * wide), BF16),
-            pltpu.VMEM((ctx, pair.shape[0], 2 * wide), BF16),
-            pltpu.VMEM((ctx, down.shape[0], block), BF16),
-            pltpu.VMEM((ctx, down.shape[0], block), BF16),
+            pltpu.VMEM((ctx, high, 2 * wide), BF16),
+            pltpu.VMEM((ctx, high, 2 * wide), BF16),
+            pltpu.VMEM((ctx, part, block), BF16),
+            pltpu.VMEM((ctx, part, block), BF16),
             pltpu.SemaphoreType.DMA((2 * (ctx - 1),)),
             pltpu.SemaphoreType.DMA((2 * (ctx - 1),)),
         ]
@@ -1582,7 +1780,7 @@
         grid=(count,),
         in_specs=[row, row, row, mat, mat, rate,
                   pl.BlockSpec((chunk, STATE, width), lambda i: (count - 1 - i, 0, 0))]
-        + [pl.BlockSpec(a.shape, lambda i: (0, 0)) for a in relay],
+        + [pl.BlockSpec(a.shape, lambda i: (0, 0)) for a in extra],
         out_specs=[row, row, red, red, rate]
         + [pl.BlockSpec(a.shape, lambda i: (0, 0)) for a in relay_out],
         out_shape=[
@@ -1601,7 +1799,7 @@
         + slots,
         compiler_params=pltpu.CompilerParams(**settings),
         name="scan_backward",
-    )(steps, drive, grad, in_b, out_b, rates, previous, *relay)
+    )(steps, drive, grad, in_b, out_b, rates, previous, *extra)
     return (
         gstep, gdrive, gin[:, 0].reshape(length, STATE), gout[:, 0].reshape(length, STATE), grate,
         relayed,
@@ -1923,9 +2121,8 @@
     ffn_scale = rms_scale(middle)
     ffn_in = (middle * ffn_scale * ffn_gain).astype(BF16)
     if ctx == 8:
-        pair_dw, down_dw, ffn_out, grad_ffn_in = ffn_both_ways(
-            ffn_in, grad_top, ffn_full, down_full, 5
-        )
+        ffn_dw, ffn_out, grad_ffn_in = ffn_both_ways(ffn_in, grad_top, ffn_full, down_full, 5)
+        ffn_dw = [ffn_dw.reshape(-1, 2 * hid_all)]
     else:
         ffn_all = gather_tokens(ffn_in, 5)
         pre = matmul(ffn_all, ffn_full)
@@ -1940,22 +2137,25 @@
         grad_ffn_in = reduce_products([grad_pair], [ffn_full], True, 7)
         down_dw = left_trans(hidden, grad_top).astype(BF16)
         pair_dw = left_trans(ffn_all, grad_pair).astype(BF16)
-    grad_ffn_in, down_dw, pair_dw = lax.optimization_barrier((grad_ffn_in, down_dw, pair_dw))
-    down_grad = scatter_fsdp(down_dw)
-    pair_grad = scatter_fsdp(pair_dw)
+        ffn_dw = [pair_dw, down_dw]
+    grad_ffn_in, ffn_dw = lax.optimization_barrier((grad_ffn_in, ffn_dw))
+    ffn_grad = [scatter_fsdp(dw) for dw in ffn_dw]
     grad_middle, grad_ffn_gain = norm_back(grad_ffn_in, middle, ffn_scale, ffn_gain)
     grad_middle = grad_middle + cotangent[0].astype(jnp.float32)
     grad_branch = (0.5 * grad_middle).astype(BF16)
     branch_all = gather_tokens(grad_branch, 8)
-    grad_attn_c = right_trans(branch_all, attn_full).astype(BF16)
     if ctx == 8:
-        grad_early, grad_attn_gain, ffn_out, out_dw = attention_backward(
-            grad_attn_c, attn_rows, attn_gain, ffn_out, (branch_attn_c, branch_ssm), branch_all,
-            attn_kept, 13,
-        )
+        grad_early, grad_attn_gain, ffn_out, out_dw, grad_norm, dots = attention_backward(
+            (attn_full, mixout_full), attn_rows, (attn_gain, gain_ssm), ssm_gated, ffn_out,
+            (branch_attn_c, branch_ssm), branch_all, attn_kept, 13,
+        )
+        dots = dots[0]
         out_dw = [out_dw.reshape(-1, model)]
         grad_attn_gain = grad_attn_gain[0]
     else:
+        grad_attn_c = right_trans(branch_all, attn_full).astype(BF16)
+        grad_norm = right_trans(branch_all, mixout_full)
+        dots = total_of(jnp.sum(grad_norm * gain_ssm * ssm_gated, axis=-1), 9)
         grad_attn = attn_to_tokens(grad_attn_c).astype(jnp.float32)
         grad_attn_raw, grad_attn_gain = norm_back(grad_attn, attn_rows, attn_scale, attn_gain)
         grad_heads = grad_attn_raw.astype(BF16).reshape(own, KV_HEADS, group_size, HEAD)
@@ -1992,15 +2192,14 @@
             left_trans(branch_attn_c, branch_all).astype(BF16),
         ]
 
-    grad_early, out_dw, pair_grad = lax.optimization_barrier((grad_early, out_dw, pair_grad))
+    grad_early, out_dw = lax.optimization_barrier((grad_early, out_dw))
     out_grad = scatter_fsdp(*out_dw)
 
     output = middle + ffn_out
 
-    grad_norm = right_trans(branch_all, mixout_full)
     grad_ssm_gain = jnp.sum(grad_norm * ssm_gated * ssm_scale, axis=0)
     scaled = grad_norm * gain_ssm
-    mean_dot = total_of(jnp.sum(scaled * ssm_gated, axis=-1), 9)[:, None] / inner
+    mean_dot = dots[:, None] / inner
     grad_gated = ssm_scale * scaled - ssm_gated * ssm_scale**3 * mean_dot
     grad_scan = grad_gated * gate_act
     grad_gate_z = grad_gated * ssm_raw * silu_slope(gate_z)
@@ -2008,10 +2207,10 @@
     grad_gate_bf = grad_gate_z.astype(BF16)
     grad_early = jnp.concatenate([grad_early, grad_gate_bf], 1)
     early_grad = scatter_fsdp(left_trans(normed_all, grad_early))
-    with_relay = ctx == 8 and hidden_units == ctx
+    with_relay = ctx == 8
     grad_steps, grad_drive, grad_input_mat, grad_output_mat, grad_rate, relayed = scan_bwd(
         steps_pad, vals_pad, padded(grad_scan), in_b, out_b, rates_log2, states,
-        *(((pair_grad, down_grad), hidden_rows, hid, 14) if with_relay else ()),
+        *((ffn_grad[0], hidden_rows, hid, down_at, model, 14) if with_relay else ()),
     )
     grad_steps, out_grad = lax.optimization_barrier((grad_steps, out_grad))
     grad_steps, grad_drive, grad_rate = (
@@ -2045,10 +2244,35 @@
     )
     grad_src = grad_src.astype(BF16)
     src_grad = scatter_fsdp(left_trans(normed_all, grad_src), step_dw)
-    grad_normed = reduce_products([grad_early, grad_src], [in_full], True, 11)
+    state_rows_all = grad_state_proj.shape[1]
+    state_cut = state_rows_all // (16 * fsdp) * 16 * fsdp
+    grad_state = grad_state_proj.T
+    head = jnp.concatenate(
+        [
+            grad_taps,
+            jnp.stack([grad_conv_bias, grad_step_bias, grad_skip, grad_ssm_gain]),
+            grad_rate,
+            grad_state[state_cut:],
+        ],
+        0,
+    )
+    head = jnp.pad(head, ((0, -head.shape[0] % (8 * fsdp)), (0, 0)))
+    grad_state = grad_state[:state_cut].astype(BF16)
+    placing = ctx == 8 and ctx == 2 * fsdp and not attn_pad
+    if placing:
+        (
+            grad_normed, query_grad, key_grad, value_grad, gates, attn_grad, mixout_grad, head,
+            grad_state,
+        ) = reduce_and_place(
+            grad_early, grad_src, in_full, early_grad, out_grad, head, grad_state,
+            (q_mine, kv_mine, mix_rows, attn_rows_mine), 11,
+        )
+    else:
+        grad_normed = reduce_products([grad_early, grad_src], [in_full], True, 11)
     if with_relay:
         gate_blocks, up_blocks, down_blocks = relayed
     else:
+        pair_grad, down_grad = ffn_grad
         pair_grad = pair_grad.reshape(-1, 2, fsdp, down_at)[..., :hid_part]
         gate_blocks = to_blocks(pair_grad[:, 0].reshape(-1, hid), hidden_units)
         up_blocks = to_blocks(pair_grad[:, 1].reshape(-1, hid), hidden_units)
@@ -2056,29 +2280,18 @@
     grad_tokens, grad_norm_gain = norm_back(grad_normed, tokens, norm_scale, norm_gain)
     grad_tokens = grad_tokens + grad_middle
 
-    channel = jnp.concatenate(
-        [
-            grad_taps,
-            jnp.stack([grad_conv_bias, grad_step_bias, grad_skip, grad_ssm_gain]),
-            grad_rate,
-            grad_state_proj.T,
-        ],
-        0,
-    )
     gains = jnp.stack([grad_norm_gain, grad_attn_gain, grad_ffn_gain])
-    channel = jnp.pad(channel, ((0, -channel.shape[0] % (8 * fsdp)), (0, 0)))
     gains = jnp.pad(gains, ((0, 5), (0, 0)))
-    if ctx == 8 and ctx == 2 * fsdp and not attn_pad:
-        (
-            query_grad, key_grad, value_grad, mixer_grad, step_grad, attn_grad, mixout_grad, channel, gains,
-        ) = finish(
-            early_grad, src_grad, out_grad, channel, gains,
-            (q_mine, kv_mine, step_rows, mix_rows, attn_rows_mine), 12,
+    if placing:
+        mixer_grad, step_grad, head, grad_state, gains = finish(
+            src_grad, gates, head, grad_state, gains, step_rows, 12
         )
     else:
+        channel = jnp.concatenate([head, grad_state.astype(jnp.float32)], 0)
         channel, gains = settle_small(channel, gains, 12)
         channel = channel.reshape(ctx, -1, fsdp, mine // fsdp).transpose(1, 2, 0, 3)
         channel = channel.reshape(-1, inner)
+        head, grad_state = channel[: head.shape[0]], channel[head.shape[0] :]
         late_at = q_mine + 2 * kv_mine
         step_grad = src_grad[early_grad.shape[0] :][:step_rows]
         src_grad = src_grad[: early_grad.shape[0]]
@@ -2104,15 +2317,17 @@
         attn_grad,
         sum_attn_gain,
         mixer_grad,
-        channel[:CONV],
-        channel[CONV],
-        channel[CONV + 4 + STATE : CONV + 4 + STATE + state_proj.shape[1]].T,
+        head[:CONV],
+        head[CONV],
+        jnp.concatenate(
+            [grad_state, head[CONV + 4 + STATE :][: state_rows_all - state_cut]], 0
+        ).T,
         step_grad,
-        channel[CONV + 1],
-        channel[CONV + 4 : CONV + 4 + STATE].T,
-        channel[CONV + 2],
+        head[CONV + 1],
+        head[CONV + 4 : CONV + 4 + STATE].T,
+        head[CONV + 2],
         mixout_grad,
-        channel[CONV + 3],
+        head[CONV + 3],
         sum_ffn_gain,
         gate_blocks,
         up_blocks,

time: 669 us -> 643 us (0.961)
  local copies, waits for them, and re-layouts: 76.3 us -> 61.6 us
  waiting for transfers between devices: 3.98 us -> 16.8 us
  matrix products: 36.6 us -> 23.8 us
  Pallas kernels: 491 us -> 480 us
    pallas_call x1 -> x2, Pallas kernels: 57 us -> 93.3 us  [the longest x1 54.3 us: ffn_both_ways(): pl.pallas_call(ffn_kernel, out_shape=[jax.ShapeDtypeStruct((fsdp, stack_r...]
    pallas_call x2 -> x1, Pallas kernels: 57.8 us -> 24.8 us  [reduce_products(): pl.pallas_call(functools.partial(reduce_kernel, bits, (trans,) * len(left...]
    pallas_call x1, Pallas kernels: 44.9 us -> 32.3 us  [finish(): pl.pallas_call(functools.partial(finish_kernel, ctx, fsdp), out_shape=[sh...]
    dot_general x4 -> x2, matrix products: 15.3 us -> 3.95 us  [right_trans(): lax.dot_general(left, right, (((1,), (1,)), ((), ())), preferred_element_...]
    reduce_scatter x5 -> x4, waiting for transfers between devices: 1.71 us -> 11.8 us  [scatter_fsdp(): return lax.psum_scatter(joined, 'fsdp', scatter_dimension=0, tiled=True)]
    unnamed x130 -> x102, local copies, waits for them, and re-layouts: 19.1 us -> 19.1 us
  transfers between devices with their start and end apart: 7 -> 6, of which waited for: 2 -> 3; matrix products, arithmetic and copies ran while one was open for 19% -> 16% of each run, Pallas kernels for 47% -> 49%
where the time goes in v4:
time: 643 us; the launch traced here: 635 us
  Pallas kernels  480 us (75%)
  local copies, waits for them, and re-layouts  61.6 us (10%)
  other arithmetic  37.5 us (6%)
  matrix products  23.8 us (4%)
  waiting for transfers between devices  16.8 us (3%)
  between operations  15.3 us (2%)
    pallas_call x1, Pallas kernels, front(): pl.pallas_call(functools.partial(front_kernel, bits, count, turned, pack_...  81.1 us
    pallas_call x1, Pallas kernels, attention_backward(): pl.pallas_call(functools.partial(attention_back_kernel, ctx, fsdp), out_s...  67.3 us
    pallas_call x1, Pallas kernels, ffn_both_ways(): pl.pallas_call(ffn_kernel, out_shape=[jax.ShapeDtypeStruct((fsdp, stack_r...  54.3 us
    pallas_call x1, Pallas kernels, attention_forward(): pl.pallas_call(functools.partial(attention_kernel, ctx, fsdp), out_shape=...  52.3 us
    pallas_call x1, Pallas kernels, scan_bwd(): pl.pallas_call(functools.partial(scan_bwd_kernel, units), grid=(count,),...  49.5 us
    pallas_call x1, Pallas kernels, reduce_and_place(): pl.pallas_call(functools.partial(back_kernel, ctx, fsdp), out_shape=[shap...  39 us
    pallas_call x1, Pallas kernels, finish(): pl.pallas_call(functools.partial(finish_kernel, ctx, fsdp), out_shape=[sh...  32.3 us
    pallas_call x2, Pallas kernels, sum_everywhere(): pl.pallas_call(functools.partial(sum_kernel, ctx), out_shape=jax.ShapeDty...  30.9 us
  transfers between devices with their start and end apart: 6, of which 3 were waited for; matrix products, arithmetic and copies ran while one was open for 16% of the time, Pallas kernels for 49%

profile of v4, /device:TPU:1, one launch (start us, length us, event | category | flops | bytes accessed | tf_op | source)
XLA Modules:
  0.0 634.9 jit_solution(11206118704787189829)
XLA Ops:
  8.5 81.1 %front.1 = (bf16[8,128,1600]{2,1,0:T(8,128)(2,1)}, bf16[8,128,1600]{2,1,0:T(8,128)(2,1)}, bf16[4,400,1080]{2,1,0:T(8,128)(2,1)}, bf16[4,112,132]{2,1,0:T(8,128)(...) custom-call(bf16[1600,128]{1,0:T(8,128)(2,1)} %bitcast.141, ...), custom_call_target="tpu_custom_call" | custom-call | tf_op jit(solution)/shard_map/front/pallas_call | solution.py:284
  93.9 7.9 %convolution_convert_fusion.proj_ref = bf16[1024,1080]{1,0:T(8,128)(2,1)S(1)} fusion(bf16[1024,1600]{1,0:T(8,128)(2,1)} %bitcast.171, bf16[1600,1080]{1,0:T(8,128)(2,1)} %bitcast.131), kind=kOutput, calls=%fused_computation.1 | convolution fusion | flops 3540049920 | bytes 8944640 | tf_op jit(solution)/shard_map/dot_general | solution.py:1810
  103.3 2.7 multiply_convert_fusion.1
  107.5 16.5 %sum_everywhere.2 = bf16[8,128,132]{2,1,0:T(8,128)(2,1)} custom-call(bf16[8,128,132]{2,1,0:T(8,128)(2,1)} %bitcast.140), custom_call_target="tpu_custom_call" | custom-call | tf_op jit(solution)/shard_map/sum_everywhere/pallas_call | solution.py:540
  124.1 1.6 pad.25.drive_ref
  125.8 2.6 compare_select_fusion
  129.9 4.2 broadcast_in_dim.16.in_ref
  134.1 3.8 broadcast_in_dim.17.out_ref
  137.9 19.2 %scan_forward.1 = (f32[1024,512]{1,0:T(8,128)S(1)}, f32[1024,16,512]{2,1,0:T(8,128)}) custom-call(f32[1024,512]{1,0:T(8,128)S(1)} %pad.24.steps_ref, f32[1024,512]{1,0:T(8,128)} %pad.25.drive_ref, bf16[1024,16,128]{2,1,0:T(8,128)(2,1)} %broadcast_in_dim.16.in_ref, bf16[1024,16,128]{2,1,0:T(8,128)(2,1)} %broadcast_in_dim.17.out_ref, f32[16,512]{1,0:T(8,128)S(1)} %pad.26.rate_ref), custom_call_target="tpu_custom_call" | custom-call | tf_op jit(solution)/shard_map/scan_forward/pallas_call | solution.py:1660
  158.4 3.2 multiply_reduce_fusion.6
  161.6 5.8 total_of.1
  168.1 52.3 %attention_forward.1 = (bf16[8,128,200]{2,1,0:T(8,128)(2,1)}, f32[128,1600]{1,0:T(8,128)}, bf16[5,1024,640]{2,1,0:T(8,128)(2,1)}, f32[5,1,640]{2,1,0:T(1,128)}, ...) custom-call(bf16[1024,1080]{1,0:T(8,128)(2,1)} %copy-done.9, ...), custom_call_target="tpu_custom_call" | custom-call | tf_op jit(solution)/shard_map/attention_forward/pallas_call | solution.py:950
  221.7 1.5 slice.181
  223.2 1.3 slice.180
  224.6 3.2 slice.182
  227.8 1.5 reshape.214.refs_3_.mix_w
  230.4 24.8 %reduce_products.1 = f32[128,1600]{1,0:T(8,128)} custom-call(bf16[8,128,200]{2,1,0:T(8,128)(2,1)} %get-tuple-element.77.refs_0_, bf16[8,128,400]{2,1,0:T(8,128)(2,1)} %bitcast.120, bf16[200,1600]{1,0:T(8,128)(2,1)} %reshape.213.refs_2_.attn_w, bf16[400,1600]{1,0:T(8,128)(2,1)} %reshape.214.refs_3_.mix_w), custom_call_target="tpu_custom_call" | custom-call | tf_op jit(solution)/shard_map/reduce_products/pallas_call | solution.py:434
  255.2 1.4 multiply_reduce_fusion.9
  257.7 4.2 all-gather.4.cloned.1.call-done.pair_w
  261.9 54.3 %ffn_both_ways.1 = (bf16[4,608,1408]{2,1,0:T(8,128)(2,1)}, bf16[8,128,1600]{2,1,0:T(8,128)(2,1)}, f32[128,1600]{1,0:T(8,128)}) custom-call(bf16[128,1600]{1,0:T(8,128)(2,1)} %multiply_convert_fusion.3.x_ref, bf16[8,128,1600]{2,1,0:T(8,128)(2,1)} %get-tuple-element.83.top_ref, bf16[1600,1408]{1,0:T(8,128)(2,1)} %all-gather.4.cloned.1.call-done.pair_w, ...), custom_call_target="tpu_custom_call" | custom-call | tf_op jit(solution)/shard_map/ffn_both_ways/pallas_call | solution.py:817
  317.8 1.4 multiply_convert_fusion.2
  319.2 23.0 %gather_shards.1 = bf16[8,128,1600]{2,1,0:T(8,128)(2,1)} custom-call(bf16[128,1600]{1,0:T(8,128)(2,1)} %get-tuple-element.217.x_ref), custom_call_target="tpu_custom_call" | custom-call | tf_op jit(solution)/shard_map/gather_shards/pallas_call | solution.py:136
  342.2 67.3 %attention_backward.1 = (bf16[1024,280]{1,0:T(8,128)(2,1)}, f32[1,1600]{1,0:T(1,128)}, f32[128,1600]{1,0:T(8,128)}, bf16[4,160,1600]{2,1,0:T(8,128)(2,1)}, f32[1024,400]{1,0:T(8,128)}, /*index=5*/f32[8,1024]{1,0:T(8,128)}) custom-call(bf16[200,1600]{1,0:T(8,128)(2,1)} %reshape.213.refs_2_.attn_w, bf16[400,1600]{1,0:T(8,128)(2,1)} %reshape.214.refs_3_.mix_w, ...), custom_call_target="tpu_custom_call" | custom-call | tf_op jit(solution)/shard_map/attention_backward/pallas_call | solution.py:1128
  411.2 5.3 multiply_reduce_fusion.1
  419.0 4.3 convolution_convert_fusion.1
  423.5 1.4 copy-done.10
  424.9 1.5 pad.27.grad_ref
  426.4 8.0 %reduce-scatter.5.cloned.1.call-done.refs_0_ = bf16[608,1408]{1,0:T(8,128)(2,1)} async-done(((bf16[2432,1408]{1,0:T(8,128)(2,1)}), bf16[608,1408]{1,0:T(8,128)(2,1)}) %reduce-scatter.5.cloned.1.call-update) | async-done | bytes 1712144 | tf_op jit(solution)/shard_map/reduce_scatter | solution.py:1919
  434.4 49.5 %scan_backward.1 = (f32[1024,512]{1,0:T(8,128)}, f32[1024,512]{1,0:T(8,128)}, f32[8,8,2048]{2,1,0:T(8,128)}, f32[8,8,2048]{2,1,0:T(8,128)}, f32[16,512]{1,0:T(8,...) custom-call(f32[1024,512]{1,0:T(8,128)} %copy-done, f32[1024,512]{1,0:T(8,128)} %pad.25.drive_ref, ...), custom_call_target="tpu_custom_call" | custom-call | tf_op jit(solution)/shard_map/scan_backward/pallas_call | solution.py:1778
  483.9 2.8 fusion.28
  491.7 14.4 %sum_everywhere.3 = bf16[8,128,132]{2,1,0:T(8,128)(2,1)} custom-call(bf16[8,128,132]{2,1,0:T(8,128)(2,1)} %pad_maximum_fusion.1.x_ref), custom_call_target="tpu_custom_call" | custom-call | tf_op jit(solution)/shard_map/sum_everywhere/pallas_call | solution.py:540
  506.1 3.5 multiply_multiply_fusion
  509.6 3.6 fusion.26
  513.3 2.8 convolution_convert_fusion.2
  516.1 3.4 copy.112
  519.5 1.4 convolution_convert_fusion.4
  521.2 3.1 maximum_maximum_fusion
  528.6 3.8 reduce-scatter.9.cloned.1.call-done.early_ref
  532.4 39.0 %reduce_and_place.1 = (f32[128,1600]{1,0:T(8,128)}, f32[400,200]{1,0:T(8,128)}, f32[400,40]{1,0:T(8,128)}, f32[400,40]{1,0:T(8,128)}, bf16[8,400,100]{2,1,0:T(8,...) custom-call(bf16[8,128,680]{2,1,0:T(8,128)(2,1)} %bitcast.125, ...), custom_call_target="tpu_custom_call" | custom-call | tf_op jit(solution)/shard_map/reduce_and_place/pallas_call | solution.py:1298
  571.5 1.4 fusion.17
  572.9 1.6 fusion.14
  578.4 1.4 copy.103
  580.4 32.3 %finish.1 = (f32[400,800]{1,0:T(8,128)}, f32[25,400]{1,0:T(8,128)}, f32[32,3200]{1,0:T(8,128)}, f32[128,3200]{1,0:T(8,128)}, f32[8,1600]{1,0:T(8,128)}) custom-call(bf16[432,400]{1,0:T(8,128)(2,1)} %reduce-scatter.11.cloned.1.call-done.src_ref, bf16[8,400,100]{2,1,0:T(8,128)(2,1)} %get-tuple-element.111.gate_ref, f32[32,400]{1,0:T(8,128)} %get-tuple-element.112.head_ref, ...), custom_call_target="tpu_custom_call" | custom-call | tf_op jit(solution)/shard_map/finish/pallas_call | solution.py:1414
  612.7 1.6 fusion.31
  614.4 1.6 slice_bitcast_fusion
  616.0 1.9 slice_reduce_fusion
  617.9 1.6 slice_reduce_fusion.4
  619.5 2.9 maximum_bitcast_fusion
  (172 shorter events, 40.5 us)
Async XLA Ops:
  7.2 214.6 %all-gather.6.cloned.1.call-start = ((), (), s32[]{:S(2)}) async-start(), calls=%async_computation.9 | async-start | bytes 5591040 | tf_op jit(solution)/shard_map/all_gather | solution.py:2014
  89.6 2.0 copy-start.31
  89.7 172.2 %all-gather.4.cloned.1.call-start = ((), (), s32[]{:S(2)}) async-start(), calls=%async_computation.4 | async-start | bytes 5632000 | tf_op jit(solution)/shard_map/all_gather | solution.py:1870
  90.4 344.0 %reduce-scatter.5.cloned.1.call-start = ((), (), s32[]{:S(2)}) async-start(), calls=%async_computation.5 | async-start | bytes 8560640 | tf_op jit(solution)/shard_map/reduce_scatter | solution.py:1919
  101.8 1.5 copy-start.9
  102.3 3.8 copy-start.7
  106.0 18.0 %copy-start.32 = (bf16[4,32,400]{2,1,0:T(8,128)(2,1)S(1)}, bf16[4,32,400]{2,1,0:T(8,128)(2,1)}, u32[]{:S(2)}) copy-start(bf16[4,32,400]{2,1,0:T(8,128)(2,1)} %get-tuple-element.79) | copy-start | bytes 307204
  124.0 1.8 copy-start.18
  128.5 9.4 %copy-start = (f32[1024,512]{1,0:T(8,128)}, f32[1024,512]{1,0:T(8,128)S(1)}, u32[]{:S(2)}) copy-start(f32[1024,512]{1,0:T(8,128)S(1)} %pad.24.steps_ref) | copy-start | bytes 6291460
  129.7 8.2 %copy-start.3 = (f32[16,512]{1,0:T(8,128)}, f32[16,512]{1,0:T(8,128)S(1)}, u32[]{:S(2)}) copy-start(f32[16,512]{1,0:T(8,128)S(1)} %pad.26.rate_ref) | copy-start | bytes 98308
  157.1 4.5 copy-start.1
  158.4 9.1 %copy-start.40 = (f32[1600]{0:T(1024)S(1)}, f32[1600]{0:T(1024)}, u32[]{:S(2)}) copy-start(f32[1600]{0:T(1024)} %param.29) | copy-start | bytes 19204
  161.6 60.1 %copy-start.4 = (f32[1024,400]{1,0:T(8,128)}, f32[1024,400]{1,0:T(8,128)S(1)}, u32[]{:S(2)}) copy-start(f32[1024,400]{1,0:T(8,128)S(1)} %get-tuple-element.222.gated_ref) | copy-start | bytes 4915204
  167.5 53.0 %copy-start.36 = (f32[8,128]{1,0:T(8,128)S(1)}, f32[8,128]{1,0:T(8,128)}, u32[]{:S(2)}) copy-start(f32[8,128]{1,0:T(8,128)} %total_of.1) | copy-start | bytes 12292
  220.5 2.7 copy-start.38
  230.4 24.8 %copy-start.12 = (bf16[1,128,1600]{2,1,0:T(8,128)(2,1)S(1)}, bf16[1,128,1600]{2,1,0:T(8,128)(2,1)}, u32[]{:S(2)}) copy-start(bf16[1,128,1600]{2,1,0:T(8,128)(2,1)} %copy.83) | copy-start | bytes 1228804
  255.2 1.5 copy-start.33
  256.7 61.2 %copy-start.5 = (f32[128,1600]{1,0:T(8,128)}, f32[128,1600]{1,0:T(8,128)S(1)}, u32[]{:S(2)}) copy-start(f32[128,1600]{1,0:T(8,128)S(1)} %get-tuple-element.220) | copy-start | bytes 2457604
  316.2 1.4 copy-start.16
  316.2 167.7 %reduce-scatter.7.cloned.1.call-start = ((), (), s32[]{:S(2)}) async-start(), calls=%async_computation.6 | async-start | bytes 2662400 | tf_op jit(solution)/shard_map/reduce_scatter | solution.py:1919
  409.6 1.6 copy-start.2
  409.6 1.6 copy-start.39
  409.6 122.8 %reduce-scatter.9.cloned.1.call-start = ((), (), s32[]{:S(2)}) async-start(), calls=%async_computation.7 | async-start | bytes 3072000 | tf_op jit(solution)/shard_map/reduce_scatter | solution.py:1919
  411.2 5.3 copy-start.26
  416.5 2.5 copy-start.42
  423.3 1.6 copy-start.10
  423.3 157.1 %reduce-scatter.11.cloned.1.call-start = ((), (), s32[]{:S(2)}) async-start(), calls=%async_computation.8 | async-start | bytes 2211840 | tf_op jit(solution)/shard_map/reduce_scatter | solution.py:1919
  490.5 15.6 %copy-start.11 = (f32[1024,400]{1,0:T(8,128)S(1)}, f32[1024,400]{1,0:T(8,128)}, u32[]{:S(2)}) copy-start(f32[1024,400]{1,0:T(8,128)} %get-tuple-element.214) | copy-start | bytes 4915204
  506.1 3.5 copy-start.8
  509.6 3.7 copy-start.43
  513.3 2.8 copy-start.15
  521.1 3.2 copy-start.6
  524.4 2.5 copy-start.19
  525.7 2.2 copy-start.37
  532.4 39.0 %copy-start.13 = (bf16[1,128,1600]{2,1,0:T(8,128)(2,1)S(1)}, bf16[1,128,1600]{2,1,0:T(8,128)(2,1)}, u32[]{:S(2)}) copy-start(bf16[1,128,1600]{2,1,0:T(8,128)(2,1)} %copy.83) | copy-start | bytes 1228804
  532.4 39.0 %copy-start.34 = (f32[1600]{0:T(1024)S(1)}, f32[1600]{0:T(1024)}, u32[]{:S(2)}) copy-start(f32[1600]{0:T(1024)} %param.24) | copy-start | bytes 19204
  532.4 40.5 %copy-start.17 = (f32[128,1600]{1,0:T(8,128)S(1)}, f32[128,1600]{1,0:T(8,128)}, u32[]{:S(2)}) copy-start(f32[128,1600]{1,0:T(8,128)} %get-tuple-element.218) | copy-start | bytes 2457604
  572.9 2.8 copy-start.25
  574.5 2.4 copy-start.30
  574.5 3.1 copy-start.29
  574.5 3.8 copy-start.22
  575.7 4.1 copy-start.41
  612.7 9.6 %copy-start.28 = (f32[400,200]{1,0:T(8,128)S(1)}, f32[400,200]{1,0:T(8,128)}, u32[]{:S(2)}) copy-start(f32[400,200]{1,0:T(8,128)} %get-tuple-element.302) | copy-start | bytes 960004
  619.4 3.6 copy-start.27
  619.5 4.4 copy-start.21
  622.3 2.6 copy-start.35
  623.1 2.5 copy-start.24
  623.8 2.8 copy-start.23
  (2 other events, 2.2 us)
Sparse Core Ops, SparseCore 0:
  89.8 86.0 all-gather.5
  177.4 84.3 all-gather.3
  316.3 117.9 reduce-scatter.4
  436.6 44.7 reduce-scatter.6
  483.5 48.8 reduce-scatter.8
  534.6 41.1 reduce-scatter.10

commit v5 on v4

--- a/solution.py
+++ b/solution.py
@@ -971,6 +971,27 @@
         compiler_params=params(collective_id),
         name="attention_forward",
     )(projected, gain[None])
+
+
+def stacked_rows(rows):
+    return rows + -rows % 16
+
+
+def folded(model, span, high):
+    out = [(0, g * high, g * span, 0, high) for g in range(model // span)]
+    spill = model % span
+    if spill:
+        pieces = span // spill
+        tall = -(-high // pieces)
+        for k in range(pieces):
+            low, up = k * tall, min(high, (k + 1) * tall)
+            if low < up:
+                out.append((k * spill, model // span * high, model - spill, low, up))
+    return out
+
+
+def folded_rows(model, span, high):
+    return stacked_rows(max(row + up - low for _, row, _, low, up in folded(model, span, high)))
 
 
 def attention_back_kernel(
@@ -1017,16 +1038,24 @@
     beside = [add_parts] + ffn_sum.turns()
     values = rows_ref[...]
     scale = lax.rsqrt(jnp.mean(values * values, axis=-1, keepdims=True) + EPSILON)
-    at = 0
+    at, span = 0, dw_ref.shape[2]
+    high = stacked_rows((ssm_ref.shape[1] + branch_ref.shape[1]) // fsdp)
+    dw_ref[...] = jnp.zeros(dw_ref.shape, BF16)
     for ref in (ssm_ref, branch_ref):
         wide = ref.shape[1] // fsdp
         weights = lax.dot_general(
             ref[...], top_ref[...], (((0,), (0,)), ((), ())), preferred_element_type=jnp.float32
         ).astype(BF16)
         for f in range(fsdp):
-            dw_ref[f, at : at + wide] = weights[f * wide : (f + 1) * wide]
+            mine = weights[f * wide : (f + 1) * wide]
+            for lane, row, first, low, up in folded(model, span, high):
+                begin, end = max(low, at), min(up, at + wide)
+                if begin < end:
+                    lanes = min(span, model - first)
+                    dw_ref[f, row + begin - low : row + end - low, lane : lane + lanes] = mine[
+                        begin - at : end - at, first : first + lanes
+                    ]
         at += wide
-    dw_ref[:, at:] = jnp.zeros((fsdp, dw_ref.shape[1] - at, model), BF16)
     for copy in come:
         copy.wait_recv()
     part = model // fsdp
@@ -1114,7 +1143,7 @@
     copies.finish()
 
 
-def attention_backward(weights, rows, gains, gated, parts, branches, top, kept, collective_id):
+def attention_backward(weights, rows, gains, gated, parts, branches, top, kept, span, collective_id):
     ctx, fsdp, bits = lax.axis_size("ctx"), lax.axis_size("fsdp"), ctx_bits()
     prob = kept[0]
     own, model = rows.shape
@@ -1131,7 +1160,7 @@
             shape((length, q_mine + 2 * kv_mine), BF16),
             shape((1, model), jnp.float32),
             shape((own, model), jnp.float32),
-            shape((fsdp, dw_rows + -dw_rows % 16, model), BF16),
+            shape((fsdp, folded_rows(model, span, stacked_rows(dw_rows)), span), BF16),
             shape(gated.shape, jnp.float32),
             shape((8, length), jnp.float32),
         ],
@@ -1198,7 +1227,7 @@
 
 
 def back_kernel(
-    size, fsdp, first_ref, second_ref, weight_ref, early_ref, stack_ref, head_ref, state_ref,
+    size, fsdp, first_ref, second_ref, weight_ref, early_ref, head_ref, state_ref,
     sum_ref, query_out, key_out, value_out, gate_recv, attn_out, mix_out, head_sum, state_sum,
     first_w, second_w, head_inbox, state_inbox, c_send, r_send, r_recv,
     ctx_send, ctx_recv, line_send, line_recv, part_ref, *inbox,
@@ -1222,11 +1251,19 @@
         to = (row + turn) % fsdp
         for ref, box, _ in small:
             bands.append(line.send(ref.at[band_of(ref, to)], box.at[turn - 1], to))
+    span, tall = early_ref.shape[1], r_send.shape[1]
     for d in range(size):
-        r_send[d] = stack_ref[:, d * block : (d + 1) * block]
+        for lane, begin, first, low, up in folded(size * block, span, tall):
+            lanes = min(span, size * block - first)
+            left, right = max(d * block, first), min((d + 1) * block, first + lanes)
+            if left < right:
+                at = lane + left - first
+                r_send[d, low:up, left - d * block : right - d * block] = early_ref[
+                    rows + begin : rows + begin + up - low, at : at + right - left
+                ]
         if d >= fsdp:
             at = late + (d - fsdp) * width
-            c_send[d] = early_ref[:, at : at + width]
+            c_send[d] = early_ref[:rows, at : at + width]
     gates = SomeExchange(across, c_send, gate_recv, me, size, lambda d: d >= fsdp)
     gates.start()
     moved = exchange(across, r_send, r_recv, me, size)
@@ -1263,9 +1300,9 @@
     def _():
         gate_recv[...] = jnp.zeros(gate_recv.shape, BF16)
 
-    query_out[...] = early_ref[:, :q_mine].astype(jnp.float32)
-    key_out[...] = early_ref[:, q_mine : q_mine + kv_mine].astype(jnp.float32)
-    value_out[...] = early_ref[:, q_mine + kv_mine : late].astype(jnp.float32)
+    query_out[...] = early_ref[:rows, :q_mine].astype(jnp.float32)
+    key_out[...] = early_ref[:rows, q_mine : q_mine + kv_mine].astype(jnp.float32)
+    value_out[...] = early_ref[:rows, q_mine + kv_mine : late].astype(jnp.float32)
     for turn in turns[2:]:
         turn()
     for copy in moved:
@@ -1282,12 +1319,12 @@
     line.finish()
 
 
-def reduce_and_place(first, second, weight, early, stack, head, state, sizes, collective_id):
+def reduce_and_place(first, second, weight, early, head, state, sizes, collective_id):
     ctx, fsdp, bits = lax.axis_size("ctx"), lax.axis_size("fsdp"), ctx_bits()
     q_mine, kv_mine, mix_rows, attn_rows = sizes
     own, columns = first.shape[0] // ctx, weight.shape[0]
-    rows, mine = early.shape[0], second.shape[1]
-    width, block = mine // fsdp, stack.shape[1] // ctx
+    rows, mine = columns // fsdp, second.shape[1]
+    width, block, tall = mine // fsdp, columns // ctx, stacked_rows(mix_rows + attn_rows)
     boxes, count = reducer_boxes(ctx, bits, own, columns)
     ctx_sems = pltpu.SemaphoreType.DMA((count + 2 * (ctx - 1),))
     line_sems = pltpu.SemaphoreType.DMA((4 * (fsdp - 1),))
@@ -1304,7 +1341,7 @@
             shape(*head.shape),
             jax.ShapeDtypeStruct(state.shape, BF16),
         ],
-        in_specs=[IN_VMEM] * 7,
+        in_specs=[IN_VMEM] * 6,
         out_specs=[IN_VMEM] * 9,
         scratch_shapes=[
             pltpu.VMEM((columns, first.shape[1]), BF16),
@@ -1312,15 +1349,15 @@
             pltpu.VMEM((fsdp - 1, head.shape[0] // fsdp, mine), jnp.float32),
             pltpu.VMEM((fsdp - 1, state.shape[0] // fsdp, mine), BF16),
             pltpu.VMEM((ctx, rows, width), BF16),
-            pltpu.VMEM((ctx, stack.shape[0], block), BF16),
-            pltpu.VMEM((ctx, stack.shape[0], block), BF16),
+            pltpu.VMEM((ctx, tall, block), BF16),
+            pltpu.VMEM((ctx, tall, block), BF16),
             ctx_sems, ctx_sems, line_sems, line_sems,
         ]
         + boxes,
         compiler_params=params(collective_id),
         name="reduce_and_place",
     )(
-        first.reshape(ctx, own, -1), second.reshape(ctx, own, -1), weight, early, stack, head, state
+        first.reshape(ctx, own, -1), second.reshape(ctx, own, -1), weight, early, head, state
     )
 
 
@@ -1617,6 +1654,39 @@
     }
 
 
+def weight_kernel(fsdp, count, *refs):
+    lefts, rights, rest, out_ref = refs[:count], refs[count : 2 * count], refs[2 * count : -1], refs[-1]
+    for f in range(fsdp):
+        at = 0
+        for left, right in zip(lefts, rights):
+            high, wide = left.shape[1] // fsdp, right.shape[1]
+            out_ref[f, at : at + high, :wide] = lax.dot_general(
+                left[:, f * high : (f + 1) * high], right[...], (((0,), (0,)), ((), ())),
+                preferred_element_type=jnp.float32,
+            ).astype(BF16)
+            if wide < out_ref.shape[2]:
+                out_ref[f, at : at + high, wide:] = jnp.zeros((high, out_ref.shape[2] - wide), BF16)
+            at += high
+        for ref in rest:
+            out_ref[f, at : at + ref.shape[1]] = ref[f]
+            at += ref.shape[1]
+        if at < out_ref.shape[1]:
+            out_ref[f, at:] = jnp.zeros((out_ref.shape[1] - at, out_ref.shape[2]), BF16)
+
+
+def weight_gradients(pairs, given, span):
+    fsdp = lax.axis_size("fsdp")
+    rows = sum(left.shape[1] // fsdp for left, _ in pairs) + sum(part.shape[1] for part in given)
+    return pl.pallas_call(
+        functools.partial(weight_kernel, fsdp, len(pairs)),
+        out_shape=jax.ShapeDtypeStruct((fsdp, stacked_rows(rows), span), BF16),
+        in_specs=[IN_VMEM] * (2 * len(pairs) + len(given)),
+        out_specs=IN_VMEM,
+        compiler_params=pltpu.CompilerParams(vmem_limit_bytes=VMEM_LIMIT),
+        name="weight_gradients",
+    )(*[left for left, _ in pairs], *[right for _, right in pairs], *given)
+
+
 def scan_fwd_kernel(steps_ref, drive_ref, in_ref, out_ref, rate_ref, scan_ref, prev_ref, state_ref):
     tiles = steps_ref.shape[1] // LANES
     chunk = steps_ref.shape[0]
@@ -1690,53 +1760,63 @@
         carry_ref[...] = jnp.zeros_like(carry_ref)
         grate_ref[...] = jnp.zeros_like(grate_ref)
 
-    for j in range(tiles):
-        lanes = slice(j * LANES, (j + 1) * LANES)
-        rates = rate_ref[:, lanes]
+    for first in range(0, tiles, 4):
+        tile_lanes = [slice(j * LANES, (j + 1) * LANES) for j in range(first, min(first + 4, tiles))]
+        tile_rates = [rate_ref[:, lanes] for lanes in tile_lanes]
 
         def group(k, kept):
-            carry, acc = kept
+            carries, sums = list(kept[0]), list(kept[1])
             base = pl.multiple_of(chunk - 8 - k * 8, 8)
-            step_8 = steps_ref[pl.ds(base, 8), lanes]
-            x_8 = drive_ref[pl.ds(base, 8), lanes]
-            drive_8 = step_8 * x_8
-            grad_8 = grad_ref[pl.ds(base, 8), lanes]
-            held_rows, dot_rows = [None] * 8, [None] * 8
+            rows_8 = pl.ds(base, 8)
+            step_8 = [steps_ref[rows_8, lanes] for lanes in tile_lanes]
+            x_8 = [drive_ref[rows_8, lanes] for lanes in tile_lanes]
+            grad_8 = [grad_ref[rows_8, lanes] for lanes in tile_lanes]
+            drive_8 = [step * x for step, x in zip(step_8, x_8)]
+            held_rows = [[None] * 8 for _ in tile_lanes]
+            dot_rows = [[None] * 8 for _ in tile_lanes]
             for t in range(7, -1, -1):
                 in_t = in_ref[base + t].astype(jnp.float32)
                 out_t = out_ref[base + t].astype(jnp.float32)
-                previous = prev_ref[base + t, :, lanes]
-                step_t = step_8[t : t + 1]
-                drive_t = drive_8[t : t + 1]
-                grad_t = grad_8[t : t + 1]
-                decay = jnp.exp2(step_t * rates)
-                adjoint = grad_t * out_t + carry
-                carry = decay * adjoint
-                held = carry * previous
-                state = decay * previous + drive_t * in_t
-                acc = acc + held * step_t
-                held_rows[t] = jnp.sum(held * rates, axis=0, keepdims=True)
-                dot_rows[t] = jnp.sum(adjoint * in_t, axis=0, keepdims=True)
-                part_in = adjoint * drive_t
-                part_out = state * grad_t
+                part_in = part_out = None
+                for n, lanes in enumerate(tile_lanes):
+                    rates = tile_rates[n]
+                    previous = prev_ref[base + t, :, lanes]
+                    step_t = step_8[n][t : t + 1]
+                    drive_t = drive_8[n][t : t + 1]
+                    grad_t = grad_8[n][t : t + 1]
+                    decay = jnp.exp2(step_t * rates)
+                    adjoint = grad_t * out_t + carries[n]
+                    carries[n] = decay * adjoint
+                    held = carries[n] * previous
+                    state = decay * previous + drive_t * in_t
+                    sums[n] = sums[n] + held * step_t
+                    held_rows[n][t] = jnp.sum(held * rates, axis=0, keepdims=True)
+                    dot_rows[n][t] = jnp.sum(adjoint * in_t, axis=0, keepdims=True)
+                    more_in, more_out = adjoint * drive_t, state * grad_t
+                    part_in = more_in if part_in is None else part_in + more_in
+                    part_out = more_out if part_out is None else part_out + more_out
                 at = pl.ds(pl.multiple_of((base + t) * STATE, STATE), STATE)
-                if j == 0:
+                if first == 0:
                     pin_ref[at] = part_in
                     pout_ref[at] = part_out
                 else:
                     pin_ref[at] += part_in
                     pout_ref[at] += part_out
-            held_8 = jnp.concatenate(held_rows, 0)
-            dot_8 = jnp.concatenate(dot_rows, 0)
-            gstep_ref[pl.ds(base, 8), lanes] = held_8 * 0.6931471805599453 + x_8 * dot_8
-            gdrive_ref[pl.ds(base, 8), lanes] = step_8 * dot_8
-            return carry, acc
-
-        carry, acc = lax.fori_loop(
-            0, chunk // 8, group, (carry_ref[:, lanes], grate_ref[:, lanes])
-        )
-        carry_ref[:, lanes] = carry
-        grate_ref[:, lanes] = acc
+            for n, lanes in enumerate(tile_lanes):
+                held_8 = jnp.concatenate(held_rows[n], 0)
+                dot_8 = jnp.concatenate(dot_rows[n], 0)
+                gstep_ref[rows_8, lanes] = held_8 * 0.6931471805599453 + x_8[n] * dot_8
+                gdrive_ref[rows_8, lanes] = step_8[n] * dot_8
+            return tuple(carries), tuple(sums)
+
+        start = (
+            tuple(carry_ref[:, lanes] for lanes in tile_lanes),
+            tuple(grate_ref[:, lanes] for lanes in tile_lanes),
+        )
+        carries, sums = lax.fori_loop(0, chunk // 8, group, start)
+        for n, lanes in enumerate(tile_lanes):
+            carry_ref[:, lanes] = carries[n]
+            grate_ref[:, lanes] = sums[n]
     ones = jnp.ones((8, LANES), jnp.float32)
     dims = (((1,), (1,)), ((), ()))
     gin_ref[0] = lax.dot_general(ones, pin_ref[...], dims, preferred_element_type=jnp.float32)
@@ -2144,13 +2224,15 @@
     grad_middle = grad_middle + cotangent[0].astype(jnp.float32)
     grad_branch = (0.5 * grad_middle).astype(BF16)
     branch_all = gather_tokens(grad_branch, 8)
+    placing = ctx == 8 and ctx == 2 * fsdp and not attn_pad
+    early_wide = q_mine + 2 * kv_mine + mine
+    early_span = early_wide + -early_wide % LANES
     if ctx == 8:
         grad_early, grad_attn_gain, ffn_out, out_dw, grad_norm, dots = attention_backward(
             (attn_full, mixout_full), attn_rows, (attn_gain, gain_ssm), ssm_gated, ffn_out,
-            (branch_attn_c, branch_ssm), branch_all, attn_kept, 13,
+            (branch_attn_c, branch_ssm), branch_all, attn_kept, early_span, 13,
         )
         dots = dots[0]
-        out_dw = [out_dw.reshape(-1, model)]
         grad_attn_gain = grad_attn_gain[0]
     else:
         grad_attn_c = right_trans(branch_all, attn_full).astype(BF16)
@@ -2193,7 +2275,8 @@
         ]
 
     grad_early, out_dw = lax.optimization_barrier((grad_early, out_dw))
-    out_grad = scatter_fsdp(*out_dw)
+    if not placing:
+        out_grad = scatter_fsdp(*out_dw)
 
     output = middle + ffn_out
 
@@ -2206,13 +2289,17 @@
     grad_skip = jnp.sum(grad_scan * conv_vals, axis=0)
     grad_gate_bf = grad_gate_z.astype(BF16)
     grad_early = jnp.concatenate([grad_early, grad_gate_bf], 1)
-    early_grad = scatter_fsdp(left_trans(normed_all, grad_early))
+    if placing:
+        early_dw = weight_gradients([(normed_all, grad_early)], [out_dw], early_span)
+        early_dw = early_dw.reshape(-1, early_span)
+    else:
+        early_dw = left_trans(normed_all, grad_early)
+    early_grad = scatter_fsdp(early_dw)
     with_relay = ctx == 8
     grad_steps, grad_drive, grad_input_mat, grad_output_mat, grad_rate, relayed = scan_bwd(
         steps_pad, vals_pad, padded(grad_scan), in_b, out_b, rates_log2, states,
         *((ffn_grad[0], hidden_rows, hid, down_at, model, 14) if with_relay else ()),
     )
-    grad_steps, out_grad = lax.optimization_barrier((grad_steps, out_grad))
     grad_steps, grad_drive, grad_rate = (
         grad_steps[:, :mine],
         grad_drive[:, :mine],
@@ -2221,7 +2308,6 @@
     grad_pre_full = grad_steps * jax.nn.sigmoid(step_pre)
     grad_step_bias = jnp.sum(grad_pre_full, axis=0)
     grad_pre = grad_pre_full.astype(BF16)
-    step_dw = left_trans(step_low, grad_pre)
     grad_projected = sum_everywhere(
         jnp.concatenate(
             [right_trans(grad_pre, step_full), grad_input_mat, grad_output_mat], 1
@@ -2243,7 +2329,12 @@
         for tap in range(CONV)
     )
     grad_src = grad_src.astype(BF16)
-    src_grad = scatter_fsdp(left_trans(normed_all, grad_src), step_dw)
+    if placing:
+        src_dw = weight_gradients([(normed_all, grad_src), (step_low, grad_pre)], [], mine)
+        src_dw, early_grad = lax.optimization_barrier((src_dw, early_grad))
+        src_grad = scatter_fsdp(src_dw.reshape(-1, mine))
+    else:
+        src_grad = scatter_fsdp(left_trans(normed_all, grad_src), left_trans(step_low, grad_pre))
     state_rows_all = grad_state_proj.shape[1]
     state_cut = state_rows_all // (16 * fsdp) * 16 * fsdp
     grad_state = grad_state_proj.T
@@ -2258,13 +2349,12 @@
     )
     head = jnp.pad(head, ((0, -head.shape[0] % (8 * fsdp)), (0, 0)))
     grad_state = grad_state[:state_cut].astype(BF16)
-    placing = ctx == 8 and ctx == 2 * fsdp and not attn_pad
     if placing:
         (
             grad_normed, query_grad, key_grad, value_grad, gates, attn_grad, mixout_grad, head,
             grad_state,
         ) = reduce_and_place(
-            grad_early, grad_src, in_full, early_grad, out_grad, head, grad_state,
+            grad_early, grad_src, in_full, early_grad, head, grad_state,
             (q_mine, kv_mine, mix_rows, attn_rows_mine), 11,
         )
     else:

time: 643 us -> 639 us (level)
  waiting for transfers between devices: 16.8 us -> 3.23 us
  Pallas kernels: 480 us -> 490 us
  matrix products: 23.8 us -> 15.8 us
    pallas_call x0 -> x2, Pallas kernels: none -> 16.4 us  [weight_gradients(): pl.pallas_call(functools.partial(weight_kernel, fsdp, len(pairs)), out_sh...]
    reduce_scatter x4 -> x3, waiting for transfers between devices: 11.8 us -> 2.47 us  [scatter_fsdp(): return lax.psum_scatter(joined, 'fsdp', scatter_dimension=0, tiled=True)]
    dot_general x4 -> x1, matrix products: 8.85 us -> 1.37 us  [left_trans(): lax.dot_general(left, right, (((0,), (0,)), ((), ())), preferred_element_...]
    unnamed x102 -> x126, local copies, waits for them, and re-layouts: 19.1 us -> 17.9 us
  transfers between devices with their start and end apart: 6 -> 5, of which waited for: 3 -> 1; matrix products, arithmetic and copies ran while one was open for 16% -> 16% of each run, Pallas kernels for 49% -> 51%
where the time goes in v5:
time: 639 us; the launch traced here: 630 us
  Pallas kernels  490 us (77%)
  local copies, waits for them, and re-layouts  66.9 us (10%)
  other arithmetic  38.8 us (6%)
  matrix products  15.8 us (2%)
  between operations  15 us (2%)
    pallas_call x1, Pallas kernels, front(): pl.pallas_call(functools.partial(front_kernel, bits, count, turned, pack_...  81.1 us
    pallas_call x1, Pallas kernels, attention_backward(): pl.pallas_call(functools.partial(attention_back_kernel, ctx, fsdp), out_s...  67.2 us
    pallas_call x1, Pallas kernels, ffn_both_ways(): pl.pallas_call(ffn_kernel, out_shape=[jax.ShapeDtypeStruct((fsdp, stack_r...  53.7 us
    pallas_call x1, Pallas kernels, attention_forward(): pl.pallas_call(functools.partial(attention_kernel, ctx, fsdp), out_shape=...  52.5 us
    pallas_call x1, Pallas kernels, scan_bwd(): pl.pallas_call(functools.partial(scan_bwd_kernel, units), grid=(count,),...  44 us
    pallas_call x1, Pallas kernels, reduce_and_place(): pl.pallas_call(functools.partial(back_kernel, ctx, fsdp), out_shape=[shap...  39.2 us
    pallas_call x1, Pallas kernels, finish(): pl.pallas_call(functools.partial(finish_kernel, ctx, fsdp), out_shape=[sh...  31.9 us
    pallas_call x2, Pallas kernels, sum_everywhere(): pl.pallas_call(functools.partial(sum_kernel, ctx), out_shape=jax.ShapeDty...  30.9 us
  transfers between devices with their start and end apart: 5, of which 1 were waited for; matrix products, arithmetic and copies ran while one was open for 16% of the time, Pallas kernels for 51%

profile of v5, /device:TPU:1, one launch (start us, length us, event | category | flops | bytes accessed | tf_op | source)
XLA Modules:
  0.0 630.3 jit_solution(8212365541662917048)
XLA Ops:
  8.5 81.1 %front.1 = (bf16[8,128,1600]{2,1,0:T(8,128)(2,1)}, bf16[8,128,1600]{2,1,0:T(8,128)(2,1)}, bf16[4,400,1080]{2,1,0:T(8,128)(2,1)}, bf16[4,112,132]{2,1,0:T(8,128)(...) custom-call(bf16[1600,128]{1,0:T(8,128)(2,1)} %bitcast.137, ...), custom_call_target="tpu_custom_call" | custom-call | tf_op jit(solution)/shard_map/front/pallas_call | solution.py:284
  90.7 2.0 copy.79
  92.7 1.6 slice.140
  94.3 1.8 copy.84
  97.1 1.5 dynamic-slice_bitcast_fusion.11
  99.7 7.4 %convolution_convert_fusion.proj_ref = bf16[1024,1080]{1,0:T(8,128)(2,1)S(1)} fusion(bf16[1024,1600]{1,0:T(8,128)(2,1)S(1)} %bitcast.116, bf16[1600,1080]{1,0:T(8,128)(2,1)} %bitcast.128), kind=kOutput, calls=%fused_computation.1 | convolution fusion | flops 3540049920 | bytes 8944640 | tf_op jit(solution)/shard_map/dot_general | solution.py:1890
  108.5 2.7 multiply_convert_fusion.1
  112.7 16.3 %sum_everywhere.2 = bf16[8,128,132]{2,1,0:T(8,128)(2,1)} custom-call(bf16[8,128,132]{2,1,0:T(8,128)(2,1)} %bitcast.136), custom_call_target="tpu_custom_call" | custom-call | tf_op jit(solution)/shard_map/sum_everywhere/pallas_call | solution.py:540
  129.1 1.6 pad.25.drive_ref
  130.8 2.6 compare_select_fusion
  134.9 3.8 broadcast_in_dim.14.in_ref
  138.8 3.8 broadcast_in_dim.15.out_ref
  142.5 19.5 %scan_forward.1 = (f32[1024,512]{1,0:T(8,128)S(1)}, f32[1024,16,512]{2,1,0:T(8,128)}) custom-call(f32[1024,512]{1,0:T(8,128)S(1)} %pad.24.steps_ref, f32[1024,512]{1,0:T(8,128)} %pad.25.drive_ref, bf16[1024,16,128]{2,1,0:T(8,128)(2,1)} %broadcast_in_dim.14.in_ref, bf16[1024,16,128]{2,1,0:T(8,128)(2,1)} %broadcast_in_dim.15.out_ref, f32[16,512]{1,0:T(8,128)S(1)} %pad.26.rate_ref), custom_call_target="tpu_custom_call" | custom-call | tf_op jit(solution)/shard_map/scan_forward/pallas_call | solution.py:1730
  163.4 3.2 multiply_reduce_fusion.6
  166.6 5.9 total_of.1
  173.1 52.5 %attention_forward.1 = (bf16[8,128,200]{2,1,0:T(8,128)(2,1)}, f32[128,1600]{1,0:T(8,128)}, bf16[5,1024,640]{2,1,0:T(8,128)(2,1)}, f32[5,1,640]{2,1,0:T(1,128)}, ...) custom-call(bf16[1024,1080]{1,0:T(8,128)(2,1)} %copy-done.8, ...), custom_call_target="tpu_custom_call" | custom-call | tf_op jit(solution)/shard_map/attention_forward/pallas_call | solution.py:950
  226.9 1.5 slice.181
  229.7 3.2 slice.182
  232.9 1.5 reshape.202.refs_3_.mix_w
  235.6 24.8 %reduce_products.1 = f32[128,1600]{1,0:T(8,128)} custom-call(bf16[8,128,200]{2,1,0:T(8,128)(2,1)} %get-tuple-element.77.refs_0_, bf16[8,128,400]{2,1,0:T(8,128)(2,1)} %bitcast.120, bf16[200,1600]{1,0:T(8,128)(2,1)} %reshape.201.refs_2_.attn_w, bf16[400,1600]{1,0:T(8,128)(2,1)} %reshape.202.refs_3_.mix_w), custom_call_target="tpu_custom_call" | custom-call | tf_op jit(solution)/shard_map/reduce_products/pallas_call | solution.py:434
  260.5 1.9 multiply_reduce_fusion.9
  263.3 53.7 %ffn_both_ways.1 = (bf16[4,608,1408]{2,1,0:T(8,128)(2,1)}, bf16[8,128,1600]{2,1,0:T(8,128)(2,1)}, f32[128,1600]{1,0:T(8,128)}) custom-call(bf16[128,1600]{1,0:T(8,128)(2,1)} %multiply_convert_fusion.3.x_ref, bf16[8,128,1600]{2,1,0:T(8,128)(2,1)} %get-tuple-element.83.top_ref, bf16[1600,1408]{1,0:T(8,128)(2,1)} %all-gather.4.cloned.1.call-done.pair_w, ...), custom_call_target="tpu_custom_call" | custom-call | tf_op jit(solution)/shard_map/ffn_both_ways/pallas_call | solution.py:817
  317.1 2.0 copy.80
  319.4 2.4 multiply_convert_fusion.2
  321.8 23.1 %gather_shards.1 = bf16[8,128,1600]{2,1,0:T(8,128)(2,1)} custom-call(bf16[128,1600]{1,0:T(8,128)(2,1)} %get-tuple-element.217.x_ref), custom_call_target="tpu_custom_call" | custom-call | tf_op jit(solution)/shard_map/gather_shards/pallas_call | solution.py:136
  344.9 67.2 %attention_backward.1 = (bf16[1024,280]{1,0:T(8,128)(2,1)}, f32[1,1600]{1,0:T(1,128)}, f32[128,1600]{1,0:T(8,128)}, bf16[4,336,768]{2,1,0:T(8,128)(2,1)}, f32[1024,400]{1,0:T(8,128)}, /*index=5*/f32[8,1024]{1,0:T(8,128)}) custom-call(bf16[200,1600]{1,0:T(8,128)(2,1)} %reshape.201.refs_2_.attn_w, bf16[400,1600]{1,0:T(8,128)(2,1)} %reshape.202.refs_3_.mix_w, ...), custom_call_target="tpu_custom_call" | custom-call | tf_op jit(solution)/shard_map/attention_backward/pallas_call | solution.py:1157
  412.9 5.5 multiply_reduce_fusion.1
  418.5 1.8 pad_maximum_fusion.refs_1_
  420.2 8.9 %weight_gradients.3 = bf16[4,736,768]{2,1,0:T(8,128)(2,1)} custom-call(bf16[1024,1600]{1,0:T(8,128)(2,1)} %bitcast.114, bf16[1024,680]{1,0:T(8,128)(2,1)} %pad_maximum_fusion.refs_1_, bf16[4,336,768]{2,1,0:T(8,128)(2,1)} %get-tuple-element.106.refs_2_), custom_call_target="tpu_custom_call" | custom-call | tf_op jit(solution)/shard_map/weight_gradients/pallas_call | solution.py:1680
  430.9 3.1 pad.27.grad_ref
  433.9 2.5 reduce-scatter.4.cloned.1.call-done.refs_0_
  436.4 44.0 %scan_backward.1 = (f32[1024,512]{1,0:T(8,128)}, f32[1024,512]{1,0:T(8,128)}, f32[8,8,2048]{2,1,0:T(8,128)}, f32[8,8,2048]{2,1,0:T(8,128)}, f32[16,512]{1,0:T(8,...) custom-call(f32[1024,512]{1,0:T(8,128)} %copy-done, f32[1024,512]{1,0:T(8,128)} %pad.25.drive_ref, ...), custom_call_target="tpu_custom_call" | custom-call | tf_op jit(solution)/shard_map/scan_backward/pallas_call | solution.py:1858
  480.4 2.8 fusion.27
  484.4 1.8 copy.90
  490.5 2.5 pad_maximum_fusion.1.x_ref
  492.9 14.5 %sum_everywhere.3 = bf16[8,128,132]{2,1,0:T(8,128)(2,1)} custom-call(bf16[8,128,132]{2,1,0:T(8,128)(2,1)} %pad_maximum_fusion.1.x_ref), custom_call_target="tpu_custom_call" | custom-call | tf_op jit(solution)/shard_map/sum_everywhere/pallas_call | solution.py:540
  507.6 3.6 multiply_multiply_fusion
  511.2 4.2 fusion.25
  515.4 7.6 %weight_gradients.2 = bf16[4,432,400]{2,1,0:T(8,128)(2,1)} custom-call(bf16[1024,1600]{1,0:T(8,128)(2,1)} %bitcast.115, bf16[1024,100]{1,0:T(8,128)(2,1)} %slice.176.refs_1_, bf16[1024,400]{1,0:T(8,128)(2,1)} %get-tuple-element.227.refs_2_, bf16[1024,400]{1,0:T(8,128)(2,1)} %copy-done.10), custom_call_target="tpu_custom_call" | custom-call | tf_op jit(solution)/shard_map/weight_gradients/pallas_call | solution.py:1680
  528.3 39.2 %reduce_and_place.1 = (f32[128,1600]{1,0:T(8,128)}, f32[400,200]{1,0:T(8,128)}, f32[400,40]{1,0:T(8,128)}, f32[400,40]{1,0:T(8,128)}, bf16[8,400,100]{2,1,0:T(8,...) custom-call(bf16[8,128,680]{2,1,0:T(8,128)(2,1)} %bitcast.113, ...), custom_call_target="tpu_custom_call" | custom-call | tf_op jit(solution)/shard_map/reduce_and_place/pallas_call | solution.py:1335
  569.0 1.6 fusion.14
  574.5 1.4 copy.97
  576.5 31.9 %finish.1 = (f32[400,800]{1,0:T(8,128)}, f32[25,400]{1,0:T(8,128)}, f32[32,3200]{1,0:T(8,128)}, f32[128,3200]{1,0:T(8,128)}, f32[8,1600]{1,0:T(8,128)}) custom-call(bf16[432,400]{1,0:T(8,128)(2,1)} %reduce-scatter.8.cloned.1.call-done.src_ref, bf16[8,400,100]{2,1,0:T(8,128)(2,1)} %get-tuple-element.111.gate_ref, f32[32,400]{1,0:T(8,128)} %get-tuple-element.112.head_ref, ...), custom_call_target="tpu_custom_call" | custom-call | tf_op jit(solution)/shard_map/finish/pallas_call | solution.py:1451
  608.5 1.6 fusion.30
  610.1 1.6 slice_bitcast_fusion
  611.7 1.9 slice_reduce_fusion
  613.6 1.6 slice_reduce_fusion.4
  615.2 2.9 maximum_bitcast_fusion
  (187 shorter events, 40.4 us)
Async XLA Ops:
  7.2 219.7 %all-gather.6.cloned.1.call-start = ((), (), s32[]{:S(2)}) async-start(), calls=%async_computation.7 | async-start | bytes 5591040 | tf_op jit(solution)/shard_map/all_gather | solution.py:2094
  89.7 10.0 %copy-start.9 = (bf16[8,128,1600]{2,1,0:T(8,128)(2,1)S(1)}, bf16[8,128,1600]{2,1,0:T(8,128)(2,1)}, u32[]{:S(2)}) copy-start(bf16[8,128,1600]{2,1,0:T(8,128)(2,1)} %get-tuple-element.75) | copy-start | bytes 9830404
  89.7 173.6 %all-gather.4.cloned.1.call-start = ((), (), s32[]{:S(2)}) async-start(), calls=%async_computation.3 | async-start | bytes 5632000 | tf_op jit(solution)/shard_map/all_gather | solution.py:1950
  90.5 345.9 %reduce-scatter.4.cloned.1.call-start = ((), (), s32[]{:S(2)}) async-start(), calls=%async_computation.4 | async-start | bytes 8560640 | tf_op jit(solution)/shard_map/reduce_scatter | solution.py:1999
  99.6 8.9 %copy-start.38 = (f32[1,400]{1,0:T(1,128)}, f32[1,400]{1,0:T(1,128)S(1)}, u32[]{:S(2)}) copy-start(f32[1,400]{1,0:T(1,128)S(1)} %get-tuple-element.257) | copy-start | bytes 4804
  99.6 8.9 %copy-start.40 = (f32[1,400]{1,0:T(1,128)}, f32[1,400]{1,0:T(1,128)S(1)}, u32[]{:S(2)}) copy-start(f32[1,400]{1,0:T(1,128)S(1)} %get-tuple-element.258) | copy-start | bytes 4804
  99.6 8.9 %copy-start.42 = (f32[1,400]{1,0:T(1,128)}, f32[1,400]{1,0:T(1,128)S(1)}, u32[]{:S(2)}) copy-start(f32[1,400]{1,0:T(1,128)S(1)} %get-tuple-element.259) | copy-start | bytes 4804
  99.6 8.9 %copy-start.44 = (f32[1,400]{1,0:T(1,128)}, f32[1,400]{1,0:T(1,128)S(1)}, u32[]{:S(2)}) copy-start(f32[1,400]{1,0:T(1,128)S(1)} %get-tuple-element.260) | copy-start | bytes 4804
  107.5 3.7 copy-start.6
  111.2 17.8 %copy-start.30 = (bf16[4,32,400]{2,1,0:T(8,128)(2,1)S(1)}, bf16[4,32,400]{2,1,0:T(8,128)(2,1)}, u32[]{:S(2)}) copy-start(bf16[4,32,400]{2,1,0:T(8,128)(2,1)} %get-tuple-element.79) | copy-start | bytes 307204
  112.7 18.1 %copy-start.53 = (f32[1,100]{1,0:T(1,128)S(1)}, f32[1,100]{1,0:T(1,128)}, u32[]{:S(2)}) copy-start(f32[1,100]{1,0:T(1,128)} %get-tuple-element.247) | copy-start | bytes 1204
  112.7 18.1 %copy-start.54 = (f32[1,100]{1,0:T(1,128)S(1)}, f32[1,100]{1,0:T(1,128)}, u32[]{:S(2)}) copy-start(f32[1,100]{1,0:T(1,128)} %get-tuple-element.248) | copy-start | bytes 1204
  129.1 4.3 copy-start.24
  133.6 9.0 %copy-start = (f32[1024,512]{1,0:T(8,128)}, f32[1024,512]{1,0:T(8,128)S(1)}, u32[]{:S(2)}) copy-start(f32[1024,512]{1,0:T(8,128)S(1)} %pad.24.steps_ref) | copy-start | bytes 6291460
  134.7 7.8 %copy-start.3 = (f32[16,512]{1,0:T(8,128)}, f32[16,512]{1,0:T(8,128)S(1)}, u32[]{:S(2)}) copy-start(f32[16,512]{1,0:T(8,128)S(1)} %pad.26.rate_ref) | copy-start | bytes 98308
  162.0 4.5 copy-start.1
  163.3 249.5 %copy-start.46 = (f32[1,400]{1,0:T(1,128)}, f32[1,400]{1,0:T(1,128)S(1)}, u32[]{:S(2)}) copy-start(f32[1,400]{1,0:T(1,128)S(1)} %pad_maximum_fusion.5) | copy-start | bytes 4804
  163.3 9.1 %copy-start.49 = (f32[1600]{0:T(1024)S(1)}, f32[1600]{0:T(1024)}, u32[]{:S(2)}) copy-start(f32[1600]{0:T(1024)} %param.29) | copy-start | bytes 19204
  166.6 60.3 %copy-start.4 = (f32[1024,400]{1,0:T(8,128)}, f32[1024,400]{1,0:T(8,128)S(1)}, u32[]{:S(2)}) copy-start(f32[1024,400]{1,0:T(8,128)S(1)} %get-tuple-element.222.gated_ref) | copy-start | bytes 4915204
  172.5 53.2 %copy-start.34 = (f32[8,128]{1,0:T(8,128)S(1)}, f32[8,128]{1,0:T(8,128)}, u32[]{:S(2)}) copy-start(f32[8,128]{1,0:T(8,128)} %total_of.1) | copy-start | bytes 12292
  235.6 24.8 %copy-start.12 = (bf16[1,128,1600]{2,1,0:T(8,128)(2,1)S(1)}, bf16[1,128,1600]{2,1,0:T(8,128)(2,1)}, u32[]{:S(2)}) copy-start(bf16[1,128,1600]{2,1,0:T(8,128)(2,1)} %copy.79) | copy-start | bytes 1228804
  317.1 205.9 %reduce-scatter.6.cloned.1.call-start = ((), (), s32[]{:S(2)}) async-start(), calls=%async_computation.5 | async-start | bytes 5652480 | tf_op jit(solution)/shard_map/reduce_scatter | solution.py:1999
  344.9 68.0 %copy-start.2 = (f32[1024,512]{1,0:T(8,128)S(1)}, f32[1024,512]{1,0:T(8,128)}, u32[]{:S(2)}) copy-start(f32[1024,512]{1,0:T(8,128)} %copy-done.1) | copy-start | bytes 6291460
  344.9 68.0 %copy-start.5 = (f32[1024,400]{1,0:T(8,128)S(1)}, f32[1024,400]{1,0:T(8,128)}, u32[]{:S(2)}) copy-start(f32[1024,400]{1,0:T(8,128)} %copy-done.4) | copy-start | bytes 4915204
  344.9 68.0 %copy-start.37 = (f32[1,400]{1,0:T(1,128)S(1)}, f32[1,400]{1,0:T(1,128)}, u32[]{:S(2)}) copy-start(f32[1,400]{1,0:T(1,128)} %copy-done.36) | copy-start | bytes 4804
  412.9 5.5 copy-start.23
  429.1 147.4 %reduce-scatter.8.cloned.1.call-start = ((), (), s32[]{:S(2)}) async-start(), calls=%async_computation.6 | async-start | bytes 2211840 | tf_op jit(solution)/shard_map/reduce_scatter | solution.py:1999
  436.4 44.0 %copy-start.17 = (f32[1024,400]{1,0:T(8,128)S(1)}, f32[1024,400]{1,0:T(8,128)}, u32[]{:S(2)}) copy-start(f32[1024,400]{1,0:T(8,128)} %get-tuple-element.266) | copy-start | bytes 4915204
  483.2 9.7 %copy-start.10 = (bf16[1024,400]{1,0:T(8,128)(2,1)}, bf16[1024,400]{1,0:T(8,128)(2,1)S(1)}, u32[]{:S(2)}) copy-start(bf16[1024,400]{1,0:T(8,128)(2,1)S(1)} %get-tuple-element.216.refs_3_) | copy-start | bytes 2457604
  490.5 17.0 %copy-start.11 = (f32[1024,400]{1,0:T(8,128)S(1)}, f32[1024,400]{1,0:T(8,128)}, u32[]{:S(2)}) copy-start(f32[1024,400]{1,0:T(8,128)} %get-tuple-element.214) | copy-start | bytes 4915204
  490.5 17.0 %copy-start.47 = (f32[1,400]{1,0:T(1,128)S(1)}, f32[1,400]{1,0:T(1,128)}, u32[]{:S(2)}) copy-start(f32[1,400]{1,0:T(1,128)} %copy-done.46) | copy-start | bytes 4804
  507.5 3.6 copy-start.7
  507.5 3.6 copy-start.39
  507.5 3.6 copy-start.41
  507.5 3.6 copy-start.43
  507.5 3.6 copy-start.45
  515.4 7.6 %copy-start.55 = (f32[128]{0:T(128)S(1)}, f32[128]{0:T(128)}, u32[]{:S(2)}) copy-start(f32[128]{0:T(128)} %get-tuple-element.230) | copy-start | bytes 1540
  524.3 3.3 copy-start.35
  524.3 3.3 copy-start.48
  524.3 3.3 copy-start.50
  524.4 3.3 copy-start.51
  528.3 39.2 %copy-start.32 = (f32[1600]{0:T(1024)S(1)}, f32[1600]{0:T(1024)}, u32[]{:S(2)}) copy-start(f32[1600]{0:T(1024)} %param.24) | copy-start | bytes 19204
  528.3 40.7 %copy-start.14 = (f32[128,1600]{1,0:T(8,128)S(1)}, f32[128,1600]{1,0:T(8,128)}, u32[]{:S(2)}) copy-start(f32[128,1600]{1,0:T(8,128)} %get-tuple-element.218) | copy-start | bytes 2457604
  570.6 3.8 copy-start.19
  571.8 4.1 copy-start.52
  608.5 9.6 %copy-start.27 = (f32[400,200]{1,0:T(8,128)S(1)}, f32[400,200]{1,0:T(8,128)}, u32[]{:S(2)}) copy-start(f32[400,200]{1,0:T(8,128)} %get-tuple-element.302) | copy-start | bytes 960004
  615.2 3.6 copy-start.26
  615.2 4.4 copy-start.18
  (13 other events, 30.1 us)
Sparse Core Ops, SparseCore 0:
  89.8 86.0 all-gather.5
  177.5 84.3 all-gather.3
  317.2 119.1 reduce-scatter.3
  438.6 82.5 reduce-scatter.5
  523.5 45.0 reduce-scatter.7
